TPU v7x, 32 devices: a whole 2x2x4 slice. The times are simulated.
32 devices in a mesh: dp: 2 (over x), expert: 16 (over z, y, core).
Axes of the slice: x: 2, y: 2, z: 4, core: 2. Of those that a mesh axis runs over, the one named last changes fastest.
Arguments:
- queries: bfloat16 [2048, 2048], P('expert', 'dp'), may hold values from -160 to 160
- kv_pool: bfloat16 [2, 128, 64, 2048], P(None, 'expert', None, 'dp'), may hold values from -6 to 6
- page_table: int32 [32, 4], P('expert'), may hold values from 0 to 127, as said below
- ctx_lens: int32 [2048], P('expert'), may hold values from 2 to 256, as said below
- w_out: bfloat16 [2048, 2048], P('dp', 'expert'), may hold values from -0.59765625 to 0.59765625
- residual: bfloat16 [2048, 2048], P(('expert', 'dp')), may hold values from -3 to 3
- moe_gain: float32 [2048], replicated, may hold values from 0.25 to 1.75
- expert_ids: int32 [2048, 6], P(('expert', 'dp')), may hold values from 0 to 15, all different within a row; in each aligned block of 64 rows (0 to 63, 64 to 127, ...) at most 48 rows name the same one
- route_weights: float32 [2048, 6], P(('expert', 'dp')), may hold values from 0.05 to 0.4
- w_gate: bfloat16 [16, 2048, 1408], P('expert', 'dp'), may hold values from -0.125 to 0.125
- w_up: bfloat16 [16, 2048, 1408], P('expert', 'dp'), may hold values from -0.125 to 0.125
- w_down: bfloat16 [16, 1408, 2048], P('expert', 'dp'), may hold values from -0.15625 to 0.15625
- final_gain: float32 [2048], replicated, may hold values from 0.25 to 1.75
Outputs:
- layer_out: bfloat16 [2048, 2048], P(('expert', 'dp'))
Inputs may be any that keep to these rules, and one draw needn't show every extreme that they name: `page_table`: the 4 pages of sequence s are distinct pages of group s // 2, which owns pages g * 8 to g * 8 + 7; every page belongs to exactly one sequence. `ctx_lens`: the first row of every sequence reads all 256 positions. `expert_ids`: each row names 6 distinct experts; among the 64 rows of one device (aligned blocks of 64 rows) no expert is named more than 48 times.
All inputs are finite; a program needn't handle non-finite values.
Results may differ from a plain program's by a relative error of at most 0.017.
Values may be sent and summed in bfloat16 or wider, within the bound.
No kernel may reach another device: no remote copies, remote signals or barrier semaphores. Data moves between devices by JAX's collectives and lax.ppermute only.
A program may use at most 128 MiB of HBM per device.

v0:
```python
import math

import jax
import jax.numpy as jnp
from jax import lax
from jax.sharding import PartitionSpec as P

HD = 128
TOP = 6
CTX = 256


def normalize(values, gain):
    mean_sq = jnp.mean(values * values, axis=-1, keepdims=True)
    return values * lax.rsqrt(mean_sq + 1e-06) * gain


def fetch_experts(w_gate, w_up, w_down):
    return (
        lax.all_gather(w_gate, "dp", axis=1, tiled=True),
        lax.all_gather(w_up, "dp", axis=1, tiled=True),
        lax.all_gather(w_down, "dp", axis=1, tiled=True),
    )


def shards(
    queries,
    kv_pool,
    page_table,
    ctx_lens,
    w_out,
    residual,
    moe_gain,
    expert_ids,
    route_weights,
    w_gate,
    w_up,
    w_down,
    final_gain,
):
    replicas = None
    scale = 1.0 / math.sqrt(HD)
    group_rows = queries.shape[0]
    local_feats = queries.shape[1]
    local_heads = local_feats // HD
    seq_count = page_table.shape[0]
    seq_rows = group_rows // seq_count
    pool_here = kv_pool.shape[1]
    local_pages = page_table - lax.axis_index("expert") * pool_here
    keys = kv_pool[0][local_pages].reshape(seq_count, CTX, local_heads, HD)
    values = kv_pool[1][local_pages].reshape(seq_count, CTX, local_heads, HD)
    asked = queries.reshape(seq_count, seq_rows, local_heads, HD)
    scores = jnp.einsum("sqhd,skhd->shqk", asked, keys, preferred_element_type=jnp.float32) * scale
    lengths = ctx_lens.reshape(seq_count, seq_rows)
    visible = (jnp.arange(CTX, dtype=jnp.int32)[None, None, :] < lengths[:, :, None])[:, None]
    scores = jnp.where(visible, scores, -1e30)
    top_score = jnp.max(scores, axis=-1, keepdims=True)
    expo = jnp.where(visible, jnp.exp(scores - top_score), 0.0)
    probs = (expo / jnp.sum(expo, axis=-1, keepdims=True)).astype(jnp.bfloat16)
    mixed = jnp.einsum("shqk,skhd->sqhd", probs, values, preferred_element_type=jnp.float32)
    context = mixed.astype(jnp.bfloat16).reshape(group_rows, local_feats)
    columns = lax.all_gather(w_out, "expert", axis=1, tiled=True)
    projected = lax.psum_scatter(
        jnp.dot(context, columns, preferred_element_type=jnp.float32).astype(jnp.bfloat16),
        "dp",
        scatter_dimension=0,
        tiled=True,
    ).astype(jnp.float32)
    hidden_state = residual.astype(jnp.float32) + projected
    moe_input = normalize(hidden_state, moe_gain).astype(jnp.bfloat16)
    rows_here = moe_input.shape[0]
    experts = lax.axis_size("expert")
    slots = max(2, min(rows_here, 2 * rows_here * TOP // experts))
    flat_ids = expert_ids.reshape(-1)
    marks = (flat_ids[:, None] == jnp.arange(experts, dtype=jnp.int32)[None, :]).astype(jnp.int32)
    before = jnp.sum((jnp.cumsum(marks, axis=0) - 1) * marks, axis=1)
    target = (flat_ids * slots + before).reshape(rows_here, TOP)
    placing = jnp.any(
        jnp.arange(experts * slots, dtype=jnp.int32)[:, None, None] == target[None], axis=-1
    )
    outbound = jnp.dot(placing.astype(jnp.bfloat16), moe_input, preferred_element_type=jnp.float32)
    outbound = outbound.astype(jnp.bfloat16).reshape(experts, slots, moe_input.shape[1])
    replicas = fetch_experts(w_gate, w_up, w_down)
    gate_full, up_full, down_full = replicas
    arrived = lax.all_to_all(outbound, "expert", split_axis=0, concat_axis=0, tiled=True)
    flat = arrived.reshape(-1, arrived.shape[2])
    gate = jnp.dot(flat, gate_full[0], preferred_element_type=jnp.float32)
    up_part = jnp.dot(flat, up_full[0], preferred_element_type=jnp.float32)
    expert_mid = (jax.nn.silu(gate) * up_part).astype(jnp.bfloat16)
    done = jnp.dot(expert_mid, down_full[0], preferred_element_type=jnp.float32).astype(
        jnp.bfloat16
    )
    done = done.reshape(arrived.shape[0], arrived.shape[1], arrived.shape[2])
    returned = lax.all_to_all(done, "expert", split_axis=0, concat_axis=0, tiled=True)
    answers = returned.reshape(experts * slots, returned.shape[2])[target]
    moe = jnp.sum(route_weights[:, :, None] * answers.astype(jnp.float32), axis=1)
    combined = hidden_state + moe
    return normalize(combined, final_gain).astype(jnp.bfloat16)


def solution(mesh):
    return jax.shard_map(
        shards,
        mesh=mesh,
        in_specs=(
            P("expert", "dp"),
            P(None, "expert", None, "dp"),
            P("expert", None),
            P("expert"),
            P("dp", "expert"),
            P(("expert", "dp"), None),
            P(),
            P(("expert", "dp"), None),
            P(("expert", "dp"), None),
            P("expert", "dp", None),
            P("expert", "dp", None),
            P("expert", "dp", None),
            P(),
        ),
        out_specs=P(("expert", "dp"), None),
        check_vma=False,
    )
```

profile of v0, /device:TPU:13, one launch (start us, length us, event | category | flops | bytes accessed | tf_op | source)
XLA Modules:
  0.0 420.9 jit_solution(1505002363644902309)
XLA Ops:
  6.5 0.7 all-gather.5.cloned.1.call-update
  7.3 0.7 compare_select_fusion.1
  8.1 1.8 slice_bitcast_fusion
  9.9 0.6 gather_fusion.1
  10.6 0.3 copy.51
  10.9 0.8 copy.52
  11.7 0.6 gather_fusion
  12.3 0.3 copy.53
  12.7 1.6 fusion.34
  14.3 1.6 fusion.18
  16.1 45.5 %all-gather.5.cloned.1.call-done = bf16[1024,2048]{1,0:T(8,128)(2,1)} async-done(((bf16[1024,128]{1,0:T(8,128)(2,1)}), bf16[1024,2048]{1,0:T(8,128)(2,1)}) %all-gather.5.cloned.1.call-update) | async-done | bytes 4194320 | tf_op jit(solution)/shard_map/all_gather | solution.py:62
  61.6 3.7 convolution_convert_fusion.1
  65.4 0.7 all-gather.9.cloned.1.call-update
  66.1 0.5 all-gather.11.cloned.1.call-update
  67.0 0.9 reduce-window.6
  68.7 11.7 %reduce-scatter.2.cloned.1.call-done = bf16[64,2048]{1,0:T(8,128)(2,1)} async-done(((bf16[128,2048]{1,0:T(8,128)(2,1)}), bf16[64,2048]{1,0:T(8,128)(2,1)}) %reduce-scatter.2.cloned.1.call-update) | async-done | bytes 262160 | tf_op jit(solution)/shard_map/reduce_scatter | solution.py:63
  80.5 1.1 multiply_reduce_fusion.2
  81.6 3.6 convolution_convert_fusion
  85.3 6.4 %all-to-all-start = ((bf16[16,48,2048]{2,1,0:T(8,128)(2,1)}), bf16[16,48,2048]{2,1,0:T(8,128)(2,1)S(1)}, u32[]{:S(2)}, u32[]{:S(2)}) async-start(bf16[16,48,2048]{2,1,0:T(8,128)(2,1)} %bitcast.5), calls=%async_computation.1 | async-start | bytes 6291456 | tf_op jit(solution)/shard_map/all_to_all | solution.py:85
  91.9 0.4 all-gather.7.cloned.1.call-update
  92.2 64.4 %all-gather.9.cloned.1.call-done = bf16[1,2048,1408]{2,1,0:T(8,128)(2,1)} async-done(((bf16[1,1024,1408]{2,1,0:T(8,128)(2,1)}), bf16[1,2048,1408]{2,1,0:T(8,128)(2,1)}) %all-gather.9.cloned.1.call-update) | async-done | bytes 5767184 | tf_op jit(solution)/shard_map/all_gather | solution.py:21
  156.6 4.9 %all-to-all-done = bf16[16,48,2048]{2,1,0:T(8,128)(2,1)S(1)} async-done(((bf16[16,48,2048]{2,1,0:T(8,128)(2,1)}), bf16[16,48,2048]{2,1,0:T(8,128)(2,1)S(1)}, u32[]{:S(2)}, u32[]{:S(2)}) %all-to-all-start) | async-done | bytes 3145760 | tf_op jit(solution)/shard_map/all_to_all | solution.py:85
  161.6 9.2 %fusion.3 = f32[768,1408]{1,0:T(8,128)} fusion(bf16[768,2048]{1,0:T(8,128)(2,1)S(1)} %bitcast.70, bf16[1,2048,1408]{2,1,0:T(8,128)(2,1)} %all-gather.9.cloned.1.call-done), kind=kOutput, calls=%fused_computation.6 | convolution fusion | flops 4429185024 | bytes 13238272 | tf_op jit(solution)/shard_map/dot_general | solution.py:88
  170.7 61.9 %all-gather.11.cloned.1.call-done = bf16[1,1408,2048]{2,1,0:T(8,128)(2,1)} async-done(((bf16[1,704,2048]{2,1,0:T(8,128)(2,1)}), bf16[1,1408,2048]{2,1,0:T(8,128)(2,1)}) %all-gather.11.cloned.1.call-update) | async-done | bytes 5767184 | tf_op jit(solution)/shard_map/all_gather | solution.py:22
  232.6 76.0 %all-gather.7.cloned.1.call-done = bf16[1,2048,1408]{2,1,0:T(8,128)(2,1)} async-done(((bf16[1,1024,1408]{2,1,0:T(8,128)(2,1)}), bf16[1,2048,1408]{2,1,0:T(8,128)(2,1)}) %all-gather.7.cloned.1.call-update) | async-done | bytes 5767184 | tf_op jit(solution)/shard_map/all_gather | solution.py:20
  308.6 17.5 %fusion.9 = bf16[768,2048]{1,0:T(8,128)(2,1)} fusion(bf16[1,1408,2048]{2,1,0:T(8,128)(2,1)} %all-gather.11.cloned.1.call-done, f32[768,1408]{1,0:T(8,128)} %fusion.3, bf16[768,2048]{1,0:T(8,128)(2,1)S(1)} %bitcast.71, bf16[1,2048,1408]{2,1,0:T(8,128)(2,1)} %all-gather.7.cloned.1.call-done), kind=kOutput, calls=%fused_computation.13 | convolution fusion | flops 8866430976 | bytes 22151168 | tf_op jit(solution)/shard_map/dot_general | solution.py:90
  326.1 6.5 %all-to-all-start.1 = ((bf16[16,48,2048]{2,1,0:T(8,128)(2,1)}), bf16[16,48,2048]{2,1,0:T(8,128)(2,1)S(1)}, u32[]{:S(2)}, u32[]{:S(2)}) async-start(bf16[16,48,2048]{2,1,0:T(8,128)(2,1)} %bitcast.72), calls=%async_computation.2 | async-start | bytes 6291456 | tf_op jit(solution)/shard_map/all_to_all | solution.py:94
  332.9 69.5 %all-to-all-done.1 = bf16[16,48,2048]{2,1,0:T(8,128)(2,1)S(1)} async-done(((bf16[16,48,2048]{2,1,0:T(8,128)(2,1)}), bf16[16,48,2048]{2,1,0:T(8,128)(2,1)S(1)}, u32[]{:S(2)}, u32[]{:S(2)}) %all-to-all-start.1) | async-done | bytes 3145760 | tf_op jit(solution)/shard_map/all_to_all | solution.py:94
  402.5 3.1 gather_fusion.2
  405.6 3.9 reshape.118
  409.5 3.7 multiply_reduce_fusion
  413.5 0.8 multiply_convert_fusion.1
  (47 shorter events, 2.6 us)
Async XLA Ops:
  6.5 55.0 %all-gather.5.cloned.1.call-start = ((), (), s32[]{:S(2)}) async-start(), calls=%async_computation.3 | async-start | bytes 4456448 | tf_op jit(solution)/shard_map/all_gather | solution.py:62
  7.3 73.2 %reduce-scatter.2.cloned.1.call-start = ((), (), s32[]{:S(2)}) async-start(), calls=%async_computation.4 | async-start | bytes 786432 | tf_op jit(solution)/shard_map/reduce_scatter | solution.py:63
  8.1 2.8 copy-start.2
  8.1 3.5 copy-start.8
  11.6 1.1 copy-start.3
  65.3 1.3 copy-start.4
  65.3 15.2 %copy-start = (bf16[64,2048]{1,0:T(8,128)(2,1)S(1)}, bf16[64,2048]{1,0:T(8,128)(2,1)}, u32[]{:S(2)}) copy-start(bf16[64,2048]{1,0:T(8,128)(2,1)} %param.18) | copy-start | bytes 786436
  65.3 16.3 %copy-start.5 = (f32[2048]{0:T(1024)S(1)}, f32[2048]{0:T(1024)}, u32[]{:S(2)}) copy-start(f32[2048]{0:T(1024)} %param.19) | copy-start | bytes 24580
  65.3 91.3 %all-gather.9.cloned.1.call-start = ((), (), s32[]{:S(2)}) async-start(), calls=%async_computation.6 | async-start | bytes 8650752 | tf_op jit(solution)/shard_map/all_gather | solution.py:21
  66.0 166.5 %all-gather.11.cloned.1.call-start = ((), (), s32[]{:S(2)}) async-start(), calls=%async_computation.7 | async-start | bytes 8650752 | tf_op jit(solution)/shard_map/all_gather | solution.py:22
  85.3 76.3 %all-to-all-start = ((bf16[16,48,2048]{2,1,0:T(8,128)(2,1)}), bf16[16,48,2048]{2,1,0:T(8,128)(2,1)S(1)}, u32[]{:S(2)}, u32[]{:S(2)}) async-start(bf16[16,48,2048]{2,1,0:T(8,128)(2,1)} %bitcast.5), calls=%async_computation.1 | async-start | bytes 6291456 | tf_op jit(solution)/shard_map/all_to_all | solution.py:85
  91.7 216.9 %all-gather.7.cloned.1.call-start = ((), (), s32[]{:S(2)}) async-start(), calls=%async_computation.5 | async-start | bytes 8650752 | tf_op jit(solution)/shard_map/all_gather | solution.py:20
  326.1 6.7 %copy-start.7 = (f32[64,6]{0,1:T(8,128)S(1)}, f32[64,6]{0,1:T(8,128)}, u32[]{:S(2)}) copy-start(f32[64,6]{0,1:T(8,128)} %param.21) | copy-start | bytes 4612
  326.1 76.4 %all-to-all-start.1 = ((bf16[16,48,2048]{2,1,0:T(8,128)(2,1)}), bf16[16,48,2048]{2,1,0:T(8,128)(2,1)S(1)}, u32[]{:S(2)}, u32[]{:S(2)}) async-start(bf16[16,48,2048]{2,1,0:T(8,128)(2,1)} %bitcast.72), calls=%async_computation.2 | async-start | bytes 6291456 | tf_op jit(solution)/shard_map/all_to_all | solution.py:94
  405.6 7.7 %copy-start.1 = (bf16[64,2048]{1,0:T(8,128)(2,1)S(1)}, bf16[64,2048]{1,0:T(8,128)(2,1)}, u32[]{:S(2)}) copy-start(bf16[64,2048]{1,0:T(8,128)(2,1)} %reduce-scatter.2.cloned.1.call-done) | copy-start | bytes 786436
  409.5 4.0 copy-start.6
Sparse Core Ops, SparseCore 0:
  9.5 52.0 all-gather.4
  65.4 14.9 reduce-scatter.1
  82.1 74.4 all-gather.8
  158.1 74.4 all-gather.10
  234.0 74.4 all-gather.6
where the time goes:
time: 421 us
  waiting for transfers between devices  336 us (80%)
  matrix products  37.2 us (9%)
  between operations  13.3 us (3%)
  starting transfers between devices  13.2 us (3%)
  local copies, waits for them, and re-layouts  12.9 us (3%)
  other arithmetic  7.99 us (2%)
    all_gather x1, waiting for transfers between devices, fetch_experts(): lax.all_gather(w_gate, 'dp', axis=1, tiled=True)  76 us
    all_to_all x1, waiting for transfers between devices, shards(): lax.all_to_all(done, 'expert', split_axis=0, concat_axis=0, tiled=True)  69.5 us
    all_gather x1, waiting for transfers between devices, fetch_experts(): lax.all_gather(w_up, 'dp', axis=1, tiled=True)  64.4 us
    all_gather x1, waiting for transfers between devices, fetch_experts(): lax.all_gather(w_down, 'dp', axis=1, tiled=True)  61.9 us
    all_gather x1, waiting for transfers between devices, shards(): columns = lax.all_gather(w_out, 'expert', axis=1, tiled=True)  45.5 us
    dot_general x1, matrix products, shards(): jnp.dot(expert_mid, down_full[0], preferred_element_type=jnp.float32)  17.5 us
    reduce_scatter x1, waiting for transfers between devices, shards(): lax.psum_scatter(jnp.dot(context, columns, preferred_element_type=jnp.flo...  11.7 us
    dot_general x1, matrix products, shards(): up_part = jnp.dot(flat, up_full[0], preferred_element_type=jnp.float32)  9.18 us
  transfers between devices with their start and end apart: 7, of which 7 were waited for; matrix products, arithmetic and copies ran while one was open for 6% of the time, Pallas kernels for 0%

commit v1 on v0

--- a/solution.py
+++ b/solution.py
@@ -1,13 +1,17 @@
+import functools
 import math
 
 import jax
 import jax.numpy as jnp
 from jax import lax
+from jax.experimental import pallas as pl
+from jax.experimental.pallas import tpu as pltpu
 from jax.sharding import PartitionSpec as P
 
 HD = 128
 TOP = 6
 CTX = 256
+MIB = 1024 * 1024
 
 
 def normalize(values, gain):
@@ -15,30 +19,7 @@
     return values * lax.rsqrt(mean_sq + 1e-06) * gain
 
 
-def fetch_experts(w_gate, w_up, w_down):
-    return (
-        lax.all_gather(w_gate, "dp", axis=1, tiled=True),
-        lax.all_gather(w_up, "dp", axis=1, tiled=True),
-        lax.all_gather(w_down, "dp", axis=1, tiled=True),
-    )
-
-
-def shards(
-    queries,
-    kv_pool,
-    page_table,
-    ctx_lens,
-    w_out,
-    residual,
-    moe_gain,
-    expert_ids,
-    route_weights,
-    w_gate,
-    w_up,
-    w_down,
-    final_gain,
-):
-    replicas = None
+def attend(queries, kv_pool, page_table, ctx_lens):
     scale = 1.0 / math.sqrt(HD)
     group_rows = queries.shape[0]
     local_feats = queries.shape[1]
@@ -58,7 +39,25 @@
     expo = jnp.where(visible, jnp.exp(scores - top_score), 0.0)
     probs = (expo / jnp.sum(expo, axis=-1, keepdims=True)).astype(jnp.bfloat16)
     mixed = jnp.einsum("shqk,skhd->sqhd", probs, values, preferred_element_type=jnp.float32)
-    context = mixed.astype(jnp.bfloat16).reshape(group_rows, local_feats)
+    return mixed.astype(jnp.bfloat16).reshape(group_rows, local_feats)
+
+
+def dispatched(
+    queries,
+    kv_pool,
+    page_table,
+    ctx_lens,
+    w_out,
+    residual,
+    moe_gain,
+    expert_ids,
+    route_weights,
+    w_gate,
+    w_up,
+    w_down,
+    final_gain,
+):
+    context = attend(queries, kv_pool, page_table, ctx_lens)
     columns = lax.all_gather(w_out, "expert", axis=1, tiled=True)
     projected = lax.psum_scatter(
         jnp.dot(context, columns, preferred_element_type=jnp.float32).astype(jnp.bfloat16),
@@ -80,8 +79,9 @@
     )
     outbound = jnp.dot(placing.astype(jnp.bfloat16), moe_input, preferred_element_type=jnp.float32)
     outbound = outbound.astype(jnp.bfloat16).reshape(experts, slots, moe_input.shape[1])
-    replicas = fetch_experts(w_gate, w_up, w_down)
-    gate_full, up_full, down_full = replicas
+    gate_full = lax.all_gather(w_gate, "dp", axis=1, tiled=True)
+    up_full = lax.all_gather(w_up, "dp", axis=1, tiled=True)
+    down_full = lax.all_gather(w_down, "dp", axis=1, tiled=True)
     arrived = lax.all_to_all(outbound, "expert", split_axis=0, concat_axis=0, tiled=True)
     flat = arrived.reshape(-1, arrived.shape[2])
     gate = jnp.dot(flat, gate_full[0], preferred_element_type=jnp.float32)
@@ -98,9 +98,327 @@
     return normalize(combined, final_gain).astype(jnp.bfloat16)
 
 
+def place(z, y, c):
+    return (z * 2 + y) * 2 + c
+
+
+def shift_z(values, depth, step):
+    pairs = [
+        (place((z + step) % depth, y, c), place(z, y, c))
+        for z in range(depth)
+        for y in range(2)
+        for c in range(2)
+    ]
+    return lax.ppermute(values, "expert", pairs)
+
+
+def flip_y(values, depth):
+    pairs = [
+        (place(z, 1 - y, c), place(z, y, c))
+        for z in range(depth)
+        for y in range(2)
+        for c in range(2)
+    ]
+    return lax.ppermute(values, "expert", pairs)
+
+
+def flip_core(values, depth):
+    pairs = [
+        (place(z, y, 1 - c), place(z, y, c))
+        for z in range(depth)
+        for y in range(2)
+        for c in range(2)
+    ]
+    return lax.ppermute(values, "expert", pairs)
+
+
+def flip_x(values):
+    return lax.ppermute(values, "dp", [(0, 1), (1, 0)])
+
+
+def project_kernel(depth, ctx_ref, *refs):
+    pieces, (own_ref, send_ref) = refs[:-2], refs[-2:]
+    half = own_ref.shape[0]
+    width = pieces[0].shape[2]
+    chunk = pieces[0].shape[1]
+    me = lax.axis_index("expert")
+    x = lax.axis_index("dp")
+    c = lax.rem(me, 2)
+    y = lax.rem(lax.div(me, 2), 2)
+    z = lax.div(me, 4)
+    mine = ctx_ref[pl.ds(pl.multiple_of(x * half, half), half), :]
+    theirs = ctx_ref[pl.ds(pl.multiple_of((1 - x) * half, half), half), :]
+    rows = jnp.concatenate([mine, theirs], axis=0)
+    for piece in range(4):
+        flips = ((0, 0), (1, 0), (0, 1), (1, 1))[piece]
+        at_y = y if flips[0] == 0 else 1 - y
+        at_c = c if flips[1] == 0 else 1 - c
+        for r in range(depth):
+            total = None
+            for k in range(2):
+                part = jnp.dot(
+                    rows[:, k * chunk : (k + 1) * chunk],
+                    pieces[2 * piece + k][r],
+                    preferred_element_type=jnp.float32,
+                )
+                total = part if total is None else total + part
+            index = (lax.rem(z + r, depth) * 2 + at_y) * 2 + at_c
+            columns = pl.ds(pl.multiple_of(index * width, width), width)
+            own_ref[:, columns] = total[:half]
+            send_ref[:, columns] = total[half:].astype(send_ref.dtype)
+
+
+def project(context, pieces, depth):
+    rows, feats = context.shape
+    width = pieces[0].shape[2]
+    columns = width * 4 * depth
+    return pl.pallas_call(
+        functools.partial(project_kernel, depth),
+        out_shape=(
+            jax.ShapeDtypeStruct((rows // 2, columns), jnp.float32),
+            jax.ShapeDtypeStruct((rows // 2, columns), jnp.bfloat16),
+        ),
+        compiler_params=pltpu.CompilerParams(vmem_limit_bytes=24 * MIB),
+        cost_estimate=pl.CostEstimate(
+            flops=2 * rows * feats * columns,
+            bytes_accessed=2 * feats * columns + 4 * rows * columns,
+            transcendentals=0,
+        ),
+        name="project",
+    )(context, *pieces)
+
+
+def experts_kernel(
+    tile, out_tile, a8, ya, b8, xb, share, *refs
+):
+    weights, refs = refs[:10], refs[10:]
+    outs, (rows, gate, up, down, mid, row_sem, weight_sem, down_sem) = refs[:4], refs[4:]
+    x = lax.axis_index("dp")
+    feats = rows.shape[1]
+    half = feats // 2
+    width = gate.shape[2]
+    tiles = width // tile
+    part = a8.shape[0]
+    near = pl.ds(pl.multiple_of(x * half, half), half)
+    far = pl.ds(pl.multiple_of((1 - x) * half, half), half)
+
+    row_copies = []
+    for i, piece in enumerate((a8, ya, b8, xb)):
+        for s, lanes in enumerate((near, far)):
+            copy = pltpu.make_async_copy(
+                piece.at[:, lanes],
+                rows.at[pl.ds(i * part, part), pl.ds(s * half, half)],
+                row_sem.at[2 * i + s],
+            )
+            copy.start()
+            row_copies.append(copy)
+    weight_copies = []
+    down_copies = []
+    for e in range(2):
+        gate_own, gate_far, up_own, up_far, down_e = weights[5 * e : 5 * e + 5]
+        for j in range(tiles):
+            group = []
+            for n, (source, target, s) in enumerate(
+                (
+                    (gate_own, gate, 0),
+                    (gate_far, gate, 1),
+                    (up_own, up, 0),
+                    (up_far, up, 1),
+                )
+            ):
+                copy = pltpu.make_async_copy(
+                    source.at[:, pl.ds(j * tile, tile)],
+                    target.at[e, pl.ds(s * half, half), pl.ds(j * tile, tile)],
+                    weight_sem.at[(e * tiles + j) * 4 + n],
+                )
+                copy.start()
+                group.append(copy)
+            weight_copies.append(group)
+    for e in range(2):
+        copy = pltpu.make_async_copy(
+            weights[5 * e + 4], down.at[pl.ds(e * width, width), :], down_sem.at[e]
+        )
+        copy.start()
+        down_copies.append(copy)
+
+    for copy in row_copies:
+        copy.wait()
+    for e in range(2):
+        scale = share[:, e : e + 1]
+        for j in range(tiles):
+            for copy in weight_copies[e * tiles + j]:
+                copy.wait()
+            lanes = pl.ds(j * tile, tile)
+            g = jnp.dot(rows[...], gate[e, :, lanes], preferred_element_type=jnp.float32)
+            u = jnp.dot(rows[...], up[e, :, lanes], preferred_element_type=jnp.float32)
+            h = g / (1.0 + jnp.exp(-g)) * u * scale
+            mid[:, pl.ds(e * width + j * tile, tile)] = h.astype(mid.dtype)
+    for copy in down_copies:
+        copy.wait()
+    for n in range(feats // out_tile):
+        lanes = pl.ds(n * out_tile, out_tile)
+        total = jnp.dot(mid[...], down[:, lanes], preferred_element_type=jnp.float32)
+        for i, out in enumerate(outs):
+            out[:, lanes] = total[i * part : (i + 1) * part].astype(out.dtype)
+
+
+def run_experts(pieces, share, weights):
+    part, feats = pieces[0].shape
+    half, width = weights[0].shape
+    total = 4 * part
+    tile = 256
+    any_spec = pl.BlockSpec(memory_space=pl.ANY)
+    vmem_spec = pl.BlockSpec(memory_space=pltpu.VMEM)
+    return pl.pallas_call(
+        functools.partial(experts_kernel, tile, 512),
+        out_shape=tuple(
+            jax.ShapeDtypeStruct((part, feats), kind)
+            for kind in (jnp.float32, jnp.bfloat16, jnp.float32, jnp.bfloat16)
+        ),
+        in_specs=[any_spec] * 4 + [vmem_spec] + [any_spec] * 10,
+        out_specs=(vmem_spec,) * 4,
+        scratch_shapes=[
+            pltpu.VMEM((total, feats), jnp.bfloat16),
+            pltpu.VMEM((2, feats, width), jnp.bfloat16),
+            pltpu.VMEM((2, feats, width), jnp.bfloat16),
+            pltpu.VMEM((2 * width, feats), jnp.bfloat16),
+            pltpu.VMEM((total, 2 * width), jnp.bfloat16),
+            pltpu.SemaphoreType.DMA((8,)),
+            pltpu.SemaphoreType.DMA((8 * (width // tile),)),
+            pltpu.SemaphoreType.DMA((2,)),
+        ],
+        compiler_params=pltpu.CompilerParams(vmem_limit_bytes=40 * MIB),
+        cost_estimate=pl.CostEstimate(
+            flops=2 * total * feats * width * 6,
+            bytes_accessed=12 * feats * width + 12 * total * feats,
+            transcendentals=total * width * 2,
+        ),
+        name="experts",
+    )(*pieces, share, *weights)
+
+
+def gathered(
+    queries,
+    kv_pool,
+    page_table,
+    ctx_lens,
+    w_out,
+    residual,
+    moe_gain,
+    expert_ids,
+    route_weights,
+    w_gate,
+    w_up,
+    w_down,
+    final_gain,
+):
+    experts = lax.axis_size("expert")
+    depth = experts // 4
+    me = lax.axis_index("expert")
+    x = lax.axis_index("dp")
+    c = me % 2
+    y = (me // 2) % 2
+    z = me // 4
+    first = x == 0
+    feats = residual.shape[1]
+    block = residual.shape[0]
+    units = w_gate.shape[2]
+    units_here = w_down.shape[1]
+    width = -(-units_here // 256) * 256
+
+    def halves(weights):
+        low, high = weights[:, :width], weights[:, units - width :]
+        return jnp.where(first, low, high), jnp.where(first, high, low)
+
+    gate_own, gate_sent = halves(w_gate[0])
+    up_own, up_sent = halves(w_up[0])
+    gate_far = flip_x(gate_sent)
+    up_far = flip_x(up_sent)
+    blank = jnp.zeros((width - units_here, feats), w_down.dtype)
+    down_own = jnp.where(
+        first,
+        jnp.concatenate([w_down[0], blank], axis=0),
+        jnp.concatenate([blank, w_down[0]], axis=0),
+    )
+    here = [gate_own, gate_far, up_own, up_far, down_own]
+    weights = here + [flip_core(array, depth) for array in here]
+
+    near, across, near_core, across_core = [], [], [], []
+    chunk = w_out.shape[0] // 2
+    for k in range(2):
+        own = w_out[k * chunk : (k + 1) * chunk]
+        line = jnp.stack([own] + [shift_z(own, depth, s) for s in range(1, depth)])
+        near.append(line)
+        near_core.append(flip_core(line, depth))
+        other = flip_y(line, depth)
+        across.append(other)
+        across_core.append(flip_core(other, depth))
+
+    named = expert_ids[:, :, None] == jnp.arange(experts, dtype=jnp.int32)[None, None, :]
+    share = jnp.sum(jnp.where(named, route_weights[:, :, None], 0.0), axis=1)
+    share = lax.all_gather(share, ("expert", "dp"), axis=0, tiled=True)
+    both = jnp.stack([me, me + 1 - 2 * c])
+    pick = (jnp.arange(experts, dtype=jnp.int32)[:, None] == both[None, :]).astype(jnp.float32)
+    share = jnp.dot(share, pick, precision=lax.Precision.HIGHEST)
+    share = share.reshape(experts * 2, 2, 2, block // 4, 2)
+    line_z = (z + jnp.arange(depth, dtype=jnp.int32)) % depth
+
+    def blocks(dx, dy):
+        at_x = x if dx == 0 else 1 - x
+        at_y = y if dy == 0 else 1 - y
+        return place(line_z, at_y, c) * 2 + at_x
+
+    order_a = jnp.concatenate([blocks(0, 0), blocks(1, 0), blocks(0, 1), blocks(1, 1)])
+    order_b = jnp.concatenate([blocks(0, 0), blocks(0, 1), blocks(1, 0), blocks(1, 1)])
+    share_a = jnp.take(share[:, :, 0], order_a, axis=0)
+    share_b = jnp.take(share[:, :, 1], order_b, axis=0)
+
+    context = attend(queries, kv_pool, page_table, ctx_lens)
+    own, sent = project(context, near + across + near_core + across_core, depth)
+    projected = own + flip_x(sent).astype(jnp.float32)
+    hidden_state = residual.astype(jnp.float32) + projected
+    moe_input = normalize(hidden_state, moe_gain).astype(jnp.bfloat16)
+
+    quarter = block // 4
+    part = depth * quarter
+    moe = []
+    for k in range(2):
+        mine = moe_input[2 * quarter * k : 2 * quarter * (k + 1)]
+        line = jnp.stack([mine] + [shift_z(mine, depth, s) for s in range(1, depth)])
+        line_a, line_b = line[:, :quarter], line[:, quarter:]
+        line_a = line_a.reshape(part, feats)
+        line_b = line_b.reshape(part, feats)
+        a8 = jnp.concatenate([line_a, flip_x(line_a)], axis=0)
+        b8 = jnp.concatenate([line_b, flip_y(line_b, depth)], axis=0)
+        ya = flip_y(a8, depth)
+        xb = flip_x(b8)
+        shares = jnp.concatenate(
+            [share_a[:, k].reshape(4 * part, 2), share_b[:, k].reshape(4 * part, 2)], axis=0
+        )
+        out_a, out_ya, out_b, out_xb = run_experts([a8, ya, b8, xb], shares, weights)
+        back_a = flip_y(out_ya, depth).astype(jnp.float32)
+        back_b = flip_x(out_xb).astype(jnp.float32)
+        sum_a = out_a + back_a
+        sum_b = out_b + back_b
+        last_a = flip_x(sum_a[part:].astype(jnp.bfloat16)).astype(jnp.float32)
+        last_b = flip_y(sum_b[part:].astype(jnp.bfloat16), depth).astype(jnp.float32)
+        full_a = (sum_a[:part] + last_a).reshape(depth, quarter, feats)
+        full_b = (sum_b[:part] + last_b).reshape(depth, quarter, feats)
+        full = jnp.concatenate([full_a, full_b], axis=1)
+        total = full[0]
+        for s in range(1, depth):
+            total = total + shift_z(full[s].astype(jnp.bfloat16), depth, depth - s).astype(
+                jnp.float32
+            )
+        moe.append(total)
+    combined = hidden_state + jnp.concatenate(moe, axis=0)
+    return normalize(combined, final_gain).astype(jnp.bfloat16)
+
+
 def solution(mesh):
+    few = mesh.shape["dp"] == 2 and mesh.shape["expert"] == 16
     return jax.shard_map(
-        shards,
+        gathered if few else dispatched,
         mesh=mesh,
         in_specs=(
             P("expert", "dp"),

time: 421 us -> 300 us (0.71)
  the two profiles are of different devices: /device:TPU:13 before, /device:TPU:0 now
where the time goes in v1:
time: 300 us
  waiting for transfers between devices  115 us (38%)
  blocking collectives  67.4 us (22%)
  starting transfers between devices  43.4 us (14%)
  Pallas kernels  29.2 us (10%)
  other arithmetic  22.9 us (8%)
  local copies, waits for them, and re-layouts  17.1 us (6%)
  matrix products  4.55 us (2%)
    all_gather x1, blocking collectives, gathered(): share = lax.all_gather(share, ('expert', 'dp'), axis=0, tiled=True)  67.4 us
    ppermute x11, waiting for transfers between devices, flip_x(): return lax.ppermute(values, 'dp', [(0, 1), (1, 0)])  52.9 us
    ppermute x18, waiting for transfers between devices, shift_z(): return lax.ppermute(values, 'expert', pairs)  31.2 us
    ppermute x10, waiting for transfers between devices, flip_y(): return lax.ppermute(values, 'expert', pairs)  29.9 us
    pallas_call x2, Pallas kernels, run_experts(): pl.pallas_call(functools.partial(experts_kernel, tile, 512), out_shape=tu...  26.1 us
    ppermute x18, starting transfers between devices, shift_z(): return lax.ppermute(values, 'expert', pairs)  23.7 us
    ppermute x11, starting transfers between devices, flip_x(): return lax.ppermute(values, 'dp', [(0, 1), (1, 0)])  11.7 us
    select_n x2, other arithmetic, halves(): return (jnp.where(first, low, high), jnp.where(first, high, low))  7.07 us
  transfers between devices with their start and end apart: 48, of which 18 were waited for; matrix products, arithmetic and copies ran while one was open for 13% of the time, Pallas kernels for 10%

profile of v1, /device:TPU:0, one launch (start us, length us, event | category | flops | bytes accessed | tf_op | source)
XLA Modules:
  0.0 299.9 jit_solution(17951875995682369895)
XLA Ops:
  0.0 1.7 slice_bitcast_fusion.10
  1.7 5.0 %collective-permute-start = (bf16[512,128]{1,0:T(8,128)(2,1)S(1)}, bf16[512,128]{1,0:T(8,128)(2,1)S(1)}, u32[]{:S(2)}, u32[]{:S(2)}) collective-permute-start(bf16[512,128]{1,0:T(8,128)(2,1)S(1)} %get-tuple-element.55), channel_id=1, source_target_pairs={{4,0},{5,1},{6,2},{7,3},{8,4},{9,5},{10,6},{11,7},{12,8},{13,9},{1... | collective-permute-start | bytes 393224 | tf_op jit(solution)/shard_map/ppermute | solution.py:112
  7.8 1.9 collective-permute-start.4
  11.9 2.8 slice_bitcast_fusion
  14.7 1.8 gather_fusion.1
  20.6 67.4 %all-gather = f32[32,64,16]{1,2,0:T(8,128)S(1)} all-gather(f32[1,64,16]{1,2,0:T(8,128)S(1)} %bitcast.148), channel_id=1, replica_groups=mesh['dp'=2,'expert'=16] {'expert','dp'}, dimensions={0}, use_global_device_ids=true | all-gather | bytes 135168 | tf_op jit(solution)/shard_map/all_gather | solution.py:359
  88.3 3.3 %broadcast_select_fusion.2 = (bf16[1024,768]{1,0:T(8,128)(2,1)}, bf16[1024,768]{1,0:T(8,128)(2,1)S(1)}) fusion(pred[]{:T(512)S(6)} %eq.40, bf16[1024,1408]{1,0:T(8,128)(2,1)} %bitcast.126), kind=kLoop, calls=%fused_computation.8 | loop fusion | flops 1572864 | bytes 6291457 | tf_op jit(solution)/shard_map/jit(_where)/select_n | solution.py:331
  91.6 2.4 fusion.32
  94.1 1.9 fusion.6
  98.6 2.7 collective-permute-done.3
  104.6 8.9 %collective-permute-done.6.refs_2_ = bf16[4,512,128]{2,1,0:T(8,128)(2,1)S(1)} collective-permute-done((bf16[4,512,128]{2,1,0:T(8,128)(2,1)S(1)}, bf16[4,512,128]{2,1,0:T(8,128)(2,1)S(1)}, u32[]{:S(2)}, u32[]{:S(2)}) %collective-permute-start.6) | collective-permute-done | bytes 524320 | tf_op jit(solution)/shard_map/ppermute | solution.py:122
  113.4 8.9 %collective-permute-done.7.refs_3_ = bf16[4,512,128]{2,1,0:T(8,128)(2,1)} collective-permute-done((bf16[4,512,128]{2,1,0:T(8,128)(2,1)S(1)}, bf16[4,512,128]{2,1,0:T(8,128)(2,1)}, u32[]{:S(2)}, u32[]{:S(2)}) %collective-permute-start.7) | collective-permute-done | bytes 524320 | tf_op jit(solution)/shard_map/ppermute | solution.py:122
  124.5 3.7 %broadcast_select_fusion = (bf16[1024,768]{1,0:T(8,128)(2,1)}, bf16[1024,768]{1,0:T(8,128)(2,1)}) fusion(pred[]{:T(512)S(6)} %eq.40, bf16[1024,1408]{1,0:T(8,128)(2,1)} %bitcast.127), kind=kLoop, calls=%fused_computation.6 | loop fusion | flops 1572864 | bytes 6291457 | tf_op jit(solution)/shard_map/jit(_where)/select_n | solution.py:331
  128.6 3.1 %project.1 = (f32[64,2048]{1,0:T(8,128)S(1)}, bf16[64,2048]{1,0:T(8,128)(2,1)S(1)}) custom-call(bf16[128,1024]{1,0:T(8,128)(2,1)S(1)} %bitcast.115, bf16[4,512,128]{2,1,0:T(8,128)(2,1)S(1)} %pad_maximum_fusion.2.refs_0_, bf16[4,512,128]{2,1,0:T(8,128)(2,1)S(1)} %pad_maximum_fusion.3.refs_1_, bf16[4,512,128]{2,1,0:T(8,128)(2,1)S(1)} %collective-permute-done.6.refs_2_, ...), custom_call_target="tpu_custom_call" | custom-call | flops 536870912 | bytes 5242880 | tf_op jit(solution)/shard_map/project/pallas_call | solution.py:175
  131.6 1.8 collective-permute-start.12
  133.4 2.4 pad_select_fusion.refs_4_
  135.8 35.0 %collective-permute-done.12 = bf16[64,2048]{1,0:T(8,128)(2,1)S(1)} collective-permute-done((bf16[64,2048]{1,0:T(8,128)(2,1)S(1)}, bf16[64,2048]{1,0:T(8,128)(2,1)S(1)}, u32[]{:S(2)}, u32[]{:S(2)}) %collective-permute-start.12) | collective-permute-done | bytes 262176 | tf_op jit(solution)/shard_map/ppermute | solution.py:136
  172.8 2.6 collective-permute-start.14
  175.4 3.0 %collective-permute-done.13 = bf16[32,2048]{1,0:T(8,128)(2,1)S(1)} collective-permute-done((bf16[32,2048]{1,0:T(8,128)(2,1)S(1)}, bf16[32,2048]{1,0:T(8,128)(2,1)S(1)}, u32[]{:S(2)}, u32[]{:S(2)}) %collective-permute-start.13) | collective-permute-done | bytes 131104 | tf_op jit(solution)/shard_map/ppermute | solution.py:112
  178.5 2.6 collective-permute-start.34
  181.0 7.9 %collective-permute-done.14 = bf16[32,2048]{1,0:T(8,128)(2,1)S(1)} collective-permute-done((bf16[32,2048]{1,0:T(8,128)(2,1)S(1)}, bf16[32,2048]{1,0:T(8,128)(2,1)S(1)}, u32[]{:S(2)}, u32[]{:S(2)}) %collective-permute-start.14) | collective-permute-done | bytes 131104 | tf_op jit(solution)/shard_map/ppermute | solution.py:112
  190.1 7.6 %collective-permute-done.35 = bf16[32,2048]{1,0:T(8,128)(2,1)} collective-permute-done((bf16[32,2048]{1,0:T(8,128)(2,1)}, bf16[32,2048]{1,0:T(8,128)(2,1)}, u32[]{:S(2)}, u32[]{:S(2)}) %collective-permute-start.35) | collective-permute-done | bytes 131104 | tf_op jit(solution)/shard_map/ppermute | solution.py:112
  204.3 6.2 %collective-permute-done.18 = bf16[64,2048]{1,0:T(8,128)(2,1)S(1)} collective-permute-done((bf16[64,2048]{1,0:T(8,128)(2,1)S(1)}, bf16[64,2048]{1,0:T(8,128)(2,1)S(1)}, u32[]{:S(2)}, u32[]{:S(2)}) %collective-permute-start.18) | collective-permute-done | bytes 262176 | tf_op jit(solution)/shard_map/ppermute | solution.py:122
  214.2 3.7 %collective-permute-done.39 = bf16[64,2048]{1,0:T(8,128)(2,1)S(1)} collective-permute-done((bf16[64,2048]{1,0:T(8,128)(2,1)S(1)}, bf16[64,2048]{1,0:T(8,128)(2,1)S(1)}, u32[]{:S(2)}, u32[]{:S(2)}) %collective-permute-start.39) | collective-permute-done | bytes 262176 | tf_op jit(solution)/shard_map/ppermute | solution.py:122
  223.3 7.1 %collective-permute-done.19.xb = bf16[128,2048]{1,0:T(8,128)(2,1)} collective-permute-done((bf16[128,2048]{1,0:T(8,128)(2,1)}, bf16[128,2048]{1,0:T(8,128)(2,1)}, u32[]{:S(2)}, u32[]{:S(2)}) %collective-permute-start.19) | collective-permute-done | bytes 524320 | tf_op jit(solution)/shard_map/ppermute | solution.py:136
  232.5 13.3 %experts.2 = (f32[128,2048]{1,0:T(8,128)S(1)}, bf16[128,2048]{1,0:T(8,128)(2,1)S(1)}, f32[128,2048]{1,0:T(8,128)S(1)}, bf16[128,2048]{1,0:T(8,128)(2,1)S(1)}) custom-call(bf16[128,2048]{1,0:T(8,128)(2,1)} %pad_maximum_fusion.5.a8, bf16[128,2048]{1,0:T(8,128)(2,1)} %collective-permute-done.17.ya, bf16[128,2048]{1,0:T(8,128)(2,1)} %pad_maximum_fusion.6.b8, ...), custom_call_target="tpu_custom_call" | custom-call | flops 9663676416 | bytes 31457280 | tf_op jit(solution)/shard_map/experts/pallas_call | solution.py:272
  247.8 12.8 %experts.3 = (f32[128,2048]{1,0:T(8,128)S(1)}, bf16[128,2048]{1,0:T(8,128)(2,1)S(1)}, f32[128,2048]{1,0:T(8,128)S(1)}, bf16[128,2048]{1,0:T(8,128)(2,1)S(1)}) custom-call(bf16[128,2048]{1,0:T(8,128)(2,1)S(1)} %pad_maximum_fusion.8.a8, bf16[128,2048]{1,0:T(8,128)(2,1)S(1)} %collective-permute-done.38.ya, bf16[128,2048]{1,0:T(8,128)(2,1)S(1)} %pad_maximum_fusion.9.b8, ...), custom_call_target="tpu_custom_call" | custom-call | flops 9663676416 | bytes 31457280 | tf_op jit(solution)/shard_map/experts/pallas_call | solution.py:272
  265.2 10.4 %collective-permute-done.43 = bf16[128,2048]{1,0:T(8,128)(2,1)S(1)} collective-permute-done((bf16[128,2048]{1,0:T(8,128)(2,1)S(1)}, bf16[128,2048]{1,0:T(8,128)(2,1)S(1)}, u32[]{:S(2)}, u32[]{:S(2)}) %collective-permute-start.43) | collective-permute-done | bytes 524320 | tf_op jit(solution)/shard_map/ppermute | solution.py:136
  278.1 2.2 collective-permute-done.30
  280.5 2.1 collective-permute-start.31
  289.8 5.1 %collective-permute-done.32 = bf16[32,2048]{1,0:T(8,128)(2,1)S(1)} collective-permute-done((bf16[32,2048]{1,0:T(8,128)(2,1)S(1)}, bf16[32,2048]{1,0:T(8,128)(2,1)S(1)}, u32[]{:S(2)}, u32[]{:S(2)}) %collective-permute-start.32) | collective-permute-done | bytes 131104 | tf_op jit(solution)/shard_map/ppermute | solution.py:112
  295.0 3.9 %collective-permute-done.46 = bf16[32,2048]{1,0:T(8,128)(2,1)S(1)} collective-permute-done((bf16[32,2048]{1,0:T(8,128)(2,1)S(1)}, bf16[32,2048]{1,0:T(8,128)(2,1)S(1)}, u32[]{:S(2)}, u32[]{:S(2)}) %collective-permute-start.46) | collective-permute-done | bytes 131104 | tf_op jit(solution)/shard_map/ppermute | solution.py:112
  (199 shorter events, 54.1 us)
Async XLA Ops:
  1.7 94.5 %collective-permute-start = (bf16[512,128]{1,0:T(8,128)(2,1)S(1)}, bf16[512,128]{1,0:T(8,128)(2,1)S(1)}, u32[]{:S(2)}, u32[]{:S(2)}) collective-permute-start(bf16[512,128]{1,0:T(8,128)(2,1)S(1)} %get-tuple-element.55), channel_id=1, source_target_pairs={{4,0},{5,1},{6,2},{7,3},{8,4},{9,5},{10,6},{11,7},{12,8},{13,9},{1... | collective-permute-start | bytes 393224 | tf_op jit(solution)/shard_map/ppermute | solution.py:112
  6.7 90.6 %collective-permute-start.1 = (bf16[512,128]{1,0:T(8,128)(2,1)S(1)}, bf16[512,128]{1,0:T(8,128)(2,1)}, u32[]{:S(2)}, u32[]{:S(2)}) collective-permute-start(bf16[512,128]{1,0:T(8,128)(2,1)S(1)} %get-tuple-element.55), channel_id=1, source_target_pairs={{8,0},{9,1},{10,2},{11,3},{12,4},{13,5},{14,6},{15,7},{0,8},{1,9},... | collective-permute-start | bytes 393224 | tf_op jit(solution)/shard_map/ppermute | solution.py:112
  6.7 90.7 %collective-permute-start.2 = (bf16[512,128]{1,0:T(8,128)(2,1)S(1)}, bf16[512,128]{1,0:T(8,128)(2,1)}, u32[]{:S(2)}, u32[]{:S(2)}) collective-permute-start(bf16[512,128]{1,0:T(8,128)(2,1)S(1)} %get-tuple-element.55), channel_id=1, source_target_pairs={{12,0},{13,1},{14,2},{15,3},{0,4},{1,5},{2,6},{3,7},{4,8},{5,9},{6... | collective-permute-start | bytes 393224 | tf_op jit(solution)/shard_map/ppermute | solution.py:112
  7.8 90.8 %collective-permute-start.4 = (bf16[512,128]{1,0:T(8,128)(2,1)S(1)}, bf16[512,128]{1,0:T(8,128)(2,1)}, u32[]{:S(2)}, u32[]{:S(2)}) collective-permute-start(bf16[512,128]{1,0:T(8,128)(2,1)S(1)} %get-tuple-element.54), channel_id=1, source_target_pairs={{8,0},{9,1},{10,2},{11,3},{12,4},{13,5},{14,6},{15,7},{0,8},{1,9},... | collective-permute-start | bytes 393224 | tf_op jit(solution)/shard_map/ppermute | solution.py:112
  9.7 88.9 %collective-permute-start.5 = (bf16[512,128]{1,0:T(8,128)(2,1)S(1)}, bf16[512,128]{1,0:T(8,128)(2,1)}, u32[]{:S(2)}, u32[]{:S(2)}) collective-permute-start(bf16[512,128]{1,0:T(8,128)(2,1)S(1)} %get-tuple-element.54), channel_id=1, source_target_pairs={{12,0},{13,1},{14,2},{15,3},{0,4},{1,5},{2,6},{3,7},{4,8},{5,9},{6... | collective-permute-start | bytes 393224 | tf_op jit(solution)/shard_map/ppermute | solution.py:112
  97.3 103.1 %collective-permute-start.20 = (bf16[1024,768]{1,0:T(8,128)(2,1)}, bf16[1024,768]{1,0:T(8,128)(2,1)}, u32[]{:S(2)}, u32[]{:S(2)}) collective-permute-start(bf16[1024,768]{1,0:T(8,128)(2,1)} %get-tuple-element.34), channel_id=1, source_target_pairs={{0,16},{16,0},{1,17},{17,1},{2,18},{18,2},{3,19},{19,3},{4,20},{20... | collective-permute-start | bytes 4718600 | tf_op jit(solution)/shard_map/ppermute | solution.py:136
  98.5 14.9 %collective-permute-start.6 = (bf16[4,512,128]{2,1,0:T(8,128)(2,1)S(1)}, bf16[4,512,128]{2,1,0:T(8,128)(2,1)S(1)}, u32[]{:S(2)}, u32[]{:S(2)}) collective-permute-start(bf16[4,512,128]{2,1,0:T(8,128)(2,1)S(1)} %pad_maximum_fusion.2.refs_0_), channel_id=1, source_target_pairs={{2,0},{3,1},{0,2},{1,3},{6,4},{7,5},{4,6},{5,7},{10,8},{11,9},{8,1... | collective-permute-start | bytes 1572872 | tf_op jit(solution)/shard_map/ppermute | solution.py:122
  103.1 19.3 %collective-permute-start.7 = (bf16[4,512,128]{2,1,0:T(8,128)(2,1)S(1)}, bf16[4,512,128]{2,1,0:T(8,128)(2,1)}, u32[]{:S(2)}, u32[]{:S(2)}) collective-permute-start(bf16[4,512,128]{2,1,0:T(8,128)(2,1)S(1)} %pad_maximum_fusion.3.refs_1_), channel_id=1, source_target_pairs={{2,0},{3,1},{0,2},{1,3},{6,4},{7,5},{4,6},{5,7},{10,8},{11,9},{8,1... | collective-permute-start | bytes 1572872 | tf_op jit(solution)/shard_map/ppermute | solution.py:122
  104.0 24.3 %collective-permute-start.8 = (bf16[4,512,128]{2,1,0:T(8,128)(2,1)S(1)}, bf16[4,512,128]{2,1,0:T(8,128)(2,1)}, u32[]{:S(2)}, u32[]{:S(2)}) collective-permute-start(bf16[4,512,128]{2,1,0:T(8,128)(2,1)S(1)} %pad_maximum_fusion.2.refs_0_), channel_id=1, source_target_pairs={{1,0},{0,1},{3,2},{2,3},{5,4},{4,5},{7,6},{6,7},{9,8},{8,9},{11,10... | collective-permute-start | bytes 1572872 | tf_op jit(solution)/shard_map/ppermute | solution.py:132
  104.1 24.5 %collective-permute-start.9 = (bf16[4,512,128]{2,1,0:T(8,128)(2,1)S(1)}, bf16[4,512,128]{2,1,0:T(8,128)(2,1)}, u32[]{:S(2)}, u32[]{:S(2)}) collective-permute-start(bf16[4,512,128]{2,1,0:T(8,128)(2,1)S(1)} %pad_maximum_fusion.3.refs_1_), channel_id=1, source_target_pairs={{1,0},{0,1},{3,2},{2,3},{5,4},{4,5},{7,6},{6,7},{9,8},{8,9},{11,10... | collective-permute-start | bytes 1572872 | tf_op jit(solution)/shard_map/ppermute | solution.py:132
  113.4 15.1 %collective-permute-start.10 = (bf16[4,512,128]{2,1,0:T(8,128)(2,1)S(1)}, bf16[4,512,128]{2,1,0:T(8,128)(2,1)}, u32[]{:S(2)}, u32[]{:S(2)}) collective-permute-start(bf16[4,512,128]{2,1,0:T(8,128)(2,1)S(1)} %collective-permute-done.6.refs_2_), channel_id=1, source_target_pairs={{1,0},{0,1},{3,2},{2,3},{5,4},{4,5},{7,6},{6,7},{9,8},{8,9},{11,10... | collective-permute-start | bytes 1572872 | tf_op jit(solution)/shard_map/ppermute | solution.py:132
  128.2 72.4 %collective-permute-start.21 = (bf16[1024,768]{1,0:T(8,128)(2,1)}, bf16[1024,768]{1,0:T(8,128)(2,1)}, u32[]{:S(2)}, u32[]{:S(2)}) collective-permute-start(bf16[1024,768]{1,0:T(8,128)(2,1)} %get-tuple-element.32), channel_id=1, source_target_pairs={{0,16},{16,0},{1,17},{17,1},{2,18},{18,2},{3,19},{19,3},{4,20},{20... | collective-permute-start | bytes 4718600 | tf_op jit(solution)/shard_map/ppermute | solution.py:136
  131.6 39.2 %collective-permute-start.12 = (bf16[64,2048]{1,0:T(8,128)(2,1)S(1)}, bf16[64,2048]{1,0:T(8,128)(2,1)S(1)}, u32[]{:S(2)}, u32[]{:S(2)}) collective-permute-start(bf16[64,2048]{1,0:T(8,128)(2,1)S(1)} %get-tuple-element.17), channel_id=1, source_target_pairs={{0,16},{16,0},{1,17},{17,1},{2,18},{18,2},{3,19},{19,3},{4,20},{20... | collective-permute-start | bytes 786440 | tf_op jit(solution)/shard_map/ppermute | solution.py:136
  172.8 16.2 %collective-permute-start.14 = (bf16[32,2048]{1,0:T(8,128)(2,1)S(1)}, bf16[32,2048]{1,0:T(8,128)(2,1)S(1)}, u32[]{:S(2)}, u32[]{:S(2)}) collective-permute-start(bf16[32,2048]{1,0:T(8,128)(2,1)S(1)} %get-tuple-element.51), channel_id=1, source_target_pairs={{8,0},{9,1},{10,2},{11,3},{12,4},{13,5},{14,6},{15,7},{0,8},{1,9},... | collective-permute-start | bytes 393224 | tf_op jit(solution)/shard_map/ppermute | solution.py:112
  175.3 13.6 %collective-permute-start.15 = (bf16[32,2048]{1,0:T(8,128)(2,1)S(1)}, bf16[32,2048]{1,0:T(8,128)(2,1)S(1)}, u32[]{:S(2)}, u32[]{:S(2)}) collective-permute-start(bf16[32,2048]{1,0:T(8,128)(2,1)S(1)} %get-tuple-element.51), channel_id=1, source_target_pairs={{12,0},{13,1},{14,2},{15,3},{0,4},{1,5},{2,6},{3,7},{4,8},{5,9},{6... | collective-permute-start | bytes 393224 | tf_op jit(solution)/shard_map/ppermute | solution.py:112
  178.5 11.6 %collective-permute-start.34 = (bf16[32,2048]{1,0:T(8,128)(2,1)}, bf16[32,2048]{1,0:T(8,128)(2,1)S(1)}, u32[]{:S(2)}, u32[]{:S(2)}) collective-permute-start(bf16[32,2048]{1,0:T(8,128)(2,1)} %get-tuple-element.50), channel_id=1, source_target_pairs={{4,0},{5,1},{6,2},{7,3},{8,4},{9,5},{10,6},{11,7},{12,8},{13,9},{1... | collective-permute-start | bytes 393224 | tf_op jit(solution)/shard_map/ppermute | solution.py:112
  190.0 12.0 %collective-permute-start.22 = (bf16[1024,768]{1,0:T(8,128)(2,1)S(1)}, bf16[1024,768]{1,0:T(8,128)(2,1)}, u32[]{:S(2)}, u32[]{:S(2)}) collective-permute-start(bf16[1024,768]{1,0:T(8,128)(2,1)S(1)} %get-tuple-element.35.refs_0_), channel_id=1, source_target_pairs={{1,0},{0,1},{3,2},{2,3},{5,4},{4,5},{7,6},{6,7},{9,8},{8,9},{11,10... | collective-permute-start | bytes 4718600 | tf_op jit(solution)/shard_map/ppermute | solution.py:132
  197.8 34.7 %collective-permute-start.26 = (bf16[768,2048]{1,0:T(8,128)(2,1)}, bf16[768,2048]{1,0:T(8,128)(2,1)}, u32[]{:S(2)}, u32[]{:S(2)}) collective-permute-start(bf16[768,2048]{1,0:T(8,128)(2,1)} %pad_select_fusion.refs_4_), channel_id=1, source_target_pairs={{1,0},{0,1},{3,2},{2,3},{5,4},{4,5},{7,6},{6,7},{9,8},{8,9},{11,10... | collective-permute-start | bytes 9437192 | tf_op jit(solution)/shard_map/ppermute | solution.py:132
  200.5 32.0 %collective-permute-start.23 = (bf16[1024,768]{1,0:T(8,128)(2,1)}, bf16[1024,768]{1,0:T(8,128)(2,1)}, u32[]{:S(2)}, u32[]{:S(2)}) collective-permute-start(bf16[1024,768]{1,0:T(8,128)(2,1)} %collective-permute-done.20.refs_1_), channel_id=1, source_target_pairs={{1,0},{0,1},{3,2},{2,3},{5,4},{4,5},{7,6},{6,7},{9,8},{8,9},{11,10... | collective-permute-start | bytes 4718600 | tf_op jit(solution)/shard_map/ppermute | solution.py:132
  200.6 31.8 %collective-permute-start.25 = (bf16[1024,768]{1,0:T(8,128)(2,1)}, bf16[1024,768]{1,0:T(8,128)(2,1)}, u32[]{:S(2)}, u32[]{:S(2)}) collective-permute-start(bf16[1024,768]{1,0:T(8,128)(2,1)} %collective-permute-done.21.refs_3_), channel_id=1, source_target_pairs={{1,0},{0,1},{3,2},{2,3},{5,4},{4,5},{7,6},{6,7},{9,8},{8,9},{11,10... | collective-permute-start | bytes 4718600 | tf_op jit(solution)/shard_map/ppermute | solution.py:132
  217.9 12.5 %collective-permute-start.19 = (bf16[128,2048]{1,0:T(8,128)(2,1)}, bf16[128,2048]{1,0:T(8,128)(2,1)}, u32[]{:S(2)}, u32[]{:S(2)}) collective-permute-start(bf16[128,2048]{1,0:T(8,128)(2,1)} %pad_maximum_fusion.6.b8), channel_id=1, source_target_pairs={{0,16},{16,0},{1,17},{17,1},{2,18},{18,2},{3,19},{19,3},{4,20},{20... | collective-permute-start | bytes 1572872 | tf_op jit(solution)/shard_map/ppermute | solution.py:136
  219.2 12.5 %collective-permute-start.17 = (bf16[128,2048]{1,0:T(8,128)(2,1)}, bf16[128,2048]{1,0:T(8,128)(2,1)}, u32[]{:S(2)}, u32[]{:S(2)}) collective-permute-start(bf16[128,2048]{1,0:T(8,128)(2,1)} %pad_maximum_fusion.5.a8), channel_id=1, source_target_pairs={{2,0},{3,1},{0,2},{1,3},{6,4},{7,5},{4,6},{5,7},{10,8},{11,9},{8,1... | collective-permute-start | bytes 1572872 | tf_op jit(solution)/shard_map/ppermute | solution.py:122
  230.4 17.4 %collective-permute-start.40 = (bf16[128,2048]{1,0:T(8,128)(2,1)S(1)}, bf16[128,2048]{1,0:T(8,128)(2,1)S(1)}, u32[]{:S(2)}, u32[]{:S(2)}) collective-permute-start(bf16[128,2048]{1,0:T(8,128)(2,1)S(1)} %pad_maximum_fusion.9.b8), channel_id=1, source_target_pairs={{0,16},{16,0},{1,17},{17,1},{2,18},{18,2},{3,19},{19,3},{4,20},{20... | collective-permute-start | bytes 1572872 | tf_op jit(solution)/shard_map/ppermute | solution.py:136
  231.7 16.2 %collective-permute-start.38 = (bf16[128,2048]{1,0:T(8,128)(2,1)S(1)}, bf16[128,2048]{1,0:T(8,128)(2,1)S(1)}, u32[]{:S(2)}, u32[]{:S(2)}) collective-permute-start(bf16[128,2048]{1,0:T(8,128)(2,1)S(1)} %pad_maximum_fusion.8.a8), channel_id=1, source_target_pairs={{2,0},{3,1},{0,2},{1,3},{6,4},{7,5},{4,6},{5,7},{10,8},{11,9},{8,1... | collective-permute-start | bytes 1572872 | tf_op jit(solution)/shard_map/ppermute | solution.py:122
  245.8 17.0 %collective-permute-start.29 = (bf16[128,2048]{1,0:T(8,128)(2,1)S(1)}, bf16[128,2048]{1,0:T(8,128)(2,1)S(1)}, u32[]{:S(2)}, u32[]{:S(2)}) collective-permute-start(bf16[128,2048]{1,0:T(8,128)(2,1)S(1)} %get-tuple-element.21), channel_id=1, source_target_pairs={{0,16},{16,0},{1,17},{17,1},{2,18},{18,2},{3,19},{19,3},{4,20},{20... | collective-permute-start | bytes 1572872 | tf_op jit(solution)/shard_map/ppermute | solution.py:136
  246.7 17.5 %collective-permute-start.27 = (bf16[128,2048]{1,0:T(8,128)(2,1)S(1)}, bf16[128,2048]{1,0:T(8,128)(2,1)S(1)}, u32[]{:S(2)}, u32[]{:S(2)}) collective-permute-start(bf16[128,2048]{1,0:T(8,128)(2,1)S(1)} %get-tuple-element.19), channel_id=1, source_target_pairs={{2,0},{3,1},{0,2},{1,3},{6,4},{7,5},{4,6},{5,7},{10,8},{11,9},{8,1... | collective-permute-start | bytes 1572872 | tf_op jit(solution)/shard_map/ppermute | solution.py:122
  260.7 14.9 %collective-permute-start.43 = (bf16[128,2048]{1,0:T(8,128)(2,1)S(1)}, bf16[128,2048]{1,0:T(8,128)(2,1)S(1)}, u32[]{:S(2)}, u32[]{:S(2)}) collective-permute-start(bf16[128,2048]{1,0:T(8,128)(2,1)S(1)} %get-tuple-element.25), channel_id=1, source_target_pairs={{0,16},{16,0},{1,17},{17,1},{2,18},{18,2},{3,19},{19,3},{4,20},{20... | collective-permute-start | bytes 1572872 | tf_op jit(solution)/shard_map/ppermute | solution.py:136
  262.0 14.9 %collective-permute-start.41 = (bf16[128,2048]{1,0:T(8,128)(2,1)S(1)}, bf16[128,2048]{1,0:T(8,128)(2,1)S(1)}, u32[]{:S(2)}, u32[]{:S(2)}) collective-permute-start(bf16[128,2048]{1,0:T(8,128)(2,1)S(1)} %get-tuple-element.23), channel_id=1, source_target_pairs={{2,0},{3,1},{0,2},{1,3},{6,4},{7,5},{4,6},{5,7},{10,8},{11,9},{8,1... | collective-permute-start | bytes 1572872 | tf_op jit(solution)/shard_map/ppermute | solution.py:122
  262.9 17.3 %collective-permute-start.30 = (bf16[64,2048]{1,0:T(8,128)(2,1)S(1)}, bf16[64,2048]{1,0:T(8,128)(2,1)S(1)}, u32[]{:S(2)}, u32[]{:S(2)}) collective-permute-start(bf16[64,2048]{1,0:T(8,128)(2,1)S(1)} %slice.254), channel_id=1, source_target_pairs={{2,0},{3,1},{0,2},{1,3},{6,4},{7,5},{4,6},{5,7},{10,8},{11,9},{8,1... | collective-permute-start | bytes 786440 | tf_op jit(solution)/shard_map/ppermute | solution.py:122
  264.4 15.9 %collective-permute-start.28 = (bf16[64,2048]{1,0:T(8,128)(2,1)S(1)}, bf16[64,2048]{1,0:T(8,128)(2,1)S(1)}, u32[]{:S(2)}, u32[]{:S(2)}) collective-permute-start(bf16[64,2048]{1,0:T(8,128)(2,1)S(1)} %slice.255), channel_id=1, source_target_pairs={{0,16},{16,0},{1,17},{17,1},{2,18},{18,2},{3,19},{19,3},{4,20},{20... | collective-permute-start | bytes 786440 | tf_op jit(solution)/shard_map/ppermute | solution.py:136
  282.5 12.3 %collective-permute-start.32 = (bf16[32,2048]{1,0:T(8,128)(2,1)S(1)}, bf16[32,2048]{1,0:T(8,128)(2,1)S(1)}, u32[]{:S(2)}, u32[]{:S(2)}) collective-permute-start(bf16[32,2048]{1,0:T(8,128)(2,1)S(1)} %get-tuple-element.40), channel_id=1, source_target_pairs={{8,0},{9,1},{10,2},{11,3},{12,4},{13,5},{14,6},{15,7},{0,8},{1,9},... | collective-permute-start | bytes 393224 | tf_op jit(solution)/shard_map/ppermute | solution.py:112
  286.5 12.4 %collective-permute-start.46 = (bf16[32,2048]{1,0:T(8,128)(2,1)S(1)}, bf16[32,2048]{1,0:T(8,128)(2,1)S(1)}, u32[]{:S(2)}, u32[]{:S(2)}) collective-permute-start(bf16[32,2048]{1,0:T(8,128)(2,1)S(1)} %get-tuple-element.45), channel_id=1, source_target_pairs={{8,0},{9,1},{10,2},{11,3},{12,4},{13,5},{14,6},{15,7},{0,8},{1,9},... | collective-permute-start | bytes 393224 | tf_op jit(solution)/shard_map/ppermute | solution.py:112
  (39 other events, 339.7 us)

commit v2 on v1

--- a/solution.py
+++ b/solution.py
@@ -139,8 +139,7 @@
 def project_kernel(depth, ctx_ref, *refs):
     pieces, (own_ref, send_ref) = refs[:-2], refs[-2:]
     half = own_ref.shape[0]
-    width = pieces[0].shape[2]
-    chunk = pieces[0].shape[1]
+    width = pieces[0].shape[1]
     me = lax.axis_index("expert")
     x = lax.axis_index("dp")
     c = lax.rem(me, 2)
@@ -149,19 +148,13 @@
     mine = ctx_ref[pl.ds(pl.multiple_of(x * half, half), half), :]
     theirs = ctx_ref[pl.ds(pl.multiple_of((1 - x) * half, half), half), :]
     rows = jnp.concatenate([mine, theirs], axis=0)
-    for piece in range(4):
-        flips = ((0, 0), (1, 0), (0, 1), (1, 1))[piece]
-        at_y = y if flips[0] == 0 else 1 - y
-        at_c = c if flips[1] == 0 else 1 - c
+    for flips in range(4):
+        at_y = y if flips % 2 == 0 else 1 - y
+        at_c = c if flips < 2 else 1 - c
         for r in range(depth):
-            total = None
-            for k in range(2):
-                part = jnp.dot(
-                    rows[:, k * chunk : (k + 1) * chunk],
-                    pieces[2 * piece + k][r],
-                    preferred_element_type=jnp.float32,
-                )
-                total = part if total is None else total + part
+            total = jnp.dot(
+                rows, pieces[flips * depth + r][...], preferred_element_type=jnp.float32
+            )
             index = (lax.rem(z + r, depth) * 2 + at_y) * 2 + at_c
             columns = pl.ds(pl.multiple_of(index * width, width), width)
             own_ref[:, columns] = total[:half]
@@ -170,8 +163,7 @@
 
 def project(context, pieces, depth):
     rows, feats = context.shape
-    width = pieces[0].shape[2]
-    columns = width * 4 * depth
+    columns = pieces[0].shape[1] * 4 * depth
     return pl.pallas_call(
         functools.partial(project_kernel, depth),
         out_shape=(
@@ -189,29 +181,34 @@
 
 
 def experts_kernel(
-    tile, out_tile, a8, ya, b8, xb, share, *refs
+    tile, out_tile, count, *refs
 ):
-    weights, refs = refs[:10], refs[10:]
-    outs, (rows, gate, up, down, mid, row_sem, weight_sem, down_sem) = refs[:4], refs[4:]
+    pieces, share, weights = refs[:count], refs[count], refs[count + 1 : count + 11]
+    outs, refs = refs[count + 11 : 2 * count + 11], refs[2 * count + 11 :]
+    rows, gate, up, down, mid, row_sem, weight_sem, down_sem = refs
     x = lax.axis_index("dp")
     feats = rows.shape[1]
     half = feats // 2
     width = gate.shape[2]
     tiles = width // tile
-    part = a8.shape[0]
     near = pl.ds(pl.multiple_of(x * half, half), half)
     far = pl.ds(pl.multiple_of((1 - x) * half, half), half)
 
     row_copies = []
-    for i, piece in enumerate((a8, ya, b8, xb)):
+    offsets = []
+    at = 0
+    for i, piece in enumerate(pieces):
+        part = piece.shape[0]
+        offsets.append((at, part))
         for s, lanes in enumerate((near, far)):
             copy = pltpu.make_async_copy(
                 piece.at[:, lanes],
-                rows.at[pl.ds(i * part, part), pl.ds(s * half, half)],
+                rows.at[pl.ds(at, part), pl.ds(s * half, half)],
                 row_sem.at[2 * i + s],
             )
             copy.start()
             row_copies.append(copy)
+        at += part
     weight_copies = []
     down_copies = []
     for e in range(2):
@@ -258,32 +255,32 @@
     for n in range(feats // out_tile):
         lanes = pl.ds(n * out_tile, out_tile)
         total = jnp.dot(mid[...], down[:, lanes], preferred_element_type=jnp.float32)
-        for i, out in enumerate(outs):
-            out[:, lanes] = total[i * part : (i + 1) * part].astype(out.dtype)
-
-
-def run_experts(pieces, share, weights):
-    part, feats = pieces[0].shape
+        for (first, part), out in zip(offsets, outs):
+            out[:, lanes] = total[first : first + part].astype(out.dtype)
+
+
+def run_experts(pieces, kinds, share, weights):
+    feats = pieces[0].shape[1]
     half, width = weights[0].shape
-    total = 4 * part
+    count = len(pieces)
+    total = sum(piece.shape[0] for piece in pieces)
     tile = 256
     any_spec = pl.BlockSpec(memory_space=pl.ANY)
     vmem_spec = pl.BlockSpec(memory_space=pltpu.VMEM)
     return pl.pallas_call(
-        functools.partial(experts_kernel, tile, 512),
+        functools.partial(experts_kernel, tile, 512, count),
         out_shape=tuple(
-            jax.ShapeDtypeStruct((part, feats), kind)
-            for kind in (jnp.float32, jnp.bfloat16, jnp.float32, jnp.bfloat16)
+            jax.ShapeDtypeStruct(piece.shape, kind) for piece, kind in zip(pieces, kinds)
         ),
-        in_specs=[any_spec] * 4 + [vmem_spec] + [any_spec] * 10,
-        out_specs=(vmem_spec,) * 4,
+        in_specs=[any_spec] * count + [vmem_spec] + [any_spec] * 10,
+        out_specs=(vmem_spec,) * count,
         scratch_shapes=[
             pltpu.VMEM((total, feats), jnp.bfloat16),
             pltpu.VMEM((2, feats, width), jnp.bfloat16),
             pltpu.VMEM((2, feats, width), jnp.bfloat16),
             pltpu.VMEM((2 * width, feats), jnp.bfloat16),
             pltpu.VMEM((total, 2 * width), jnp.bfloat16),
-            pltpu.SemaphoreType.DMA((8,)),
+            pltpu.SemaphoreType.DMA((2 * count,)),
             pltpu.SemaphoreType.DMA((8 * (width // tile),)),
             pltpu.SemaphoreType.DMA((2,)),
         ],
@@ -317,8 +314,6 @@
     me = lax.axis_index("expert")
     x = lax.axis_index("dp")
     c = me % 2
-    y = (me // 2) % 2
-    z = me // 4
     first = x == 0
     feats = residual.shape[1]
     block = residual.shape[0]
@@ -333,78 +328,86 @@
     gate_own, gate_sent = halves(w_gate[0])
     up_own, up_sent = halves(w_up[0])
     gate_far = flip_x(gate_sent)
-    up_far = flip_x(up_sent)
     blank = jnp.zeros((width - units_here, feats), w_down.dtype)
     down_own = jnp.where(
         first,
         jnp.concatenate([w_down[0], blank], axis=0),
         jnp.concatenate([blank, w_down[0]], axis=0),
     )
-    here = [gate_own, gate_far, up_own, up_far, down_own]
-    weights = here + [flip_core(array, depth) for array in here]
-
-    near, across, near_core, across_core = [], [], [], []
-    chunk = w_out.shape[0] // 2
-    for k in range(2):
-        own = w_out[k * chunk : (k + 1) * chunk]
-        line = jnp.stack([own] + [shift_z(own, depth, s) for s in range(1, depth)])
-        near.append(line)
-        near_core.append(flip_core(line, depth))
-        other = flip_y(line, depth)
-        across.append(other)
-        across_core.append(flip_core(other, depth))
+    gate_own_core = flip_core(gate_own, depth)
+    up_own_core = flip_core(up_own, depth)
+    down_own_core = flip_core(down_own, depth)
+
+    near = [w_out] + [shift_z(w_out, depth, s) for s in range(1, depth)]
+    across = [flip_y(piece, depth) for piece in near]
+    columns = near + across
+    columns = columns + [flip_core(piece, depth) for piece in columns]
 
     named = expert_ids[:, :, None] == jnp.arange(experts, dtype=jnp.int32)[None, None, :]
     share = jnp.sum(jnp.where(named, route_weights[:, :, None], 0.0), axis=1)
-    share = lax.all_gather(share, ("expert", "dp"), axis=0, tiled=True)
     both = jnp.stack([me, me + 1 - 2 * c])
-    pick = (jnp.arange(experts, dtype=jnp.int32)[:, None] == both[None, :]).astype(jnp.float32)
-    share = jnp.dot(share, pick, precision=lax.Precision.HIGHEST)
-    share = share.reshape(experts * 2, 2, 2, block // 4, 2)
-    line_z = (z + jnp.arange(depth, dtype=jnp.int32)) % depth
-
-    def blocks(dx, dy):
-        at_x = x if dx == 0 else 1 - x
-        at_y = y if dy == 0 else 1 - y
-        return place(line_z, at_y, c) * 2 + at_x
-
-    order_a = jnp.concatenate([blocks(0, 0), blocks(1, 0), blocks(0, 1), blocks(1, 1)])
-    order_b = jnp.concatenate([blocks(0, 0), blocks(0, 1), blocks(1, 0), blocks(1, 1)])
-    share_a = jnp.take(share[:, :, 0], order_a, axis=0)
-    share_b = jnp.take(share[:, :, 1], order_b, axis=0)
+    pick = both[None, :] == jnp.arange(experts, dtype=jnp.int32)[:, None]
+    share_l = jnp.stack([share] + [shift_z(share, depth, s) for s in range(1, depth)])
+    share_x = flip_x(share_l)
+    share_y = flip_y(share_l, depth)
+    share_d = flip_y(share_x, depth)
+    shares = jnp.stack([share_l, share_x, share_y, share_d])
+    shares = jnp.sum(jnp.where(pick[:, None, :].swapaxes(0, 1), shares[..., None], 0.0), axis=-2)
 
     context = attend(queries, kv_pool, page_table, ctx_lens)
-    own, sent = project(context, near + across + near_core + across_core, depth)
-    projected = own + flip_x(sent).astype(jnp.float32)
-    hidden_state = residual.astype(jnp.float32) + projected
+    own, sent = project(context, columns, depth)
+    own, sent, gate_far, shares, gate_own_core, up_own_core, down_own_core = lax.optimization_barrier(
+        (own, sent, gate_far, shares, gate_own_core, up_own_core, down_own_core)
+    )
+    received, up_sent = lax.optimization_barrier((flip_x(sent), up_sent))
+    up_far = flip_x(up_sent)
+    weights = [gate_own, gate_far, up_own, up_far, down_own]
+    weights += [
+        gate_own_core,
+        flip_core(gate_far, depth),
+        up_own_core,
+        flip_core(up_far, depth),
+        down_own_core,
+    ]
+    hidden_state = residual.astype(jnp.float32) + (own + received.astype(jnp.float32))
     moe_input = normalize(hidden_state, moe_gain).astype(jnp.bfloat16)
 
-    quarter = block // 4
-    part = depth * quarter
+    chunks = 2
+    rows = block // chunks
+    part = rows // 2
     moe = []
-    for k in range(2):
-        mine = moe_input[2 * quarter * k : 2 * quarter * (k + 1)]
+    for k in range(chunks):
+        mine = moe_input[rows * k : rows * (k + 1)]
         line = jnp.stack([mine] + [shift_z(mine, depth, s) for s in range(1, depth)])
-        line_a, line_b = line[:, :quarter], line[:, quarter:]
-        line_a = line_a.reshape(part, feats)
-        line_b = line_b.reshape(part, feats)
-        a8 = jnp.concatenate([line_a, flip_x(line_a)], axis=0)
-        b8 = jnp.concatenate([line_b, flip_y(line_b, depth)], axis=0)
-        ya = flip_y(a8, depth)
-        xb = flip_x(b8)
-        shares = jnp.concatenate(
-            [share_a[:, k].reshape(4 * part, 2), share_b[:, k].reshape(4 * part, 2)], axis=0
+        line_x = flip_x(line)
+        line_y = flip_y(line, depth)
+        low = flip_y(line_x[:, :part], depth)
+        high = flip_x(line_y[:, part:])
+        share = shares[:, :, rows * k : rows * (k + 1)]
+        share = jnp.concatenate(
+            [
+                share[:3].reshape(3 * depth * rows, 2),
+                share[3, :, :part].reshape(depth * part, 2),
+                share[3, :, part:].reshape(depth * part, 2),
+            ],
+            axis=0,
         )
-        out_a, out_ya, out_b, out_xb = run_experts([a8, ya, b8, xb], shares, weights)
-        back_a = flip_y(out_ya, depth).astype(jnp.float32)
-        back_b = flip_x(out_xb).astype(jnp.float32)
-        sum_a = out_a + back_a
-        sum_b = out_b + back_b
-        last_a = flip_x(sum_a[part:].astype(jnp.bfloat16)).astype(jnp.float32)
-        last_b = flip_y(sum_b[part:].astype(jnp.bfloat16), depth).astype(jnp.float32)
-        full_a = (sum_a[:part] + last_a).reshape(depth, quarter, feats)
-        full_b = (sum_b[:part] + last_b).reshape(depth, quarter, feats)
-        full = jnp.concatenate([full_a, full_b], axis=1)
+        out_l, out_x, out_y, out_low, out_high = run_experts(
+            [piece.reshape(-1, feats) for piece in (line, line_x, line_y, low, high)],
+            (jnp.float32, jnp.float32, jnp.float32, jnp.bfloat16, jnp.bfloat16),
+            share,
+            weights,
+        )
+        out_l = out_l.reshape(line.shape)
+        out_x = out_x.reshape(line.shape)
+        out_y = out_y.reshape(line.shape)
+        back_low = flip_y(out_low, depth).reshape(low.shape).astype(jnp.float32)
+        back_high = flip_x(out_high).reshape(high.shape).astype(jnp.float32)
+        sum_x = jnp.concatenate([out_x[:, :part] + back_low, out_x[:, part:]], axis=1)
+        sum_y = jnp.concatenate([out_y[:, :part], out_y[:, part:] + back_high], axis=1)
+        back_x = flip_x(sum_x.astype(jnp.bfloat16)).astype(jnp.float32)
+        back_y = flip_y(sum_y.astype(jnp.bfloat16), depth).astype(jnp.float32)
+        full = out_l + back_x + back_y
         total = full[0]
         for s in range(1, depth):
             total = total + shift_z(full[s].astype(jnp.bfloat16), depth, depth - s).astype(

time: 300 us -> 262 us (0.87)
  blocking collectives: 67.4 us -> 0 us
  waiting for transfers between devices: 115 us -> 134 us
  local copies, waits for them, and re-layouts: 17.1 us -> 26.2 us
  starting transfers between devices: 43.4 us -> 52.1 us
  other arithmetic: 22.9 us -> 14.5 us
    all_gather x1 -> x0, blocking collectives: 67.4 us -> none  [gathered(): share = lax.all_gather(share, ('expert', 'dp'), axis=0, tiled=True)]
    ppermute x11 -> x12, waiting for transfers between devices: 52.9 us -> 66.3 us  [flip_x(): return lax.ppermute(values, 'dp', [(0, 1), (1, 0)])]
    ppermute x10 -> x14, starting transfers between devices: 6.31 us -> 19.1 us  [flip_y(): return lax.ppermute(values, 'expert', pairs)]
    unnamed x51 -> x78, local copies, waits for them, and re-layouts: 4.26 us -> 13.3 us
    ppermute x18, waiting for transfers between devices: 31.2 us -> 38.1 us  [shift_z(): return lax.ppermute(values, 'expert', pairs)]
    ppermute x10 -> x14, waiting for transfers between devices: 29.9 us -> 25.7 us  [flip_y(): return lax.ppermute(values, 'expert', pairs)]
    concatenate x6, other arithmetic: 3.91 us -> 0.32 us  [the longest x2 0.15 us: gathered(): jnp.concatenate([share[:3].reshape(3 * depth * rows, 2), share[3, :, :par...]
    select_n x1, other arithmetic: 2.41 us -> 5.92 us  [gathered(): jnp.where(first, jnp.concatenate([w_down[0], blank], axis=0), jnp.concate...]
  transfers between devices with their start and end apart: 48 -> 57, of which waited for: 18 -> 27; matrix products, arithmetic and copies ran while one was open for 13% -> 12% of each run, Pallas kernels for 10% -> 11%
where the time goes in v2:
time: 262 us; the launch traced here: 261 us
  waiting for transfers between devices  134 us (51%)
  starting transfers between devices  52.1 us (20%)
  Pallas kernels  28.9 us (11%)
  local copies, waits for them, and re-layouts  26.2 us (10%)
  other arithmetic  14.5 us (6%)
  matrix products  4.86 us (2%)
    ppermute x12, waiting for transfers between devices, flip_x(): return lax.ppermute(values, 'dp', [(0, 1), (1, 0)])  66.3 us
    ppermute x18, waiting for transfers between devices, shift_z(): return lax.ppermute(values, 'expert', pairs)  38.1 us
    pallas_call x2, Pallas kernels, run_experts(): pl.pallas_call(functools.partial(experts_kernel, tile, 512, count), out_s...  26.2 us
    ppermute x14, waiting for transfers between devices, flip_y(): return lax.ppermute(values, 'expert', pairs)  25.7 us
    ppermute x18, starting transfers between devices, shift_z(): return lax.ppermute(values, 'expert', pairs)  20.6 us
    ppermute x14, starting transfers between devices, flip_y(): return lax.ppermute(values, 'expert', pairs)  19.1 us
    unnamed x78, local copies, waits for them, and re-layouts  13.3 us
    ppermute x12, starting transfers between devices, flip_x(): return lax.ppermute(values, 'dp', [(0, 1), (1, 0)])  9.74 us
  transfers between devices with their start and end apart: 57, of which 27 were waited for; matrix products, arithmetic and copies ran while one was open for 12% of the time, Pallas kernels for 11%

profile of v2, /device:TPU:0, one launch (start us, length us, event | category | flops | bytes accessed | tf_op | source)
XLA Modules:
  0.0 261.3 jit_solution(3985183988214900485)
XLA Ops:
  0.0 5.9 %pad_select_fusion.refs_10_ = bf16[768,2048]{1,0:T(8,128)(2,1)} fusion(bf16[704,2048]{1,0:T(8,128)(2,1)} %bitcast.136, pred[]{:T(512)S(6)} %eq.16), kind=kLoop, calls=%fused_computation.3 | loop fusion | flops 1572864 | bytes 6029313 | tf_op jit(solution)/shard_map/jit(_where)/select_n | solution.py:332
  6.4 2.6 %collective-permute-start.18 = (f32[64,16]{0,1:T(8,128)S(1)}, f32[64,16]{0,1:T(8,128)S(1)}, u32[]{:S(2)}, u32[]{:S(2)}) collective-permute-start(f32[64,16]{0,1:T(8,128)S(1)} %select_reduce_fusion.1), channel_id=1, source_target_pairs={{12,0},{13,1},{14,2},{15,3},{0,4},{1,5},{2,6},{3,7},{4,8},{5,9},{6... | collective-permute-start | bytes 12296 | tf_op jit(solution)/shard_map/ppermute | solution.py:112
  12.8 2.9 %collective-permute-done.17 = f32[64,16]{0,1:T(8,128)S(1)} collective-permute-done((f32[64,16]{0,1:T(8,128)S(1)}, f32[64,16]{0,1:T(8,128)S(1)}, u32[]{:S(2)}, u32[]{:S(2)}) %collective-permute-start.17) | collective-permute-done | bytes 4128 | tf_op jit(solution)/shard_map/ppermute | solution.py:112
  26.0 14.4 %collective-permute-done.1.refs_2_ = bf16[1024,128]{1,0:T(8,128)(2,1)} collective-permute-done((bf16[1024,128]{1,0:T(8,128)(2,1)S(1)}, bf16[1024,128]{1,0:T(8,128)(2,1)}, u32[]{:S(2)}, u32[]{:S(2)}) %collective-permute-start.1) | collective-permute-done | bytes 262176 | tf_op jit(solution)/shard_map/ppermute | solution.py:112
  41.9 3.4 %broadcast_select_fusion = (bf16[1024,768]{1,0:T(8,128)(2,1)}, bf16[1024,768]{1,0:T(8,128)(2,1)S(1)}) fusion(pred[]{:T(512)S(6)} %eq.16, bf16[1024,1408]{1,0:T(8,128)(2,1)} %bitcast.135), kind=kLoop, calls=%fused_computation.4 | loop fusion | flops 1572864 | bytes 6291457 | tf_op jit(solution)/shard_map/jit(_where)/select_n | solution.py:326
  48.5 2.5 collective-permute-start.5
  52.5 5.7 %collective-permute-done.5.refs_6_ = bf16[1024,128]{1,0:T(8,128)(2,1)S(1)} collective-permute-done((bf16[1024,128]{1,0:T(8,128)(2,1)}, bf16[1024,128]{1,0:T(8,128)(2,1)S(1)}, u32[]{:S(2)}, u32[]{:S(2)}) %collective-permute-start.5) | collective-permute-done | bytes 262176 | tf_op jit(solution)/shard_map/ppermute | solution.py:122
  61.2 3.4 %collective-permute-done.9.refs_10_ = bf16[1024,128]{1,0:T(8,128)(2,1)} collective-permute-done((bf16[1024,128]{1,0:T(8,128)(2,1)}, bf16[1024,128]{1,0:T(8,128)(2,1)}, u32[]{:S(2)}, u32[]{:S(2)}) %collective-permute-start.9) | collective-permute-done | bytes 262176 | tf_op jit(solution)/shard_map/ppermute | solution.py:132
  64.8 2.8 %gather_fusion.1 = bf16[8,64,1024]{2,1,0:T(8,128)(2,1)} fusion(bf16[8,64,1024]{2,1,0:T(8,128)(2,1)} %get-tuple-element.57, s32[1024]{0:T(1024)S(1)} %pad_clamp_fusion), kind=kCustom, calls=%fused_computation.1 | custom fusion | bytes 2097184 | tf_op jit(solution)/shard_map/gather | solution.py:31
  67.6 2.5 copy.59
  71.0 2.8 %gather_fusion = bf16[8,64,1024]{2,1,0:T(8,128)(2,1)} fusion(bf16[8,64,1024]{2,1,0:T(8,128)(2,1)} %get-tuple-element.58, s32[1024]{0:T(1024)S(1)} %pad_clamp_fusion), kind=kCustom, calls=%fused_computation | custom fusion | bytes 2097184 | tf_op jit(solution)/shard_map/gather | solution.py:32
  73.8 2.5 copy.61
  76.9 2.9 %fusion.26 = (f32[2,8,64]{2,1,0:T(8,128)S(1)}, f32[2,8,64,256]{3,2,1,0:T(8,128)}) fusion(pred[2,64,256]{2,1,0:T(8,128)(4,1)S(1)} %iota_compare_fusion, bf16[2,256,8,128]{3,2,1,0:T(8,128)(2,1)} %bitcast.138, bf16[2,64,8,128]{3,2,1,0:T(8,128)(2,1)} %bitcast.141), kind=kOutput, calls=%fused_computation.85 | convolution fusion | flops 68419840 | bytes 2396160 | tf_op jit(solution)/shard_map/sub | solution.py:39
  83.6 2.7 %project.1 = (f32[64,2048]{1,0:T(8,128)S(1)}, bf16[64,2048]{1,0:T(8,128)(2,1)S(1)}) custom-call(bf16[128,1024]{1,0:T(8,128)(2,1)S(1)} %bitcast.118, bf16[1024,128]{1,0:T(8,128)(2,1)S(1)} %copy-done.2, bf16[1024,128]{1,0:T(8,128)(2,1)} %collective-permute-done.refs_1_, bf16[1024,128]{1,0:T(8,128)(2,1)} %collective-permute-done.1.refs_2_, ...), custom_call_target="tpu_custom_call" | custom-call | flops 536870912 | bytes 5242880 | tf_op jit(solution)/shard_map/project/pallas_call | solution.py:167
  86.4 10.3 %collective-permute-done.15.refs_7_ = bf16[1024,768]{1,0:T(8,128)(2,1)} collective-permute-done((bf16[1024,768]{1,0:T(8,128)(2,1)}, bf16[1024,768]{1,0:T(8,128)(2,1)}, u32[]{:S(2)}, u32[]{:S(2)}) %collective-permute-start.15) | collective-permute-done | bytes 1572896 | tf_op jit(solution)/shard_map/ppermute | solution.py:136
  97.3 7.3 %collective-permute-done.25 = bf16[64,2048]{1,0:T(8,128)(2,1)S(1)} collective-permute-done((bf16[64,2048]{1,0:T(8,128)(2,1)S(1)}, bf16[64,2048]{1,0:T(8,128)(2,1)S(1)}, u32[]{:S(2)}, u32[]{:S(2)}) %collective-permute-start.25) | collective-permute-done | bytes 262176 | tf_op jit(solution)/shard_map/ppermute | solution.py:136
  107.6 32.2 %collective-permute-done.33.refs_9_ = bf16[1024,768]{1,0:T(8,128)(2,1)} collective-permute-done((bf16[1024,768]{1,0:T(8,128)(2,1)S(1)}, bf16[1024,768]{1,0:T(8,128)(2,1)}, u32[]{:S(2)}, u32[]{:S(2)}) %collective-permute-start.33) | collective-permute-done | bytes 1572896 | tf_op jit(solution)/shard_map/ppermute | solution.py:136
  142.1 4.1 %collective-permute-done.43 = bf16[32,2048]{1,0:T(8,128)(2,1)S(1)} collective-permute-done((bf16[32,2048]{1,0:T(8,128)(2,1)S(1)}, bf16[32,2048]{1,0:T(8,128)(2,1)S(1)}, u32[]{:S(2)}, u32[]{:S(2)}) %collective-permute-start.43) | collective-permute-done | bytes 131104 | tf_op jit(solution)/shard_map/ppermute | solution.py:112
  146.7 6.3 %collective-permute-done.44 = bf16[32,2048]{1,0:T(8,128)(2,1)S(1)} collective-permute-done((bf16[32,2048]{1,0:T(8,128)(2,1)S(1)}, bf16[32,2048]{1,0:T(8,128)(2,1)S(1)}, u32[]{:S(2)}, u32[]{:S(2)}) %collective-permute-start.44) | collective-permute-done | bytes 131104 | tf_op jit(solution)/shard_map/ppermute | solution.py:112
  156.8 4.2 %collective-permute-done.29 = bf16[4,32,2048]{2,1,0:T(8,128)(2,1)S(1)} collective-permute-done((bf16[4,32,2048]{2,1,0:T(8,128)(2,1)S(1)}, bf16[4,32,2048]{2,1,0:T(8,128)(2,1)S(1)}, u32[]{:S(2)}, u32[]{:S(2)}) %collective-permute-start.29) | collective-permute-done | bytes 524320 | tf_op jit(solution)/shard_map/ppermute | solution.py:136
  163.4 4.5 %collective-permute-done.30 = bf16[4,32,2048]{2,1,0:T(8,128)(2,1)S(1)} collective-permute-done((bf16[4,32,2048]{2,1,0:T(8,128)(2,1)S(1)}, bf16[4,32,2048]{2,1,0:T(8,128)(2,1)S(1)}, u32[]{:S(2)}, u32[]{:S(2)}) %collective-permute-start.30) | collective-permute-done | bytes 524320 | tf_op jit(solution)/shard_map/ppermute | solution.py:122
  174.4 4.8 %collective-permute-done.47 = bf16[4,32,2048]{2,1,0:T(8,128)(2,1)} collective-permute-done((bf16[4,32,2048]{2,1,0:T(8,128)(2,1)}, bf16[4,32,2048]{2,1,0:T(8,128)(2,1)}, u32[]{:S(2)}, u32[]{:S(2)}) %collective-permute-start.47) | collective-permute-done | bytes 524320 | tf_op jit(solution)/shard_map/ppermute | solution.py:122
  181.7 3.1 %collective-permute-done.31 = bf16[4,16,2048]{2,1,0:T(8,128)(2,1)} collective-permute-done((bf16[4,16,2048]{2,1,0:T(8,128)(2,1)}, bf16[4,16,2048]{2,1,0:T(8,128)(2,1)}, u32[]{:S(2)}, u32[]{:S(2)}) %collective-permute-start.31) | collective-permute-done | bytes 262176 | tf_op jit(solution)/shard_map/ppermute | solution.py:122
  189.4 13.0 %experts.2 = (f32[128,2048]{1,0:T(8,128)S(1)}, f32[128,2048]{1,0:T(8,128)S(1)}, f32[128,2048]{1,0:T(8,128)S(1)}, bf16[64,2048]{1,0:T(8,128)(2,1)S(1)}, bf16[64,2048]{1,0:T(8,128)(2,1)S(1)}) custom-call(bf16[128,2048]{1,0:T(8,128)(2,1)S(1)} %bitcast.127, bf16[128,2048]{1,0:T(8,128)(2,1)S(1)} %bitcast.128, bf16[128,2048]{1,0:T(8,128)(2,1)S(1)} %bitcast.129, ...), custom_call_target="tpu_custom_call" | custom-call | flops 9663676416 | bytes 31457280 | tf_op jit(solution)/shard_map/experts/pallas_call | solution.py:270
  205.6 13.1 %experts.3 = (f32[128,2048]{1,0:T(8,128)S(1)}, f32[128,2048]{1,0:T(8,128)S(1)}, f32[128,2048]{1,0:T(8,128)S(1)}, bf16[64,2048]{1,0:T(8,128)(2,1)S(1)}, bf16[64,2048]{1,0:T(8,128)(2,1)S(1)}) custom-call(bf16[128,2048]{1,0:T(8,128)(2,1)} %bitcast.39.refs_0_, bf16[128,2048]{1,0:T(8,128)(2,1)} %bitcast.40.refs_1_, bf16[128,2048]{1,0:T(8,128)(2,1)} %bitcast.41.refs_2_, ...), custom_call_target="tpu_custom_call" | custom-call | flops 9663676416 | bytes 31457280 | tf_op jit(solution)/shard_map/experts/pallas_call | solution.py:270
  223.4 4.7 %collective-permute-done.50 = bf16[64,2048]{1,0:T(8,128)(2,1)S(1)} collective-permute-done((bf16[64,2048]{1,0:T(8,128)(2,1)S(1)}, bf16[64,2048]{1,0:T(8,128)(2,1)S(1)}, u32[]{:S(2)}, u32[]{:S(2)}) %collective-permute-start.50) | collective-permute-done | bytes 262176 | tf_op jit(solution)/shard_map/ppermute | solution.py:122
  230.4 9.5 %collective-permute-done.37 = bf16[4,32,2048]{2,1,0:T(8,128)(2,1)S(1)} collective-permute-done((bf16[4,32,2048]{2,1,0:T(8,128)(2,1)S(1)}, bf16[4,32,2048]{2,1,0:T(8,128)(2,1)S(1)}, u32[]{:S(2)}, u32[]{:S(2)}) %collective-permute-start.37) | collective-permute-done | bytes 524320 | tf_op jit(solution)/shard_map/ppermute | solution.py:136
  241.2 2.9 %collective-permute-start.42 = (bf16[32,2048]{1,0:T(8,128)(2,1)S(1)}, bf16[32,2048]{1,0:T(8,128)(2,1)S(1)}, u32[]{:S(2)}, u32[]{:S(2)}) collective-permute-start(bf16[32,2048]{1,0:T(8,128)(2,1)S(1)} %get-tuple-element.60), channel_id=1, source_target_pairs={{4,0},{5,1},{6,2},{7,3},{8,4},{9,5},{10,6},{11,7},{12,8},{13,9},{1... | collective-permute-start | bytes 393224 | tf_op jit(solution)/shard_map/ppermute | solution.py:112
  244.1 2.5 collective-permute-done.51
  248.6 2.2 collective-permute-start.56
  252.3 3.2 %collective-permute-done.54 = bf16[32,2048]{1,0:T(8,128)(2,1)S(1)} collective-permute-done((bf16[32,2048]{1,0:T(8,128)(2,1)S(1)}, bf16[32,2048]{1,0:T(8,128)(2,1)S(1)}, u32[]{:S(2)}, u32[]{:S(2)}) %collective-permute-start.54) | collective-permute-done | bytes 131104 | tf_op jit(solution)/shard_map/ppermute | solution.py:112
  255.5 4.7 %collective-permute-done.55 = bf16[32,2048]{1,0:T(8,128)(2,1)S(1)} collective-permute-done((bf16[32,2048]{1,0:T(8,128)(2,1)S(1)}, bf16[32,2048]{1,0:T(8,128)(2,1)S(1)}, u32[]{:S(2)}, u32[]{:S(2)}) %collective-permute-start.55) | collective-permute-done | bytes 131104 | tf_op jit(solution)/shard_map/ppermute | solution.py:112
  (232 shorter events, 71.0 us)
Async XLA Ops:
  5.9 90.8 %collective-permute-start.24 = (bf16[768,2048]{1,0:T(8,128)(2,1)}, bf16[768,2048]{1,0:T(8,128)(2,1)}, u32[]{:S(2)}, u32[]{:S(2)}) collective-permute-start(bf16[768,2048]{1,0:T(8,128)(2,1)} %pad_select_fusion.refs_10_), channel_id=1, source_target_pairs={{1,0},{0,1},{3,2},{2,3},{5,4},{4,5},{7,6},{6,7},{9,8},{8,9},{11,10... | collective-permute-start | bytes 9437192 | tf_op jit(solution)/shard_map/ppermute | solution.py:132
  19.2 21.1 %collective-permute-start.1 = (bf16[1024,128]{1,0:T(8,128)(2,1)S(1)}, bf16[1024,128]{1,0:T(8,128)(2,1)}, u32[]{:S(2)}, u32[]{:S(2)}) collective-permute-start(bf16[1024,128]{1,0:T(8,128)(2,1)S(1)} %copy-done.2), channel_id=1, source_target_pairs={{8,0},{9,1},{10,2},{11,3},{12,4},{13,5},{14,6},{15,7},{0,8},{1,9},... | collective-permute-start | bytes 786440 | tf_op jit(solution)/shard_map/ppermute | solution.py:112
  23.1 22.1 %collective-permute-start.2 = (bf16[1024,128]{1,0:T(8,128)(2,1)S(1)}, bf16[1024,128]{1,0:T(8,128)(2,1)S(1)}, u32[]{:S(2)}, u32[]{:S(2)}) collective-permute-start(bf16[1024,128]{1,0:T(8,128)(2,1)S(1)} %copy-done.2), channel_id=1, source_target_pairs={{12,0},{13,1},{14,2},{15,3},{0,4},{1,5},{2,6},{3,7},{4,8},{5,9},{6... | collective-permute-start | bytes 786440 | tf_op jit(solution)/shard_map/ppermute | solution.py:112
  24.7 21.2 %collective-permute-start.3 = (bf16[1024,128]{1,0:T(8,128)(2,1)S(1)}, bf16[1024,128]{1,0:T(8,128)(2,1)S(1)}, u32[]{:S(2)}, u32[]{:S(2)}) collective-permute-start(bf16[1024,128]{1,0:T(8,128)(2,1)S(1)} %copy-done.2), channel_id=1, source_target_pairs={{2,0},{3,1},{0,2},{1,3},{6,4},{7,5},{4,6},{5,7},{10,8},{11,9},{8,1... | collective-permute-start | bytes 786440 | tf_op jit(solution)/shard_map/ppermute | solution.py:122
  26.0 19.9 %collective-permute-start.7 = (bf16[1024,128]{1,0:T(8,128)(2,1)S(1)}, bf16[1024,128]{1,0:T(8,128)(2,1)S(1)}, u32[]{:S(2)}, u32[]{:S(2)}) collective-permute-start(bf16[1024,128]{1,0:T(8,128)(2,1)S(1)} %copy-done.2), channel_id=1, source_target_pairs={{1,0},{0,1},{3,2},{2,3},{5,4},{4,5},{7,6},{6,7},{9,8},{8,9},{11,10... | collective-permute-start | bytes 786440 | tf_op jit(solution)/shard_map/ppermute | solution.py:132
  45.9 14.3 %collective-permute-start.8 = (bf16[1024,128]{1,0:T(8,128)(2,1)}, bf16[1024,128]{1,0:T(8,128)(2,1)S(1)}, u32[]{:S(2)}, u32[]{:S(2)}) collective-permute-start(bf16[1024,128]{1,0:T(8,128)(2,1)} %collective-permute-done.refs_1_), channel_id=1, source_target_pairs={{1,0},{0,1},{3,2},{2,3},{5,4},{4,5},{7,6},{6,7},{9,8},{8,9},{11,10... | collective-permute-start | bytes 786440 | tf_op jit(solution)/shard_map/ppermute | solution.py:132
  58.2 28.2 %collective-permute-start.22 = (bf16[1024,768]{1,0:T(8,128)(2,1)S(1)}, bf16[1024,768]{1,0:T(8,128)(2,1)}, u32[]{:S(2)}, u32[]{:S(2)}) collective-permute-start(bf16[1024,768]{1,0:T(8,128)(2,1)S(1)} %get-tuple-element.55.refs_6_), channel_id=1, source_target_pairs={{1,0},{0,1},{3,2},{2,3},{5,4},{4,5},{7,6},{6,7},{9,8},{8,9},{11,10... | collective-permute-start | bytes 4718600 | tf_op jit(solution)/shard_map/ppermute | solution.py:132
  58.2 28.2 %collective-permute-start.23 = (bf16[1024,768]{1,0:T(8,128)(2,1)S(1)}, bf16[1024,768]{1,0:T(8,128)(2,1)}, u32[]{:S(2)}, u32[]{:S(2)}) collective-permute-start(bf16[1024,768]{1,0:T(8,128)(2,1)S(1)} %get-tuple-element.54.refs_8_), channel_id=1, source_target_pairs={{1,0},{0,1},{3,2},{2,3},{5,4},{4,5},{7,6},{6,7},{9,8},{8,9},{11,10... | collective-permute-start | bytes 4718600 | tf_op jit(solution)/shard_map/ppermute | solution.py:132
  59.7 37.1 %collective-permute-start.15 = (bf16[1024,768]{1,0:T(8,128)(2,1)}, bf16[1024,768]{1,0:T(8,128)(2,1)}, u32[]{:S(2)}, u32[]{:S(2)}) collective-permute-start(bf16[1024,768]{1,0:T(8,128)(2,1)} %get-tuple-element.56), channel_id=1, source_target_pairs={{0,16},{16,0},{1,17},{17,1},{2,18},{18,2},{3,19},{19,3},{4,20},{20... | collective-permute-start | bytes 4718600 | tf_op jit(solution)/shard_map/ppermute | solution.py:136
  104.6 35.2 %collective-permute-start.33 = (bf16[1024,768]{1,0:T(8,128)(2,1)S(1)}, bf16[1024,768]{1,0:T(8,128)(2,1)}, u32[]{:S(2)}, u32[]{:S(2)}) collective-permute-start(bf16[1024,768]{1,0:T(8,128)(2,1)S(1)} %copy-done.26), channel_id=1, source_target_pairs={{0,16},{16,0},{1,17},{17,1},{2,18},{18,2},{3,19},{19,3},{4,20},{20... | collective-permute-start | bytes 4718600 | tf_op jit(solution)/shard_map/ppermute | solution.py:136
  105.5 34.2 %collective-permute-start.26 = (bf16[32,2048]{1,0:T(8,128)(2,1)S(1)}, bf16[32,2048]{1,0:T(8,128)(2,1)S(1)}, u32[]{:S(2)}, u32[]{:S(2)}) collective-permute-start(bf16[32,2048]{1,0:T(8,128)(2,1)S(1)} %get-tuple-element.68), channel_id=1, source_target_pairs={{4,0},{5,1},{6,2},{7,3},{8,4},{9,5},{10,6},{11,7},{12,8},{13,9},{1... | collective-permute-start | bytes 393224 | tf_op jit(solution)/shard_map/ppermute | solution.py:112
  105.6 34.2 %collective-permute-start.27 = (bf16[32,2048]{1,0:T(8,128)(2,1)S(1)}, bf16[32,2048]{1,0:T(8,128)(2,1)S(1)}, u32[]{:S(2)}, u32[]{:S(2)}) collective-permute-start(bf16[32,2048]{1,0:T(8,128)(2,1)S(1)} %get-tuple-element.68), channel_id=1, source_target_pairs={{8,0},{9,1},{10,2},{11,3},{12,4},{13,5},{14,6},{15,7},{0,8},{1,9},... | collective-permute-start | bytes 393224 | tf_op jit(solution)/shard_map/ppermute | solution.py:112
  106.5 34.2 %collective-permute-start.28 = (bf16[32,2048]{1,0:T(8,128)(2,1)S(1)}, bf16[32,2048]{1,0:T(8,128)(2,1)S(1)}, u32[]{:S(2)}, u32[]{:S(2)}) collective-permute-start(bf16[32,2048]{1,0:T(8,128)(2,1)S(1)} %get-tuple-element.68), channel_id=1, source_target_pairs={{12,0},{13,1},{14,2},{15,3},{0,4},{1,5},{2,6},{3,7},{4,8},{5,9},{6... | collective-permute-start | bytes 393224 | tf_op jit(solution)/shard_map/ppermute | solution.py:112
  107.6 77.7 %collective-permute-start.34 = (bf16[1024,768]{1,0:T(8,128)(2,1)}, bf16[1024,768]{1,0:T(8,128)(2,1)}, u32[]{:S(2)}, u32[]{:S(2)}) collective-permute-start(bf16[1024,768]{1,0:T(8,128)(2,1)} %collective-permute-done.15.refs_7_), channel_id=1, source_target_pairs={{1,0},{0,1},{3,2},{2,3},{5,4},{4,5},{7,6},{6,7},{9,8},{8,9},{11,10... | collective-permute-start | bytes 4718600 | tf_op jit(solution)/shard_map/ppermute | solution.py:132
  139.8 45.6 %collective-permute-start.35 = (bf16[1024,768]{1,0:T(8,128)(2,1)}, bf16[1024,768]{1,0:T(8,128)(2,1)}, u32[]{:S(2)}, u32[]{:S(2)}) collective-permute-start(bf16[1024,768]{1,0:T(8,128)(2,1)} %collective-permute-done.33.refs_9_), channel_id=1, source_target_pairs={{1,0},{0,1},{3,2},{2,3},{5,4},{4,5},{7,6},{6,7},{9,8},{8,9},{11,10... | collective-permute-start | bytes 4718600 | tf_op jit(solution)/shard_map/ppermute | solution.py:132
  139.8 13.2 %collective-permute-start.44 = (bf16[32,2048]{1,0:T(8,128)(2,1)S(1)}, bf16[32,2048]{1,0:T(8,128)(2,1)S(1)}, u32[]{:S(2)}, u32[]{:S(2)}) collective-permute-start(bf16[32,2048]{1,0:T(8,128)(2,1)S(1)} %get-tuple-element.67), channel_id=1, source_target_pairs={{8,0},{9,1},{10,2},{11,3},{12,4},{13,5},{14,6},{15,7},{0,8},{1,9},... | collective-permute-start | bytes 393224 | tf_op jit(solution)/shard_map/ppermute | solution.py:112
  140.7 14.6 %collective-permute-start.45 = (bf16[32,2048]{1,0:T(8,128)(2,1)S(1)}, bf16[32,2048]{1,0:T(8,128)(2,1)S(1)}, u32[]{:S(2)}, u32[]{:S(2)}) collective-permute-start(bf16[32,2048]{1,0:T(8,128)(2,1)S(1)} %get-tuple-element.67), channel_id=1, source_target_pairs={{12,0},{13,1},{14,2},{15,3},{0,4},{1,5},{2,6},{3,7},{4,8},{5,9},{6... | collective-permute-start | bytes 393224 | tf_op jit(solution)/shard_map/ppermute | solution.py:112
  146.2 14.8 %collective-permute-start.29 = (bf16[4,32,2048]{2,1,0:T(8,128)(2,1)S(1)}, bf16[4,32,2048]{2,1,0:T(8,128)(2,1)S(1)}, u32[]{:S(2)}, u32[]{:S(2)}) collective-permute-start(bf16[4,32,2048]{2,1,0:T(8,128)(2,1)S(1)} %pad_maximum_fusion), channel_id=1, source_target_pairs={{0,16},{16,0},{1,17},{17,1},{2,18},{18,2},{3,19},{19,3},{4,20},{20... | collective-permute-start | bytes 1572872 | tf_op jit(solution)/shard_map/ppermute | solution.py:136
  153.0 14.8 %collective-permute-start.30 = (bf16[4,32,2048]{2,1,0:T(8,128)(2,1)S(1)}, bf16[4,32,2048]{2,1,0:T(8,128)(2,1)S(1)}, u32[]{:S(2)}, u32[]{:S(2)}) collective-permute-start(bf16[4,32,2048]{2,1,0:T(8,128)(2,1)S(1)} %pad_maximum_fusion), channel_id=1, source_target_pairs={{2,0},{3,1},{0,2},{1,3},{6,4},{7,5},{4,6},{5,7},{10,8},{11,9},{8,1... | collective-permute-start | bytes 1572872 | tf_op jit(solution)/shard_map/ppermute | solution.py:122
  156.2 14.9 %collective-permute-start.46 = (bf16[4,32,2048]{2,1,0:T(8,128)(2,1)}, bf16[4,32,2048]{2,1,0:T(8,128)(2,1)}, u32[]{:S(2)}, u32[]{:S(2)}) collective-permute-start(bf16[4,32,2048]{2,1,0:T(8,128)(2,1)} %pad_maximum_fusion.3), channel_id=1, source_target_pairs={{0,16},{16,0},{1,17},{17,1},{2,18},{18,2},{3,19},{19,3},{4,20},{20... | collective-permute-start | bytes 1572872 | tf_op jit(solution)/shard_map/ppermute | solution.py:136
  161.0 18.2 %collective-permute-start.47 = (bf16[4,32,2048]{2,1,0:T(8,128)(2,1)}, bf16[4,32,2048]{2,1,0:T(8,128)(2,1)}, u32[]{:S(2)}, u32[]{:S(2)}) collective-permute-start(bf16[4,32,2048]{2,1,0:T(8,128)(2,1)} %pad_maximum_fusion.3), channel_id=1, source_target_pairs={{2,0},{3,1},{0,2},{1,3},{6,4},{7,5},{4,6},{5,7},{10,8},{11,9},{8,1... | collective-permute-start | bytes 1572872 | tf_op jit(solution)/shard_map/ppermute | solution.py:122
  167.8 17.0 %collective-permute-start.31 = (bf16[4,16,2048]{2,1,0:T(8,128)(2,1)}, bf16[4,16,2048]{2,1,0:T(8,128)(2,1)}, u32[]{:S(2)}, u32[]{:S(2)}) collective-permute-start(bf16[4,16,2048]{2,1,0:T(8,128)(2,1)} %slice.163), channel_id=1, source_target_pairs={{2,0},{3,1},{0,2},{1,3},{6,4},{7,5},{4,6},{5,7},{10,8},{11,9},{8,1... | collective-permute-start | bytes 786440 | tf_op jit(solution)/shard_map/ppermute | solution.py:122
  171.1 14.3 %collective-permute-start.32 = (bf16[4,16,2048]{2,1,0:T(8,128)(2,1)}, bf16[4,16,2048]{2,1,0:T(8,128)(2,1)}, u32[]{:S(2)}, u32[]{:S(2)}) collective-permute-start(bf16[4,16,2048]{2,1,0:T(8,128)(2,1)} %slice.164), channel_id=1, source_target_pairs={{0,16},{16,0},{1,17},{17,1},{2,18},{18,2},{3,19},{19,3},{4,20},{20... | collective-permute-start | bytes 786440 | tf_op jit(solution)/shard_map/ppermute | solution.py:136
  179.2 26.5 %collective-permute-start.48 = (bf16[4,16,2048]{2,1,0:T(8,128)(2,1)S(1)}, bf16[4,16,2048]{2,1,0:T(8,128)(2,1)S(1)}, u32[]{:S(2)}, u32[]{:S(2)}) collective-permute-start(bf16[4,16,2048]{2,1,0:T(8,128)(2,1)S(1)} %slice.174), channel_id=1, source_target_pairs={{2,0},{3,1},{0,2},{1,3},{6,4},{7,5},{4,6},{5,7},{10,8},{11,9},{8,1... | collective-permute-start | bytes 786440 | tf_op jit(solution)/shard_map/ppermute | solution.py:122
  184.8 20.8 %collective-permute-start.49 = (bf16[4,16,2048]{2,1,0:T(8,128)(2,1)S(1)}, bf16[4,16,2048]{2,1,0:T(8,128)(2,1)S(1)}, u32[]{:S(2)}, u32[]{:S(2)}) collective-permute-start(bf16[4,16,2048]{2,1,0:T(8,128)(2,1)S(1)} %slice.175), channel_id=1, source_target_pairs={{0,16},{16,0},{1,17},{17,1},{2,18},{18,2},{3,19},{19,3},{4,20},{20... | collective-permute-start | bytes 786440 | tf_op jit(solution)/shard_map/ppermute | solution.py:136
  202.5 17.6 %collective-permute-start.36 = (bf16[64,2048]{1,0:T(8,128)(2,1)S(1)}, bf16[64,2048]{1,0:T(8,128)(2,1)S(1)}, u32[]{:S(2)}, u32[]{:S(2)}) collective-permute-start(bf16[64,2048]{1,0:T(8,128)(2,1)S(1)} %get-tuple-element.39), channel_id=1, source_target_pairs={{2,0},{3,1},{0,2},{1,3},{6,4},{7,5},{4,6},{5,7},{10,8},{11,9},{8,1... | collective-permute-start | bytes 786440 | tf_op jit(solution)/shard_map/ppermute | solution.py:122
  204.1 17.7 %collective-permute-start.38 = (bf16[64,2048]{1,0:T(8,128)(2,1)S(1)}, bf16[64,2048]{1,0:T(8,128)(2,1)S(1)}, u32[]{:S(2)}, u32[]{:S(2)}) collective-permute-start(bf16[64,2048]{1,0:T(8,128)(2,1)S(1)} %get-tuple-element.41), channel_id=1, source_target_pairs={{0,16},{16,0},{1,17},{17,1},{2,18},{18,2},{3,19},{19,3},{4,20},{20... | collective-permute-start | bytes 786440 | tf_op jit(solution)/shard_map/ppermute | solution.py:136
  220.2 19.8 %collective-permute-start.37 = (bf16[4,32,2048]{2,1,0:T(8,128)(2,1)S(1)}, bf16[4,32,2048]{2,1,0:T(8,128)(2,1)S(1)}, u32[]{:S(2)}, u32[]{:S(2)}) collective-permute-start(bf16[4,32,2048]{2,1,0:T(8,128)(2,1)S(1)} %pad_maximum_fusion.1), channel_id=1, source_target_pairs={{0,16},{16,0},{1,17},{17,1},{2,18},{18,2},{3,19},{19,3},{4,20},{20... | collective-permute-start | bytes 1572872 | tf_op jit(solution)/shard_map/ppermute | solution.py:136
  221.8 18.1 %collective-permute-start.39 = (bf16[4,32,2048]{2,1,0:T(8,128)(2,1)S(1)}, bf16[4,32,2048]{2,1,0:T(8,128)(2,1)S(1)}, u32[]{:S(2)}, u32[]{:S(2)}) collective-permute-start(bf16[4,32,2048]{2,1,0:T(8,128)(2,1)S(1)} %pad_maximum_fusion.2), channel_id=1, source_target_pairs={{2,0},{3,1},{0,2},{1,3},{6,4},{7,5},{4,6},{5,7},{10,8},{11,9},{8,1... | collective-permute-start | bytes 1572872 | tf_op jit(solution)/shard_map/ppermute | solution.py:122
  228.2 18.4 %collective-permute-start.51 = (bf16[4,32,2048]{2,1,0:T(8,128)(2,1)S(1)}, bf16[4,32,2048]{2,1,0:T(8,128)(2,1)S(1)}, u32[]{:S(2)}, u32[]{:S(2)}) collective-permute-start(bf16[4,32,2048]{2,1,0:T(8,128)(2,1)S(1)} %pad_maximum_fusion.4), channel_id=1, source_target_pairs={{0,16},{16,0},{1,17},{17,1},{2,18},{18,2},{3,19},{19,3},{4,20},{20... | collective-permute-start | bytes 1572872 | tf_op jit(solution)/shard_map/ppermute | solution.py:136
  228.9 17.7 %collective-permute-start.53 = (bf16[4,32,2048]{2,1,0:T(8,128)(2,1)S(1)}, bf16[4,32,2048]{2,1,0:T(8,128)(2,1)S(1)}, u32[]{:S(2)}, u32[]{:S(2)}) collective-permute-start(bf16[4,32,2048]{2,1,0:T(8,128)(2,1)S(1)} %pad_maximum_fusion.5), channel_id=1, source_target_pairs={{2,0},{3,1},{0,2},{1,3},{6,4},{7,5},{4,6},{5,7},{10,8},{11,9},{8,1... | collective-permute-start | bytes 1572872 | tf_op jit(solution)/shard_map/ppermute | solution.py:122
  247.0 13.3 %collective-permute-start.55 = (bf16[32,2048]{1,0:T(8,128)(2,1)S(1)}, bf16[32,2048]{1,0:T(8,128)(2,1)S(1)}, u32[]{:S(2)}, u32[]{:S(2)}) collective-permute-start(bf16[32,2048]{1,0:T(8,128)(2,1)S(1)} %get-tuple-element.64), channel_id=1, source_target_pairs={{8,0},{9,1},{10,2},{11,3},{12,4},{13,5},{14,6},{15,7},{0,8},{1,9},... | collective-permute-start | bytes 393224 | tf_op jit(solution)/shard_map/ppermute | solution.py:112
  (62 other events, 483.4 us)

commit v3 on v2

--- a/solution.py
+++ b/solution.py
@@ -180,11 +180,11 @@
     )(context, *pieces)
 
 
-def experts_kernel(
-    tile, out_tile, count, *refs
-):
-    pieces, share, weights = refs[:count], refs[count], refs[count + 1 : count + 11]
-    outs, refs = refs[count + 11 : 2 * count + 11], refs[2 * count + 11 :]
+def experts_kernel(tile, out_tile, count, n_gate, n_up, *refs):
+    per_expert = n_gate + n_up + 1
+    pieces, refs = refs[:count], refs[count:]
+    share, weights, refs = refs[0], refs[1 : 1 + 2 * per_expert], refs[1 + 2 * per_expert :]
+    outs, refs = refs[:count], refs[count:]
     rows, gate, up, down, mid, row_sem, weight_sem, down_sem = refs
     x = lax.axis_index("dp")
     feats = rows.shape[1]
@@ -211,32 +211,36 @@
         at += part
     weight_copies = []
     down_copies = []
+    sem = 0
     for e in range(2):
-        gate_own, gate_far, up_own, up_far, down_e = weights[5 * e : 5 * e + 5]
+        mine = weights[e * per_expert : (e + 1) * per_expert]
         for j in range(tiles):
             group = []
-            for n, (source, target, s) in enumerate(
-                (
-                    (gate_own, gate, 0),
-                    (gate_far, gate, 1),
-                    (up_own, up, 0),
-                    (up_far, up, 1),
-                )
-            ):
-                copy = pltpu.make_async_copy(
-                    source.at[:, pl.ds(j * tile, tile)],
-                    target.at[e, pl.ds(s * half, half), pl.ds(j * tile, tile)],
-                    weight_sem.at[(e * tiles + j) * 4 + n],
-                )
-                copy.start()
-                group.append(copy)
+            for sources, target in ((mine[:n_gate], gate), (mine[n_gate:-1], up)):
+                depth_at = 0
+                for source in sources:
+                    copy = pltpu.make_async_copy(
+                        source.at[:, pl.ds(j * tile, tile)],
+                        target.at[e, pl.ds(depth_at, source.shape[0]), pl.ds(j * tile, tile)],
+                        weight_sem.at[sem],
+                    )
+                    copy.start()
+                    group.append(copy)
+                    depth_at += source.shape[0]
+                    sem += 1
             weight_copies.append(group)
+    units = weights[-1].shape[0]
+    spare = width - units
     for e in range(2):
+        start = pl.multiple_of(e * width + x * spare, 16)
         copy = pltpu.make_async_copy(
-            weights[5 * e + 4], down.at[pl.ds(e * width, width), :], down_sem.at[e]
+            weights[(e + 1) * per_expert - 1], down.at[pl.ds(start, units), :], down_sem.at[e]
         )
         copy.start()
         down_copies.append(copy)
+        if spare:
+            blank = pl.multiple_of(e * width + (1 - x) * units, 16)
+            down[pl.ds(blank, spare), :] = jnp.zeros((spare, feats), down.dtype)
 
     for copy in row_copies:
         copy.wait()
@@ -259,20 +263,24 @@
             out[:, lanes] = total[first : first + part].astype(out.dtype)
 
 
-def run_experts(pieces, kinds, share, weights):
+def run_experts(pieces, kinds, share, experts_weights):
     feats = pieces[0].shape[1]
-    half, width = weights[0].shape
+    width = experts_weights[0][0][0].shape[1]
+    n_gate, n_up = len(experts_weights[0][0]), len(experts_weights[0][1])
+    weights = [
+        array for gate, up, down in experts_weights for array in list(gate) + list(up) + [down]
+    ]
     count = len(pieces)
     total = sum(piece.shape[0] for piece in pieces)
     tile = 256
     any_spec = pl.BlockSpec(memory_space=pl.ANY)
     vmem_spec = pl.BlockSpec(memory_space=pltpu.VMEM)
     return pl.pallas_call(
-        functools.partial(experts_kernel, tile, 512, count),
+        functools.partial(experts_kernel, tile, 512, count, n_gate, n_up),
         out_shape=tuple(
             jax.ShapeDtypeStruct(piece.shape, kind) for piece, kind in zip(pieces, kinds)
         ),
-        in_specs=[any_spec] * count + [vmem_spec] + [any_spec] * 10,
+        in_specs=[any_spec] * count + [vmem_spec] + [any_spec] * len(weights),
         out_specs=(vmem_spec,) * count,
         scratch_shapes=[
             pltpu.VMEM((total, feats), jnp.bfloat16),
@@ -281,10 +289,10 @@
             pltpu.VMEM((2 * width, feats), jnp.bfloat16),
             pltpu.VMEM((total, 2 * width), jnp.bfloat16),
             pltpu.SemaphoreType.DMA((2 * count,)),
-            pltpu.SemaphoreType.DMA((8 * (width // tile),)),
+            pltpu.SemaphoreType.DMA((2 * (n_gate + n_up) * (width // tile),)),
             pltpu.SemaphoreType.DMA((2,)),
         ],
-        compiler_params=pltpu.CompilerParams(vmem_limit_bytes=40 * MIB),
+        compiler_params=pltpu.CompilerParams(vmem_limit_bytes=34 * MIB),
         cost_estimate=pl.CostEstimate(
             flops=2 * total * feats * width * 6,
             bytes_accessed=12 * feats * width + 12 * total * feats,
@@ -321,90 +329,115 @@
     units_here = w_down.shape[1]
     width = -(-units_here // 256) * 256
 
-    def halves(weights):
-        low, high = weights[:, :width], weights[:, units - width :]
-        return jnp.where(first, low, high), jnp.where(first, high, low)
-
-    gate_own, gate_sent = halves(w_gate[0])
-    up_own, up_sent = halves(w_up[0])
-    gate_far = flip_x(gate_sent)
-    blank = jnp.zeros((width - units_here, feats), w_down.dtype)
-    down_own = jnp.where(
-        first,
-        jnp.concatenate([w_down[0], blank], axis=0),
-        jnp.concatenate([blank, w_down[0]], axis=0),
-    )
-    gate_own_core = flip_core(gate_own, depth)
-    up_own_core = flip_core(up_own, depth)
-    down_own_core = flip_core(down_own, depth)
+    def own_part(weights):
+        return jnp.where(first, weights[:, :width], weights[:, units - width :])
+
+    def sent_part(weights):
+        return jnp.where(first, weights[:, units - width :], weights[:, :width])
+
+    deep = w_gate.shape[1] * 5 // 8
+    gate_sent = [sent_part(w_gate[0, :deep]), sent_part(w_gate[0, deep:])]
+    gate_own = own_part(w_gate[0])
+    gate_far = [flip_x(piece) for piece in gate_sent]
 
     near = [w_out] + [shift_z(w_out, depth, s) for s in range(1, depth)]
-    across = [flip_y(piece, depth) for piece in near]
+    across_own = flip_y(w_out, depth)
+
+    queries, gate_sent[0], gate_sent[1], gate_own = lax.optimization_barrier(
+        (queries, gate_sent[0], gate_sent[1], gate_own)
+    )
+    context = attend(queries, kv_pool, page_table, ctx_lens)
+    near[1:], across_own, gate_far[0], context, w_up, w_down, route_weights, gate_own = (
+        lax.optimization_barrier(
+            (
+                near[1:],
+                across_own,
+                gate_far[0],
+                context,
+                w_up,
+                w_down,
+                route_weights,
+                gate_own,
+            )
+        )
+    )
+    across = [across_own] + [flip_y(piece, depth) for piece in near[1:]]
+    across[1], across[2], across[3], gate_far[1] = lax.optimization_barrier(
+        (across[1], across[2], across[3], gate_far[1])
+    )
     columns = near + across
     columns = columns + [flip_core(piece, depth) for piece in columns]
+
+    deep = w_up.shape[1] // 2
+    up_sent = [sent_part(w_up[0, :deep]), sent_part(w_up[0, deep:])]
+    up_own = own_part(w_up[0])
+    down_own = w_down[0]
+    here_core = [flip_core(array, depth) for array in (gate_own, up_own, down_own)]
 
     named = expert_ids[:, :, None] == jnp.arange(experts, dtype=jnp.int32)[None, None, :]
     share = jnp.sum(jnp.where(named, route_weights[:, :, None], 0.0), axis=1)
     both = jnp.stack([me, me + 1 - 2 * c])
-    pick = both[None, :] == jnp.arange(experts, dtype=jnp.int32)[:, None]
+    pick = both[:, None] == jnp.arange(experts, dtype=jnp.int32)[None, :]
     share_l = jnp.stack([share] + [shift_z(share, depth, s) for s in range(1, depth)])
     share_x = flip_x(share_l)
     share_y = flip_y(share_l, depth)
     share_d = flip_y(share_x, depth)
     shares = jnp.stack([share_l, share_x, share_y, share_d])
-    shares = jnp.sum(jnp.where(pick[:, None, :].swapaxes(0, 1), shares[..., None], 0.0), axis=-2)
-
-    context = attend(queries, kv_pool, page_table, ctx_lens)
+    shares = jnp.stack(
+        [jnp.sum(jnp.where(pick[i], shares, 0.0), axis=-1) for i in range(2)], axis=-1
+    )
+
     own, sent = project(context, columns, depth)
-    own, sent, gate_far, shares, gate_own_core, up_own_core, down_own_core = lax.optimization_barrier(
-        (own, sent, gate_far, shares, gate_own_core, up_own_core, down_own_core)
-    )
-    received, up_sent = lax.optimization_barrier((flip_x(sent), up_sent))
-    up_far = flip_x(up_sent)
-    weights = [gate_own, gate_far, up_own, up_far, down_own]
-    weights += [
-        gate_own_core,
-        flip_core(gate_far, depth),
-        up_own_core,
-        flip_core(up_far, depth),
-        down_own_core,
-    ]
+    own, sent, shares, here_core[0], here_core[1], here_core[2] = lax.optimization_barrier(
+        (own, sent, shares, here_core[0], here_core[1], here_core[2])
+    )
+    received, up_sent[0], up_sent[1] = lax.optimization_barrier(
+        (flip_x(sent), up_sent[0], up_sent[1])
+    )
+    up_far = [flip_x(piece) for piece in up_sent]
+    gate_far_core = [flip_core(piece, depth) for piece in gate_far]
     hidden_state = residual.astype(jnp.float32) + (own + received.astype(jnp.float32))
     moe_input = normalize(hidden_state, moe_gain).astype(jnp.bfloat16)
 
-    chunks = 2
-    rows = block // chunks
-    part = rows // 2
-    moe = []
-    for k in range(chunks):
-        mine = moe_input[rows * k : rows * (k + 1)]
-        line = jnp.stack([mine] + [shift_z(mine, depth, s) for s in range(1, depth)])
+    mid_z = depth // 2
+    ready = []
+    at = 0
+    arrived = [moe_input] + [shift_z(moe_input, depth, s) for s in range(1, depth)]
+    for rows in (block // 2, block // 2):
+        line = jnp.stack([piece[at : at + rows] for piece in arrived])
         line_x = flip_x(line)
         line_y = flip_y(line, depth)
-        low = flip_y(line_x[:, :part], depth)
-        high = flip_x(line_y[:, part:])
-        share = shares[:, :, rows * k : rows * (k + 1)]
-        share = jnp.concatenate(
-            [
-                share[:3].reshape(3 * depth * rows, 2),
-                share[3, :, :part].reshape(depth * part, 2),
-                share[3, :, part:].reshape(depth * part, 2),
-            ],
-            axis=0,
-        )
+        low = flip_y(line_x[:mid_z], depth)
+        high = flip_x(line_y[mid_z:])
+        share = shares[:, :, at : at + rows].reshape(4 * depth * rows, 2)
+        ready.append(([line, line_x, line_y, low, high], share))
+        at += rows
+
+    ready[0][0][1], up_far[0] = lax.optimization_barrier((ready[0][0][1], up_far[0]))
+    ready[0][0][3], ready[0][0][4], up_far[1] = lax.optimization_barrier(
+        (ready[0][0][3], ready[0][0][4], up_far[1])
+    )
+    up_far_core = [flip_core(piece, depth) for piece in up_far]
+    weights = [
+        ([gate_own] + gate_far, [up_own] + up_far, down_own),
+        ([here_core[0]] + gate_far_core, [here_core[1]] + up_far_core, here_core[2]),
+    ]
+
+    moe = []
+    for pieces, share in ready:
         out_l, out_x, out_y, out_low, out_high = run_experts(
-            [piece.reshape(-1, feats) for piece in (line, line_x, line_y, low, high)],
+            [piece.reshape(-1, feats) for piece in pieces],
             (jnp.float32, jnp.float32, jnp.float32, jnp.bfloat16, jnp.bfloat16),
             share,
             weights,
         )
-        out_l = out_l.reshape(line.shape)
-        out_x = out_x.reshape(line.shape)
-        out_y = out_y.reshape(line.shape)
-        back_low = flip_y(out_low, depth).reshape(low.shape).astype(jnp.float32)
-        back_high = flip_x(out_high).reshape(high.shape).astype(jnp.float32)
-        sum_x = jnp.concatenate([out_x[:, :part] + back_low, out_x[:, part:]], axis=1)
-        sum_y = jnp.concatenate([out_y[:, :part], out_y[:, part:] + back_high], axis=1)
+        out_l = out_l.reshape(pieces[0].shape)
+        out_x = out_x.reshape(pieces[0].shape)
+        out_y = out_y.reshape(pieces[0].shape)
+        back_low = flip_y(out_low, depth).reshape(pieces[3].shape).astype(jnp.float32)
+        back_high = flip_x(out_high).reshape(pieces[4].shape).astype(jnp.float32)
+        sum_x = jnp.concatenate([out_x[:mid_z] + back_low, out_x[mid_z:]], axis=0)
+        sum_y = jnp.concatenate([out_y[:mid_z], out_y[mid_z:] + back_high], axis=0)
         back_x = flip_x(sum_x.astype(jnp.bfloat16)).astype(jnp.float32)
         back_y = flip_y(sum_y.astype(jnp.bfloat16), depth).astype(jnp.float32)
         full = out_l + back_x + back_y

time: 262 us -> 255 us (0.973)
  waiting for transfers between devices: 134 us -> 126 us
  other arithmetic: 14.5 us -> 7.74 us
  starting transfers between devices: 52.1 us -> 56.9 us
  local copies, waits for them, and re-layouts: 26.2 us -> 30 us
    ppermute x18 -> x15, starting transfers between devices: 20.6 us -> 28.5 us  [shift_z(): return lax.ppermute(values, 'expert', pairs)]
    ppermute x14, starting transfers between devices: 19.1 us -> 11.4 us  [flip_y(): return lax.ppermute(values, 'expert', pairs)]
    ppermute x18 -> x15, waiting for transfers between devices: 38.1 us -> 30.5 us  [shift_z(): return lax.ppermute(values, 'expert', pairs)]
    select_n x3 -> x5, other arithmetic: 10.7 us -> 4.18 us  [the longest x3 3.83 us: sent_part(): return jnp.where(first, weights[:, units - width:], weights[:, :width])]
    ppermute x12 -> x14, starting transfers between devices: 9.74 us -> 15.2 us  [flip_x(): return lax.ppermute(values, 'dp', [(0, 1), (1, 0)])]
    squeeze x0 -> x4, local copies, waits for them, and re-layouts: none -> 4.93 us  [the longest x2 2.91 us: gathered(): gate_sent = [sent_part(w_gate[0, :deep]), sent_part(w_gate[0, deep:])]]
    ppermute x14, waiting for transfers between devices: 25.7 us -> 28.9 us  [flip_y(): return lax.ppermute(values, 'expert', pairs)]
    ppermute x12 -> x14, waiting for transfers between devices: 66.3 us -> 63.7 us  [flip_x(): return lax.ppermute(values, 'dp', [(0, 1), (1, 0)])]
  transfers between devices with their start and end apart: 57 -> 58, of which waited for: 27 -> 24; matrix products, arithmetic and copies ran while one was open for 12% -> 11% of each run, Pallas kernels for 11% -> 11%
where the time goes in v3:
time: 255 us
  waiting for transfers between devices  126 us (49%)
  starting transfers between devices  56.9 us (22%)
  local copies, waits for them, and re-layouts  30 us (12%)
  Pallas kernels  28.8 us (11%)
  other arithmetic  7.74 us (3%)
  matrix products  4.65 us (2%)
    ppermute x14, waiting for transfers between devices, flip_x(): return lax.ppermute(values, 'dp', [(0, 1), (1, 0)])  63.7 us
    ppermute x15, waiting for transfers between devices, shift_z(): return lax.ppermute(values, 'expert', pairs)  30.5 us
    ppermute x14, waiting for transfers between devices, flip_y(): return lax.ppermute(values, 'expert', pairs)  28.9 us
    ppermute x15, starting transfers between devices, shift_z(): return lax.ppermute(values, 'expert', pairs)  28.5 us
    pallas_call x2, Pallas kernels, run_experts(): pl.pallas_call(functools.partial(experts_kernel, tile, 512, count, n_gate...  26.3 us
    ppermute x14, starting transfers between devices, flip_x(): return lax.ppermute(values, 'dp', [(0, 1), (1, 0)])  15.2 us
    unnamed x82, local copies, waits for them, and re-layouts  14.6 us
    ppermute x14, starting transfers between devices, flip_y(): return lax.ppermute(values, 'expert', pairs)  11.4 us
  transfers between devices with their start and end apart: 58, of which 24 were waited for; matrix products, arithmetic and copies ran while one was open for 11% of the time, Pallas kernels for 11%

profile of v3, /device:TPU:0, one launch (start us, length us, event | category | flops | bytes accessed | tf_op | source)
XLA Modules:
  0.0 254.8 jit_solution(4820238623682719830)
XLA Ops:
  0.0 5.0 %collective-permute-start = (bf16[1024,128]{1,0:T(8,128)(2,1)}, bf16[1024,128]{1,0:T(8,128)(2,1)}, u32[]{:S(2)}, u32[]{:S(2)}) collective-permute-start(bf16[1024,128]{1,0:T(8,128)(2,1)} %refs_0_.1), channel_id=1, source_target_pairs={{4,0},{5,1},{6,2},{7,3},{8,4},{9,5},{10,6},{11,7},{12,8},{13,9},{1... | collective-permute-start | bytes 786440 | tf_op jit(solution)/shard_map/ppermute | solution.py:112
  7.6 2.8 %slice_bitcast_fusion = bf16[640,1408]{1,0:T(8,128)(2,1)} fusion(bf16[1,1024,1408]{2,1,0:T(8,128)(2,1)} %param.22), kind=kLoop, calls=%fused_computation.3 | loop fusion | bytes 3604480 | tf_op jit(solution)/shard_map/squeeze | solution.py:339
  10.4 2.7 %slice_select_fusion.2 = bf16[640,768]{1,0:T(8,128)(2,1)} fusion(bf16[640,1408]{1,0:T(8,128)(2,1)} %slice_bitcast_fusion, pred[]{:T(512)S(6)} %eq.16), kind=kLoop, calls=%fused_computation.23 | loop fusion | flops 491520 | bytes 2949121 | tf_op jit(solution)/shard_map/jit(_where)/select_n | solution.py:336
  15.8 3.1 %slice_bitcast_fusion.4 = (bf16[8,64,1024]{2,1,0:T(8,128)(2,1)}, bf16[8,64,1024]{2,1,0:T(8,128)(2,1)}) fusion(bf16[2,8,64,1024]{3,2,1,0:T(8,128)(2,1)} %param.14), kind=kLoop, calls=%fused_computation.21 | loop fusion | bytes 4194304 | tf_op jit(solution)/shard_map/squeeze | solution.py:31
  19.1 1.8 gather_fusion.1
  25.5 2.9 %fusion.20 = (f32[2,8,64]{2,1,0:T(8,128)S(1)}, f32[2,8,64,256]{3,2,1,0:T(8,128)}) fusion(pred[2,64,256]{2,1,0:T(8,128)(4,1)S(1)} %iota_compare_fusion, bf16[2,256,8,128]{3,2,1,0:T(8,128)(2,1)} %bitcast.132, bf16[2,64,8,128]{3,2,1,0:T(8,128)(2,1)S(1)} %bitcast.144), kind=kOutput, calls=%fused_computation.92 | convolution fusion | flops 68419840 | bytes 2396160 | tf_op jit(solution)/shard_map/sub | solution.py:39
  30.5 5.3 %collective-permute-done.4.refs_7_ = bf16[640,768]{1,0:T(8,128)(2,1)} collective-permute-done((bf16[640,768]{1,0:T(8,128)(2,1)}, bf16[640,768]{1,0:T(8,128)(2,1)}, u32[]{:S(2)}, u32[]{:S(2)}) %collective-permute-start.4) | collective-permute-done | bytes 983072 | tf_op jit(solution)/shard_map/ppermute | solution.py:136
  37.6 3.1 %collective-permute-start.17 = (f32[64,16]{0,1:T(8,128)S(1)}, f32[64,16]{0,1:T(8,128)S(1)}, u32[]{:S(2)}, u32[]{:S(2)}) collective-permute-start(f32[64,16]{0,1:T(8,128)S(1)} %select_reduce_fusion.2), channel_id=1, source_target_pairs={{4,0},{5,1},{6,2},{7,3},{8,4},{9,5},{10,6},{11,7},{12,8},{13,9},{1... | collective-permute-start | bytes 12296 | tf_op jit(solution)/shard_map/ppermute | solution.py:112
  45.8 2.0 collective-permute-done.19
  49.6 2.4 collective-permute-done.8.refs_8_
  54.5 4.7 %collective-permute-done.21 = f32[4,64,16]{1,2,0:T(8,128)S(1)} collective-permute-done((f32[4,64,16]{1,2,0:T(8,128)S(1)}, f32[4,64,16]{1,2,0:T(8,128)S(1)}, u32[]{:S(2)}, u32[]{:S(2)}) %collective-permute-start.21) | collective-permute-done | bytes 16416 | tf_op jit(solution)/shard_map/ppermute | solution.py:122
  61.2 7.4 %collective-permute-done.7.refs_7_ = bf16[1024,128]{1,0:T(8,128)(2,1)S(1)} collective-permute-done((bf16[1024,128]{1,0:T(8,128)(2,1)}, bf16[1024,128]{1,0:T(8,128)(2,1)S(1)}, u32[]{:S(2)}, u32[]{:S(2)}) %collective-permute-start.7) | collective-permute-done | bytes 262176 | tf_op jit(solution)/shard_map/ppermute | solution.py:122
  70.8 2.1 collective-permute-done.13.refs_12_
  73.8 2.0 slice_bitcast_fusion.1
  76.0 2.5 project.1
  79.4 7.8 %collective-permute-done.26 = bf16[64,2048]{1,0:T(8,128)(2,1)S(1)} collective-permute-done((bf16[64,2048]{1,0:T(8,128)(2,1)S(1)}, bf16[64,2048]{1,0:T(8,128)(2,1)S(1)}, u32[]{:S(2)}, u32[]{:S(2)}) %collective-permute-start.26) | collective-permute-done | bytes 262176 | tf_op jit(solution)/shard_map/ppermute | solution.py:136
  89.2 1.9 collective-permute-start.29
  91.7 4.5 %collective-permute-done.27 = bf16[64,2048]{1,0:T(8,128)(2,1)S(1)} collective-permute-done((bf16[64,2048]{1,0:T(8,128)(2,1)S(1)}, bf16[64,2048]{1,0:T(8,128)(2,1)S(1)}, u32[]{:S(2)}, u32[]{:S(2)}) %collective-permute-start.27) | collective-permute-done | bytes 262176 | tf_op jit(solution)/shard_map/ppermute | solution.py:112
  96.2 15.8 %collective-permute-done.28 = bf16[64,2048]{1,0:T(8,128)(2,1)S(1)} collective-permute-done((bf16[64,2048]{1,0:T(8,128)(2,1)S(1)}, bf16[64,2048]{1,0:T(8,128)(2,1)S(1)}, u32[]{:S(2)}, u32[]{:S(2)}) %collective-permute-start.28) | collective-permute-done | bytes 262176 | tf_op jit(solution)/shard_map/ppermute | solution.py:112
  118.0 9.1 %collective-permute-done.30 = bf16[4,32,2048]{2,1,0:T(8,128)(2,1)S(1)} collective-permute-done((bf16[4,32,2048]{2,1,0:T(8,128)(2,1)S(1)}, bf16[4,32,2048]{2,1,0:T(8,128)(2,1)S(1)}, u32[]{:S(2)}, u32[]{:S(2)}) %collective-permute-start.30) | collective-permute-done | bytes 524320 | tf_op jit(solution)/shard_map/ppermute | solution.py:136
  130.1 14.0 %collective-permute-done.35.refs_11_ = bf16[512,768]{1,0:T(8,128)(2,1)} collective-permute-done((bf16[512,768]{1,0:T(8,128)(2,1)S(1)}, bf16[512,768]{1,0:T(8,128)(2,1)}, u32[]{:S(2)}, u32[]{:S(2)}) %collective-permute-start.35) | collective-permute-done | bytes 786464 | tf_op jit(solution)/shard_map/ppermute | solution.py:136
  144.8 14.0 %collective-permute-done.34 = bf16[2,32,2048]{2,1,0:T(8,128)(2,1)S(1)} collective-permute-done((bf16[2,32,2048]{2,1,0:T(8,128)(2,1)S(1)}, bf16[2,32,2048]{2,1,0:T(8,128)(2,1)S(1)}, u32[]{:S(2)}, u32[]{:S(2)}) %collective-permute-start.34) | collective-permute-done | bytes 262176 | tf_op jit(solution)/shard_map/ppermute | solution.py:136
  162.3 11.8 %collective-permute-done.48 = bf16[4,32,2048]{2,1,0:T(8,128)(2,1)} collective-permute-done((bf16[4,32,2048]{2,1,0:T(8,128)(2,1)}, bf16[4,32,2048]{2,1,0:T(8,128)(2,1)}, u32[]{:S(2)}, u32[]{:S(2)}) %collective-permute-start.48) | collective-permute-done | bytes 524320 | tf_op jit(solution)/shard_map/ppermute | solution.py:122
  182.9 13.1 %experts.2 = (f32[128,2048]{1,0:T(8,128)S(1)}, f32[128,2048]{1,0:T(8,128)S(1)}, f32[128,2048]{1,0:T(8,128)S(1)}, bf16[64,2048]{1,0:T(8,128)(2,1)S(1)}, bf16[64,2048]{1,0:T(8,128)(2,1)S(1)}) custom-call(bf16[128,2048]{1,0:T(8,128)(2,1)S(1)} %bitcast.119, bf16[128,2048]{1,0:T(8,128)(2,1)S(1)} %bitcast.122, bf16[128,2048]{1,0:T(8,128)(2,1)S(1)} %bitcast.123, ...), custom_call_target="tpu_custom_call" | custom-call | flops 9663676416 | bytes 31457280 | tf_op jit(solution)/shard_map/experts/pallas_call | solution.py:278
  198.4 13.3 %experts.3 = (f32[128,2048]{1,0:T(8,128)S(1)}, f32[128,2048]{1,0:T(8,128)S(1)}, f32[128,2048]{1,0:T(8,128)S(1)}, bf16[64,2048]{1,0:T(8,128)(2,1)S(1)}, bf16[64,2048]{1,0:T(8,128)(2,1)S(1)}) custom-call(bf16[128,2048]{1,0:T(8,128)(2,1)} %bitcast.47.refs_0_, bf16[128,2048]{1,0:T(8,128)(2,1)} %bitcast.48.refs_1_, bf16[128,2048]{1,0:T(8,128)(2,1)} %bitcast.49.refs_2_, ...), custom_call_target="tpu_custom_call" | custom-call | flops 9663676416 | bytes 31457280 | tf_op jit(solution)/shard_map/experts/pallas_call | solution.py:278
  216.3 4.7 %collective-permute-done.51 = bf16[64,2048]{1,0:T(8,128)(2,1)S(1)} collective-permute-done((bf16[64,2048]{1,0:T(8,128)(2,1)S(1)}, bf16[64,2048]{1,0:T(8,128)(2,1)S(1)}, u32[]{:S(2)}, u32[]{:S(2)}) %collective-permute-start.51) | collective-permute-done | bytes 262176 | tf_op jit(solution)/shard_map/ppermute | solution.py:122
  223.3 9.3 %collective-permute-done.41 = bf16[4,32,2048]{2,1,0:T(8,128)(2,1)S(1)} collective-permute-done((bf16[4,32,2048]{2,1,0:T(8,128)(2,1)S(1)}, bf16[4,32,2048]{2,1,0:T(8,128)(2,1)S(1)}, u32[]{:S(2)}, u32[]{:S(2)}) %collective-permute-start.41) | collective-permute-done | bytes 524320 | tf_op jit(solution)/shard_map/ppermute | solution.py:136
  234.7 2.0 collective-permute-start.45
  236.7 2.8 %collective-permute-start.46 = (bf16[32,2048]{1,0:T(8,128)(2,1)S(1)}, bf16[32,2048]{1,0:T(8,128)(2,1)S(1)}, u32[]{:S(2)}, u32[]{:S(2)}) collective-permute-start(bf16[32,2048]{1,0:T(8,128)(2,1)S(1)} %get-tuple-element.102), channel_id=1, source_target_pairs={{4,0},{5,1},{6,2},{7,3},{8,4},{9,5},{10,6},{11,7},{12,8},{13,9},{1... | collective-permute-start | bytes 393224 | tf_op jit(solution)/shard_map/ppermute | solution.py:112
  242.7 2.0 collective-permute-start.56
  244.6 2.8 %collective-permute-start.57 = (bf16[32,2048]{1,0:T(8,128)(2,1)S(1)}, bf16[32,2048]{1,0:T(8,128)(2,1)S(1)}, u32[]{:S(2)}, u32[]{:S(2)}) collective-permute-start(bf16[32,2048]{1,0:T(8,128)(2,1)S(1)} %get-tuple-element.105), channel_id=1, source_target_pairs={{4,0},{5,1},{6,2},{7,3},{8,4},{9,5},{10,6},{11,7},{12,8},{13,9},{1... | collective-permute-start | bytes 393224 | tf_op jit(solution)/shard_map/ppermute | solution.py:112
  249.2 4.5 %collective-permute-done.56 = bf16[32,2048]{1,0:T(8,128)(2,1)S(1)} collective-permute-done((bf16[32,2048]{1,0:T(8,128)(2,1)S(1)}, bf16[32,2048]{1,0:T(8,128)(2,1)S(1)}, u32[]{:S(2)}, u32[]{:S(2)}) %collective-permute-start.56) | collective-permute-done | bytes 131104 | tf_op jit(solution)/shard_map/ppermute | solution.py:112
  (232 shorter events, 70.5 us)
Async XLA Ops:
  0.0 30.5 %collective-permute-start = (bf16[1024,128]{1,0:T(8,128)(2,1)}, bf16[1024,128]{1,0:T(8,128)(2,1)}, u32[]{:S(2)}, u32[]{:S(2)}) collective-permute-start(bf16[1024,128]{1,0:T(8,128)(2,1)} %refs_0_.1), channel_id=1, source_target_pairs={{4,0},{5,1},{6,2},{7,3},{8,4},{9,5},{10,6},{11,7},{12,8},{13,9},{1... | collective-permute-start | bytes 786440 | tf_op jit(solution)/shard_map/ppermute | solution.py:112
  5.0 25.4 %collective-permute-start.1 = (bf16[1024,128]{1,0:T(8,128)(2,1)}, bf16[1024,128]{1,0:T(8,128)(2,1)}, u32[]{:S(2)}, u32[]{:S(2)}) collective-permute-start(bf16[1024,128]{1,0:T(8,128)(2,1)} %refs_0_.1), channel_id=1, source_target_pairs={{8,0},{9,1},{10,2},{11,3},{12,4},{13,5},{14,6},{15,7},{0,8},{1,9},... | collective-permute-start | bytes 786440 | tf_op jit(solution)/shard_map/ppermute | solution.py:112
  5.1 25.4 %collective-permute-start.2 = (bf16[1024,128]{1,0:T(8,128)(2,1)}, bf16[1024,128]{1,0:T(8,128)(2,1)}, u32[]{:S(2)}, u32[]{:S(2)}) collective-permute-start(bf16[1024,128]{1,0:T(8,128)(2,1)} %refs_0_.1), channel_id=1, source_target_pairs={{12,0},{13,1},{14,2},{15,3},{0,4},{1,5},{2,6},{3,7},{4,8},{5,9},{6... | collective-permute-start | bytes 786440 | tf_op jit(solution)/shard_map/ppermute | solution.py:112
  6.1 24.4 %collective-permute-start.3 = (bf16[1024,128]{1,0:T(8,128)(2,1)}, bf16[1024,128]{1,0:T(8,128)(2,1)S(1)}, u32[]{:S(2)}, u32[]{:S(2)}) collective-permute-start(bf16[1024,128]{1,0:T(8,128)(2,1)} %refs_0_.1), channel_id=1, source_target_pairs={{2,0},{3,1},{0,2},{1,3},{6,4},{7,5},{4,6},{5,7},{10,8},{11,9},{8,1... | collective-permute-start | bytes 786440 | tf_op jit(solution)/shard_map/ppermute | solution.py:122
  13.2 22.7 %collective-permute-start.4 = (bf16[640,768]{1,0:T(8,128)(2,1)}, bf16[640,768]{1,0:T(8,128)(2,1)}, u32[]{:S(2)}, u32[]{:S(2)}) collective-permute-start(bf16[640,768]{1,0:T(8,128)(2,1)} %slice_select_fusion.2), channel_id=1, source_target_pairs={{0,16},{16,0},{1,17},{17,1},{2,18},{18,2},{3,19},{19,3},{4,20},{20... | collective-permute-start | bytes 2949128 | tf_op jit(solution)/shard_map/ppermute | solution.py:136
  35.9 42.8 %collective-permute-start.25 = (bf16[704,2048]{1,0:T(8,128)(2,1)}, bf16[704,2048]{1,0:T(8,128)(2,1)}, u32[]{:S(2)}, u32[]{:S(2)}) collective-permute-start(bf16[704,2048]{1,0:T(8,128)(2,1)} %bitcast.154), channel_id=1, source_target_pairs={{1,0},{0,1},{3,2},{2,3},{5,4},{4,5},{7,6},{6,7},{9,8},{8,9},{11,10... | collective-permute-start | bytes 8650760 | tf_op jit(solution)/shard_map/ppermute | solution.py:132
  35.9 16.2 %collective-permute-start.8 = (bf16[384,768]{1,0:T(8,128)(2,1)S(1)}, bf16[384,768]{1,0:T(8,128)(2,1)}, u32[]{:S(2)}, u32[]{:S(2)}) collective-permute-start(bf16[384,768]{1,0:T(8,128)(2,1)S(1)} %copy-done.30), channel_id=1, source_target_pairs={{0,16},{16,0},{1,17},{17,1},{2,18},{18,2},{3,19},{19,3},{4,20},{20... | collective-permute-start | bytes 1769480 | tf_op jit(solution)/shard_map/ppermute | solution.py:136
  45.3 14.5 %collective-permute-start.5 = (bf16[1024,128]{1,0:T(8,128)(2,1)}, bf16[1024,128]{1,0:T(8,128)(2,1)S(1)}, u32[]{:S(2)}, u32[]{:S(2)}) collective-permute-start(bf16[1024,128]{1,0:T(8,128)(2,1)} %collective-permute-done.refs_1_), channel_id=1, source_target_pairs={{2,0},{3,1},{0,2},{1,3},{6,4},{7,5},{4,6},{5,7},{10,8},{11,9},{8,1... | collective-permute-start | bytes 786440 | tf_op jit(solution)/shard_map/ppermute | solution.py:122
  47.8 12.4 %collective-permute-start.6 = (bf16[1024,128]{1,0:T(8,128)(2,1)}, bf16[1024,128]{1,0:T(8,128)(2,1)S(1)}, u32[]{:S(2)}, u32[]{:S(2)}) collective-permute-start(bf16[1024,128]{1,0:T(8,128)(2,1)} %collective-permute-done.1.refs_2_), channel_id=1, source_target_pairs={{2,0},{3,1},{0,2},{1,3},{6,4},{7,5},{4,6},{5,7},{10,8},{11,9},{8,1... | collective-permute-start | bytes 786440 | tf_op jit(solution)/shard_map/ppermute | solution.py:122
  88.9 23.2 %collective-permute-start.28 = (bf16[64,2048]{1,0:T(8,128)(2,1)S(1)}, bf16[64,2048]{1,0:T(8,128)(2,1)S(1)}, u32[]{:S(2)}, u32[]{:S(2)}) collective-permute-start(bf16[64,2048]{1,0:T(8,128)(2,1)S(1)} %multiply_convert_fusion.1), channel_id=1, source_target_pairs={{8,0},{9,1},{10,2},{11,3},{12,4},{13,5},{14,6},{15,7},{0,8},{1,9},... | collective-permute-start | bytes 786440 | tf_op jit(solution)/shard_map/ppermute | solution.py:112
  89.2 22.8 %collective-permute-start.29 = (bf16[64,2048]{1,0:T(8,128)(2,1)S(1)}, bf16[64,2048]{1,0:T(8,128)(2,1)S(1)}, u32[]{:S(2)}, u32[]{:S(2)}) collective-permute-start(bf16[64,2048]{1,0:T(8,128)(2,1)S(1)} %multiply_convert_fusion.1), channel_id=1, source_target_pairs={{12,0},{13,1},{14,2},{15,3},{0,4},{1,5},{2,6},{3,7},{4,8},{5,9},{6... | collective-permute-start | bytes 786440 | tf_op jit(solution)/shard_map/ppermute | solution.py:112
  91.2 38.9 %collective-permute-start.31 = (bf16[512,768]{1,0:T(8,128)(2,1)S(1)}, bf16[512,768]{1,0:T(8,128)(2,1)}, u32[]{:S(2)}, u32[]{:S(2)}) collective-permute-start(bf16[512,768]{1,0:T(8,128)(2,1)S(1)} %get-tuple-element.66), channel_id=1, source_target_pairs={{0,16},{16,0},{1,17},{17,1},{2,18},{18,2},{3,19},{19,3},{4,20},{20... | collective-permute-start | bytes 2359304 | tf_op jit(solution)/shard_map/ppermute | solution.py:136
  112.2 14.9 %collective-permute-start.30 = (bf16[4,32,2048]{2,1,0:T(8,128)(2,1)S(1)}, bf16[4,32,2048]{2,1,0:T(8,128)(2,1)S(1)}, u32[]{:S(2)}, u32[]{:S(2)}) collective-permute-start(bf16[4,32,2048]{2,1,0:T(8,128)(2,1)S(1)} %pad_maximum_fusion), channel_id=1, source_target_pairs={{0,16},{16,0},{1,17},{17,1},{2,18},{18,2},{3,19},{19,3},{4,20},{20... | collective-permute-start | bytes 1572872 | tf_op jit(solution)/shard_map/ppermute | solution.py:136
  112.8 31.3 %collective-permute-start.35 = (bf16[512,768]{1,0:T(8,128)(2,1)S(1)}, bf16[512,768]{1,0:T(8,128)(2,1)}, u32[]{:S(2)}, u32[]{:S(2)}) collective-permute-start(bf16[512,768]{1,0:T(8,128)(2,1)S(1)} %get-tuple-element.68), channel_id=1, source_target_pairs={{0,16},{16,0},{1,17},{17,1},{2,18},{18,2},{3,19},{19,3},{4,20},{20... | collective-permute-start | bytes 2359304 | tf_op jit(solution)/shard_map/ppermute | solution.py:136
  114.3 13.5 %collective-permute-start.32 = (bf16[4,32,2048]{2,1,0:T(8,128)(2,1)S(1)}, bf16[4,32,2048]{2,1,0:T(8,128)(2,1)S(1)}, u32[]{:S(2)}, u32[]{:S(2)}) collective-permute-start(bf16[4,32,2048]{2,1,0:T(8,128)(2,1)S(1)} %pad_maximum_fusion), channel_id=1, source_target_pairs={{2,0},{3,1},{0,2},{1,3},{6,4},{7,5},{4,6},{5,7},{10,8},{11,9},{8,1... | collective-permute-start | bytes 1572872 | tf_op jit(solution)/shard_map/ppermute | solution.py:122
  116.5 43.4 %collective-permute-start.47 = (bf16[4,32,2048]{2,1,0:T(8,128)(2,1)}, bf16[4,32,2048]{2,1,0:T(8,128)(2,1)}, u32[]{:S(2)}, u32[]{:S(2)}) collective-permute-start(bf16[4,32,2048]{2,1,0:T(8,128)(2,1)} %pad_maximum_fusion.3), channel_id=1, source_target_pairs={{0,16},{16,0},{1,17},{17,1},{2,18},{18,2},{3,19},{19,3},{4,20},{20... | collective-permute-start | bytes 1572872 | tf_op jit(solution)/shard_map/ppermute | solution.py:136
  127.1 16.9 %collective-permute-start.33 = (bf16[2,32,2048]{2,1,0:T(8,128)(2,1)S(1)}, bf16[2,32,2048]{2,1,0:T(8,128)(2,1)S(1)}, u32[]{:S(2)}, u32[]{:S(2)}) collective-permute-start(bf16[2,32,2048]{2,1,0:T(8,128)(2,1)S(1)} %slice.250), channel_id=1, source_target_pairs={{2,0},{3,1},{0,2},{1,3},{6,4},{7,5},{4,6},{5,7},{10,8},{11,9},{8,1... | collective-permute-start | bytes 786440 | tf_op jit(solution)/shard_map/ppermute | solution.py:122
  128.7 30.0 %collective-permute-start.34 = (bf16[2,32,2048]{2,1,0:T(8,128)(2,1)S(1)}, bf16[2,32,2048]{2,1,0:T(8,128)(2,1)S(1)}, u32[]{:S(2)}, u32[]{:S(2)}) collective-permute-start(bf16[2,32,2048]{2,1,0:T(8,128)(2,1)S(1)} %slice.251), channel_id=1, source_target_pairs={{0,16},{16,0},{1,17},{17,1},{2,18},{18,2},{3,19},{19,3},{4,20},{20... | collective-permute-start | bytes 786440 | tf_op jit(solution)/shard_map/ppermute | solution.py:136
  130.1 46.8 %collective-permute-start.36 = (bf16[640,768]{1,0:T(8,128)(2,1)}, bf16[640,768]{1,0:T(8,128)(2,1)}, u32[]{:S(2)}, u32[]{:S(2)}) collective-permute-start(bf16[640,768]{1,0:T(8,128)(2,1)} %collective-permute-done.4.refs_7_), channel_id=1, source_target_pairs={{1,0},{0,1},{3,2},{2,3},{5,4},{4,5},{7,6},{6,7},{9,8},{8,9},{11,10... | collective-permute-start | bytes 2949128 | tf_op jit(solution)/shard_map/ppermute | solution.py:132
  144.0 32.9 %collective-permute-start.38 = (bf16[512,768]{1,0:T(8,128)(2,1)}, bf16[512,768]{1,0:T(8,128)(2,1)}, u32[]{:S(2)}, u32[]{:S(2)}) collective-permute-start(bf16[512,768]{1,0:T(8,128)(2,1)} %collective-permute-done.31.refs_10_), channel_id=1, source_target_pairs={{1,0},{0,1},{3,2},{2,3},{5,4},{4,5},{7,6},{6,7},{9,8},{8,9},{11,10... | collective-permute-start | bytes 2359304 | tf_op jit(solution)/shard_map/ppermute | solution.py:132
  159.4 17.5 %collective-permute-start.39 = (bf16[512,768]{1,0:T(8,128)(2,1)}, bf16[512,768]{1,0:T(8,128)(2,1)}, u32[]{:S(2)}, u32[]{:S(2)}) collective-permute-start(bf16[512,768]{1,0:T(8,128)(2,1)} %collective-permute-done.35.refs_11_), channel_id=1, source_target_pairs={{1,0},{0,1},{3,2},{2,3},{5,4},{4,5},{7,6},{6,7},{9,8},{8,9},{11,10... | collective-permute-start | bytes 2359304 | tf_op jit(solution)/shard_map/ppermute | solution.py:132
  159.4 15.9 %collective-permute-start.37 = (bf16[384,768]{1,0:T(8,128)(2,1)}, bf16[384,768]{1,0:T(8,128)(2,1)}, u32[]{:S(2)}, u32[]{:S(2)}) collective-permute-start(bf16[384,768]{1,0:T(8,128)(2,1)} %collective-permute-done.8.refs_8_), channel_id=1, source_target_pairs={{1,0},{0,1},{3,2},{2,3},{5,4},{4,5},{7,6},{6,7},{9,8},{8,9},{11,10... | collective-permute-start | bytes 1769480 | tf_op jit(solution)/shard_map/ppermute | solution.py:132
  159.9 14.1 %collective-permute-start.48 = (bf16[4,32,2048]{2,1,0:T(8,128)(2,1)}, bf16[4,32,2048]{2,1,0:T(8,128)(2,1)}, u32[]{:S(2)}, u32[]{:S(2)}) collective-permute-start(bf16[4,32,2048]{2,1,0:T(8,128)(2,1)} %pad_maximum_fusion.3), channel_id=1, source_target_pairs={{2,0},{3,1},{0,2},{1,3},{6,4},{7,5},{4,6},{5,7},{10,8},{11,9},{8,1... | collective-permute-start | bytes 1572872 | tf_op jit(solution)/shard_map/ppermute | solution.py:122
  174.1 24.3 %collective-permute-start.49 = (bf16[2,32,2048]{2,1,0:T(8,128)(2,1)S(1)}, bf16[2,32,2048]{2,1,0:T(8,128)(2,1)S(1)}, u32[]{:S(2)}, u32[]{:S(2)}) collective-permute-start(bf16[2,32,2048]{2,1,0:T(8,128)(2,1)S(1)} %slice.262), channel_id=1, source_target_pairs={{2,0},{3,1},{0,2},{1,3},{6,4},{7,5},{4,6},{5,7},{10,8},{11,9},{8,1... | collective-permute-start | bytes 786440 | tf_op jit(solution)/shard_map/ppermute | solution.py:122
  175.4 23.1 %collective-permute-start.50 = (bf16[2,32,2048]{2,1,0:T(8,128)(2,1)S(1)}, bf16[2,32,2048]{2,1,0:T(8,128)(2,1)S(1)}, u32[]{:S(2)}, u32[]{:S(2)}) collective-permute-start(bf16[2,32,2048]{2,1,0:T(8,128)(2,1)S(1)} %slice.263), channel_id=1, source_target_pairs={{0,16},{16,0},{1,17},{17,1},{2,18},{18,2},{3,19},{19,3},{4,20},{20... | collective-permute-start | bytes 786440 | tf_op jit(solution)/shard_map/ppermute | solution.py:136
  196.0 17.7 %collective-permute-start.40 = (bf16[64,2048]{1,0:T(8,128)(2,1)S(1)}, bf16[64,2048]{1,0:T(8,128)(2,1)S(1)}, u32[]{:S(2)}, u32[]{:S(2)}) collective-permute-start(bf16[64,2048]{1,0:T(8,128)(2,1)S(1)} %get-tuple-element.81), channel_id=1, source_target_pairs={{2,0},{3,1},{0,2},{1,3},{6,4},{7,5},{4,6},{5,7},{10,8},{11,9},{8,1... | collective-permute-start | bytes 786440 | tf_op jit(solution)/shard_map/ppermute | solution.py:122
  196.6 17.8 %collective-permute-start.42 = (bf16[64,2048]{1,0:T(8,128)(2,1)S(1)}, bf16[64,2048]{1,0:T(8,128)(2,1)S(1)}, u32[]{:S(2)}, u32[]{:S(2)}) collective-permute-start(bf16[64,2048]{1,0:T(8,128)(2,1)S(1)} %get-tuple-element.83), channel_id=1, source_target_pairs={{0,16},{16,0},{1,17},{17,1},{2,18},{18,2},{3,19},{19,3},{4,20},{20... | collective-permute-start | bytes 786440 | tf_op jit(solution)/shard_map/ppermute | solution.py:136
  213.8 18.9 %collective-permute-start.41 = (bf16[4,32,2048]{2,1,0:T(8,128)(2,1)S(1)}, bf16[4,32,2048]{2,1,0:T(8,128)(2,1)S(1)}, u32[]{:S(2)}, u32[]{:S(2)}) collective-permute-start(bf16[4,32,2048]{2,1,0:T(8,128)(2,1)S(1)} %pad_maximum_fusion.1), channel_id=1, source_target_pairs={{0,16},{16,0},{1,17},{17,1},{2,18},{18,2},{3,19},{19,3},{4,20},{20... | collective-permute-start | bytes 1572872 | tf_op jit(solution)/shard_map/ppermute | solution.py:136
  214.5 18.1 %collective-permute-start.43 = (bf16[4,32,2048]{2,1,0:T(8,128)(2,1)S(1)}, bf16[4,32,2048]{2,1,0:T(8,128)(2,1)S(1)}, u32[]{:S(2)}, u32[]{:S(2)}) collective-permute-start(bf16[4,32,2048]{2,1,0:T(8,128)(2,1)S(1)} %pad_maximum_fusion.2), channel_id=1, source_target_pairs={{2,0},{3,1},{0,2},{1,3},{6,4},{7,5},{4,6},{5,7},{10,8},{11,9},{8,1... | collective-permute-start | bytes 1572872 | tf_op jit(solution)/shard_map/ppermute | solution.py:122
  221.1 19.5 %collective-permute-start.52 = (bf16[4,32,2048]{2,1,0:T(8,128)(2,1)S(1)}, bf16[4,32,2048]{2,1,0:T(8,128)(2,1)S(1)}, u32[]{:S(2)}, u32[]{:S(2)}) collective-permute-start(bf16[4,32,2048]{2,1,0:T(8,128)(2,1)S(1)} %pad_maximum_fusion.4), channel_id=1, source_target_pairs={{0,16},{16,0},{1,17},{17,1},{2,18},{18,2},{3,19},{19,3},{4,20},{20... | collective-permute-start | bytes 1572872 | tf_op jit(solution)/shard_map/ppermute | solution.py:136
  221.5 19.1 %collective-permute-start.54 = (bf16[4,32,2048]{2,1,0:T(8,128)(2,1)S(1)}, bf16[4,32,2048]{2,1,0:T(8,128)(2,1)S(1)}, u32[]{:S(2)}, u32[]{:S(2)}) collective-permute-start(bf16[4,32,2048]{2,1,0:T(8,128)(2,1)S(1)} %pad_maximum_fusion.5), channel_id=1, source_target_pairs={{2,0},{3,1},{0,2},{1,3},{6,4},{7,5},{4,6},{5,7},{10,8},{11,9},{8,1... | collective-permute-start | bytes 1572872 | tf_op jit(solution)/shard_map/ppermute | solution.py:122
  234.7 12.8 %collective-permute-start.45 = (bf16[32,2048]{1,0:T(8,128)(2,1)S(1)}, bf16[32,2048]{1,0:T(8,128)(2,1)S(1)}, u32[]{:S(2)}, u32[]{:S(2)}) collective-permute-start(bf16[32,2048]{1,0:T(8,128)(2,1)S(1)} %get-tuple-element.103), channel_id=1, source_target_pairs={{8,0},{9,1},{10,2},{11,3},{12,4},{13,5},{14,6},{15,7},{0,8},{1,9},... | collective-permute-start | bytes 393224 | tf_op jit(solution)/shard_map/ppermute | solution.py:112
  (65 other events, 427.7 us)

commit v4 on v3

v4 whole, which is shorter than its diff:
```python
import functools
import math

import jax
import jax.numpy as jnp
from jax import lax
from jax.experimental import pallas as pl
from jax.experimental.pallas import tpu as pltpu
from jax.sharding import PartitionSpec as P

HD = 128
TOP = 6
CTX = 256
MIB = 1024 * 1024


def normalize(values, gain):
    mean_sq = jnp.mean(values * values, axis=-1, keepdims=True)
    return values * lax.rsqrt(mean_sq + 1e-06) * gain


def attend(queries, kv_pool, page_table, ctx_lens):
    scale = 1.0 / math.sqrt(HD)
    group_rows = queries.shape[0]
    local_feats = queries.shape[1]
    local_heads = local_feats // HD
    seq_count = page_table.shape[0]
    seq_rows = group_rows // seq_count
    pool_here = kv_pool.shape[1]
    local_pages = page_table - lax.axis_index("expert") * pool_here
    keys = kv_pool[0][local_pages].reshape(seq_count, CTX, local_heads, HD)
    values = kv_pool[1][local_pages].reshape(seq_count, CTX, local_heads, HD)
    asked = queries.reshape(seq_count, seq_rows, local_heads, HD)
    scores = jnp.einsum("sqhd,skhd->shqk", asked, keys, preferred_element_type=jnp.float32) * scale
    lengths = ctx_lens.reshape(seq_count, seq_rows)
    visible = (jnp.arange(CTX, dtype=jnp.int32)[None, None, :] < lengths[:, :, None])[:, None]
    scores = jnp.where(visible, scores, -1e30)
    top_score = jnp.max(scores, axis=-1, keepdims=True)
    expo = jnp.where(visible, jnp.exp(scores - top_score), 0.0)
    probs = (expo / jnp.sum(expo, axis=-1, keepdims=True)).astype(jnp.bfloat16)
    mixed = jnp.einsum("shqk,skhd->sqhd", probs, values, preferred_element_type=jnp.float32)
    return mixed.astype(jnp.bfloat16).reshape(group_rows, local_feats)


def dispatched(
    queries,
    kv_pool,
    page_table,
    ctx_lens,
    w_out,
    residual,
    moe_gain,
    expert_ids,
    route_weights,
    w_gate,
    w_up,
    w_down,
    final_gain,
):
    context = attend(queries, kv_pool, page_table, ctx_lens)
    columns = lax.all_gather(w_out, "expert", axis=1, tiled=True)
    projected = lax.psum_scatter(
        jnp.dot(context, columns, preferred_element_type=jnp.float32).astype(jnp.bfloat16),
        "dp",
        scatter_dimension=0,
        tiled=True,
    ).astype(jnp.float32)
    hidden_state = residual.astype(jnp.float32) + projected
    moe_input = normalize(hidden_state, moe_gain).astype(jnp.bfloat16)
    rows_here = moe_input.shape[0]
    experts = lax.axis_size("expert")
    slots = max(2, min(rows_here, 2 * rows_here * TOP // experts))
    flat_ids = expert_ids.reshape(-1)
    marks = (flat_ids[:, None] == jnp.arange(experts, dtype=jnp.int32)[None, :]).astype(jnp.int32)
    before = jnp.sum((jnp.cumsum(marks, axis=0) - 1) * marks, axis=1)
    target = (flat_ids * slots + before).reshape(rows_here, TOP)
    placing = jnp.any(
        jnp.arange(experts * slots, dtype=jnp.int32)[:, None, None] == target[None], axis=-1
    )
    outbound = jnp.dot(placing.astype(jnp.bfloat16), moe_input, preferred_element_type=jnp.float32)
    outbound = outbound.astype(jnp.bfloat16).reshape(experts, slots, moe_input.shape[1])
    gate_full = lax.all_gather(w_gate, "dp", axis=1, tiled=True)
    up_full = lax.all_gather(w_up, "dp", axis=1, tiled=True)
    down_full = lax.all_gather(w_down, "dp", axis=1, tiled=True)
    arrived = lax.all_to_all(outbound, "expert", split_axis=0, concat_axis=0, tiled=True)
    flat = arrived.reshape(-1, arrived.shape[2])
    gate = jnp.dot(flat, gate_full[0], preferred_element_type=jnp.float32)
    up_part = jnp.dot(flat, up_full[0], preferred_element_type=jnp.float32)
    expert_mid = (jax.nn.silu(gate) * up_part).astype(jnp.bfloat16)
    done = jnp.dot(expert_mid, down_full[0], preferred_element_type=jnp.float32).astype(
        jnp.bfloat16
    )
    done = done.reshape(arrived.shape[0], arrived.shape[1], arrived.shape[2])
    returned = lax.all_to_all(done, "expert", split_axis=0, concat_axis=0, tiled=True)
    answers = returned.reshape(experts * slots, returned.shape[2])[target]
    moe = jnp.sum(route_weights[:, :, None] * answers.astype(jnp.float32), axis=1)
    combined = hidden_state + moe
    return normalize(combined, final_gain).astype(jnp.bfloat16)


def place(z, y, c):
    return (z * 2 + y) * 2 + c


def shift_z(values, depth, step):
    pairs = [
        (place((z + step) % depth, y, c), place(z, y, c))
        for z in range(depth)
        for y in range(2)
        for c in range(2)
    ]
    return lax.ppermute(values, "expert", pairs)


def flip_y(values, depth):
    pairs = [
        (place(z, 1 - y, c), place(z, y, c))
        for z in range(depth)
        for y in range(2)
        for c in range(2)
    ]
    return lax.ppermute(values, "expert", pairs)


def flip_core(values, depth):
    pairs = [
        (place(z, y, 1 - c), place(z, y, c))
        for z in range(depth)
        for y in range(2)
        for c in range(2)
    ]
    return lax.ppermute(values, "expert", pairs)


def flip_x(values):
    return lax.ppermute(values, "dp", [(0, 1), (1, 0)])


def attend_kernel(pages_ref, lens_ref, q_ref, kv_ref, out_ref):
    scale = 1.0 / math.sqrt(HD)
    seqs, slots = pages_ref.shape
    rows, feats = q_ref.shape
    each = rows // seqs
    page = kv_ref.shape[2]
    first_page = lax.axis_index("expert") * kv_ref.shape[1]
    place_in = lax.broadcasted_iota(jnp.int32, (each, slots * page), 1)
    for s in range(seqs):
        here = slice(s * each, (s + 1) * each)
        pages = [pages_ref[s, p] - first_page for p in range(slots)]
        keys = jnp.concatenate([kv_ref[0, p] for p in pages], axis=0)
        values = jnp.concatenate([kv_ref[1, p] for p in pages], axis=0)
        visible = place_in < lens_ref[here, :]
        for h in range(feats // HD):
            lanes = slice(h * HD, (h + 1) * HD)
            scores = lax.dot_general(
                q_ref[here, lanes],
                keys[:, lanes],
                (((1,), (1,)), ((), ())),
                preferred_element_type=jnp.float32,
            )
            scores = jnp.where(visible, scores * scale, -1e30)
            top_score = jnp.max(scores, axis=-1, keepdims=True)
            expo = jnp.where(visible, jnp.exp(scores - top_score), 0.0)
            probs = (expo / jnp.sum(expo, axis=-1, keepdims=True)).astype(jnp.bfloat16)
            mixed = jnp.dot(probs, values[:, lanes], preferred_element_type=jnp.float32)
            out_ref[here, lanes] = mixed.astype(out_ref.dtype)


def attend_here(queries, kv_pool, page_table, ctx_lens):
    vmem_spec = pl.BlockSpec(memory_space=pltpu.VMEM)
    return pl.pallas_call(
        attend_kernel,
        out_shape=jax.ShapeDtypeStruct(queries.shape, jnp.bfloat16),
        in_specs=[pl.BlockSpec(memory_space=pltpu.SMEM)] + [vmem_spec] * 3,
        out_specs=vmem_spec,
        compiler_params=pltpu.CompilerParams(vmem_limit_bytes=16 * MIB),
        cost_estimate=pl.CostEstimate(
            flops=4 * queries.size * CTX,
            bytes_accessed=2 * kv_pool.size + 4 * queries.size,
            transcendentals=queries.size * CTX // HD,
        ),
        name="attend",
    )(page_table, ctx_lens[:, None], queries, kv_pool)


def project_kernel(depth, ctx_ref, other_ref, *refs):
    pieces, (kept_ref, sent_ref) = refs[:-2], refs[-2:]
    half = ctx_ref.shape[0] // 2
    width = pieces[0].shape[1]
    me = lax.axis_index("expert")
    x = lax.axis_index("dp")
    y = lax.rem(lax.div(me, 2), 2)
    z = lax.div(me, 4)
    mine = pl.ds(pl.multiple_of(x * half, half), half)
    theirs = pl.ds(pl.multiple_of((1 - x) * half, half), half)
    rows = jnp.concatenate(
        [ctx_ref[mine, :], other_ref[mine, :], ctx_ref[theirs, :], other_ref[theirs, :]], axis=0
    )
    for flip in range(2):
        at_y = y if flip == 0 else 1 - y
        for r in range(depth):
            total = jnp.dot(rows, pieces[flip * depth + r][...], preferred_element_type=jnp.float32)
            index = lax.rem(z + r, depth) * 2 + at_y
            columns = pl.ds(pl.multiple_of(index * width, width), width)
            kept_ref[:, columns] = total[: 2 * half]
            sent_ref[:, columns] = total[2 * half :].astype(sent_ref.dtype)


def project(context, other, pieces, depth):
    rows, feats = context.shape
    columns = pieces[0].shape[1] * 2 * depth
    return pl.pallas_call(
        functools.partial(project_kernel, depth),
        out_shape=(
            jax.ShapeDtypeStruct((rows, columns), jnp.float32),
            jax.ShapeDtypeStruct((rows, columns), jnp.bfloat16),
        ),
        compiler_params=pltpu.CompilerParams(vmem_limit_bytes=16 * MIB),
        cost_estimate=pl.CostEstimate(
            flops=4 * rows * feats * columns,
            bytes_accessed=2 * feats * columns + 6 * rows * columns,
            transcendentals=0,
        ),
        name="project",
    )(context, other, *pieces)


def join_kernel(width, mine_ref, other_ref, residual_ref, gain_ref, share_ref, hidden_ref, out_ref):
    c = lax.rem(lax.axis_index("expert"), 2)
    feats = residual_ref.shape[1]
    for i in range(feats // (2 * width)):
        source = slice(i * width, (i + 1) * width)
        for own, ref in ((True, mine_ref), (False, other_ref)):
            index = 2 * i + (c if own else 1 - c)
            columns = pl.ds(pl.multiple_of(index * width, width), width)
            hidden_ref[:, columns] = ref[:, source]
    hidden = residual_ref[...].astype(jnp.float32) + hidden_ref[...]
    hidden_ref[...] = hidden
    mean_sq = jnp.mean(hidden * hidden, axis=-1, keepdims=True)
    out_ref[:, :feats] = (hidden * lax.rsqrt(mean_sq + 1e-06) * gain_ref[...]).astype(
        out_ref.dtype
    )
    out_ref[:, feats:] = share_ref[...]


def join(mine, other, residual, gain, share, width):
    rows, feats = residual.shape
    return pl.pallas_call(
        functools.partial(join_kernel, width),
        out_shape=(
            jax.ShapeDtypeStruct((rows, feats), jnp.float32),
            jax.ShapeDtypeStruct((rows, feats + share.shape[1]), jnp.bfloat16),
        ),
        compiler_params=pltpu.CompilerParams(vmem_limit_bytes=16 * MIB),
        cost_estimate=pl.CostEstimate(
            flops=6 * rows * feats, bytes_accessed=12 * rows * feats, transcendentals=rows
        ),
        name="join",
    )(mine, other, residual, gain[None, :], share)


def cut_kernel(width, w_ref, *refs):
    outs, sems = refs[:-1], refs[-1]
    x = lax.axis_index("dp")
    units = w_ref.shape[2]
    low = x * (units - width)
    high = (1 - x) * (units - width)
    copies = []
    at = 0
    for i, out in enumerate(outs):
        start = pl.multiple_of(high if i > 0 else low, 128)
        source_at = 0 if i == 0 else at
        copy = pltpu.make_async_copy(
            w_ref.at[0, pl.ds(source_at, out.shape[0]), pl.ds(start, width)], out, sems.at[i]
        )
        copy.start()
        copies.append(copy)
        if i > 0:
            at += out.shape[0]
    for copy in copies:
        copy.wait()


def cut(weights, width, parts):
    depth = weights.shape[1]
    shapes = [depth] + list(parts)
    any_spec = pl.BlockSpec(memory_space=pl.ANY)
    return pl.pallas_call(
        functools.partial(cut_kernel, width),
        out_shape=tuple(jax.ShapeDtypeStruct((n, width), weights.dtype) for n in shapes),
        in_specs=[any_spec],
        out_specs=(pl.BlockSpec(memory_space=pltpu.VMEM),) * len(shapes),
        scratch_shapes=[pltpu.SemaphoreType.DMA((len(shapes),))],
        cost_estimate=pl.CostEstimate(
            flops=0, bytes_accessed=8 * depth * width, transcendentals=0
        ),
        compiler_params=pltpu.CompilerParams(vmem_limit_bytes=16 * MIB),
        name="cut",
    )(weights)


SLOTS = 3


def experts_kernel(tile, out_tile, first_row, count, n_gate, n_up, *refs):
    per_expert = n_gate + n_up + 1
    pieces, refs = refs[:count], refs[count:]
    weights, refs = refs[: 2 * per_expert], refs[2 * per_expert :]
    outs, refs = refs[:count], refs[count:]
    rows, share, gate, up, down, mid, row_sem, weight_sem, down_sem = refs
    x = lax.axis_index("dp")
    me = lax.axis_index("expert")
    feats = rows.shape[2]
    blocks, each = rows.shape[0], rows.shape[1]
    half = feats // 2
    width = down.shape[0] // 2
    tiles = width // tile
    near = pl.ds(pl.multiple_of(x * half, half), half)
    far = pl.ds(pl.multiple_of((1 - x) * half, half), half)
    taken = pl.ds(first_row, each)

    row_copies = []
    spans = []
    at = 0
    for i, piece in enumerate(pieces):
        part = piece.shape[0]
        spans.append((at * each, part * each))
        here = pl.ds(at, part)
        for s, (source, target) in enumerate(
            (
                (piece.at[:, taken, near], rows.at[here, :, pl.ds(0, half)]),
                (piece.at[:, taken, far], rows.at[here, :, pl.ds(half, half)]),
                (piece.at[:, taken, pl.ds(feats, 128)], share.at[here]),
            )
        ):
            copy = pltpu.make_async_copy(source, target, row_sem.at[3 * i + s])
            copy.start()
            row_copies.append(copy)
        at += part

    def fetch(t):
        e, j = t // tiles, t % tiles
        mine = weights[e * per_expert : (e + 1) * per_expert]
        group = []
        sem = (n_gate + n_up) * (t % SLOTS)
        for sources, target in ((mine[:n_gate], gate), (mine[n_gate:-1], up)):
            depth_at = 0
            for source in sources:
                copy = pltpu.make_async_copy(
                    source.at[:, pl.ds(j * tile, tile)],
                    target.at[t % SLOTS, pl.ds(depth_at, source.shape[0]), :],
                    weight_sem.at[sem],
                )
                copy.start()
                group.append(copy)
                depth_at += source.shape[0]
                sem += 1
        return group

    weight_copies = [fetch(t) for t in range(SLOTS)]
    units = weights[-1].shape[0]
    spare = width - units
    down_copies = []
    for e in range(2):
        start = pl.multiple_of(e * width + x * spare, 16)
        copy = pltpu.make_async_copy(
            weights[(e + 1) * per_expert - 1], down.at[pl.ds(start, units), :], down_sem.at[e]
        )
        copy.start()
        down_copies.append(copy)
        if spare:
            blank = pl.multiple_of(e * width + (1 - x) * units, 16)
            down[pl.ds(blank, spare), :] = jnp.zeros((spare, feats), down.dtype)

    for copy in row_copies:
        copy.wait()
    total_rows = blocks * each
    shares = share[...].reshape(total_rows, 128).astype(jnp.float32)
    lane = lax.broadcasted_iota(jnp.int32, (total_rows, 128), 1)
    experts = lax.axis_size("expert")
    for t in range(2 * tiles):
        e, j = t // tiles, t % tiles
        if j == 0:
            chosen = me if e == 0 else me + 1 - 2 * lax.rem(me, 2)
            hit = (lane == chosen) | (lane == chosen + experts)
            scale = jnp.sum(jnp.where(hit, shares, 0.0), axis=1, keepdims=True)
        for copy in weight_copies[t]:
            copy.wait()
        values = rows[...].reshape(total_rows, feats)
        g = jnp.dot(values, gate[t % SLOTS], preferred_element_type=jnp.float32)
        u = jnp.dot(values, up[t % SLOTS], preferred_element_type=jnp.float32)
        h = g / (1.0 + jnp.exp(-g)) * u * scale
        mid[:, pl.ds(t * tile, tile)] = h.astype(mid.dtype)
        if t + SLOTS < 2 * tiles:
            weight_copies.append(fetch(t + SLOTS))
    for copy in down_copies:
        copy.wait()
    for n in range(feats // out_tile):
        lanes = pl.ds(n * out_tile, out_tile)
        total = jnp.dot(mid[...], down[:, lanes], preferred_element_type=jnp.float32)
        for (first, part), out in zip(spans, outs):
            out[:, lanes] = total[first : first + part].astype(out.dtype)


def run_experts(pieces, kinds, first_row, each, experts_weights):
    feats = experts_weights[0][2].shape[1]
    width = experts_weights[0][0][0].shape[1]
    n_gate, n_up = len(experts_weights[0][0]), len(experts_weights[0][1])
    weights = [
        array for gate, up, down in experts_weights for array in list(gate) + list(up) + [down]
    ]
    count = len(pieces)
    blocks = sum(piece.shape[0] for piece in pieces)
    total = blocks * each
    tile = 256
    any_spec = pl.BlockSpec(memory_space=pl.ANY)
    vmem_spec = pl.BlockSpec(memory_space=pltpu.VMEM)
    return pl.pallas_call(
        functools.partial(experts_kernel, tile, 512, first_row, count, n_gate, n_up),
        out_shape=tuple(
            jax.ShapeDtypeStruct((piece.shape[0] * each, feats), kind)
            for piece, kind in zip(pieces, kinds)
        ),
        in_specs=[any_spec] * (count + len(weights)),
        out_specs=(vmem_spec,) * count,
        scratch_shapes=[
            pltpu.VMEM((blocks, each, feats), jnp.bfloat16),
            pltpu.VMEM((blocks, each, 128), jnp.bfloat16),
            pltpu.VMEM((SLOTS, feats, tile), jnp.bfloat16),
            pltpu.VMEM((SLOTS, feats, tile), jnp.bfloat16),
            pltpu.VMEM((2 * width, feats), jnp.bfloat16),
            pltpu.VMEM((total, 2 * width), jnp.bfloat16),
            pltpu.SemaphoreType.DMA((3 * count,)),
            pltpu.SemaphoreType.DMA((SLOTS * (n_gate + n_up),)),
            pltpu.SemaphoreType.DMA((2,)),
        ],
        compiler_params=pltpu.CompilerParams(vmem_limit_bytes=30 * MIB),
        cost_estimate=pl.CostEstimate(
            flops=2 * total * feats * width * 6,
            bytes_accessed=12 * feats * width + 12 * total * feats,
            transcendentals=total * width * 2,
        ),
        name="experts",
    )(*pieces, *weights)


def send_sides(out_l, out_x, out_y, far, k, depth):
    if k % 2 == 0:
        out_x = out_x + far.astype(jnp.float32)
    else:
        out_y = out_y + far.astype(jnp.float32)
    return (
        out_l,
        flip_x(out_x.astype(jnp.bfloat16)),
        flip_y(out_y.astype(jnp.bfloat16), depth),
    )


def send_line(out_l, back_x, back_y, depth):
    full = out_l + back_x.astype(jnp.float32) + back_y.astype(jnp.float32)
    full = full.reshape(depth, -1, full.shape[1])
    total = full[0]
    for s in range(1, depth):
        back = shift_z(full[s].astype(jnp.bfloat16), depth, depth - s)
        total = total + back.astype(jnp.float32)
    return total


def gathered(
    queries,
    kv_pool,
    page_table,
    ctx_lens,
    w_out,
    residual,
    moe_gain,
    expert_ids,
    route_weights,
    w_gate,
    w_up,
    w_down,
    final_gain,
):
    experts = lax.axis_size("expert")
    depth = experts // 4
    feats = residual.shape[1]
    block = residual.shape[0]
    units_here = w_down.shape[1]
    width = -(-units_here // 256) * 256
    barrier = lax.optimization_barrier

    near = [w_out] + [shift_z(w_out, depth, s) for s in range(1, depth)]
    across_own = flip_y(w_out, depth)

    feats_here = w_gate.shape[1]
    early = feats_here * 7 // 16
    gate_own, *gate_sent = cut(w_gate, width, (early, feats_here - early))
    gate_far = [flip_x(piece) for piece in gate_sent]
    queries, gate_sent = barrier((queries, gate_sent))
    context = attend_here(queries, kv_pool, page_table, ctx_lens)
    near[1:], across_own, gate_far[0], gate_sent[1], w_up, w_down, gate_own, context = barrier(
        (near[1:], across_own, gate_far[0], gate_sent[1], w_up, w_down, gate_own, context)
    )
    other = flip_core(context, depth)
    gate_far[1] = flip_x(gate_sent[1])
    across = [across_own] + [flip_y(piece, depth) for piece in near[1:]]
    early = feats_here // 4
    up_own, *up_sent = cut(w_up, width, (early, feats_here - early))
    up_early = flip_x(up_sent[0])
    down_own = w_down[0]
    here_core = [flip_core(array, depth) for array in (gate_own, up_own, down_own)]

    named = expert_ids[:, :, None] == jnp.arange(experts, dtype=jnp.int32)[None, None, :]
    share = jnp.sum(jnp.where(named, route_weights[:, :, None], 0.0), axis=1)
    share_high = share.astype(jnp.bfloat16)
    share_low = (share - share_high.astype(jnp.float32)).astype(jnp.bfloat16)
    share = jnp.concatenate(
        [share_high, share_low, jnp.zeros((block, 128 - 2 * experts), jnp.bfloat16)], axis=1
    )

    across, share, here_core = barrier((across, share, here_core))
    kept, sent = project(context, other, near + across, depth)
    kept, sent, gate_far[1] = barrier((kept, sent, gate_far[1]))
    received, up_sent[1], up_early = barrier((flip_x(sent), up_sent[1], up_early))
    up_far = [up_early, flip_x(up_sent[1])]
    gate_far_core = [flip_core(piece, depth) for piece in gate_far]
    total = kept + received.astype(jnp.float32)
    back = flip_core(total[block:], depth)
    hidden_state, message = join(total[:block], back, residual, moe_gain, share, w_out.shape[1])

    line = jnp.stack([message] + [shift_z(message, depth, s) for s in range(1, depth)])
    line_x, up_far[1] = barrier((flip_x(line), up_far[1]))
    line_y = flip_y(line, depth)
    mid_z = depth // 2
    low = flip_y(line_x[:mid_z], depth)
    high = flip_x(line_y[mid_z:])
    up_far_core = [flip_core(piece, depth) for piece in up_far]
    weights = [
        ([gate_own] + gate_far, [up_own] + up_far, down_own),
        ([here_core[0]] + gate_far_core, [here_core[1]] + up_far_core, here_core[2]),
    ]

    moe = []
    diagonal = []
    sides = []
    at = 0
    quarter = block // 4
    for k, each in enumerate((quarter, 2 * quarter, quarter)):
        outs = run_experts(
            [line, line_x, line_y, low, high],
            (jnp.float32, jnp.float32, jnp.float32, jnp.bfloat16, jnp.bfloat16),
            at,
            each,
            weights,
        )
        at += each
        if k > 0:
            outs, diagonal[k - 1] = barrier((outs, diagonal[k - 1]))
            sides.append(send_sides(*diagonal[k - 1], k - 1, depth))
        if k > 1:
            outs, sides[k - 2] = barrier((outs, sides[k - 2]))
            moe.append(send_line(*sides[k - 2], depth))
        line, outs = barrier((line, outs))
        out_l, out_x, out_y, out_low, out_high = outs
        far = jnp.concatenate([out_low, out_high], axis=0)
        far = flip_y(far, depth) if k % 2 == 0 else flip_x(far)
        diagonal.append((out_l, out_x, out_y, far))
    sides.append(send_sides(*diagonal[-1], len(diagonal) - 1, depth))
    for side in sides[-2:]:
        moe.append(send_line(*side, depth))
    combined = hidden_state + jnp.concatenate(moe, axis=0)
    return normalize(combined, final_gain).astype(jnp.bfloat16)


def solution(mesh):
    few = mesh.shape["dp"] == 2 and mesh.shape["expert"] == 16
    return jax.shard_map(
        gathered if few else dispatched,
        mesh=mesh,
        in_specs=(
            P("expert", "dp"),
            P(None, "expert", None, "dp"),
            P("expert", None),
            P("expert"),
            P("dp", "expert"),
            P(("expert", "dp"), None),
            P(),
            P(("expert", "dp"), None),
            P(("expert", "dp"), None),
            P("expert", "dp", None),
            P("expert", "dp", None),
            P("expert", "dp", None),
            P(),
        ),
        out_specs=P(("expert", "dp"), None),
        check_vma=False,
    )
```

time: 255 us -> 245 us (0.961)
  local copies, waits for them, and re-layouts: 30 us -> 12.8 us
  Pallas kernels: 28.8 us -> 42.5 us
  waiting for transfers between devices: 126 us -> 139 us
  starting transfers between devices: 56.9 us -> 47.7 us
  other arithmetic: 7.74 us -> 2.2 us
  matrix products: 4.65 us -> 0 us
    ppermute x14 -> x11, waiting for transfers between devices: 63.7 us -> 47.8 us  [flip_x(): return lax.ppermute(values, 'dp', [(0, 1), (1, 0)])]
    ppermute x14 -> x11, waiting for transfers between devices: 28.9 us -> 44.4 us  [flip_y(): return lax.ppermute(values, 'expert', pairs)]
    pallas_call x2 -> x7, Pallas kernels: 26.3 us -> 40 us  [the longest x3 30.7 us: run_experts(): pl.pallas_call(functools.partial(experts_kernel, tile, 512, first_row, co...]
    ppermute x15, waiting for transfers between devices: 30.5 us -> 41.9 us  [shift_z(): return lax.ppermute(values, 'expert', pairs)]
    squeeze x5 -> x0, local copies, waits for them, and re-layouts: 8.05 us -> none  [the longest x1 3.12 us: attend(): keys = kv_pool[0][local_pages].reshape(seq_count, CTX, local_heads, HD)]
    ppermute x15, starting transfers between devices: 28.5 us -> 21.6 us  [shift_z(): return lax.ppermute(values, 'expert', pairs)]
    ppermute x14 -> x11, starting transfers between devices: 15.2 us -> 10.5 us  [flip_x(): return lax.ppermute(values, 'dp', [(0, 1), (1, 0)])]
    select_n x6 -> x0, other arithmetic: 4.18 us -> none  [the longest x3 3.83 us: sent_part(): return jnp.where(first, weights[:, units - width:], weights[:, :width])]
  transfers between devices with their start and end apart: 58 -> 46, of which waited for: 24 -> 25; matrix products, arithmetic and copies ran while one was open for 11% -> 1% of each run, Pallas kernels for 11% -> 13%
where the time goes in v4:
time: 245 us; the launch traced here: 244 us
  waiting for transfers between devices  139 us (57%)
  starting transfers between devices  47.7 us (19%)
  Pallas kernels  42.5 us (17%)
  local copies, waits for them, and re-layouts  12.8 us (5%)
    ppermute x11, waiting for transfers between devices, flip_x(): return lax.ppermute(values, 'dp', [(0, 1), (1, 0)])  47.8 us
    ppermute x11, waiting for transfers between devices, flip_y(): return lax.ppermute(values, 'expert', pairs)  44.4 us
    ppermute x15, waiting for transfers between devices, shift_z(): return lax.ppermute(values, 'expert', pairs)  41.9 us
    pallas_call x3, Pallas kernels, run_experts(): pl.pallas_call(functools.partial(experts_kernel, tile, 512, first_row, co...  30.7 us
    ppermute x15, starting transfers between devices, shift_z(): return lax.ppermute(values, 'expert', pairs)  21.6 us
    ppermute x11, starting transfers between devices, flip_y(): return lax.ppermute(values, 'expert', pairs)  14.1 us
    unnamed x46, local copies, waits for them, and re-layouts  12.2 us
    ppermute x11, starting transfers between devices, flip_x(): return lax.ppermute(values, 'dp', [(0, 1), (1, 0)])  10.5 us
  transfers between devices with their start and end apart: 46, of which 25 were waited for; matrix products, arithmetic and copies ran while one was open for 1% of the time, Pallas kernels for 13%

profile of v4, /device:TPU:0, one launch (start us, length us, event | category | flops | bytes accessed | tf_op | source)
XLA Modules:
  0.0 244.5 jit_solution(4391224814082086259)
XLA Ops:
  0.0 1.8 copy-done.1
  1.8 1.9 cut.2
  3.7 3.0 %collective-permute-start.4 = (bf16[448,768]{1,0:T(8,128)(2,1)}, bf16[448,768]{1,0:T(8,128)(2,1)}, u32[]{:S(2)}, u32[]{:S(2)}) collective-permute-start(bf16[448,768]{1,0:T(8,128)(2,1)} %get-tuple-element.101), channel_id=1, source_target_pairs={{0,16},{16,0},{1,17},{17,1},{2,18},{18,2},{3,19},{19,3},{4,20},{20... | collective-permute-start | bytes 2064392 | tf_op jit(solution)/shard_map/ppermute | solution.py:136
  6.7 3.6 %collective-permute-start = (bf16[1024,128]{1,0:T(8,128)(2,1)}, bf16[1024,128]{1,0:T(8,128)(2,1)S(1)}, u32[]{:S(2)}, u32[]{:S(2)}) collective-permute-start(bf16[1024,128]{1,0:T(8,128)(2,1)} %refs_0_.1), channel_id=1, source_target_pairs={{4,0},{5,1},{6,2},{7,3},{8,4},{9,5},{10,6},{11,7},{12,8},{13,9},{1... | collective-permute-start | bytes 786440 | tf_op jit(solution)/shard_map/ppermute | solution.py:112
  15.5 5.8 %attend.1.ctx_ref = bf16[128,1024]{1,0:T(8,128)(2,1)S(1)} custom-call(s32[2,4]{1,0:T(2,128)S(1)} %copy-done.15, s32[128,1]{1,0:T(8,128)S(1)} %copy.20.lens_ref, bf16[128,1024]{1,0:T(8,128)(2,1)S(1)} %copy-done.4, bf16[2,8,64,1024]{3,2,1,0:T(8,128)(2,1)S(1)} %copy-done.3), custom_call_target="tpu_custom_call" | custom-call | flops 134217728 | bytes 2621440 | tf_op jit(solution)/shard_map/attend/pallas_call | solution.py:171
  21.3 11.3 %collective-permute-done.1.refs_2_ = bf16[1024,128]{1,0:T(8,128)(2,1)} collective-permute-done((bf16[1024,128]{1,0:T(8,128)(2,1)}, bf16[1024,128]{1,0:T(8,128)(2,1)}, u32[]{:S(2)}, u32[]{:S(2)}) %collective-permute-start.1) | collective-permute-done | bytes 262176 | tf_op jit(solution)/shard_map/ppermute | solution.py:112
  40.3 7.1 %collective-permute-done.6.refs_5_ = bf16[1024,128]{1,0:T(8,128)(2,1)S(1)} collective-permute-done((bf16[1024,128]{1,0:T(8,128)(2,1)S(1)}, bf16[1024,128]{1,0:T(8,128)(2,1)S(1)}, u32[]{:S(2)}, u32[]{:S(2)}) %collective-permute-start.6) | collective-permute-done | bytes 262176 | tf_op jit(solution)/shard_map/ppermute | solution.py:122
  48.7 4.0 %collective-permute-done.7.refs_6_ = bf16[1024,128]{1,0:T(8,128)(2,1)S(1)} collective-permute-done((bf16[1024,128]{1,0:T(8,128)(2,1)}, bf16[1024,128]{1,0:T(8,128)(2,1)S(1)}, u32[]{:S(2)}, u32[]{:S(2)}) %collective-permute-start.7) | collective-permute-done | bytes 262176 | tf_op jit(solution)/shard_map/ppermute | solution.py:122
  55.1 6.6 %collective-permute-done.8.refs_7_ = bf16[1024,128]{1,0:T(8,128)(2,1)} collective-permute-done((bf16[1024,128]{1,0:T(8,128)(2,1)}, bf16[1024,128]{1,0:T(8,128)(2,1)}, u32[]{:S(2)}, u32[]{:S(2)}) %collective-permute-start.8) | collective-permute-done | bytes 262176 | tf_op jit(solution)/shard_map/ppermute | solution.py:122
  66.1 2.4 project.1
  68.5 2.5 %collective-permute-done.12.refs_7_ = bf16[576,768]{1,0:T(8,128)(2,1)} collective-permute-done((bf16[576,768]{1,0:T(8,128)(2,1)}, bf16[576,768]{1,0:T(8,128)(2,1)}, u32[]{:S(2)}, u32[]{:S(2)}) %collective-permute-start.12) | collective-permute-done | bytes 884768 | tf_op jit(solution)/shard_map/ppermute | solution.py:136
  71.6 7.8 %collective-permute-done.14.refs_9_ = bf16[256,768]{1,0:T(8,128)(2,1)S(1)} collective-permute-done((bf16[256,768]{1,0:T(8,128)(2,1)}, bf16[256,768]{1,0:T(8,128)(2,1)S(1)}, u32[]{:S(2)}, u32[]{:S(2)}) %collective-permute-start.14) | collective-permute-done | bytes 393248 | tf_op jit(solution)/shard_map/ppermute | solution.py:136
  79.4 3.9 %collective-permute-done.13 = bf16[128,1024]{1,0:T(8,128)(2,1)S(1)} collective-permute-done((bf16[128,1024]{1,0:T(8,128)(2,1)S(1)}, bf16[128,1024]{1,0:T(8,128)(2,1)S(1)}, u32[]{:S(2)}, u32[]{:S(2)}) %collective-permute-start.13) | collective-permute-done | bytes 262176 | tf_op jit(solution)/shard_map/ppermute | solution.py:136
  85.3 2.9 %collective-permute-start.17 = (bf16[64,2176]{1,0:T(8,128)(2,1)S(1)}, bf16[64,2176]{1,0:T(8,128)(2,1)S(1)}, u32[]{:S(2)}, u32[]{:S(2)}) collective-permute-start(bf16[64,2176]{1,0:T(8,128)(2,1)S(1)} %get-tuple-element.129), channel_id=1, source_target_pairs={{8,0},{9,1},{10,2},{11,3},{12,4},{13,5},{14,6},{15,7},{0,8},{1,9},... | collective-permute-start | bytes 835592 | tf_op jit(solution)/shard_map/ppermute | solution.py:112
  88.2 1.9 collective-permute-start.18
  90.7 3.3 %collective-permute-done.16 = bf16[64,2176]{1,0:T(8,128)(2,1)S(1)} collective-permute-done((bf16[64,2176]{1,0:T(8,128)(2,1)S(1)}, bf16[64,2176]{1,0:T(8,128)(2,1)S(1)}, u32[]{:S(2)}, u32[]{:S(2)}) %collective-permute-start.16) | collective-permute-done | bytes 278560 | tf_op jit(solution)/shard_map/ppermute | solution.py:112
  94.0 19.0 %collective-permute-done.17 = bf16[64,2176]{1,0:T(8,128)(2,1)S(1)} collective-permute-done((bf16[64,2176]{1,0:T(8,128)(2,1)S(1)}, bf16[64,2176]{1,0:T(8,128)(2,1)S(1)}, u32[]{:S(2)}, u32[]{:S(2)}) %collective-permute-start.17) | collective-permute-done | bytes 278560 | tf_op jit(solution)/shard_map/ppermute | solution.py:112
  115.3 3.8 %collective-permute-done.20.refs_10_ = bf16[768,768]{1,0:T(8,128)(2,1)S(1)} collective-permute-done((bf16[768,768]{1,0:T(8,128)(2,1)S(1)}, bf16[768,768]{1,0:T(8,128)(2,1)S(1)}, u32[]{:S(2)}, u32[]{:S(2)}) %collective-permute-start.20) | collective-permute-done | bytes 1179680 | tf_op jit(solution)/shard_map/ppermute | solution.py:136
  119.0 22.1 %collective-permute-done.19.refs_1_ = bf16[4,64,2176]{2,1,0:T(8,128)(2,1)S(1)} collective-permute-done((bf16[4,64,2176]{2,1,0:T(8,128)(2,1)S(1)}, bf16[4,64,2176]{2,1,0:T(8,128)(2,1)S(1)}, u32[]{:S(2)}, u32[]{:S(2)}) %collective-permute-start.19) | collective-permute-done | bytes 1114144 | tf_op jit(solution)/shard_map/ppermute | solution.py:136
  146.8 10.0 %collective-permute-done.22.refs_3_ = bf16[2,64,2176]{2,1,0:T(8,128)(2,1)S(1)} collective-permute-done((bf16[2,64,2176]{2,1,0:T(8,128)(2,1)S(1)}, bf16[2,64,2176]{2,1,0:T(8,128)(2,1)S(1)}, u32[]{:S(2)}, u32[]{:S(2)}) %collective-permute-start.22) | collective-permute-done | bytes 557088 | tf_op jit(solution)/shard_map/ppermute | solution.py:122
  158.2 8.5 %experts.3 = (f32[64,2048]{1,0:T(8,128)S(1)}, f32[64,2048]{1,0:T(8,128)S(1)}, f32[64,2048]{1,0:T(8,128)S(1)}, bf16[32,2048]{1,0:T(8,128)(2,1)S(1)}, bf16[32,2048]{1,0:T(8,128)(2,1)S(1)}) custom-call(bf16[4,64,2176]{2,1,0:T(8,128)(2,1)S(1)} %pad_maximum_fusion.refs_0_, bf16[4,64,2176]{2,1,0:T(8,128)(2,1)S(1)} %collective-permute-done.19.refs_1_, ...), custom_call_target="tpu_custom_call" | custom-call | flops 4831838208 | bytes 25165824 | tf_op jit(solution)/shard_map/experts/pallas_call | solution.py:418
  167.3 13.7 %experts.4 = (f32[128,2048]{1,0:T(8,128)S(1)}, f32[128,2048]{1,0:T(8,128)S(1)}, f32[128,2048]{1,0:T(8,128)S(1)}, bf16[64,2048]{1,0:T(8,128)(2,1)S(1)}, bf16[64,2048]{1,0:T(8,128)(2,1)S(1)}) custom-call(bf16[4,64,2176]{2,1,0:T(8,128)(2,1)S(1)} %pad_maximum_fusion.refs_0_, bf16[4,64,2176]{2,1,0:T(8,128)(2,1)S(1)} %collective-permute-done.19.refs_1_, ...), custom_call_target="tpu_custom_call" | custom-call | flops 9663676416 | bytes 31457280 | tf_op jit(solution)/shard_map/experts/pallas_call | solution.py:418
  184.9 8.5 %experts.5 = (f32[64,2048]{1,0:T(8,128)S(1)}, f32[64,2048]{1,0:T(8,128)S(1)}, f32[64,2048]{1,0:T(8,128)S(1)}, bf16[32,2048]{1,0:T(8,128)(2,1)S(1)}, bf16[32,2048]{1,0:T(8,128)(2,1)S(1)}) custom-call(bf16[4,64,2176]{2,1,0:T(8,128)(2,1)S(1)} %pad_maximum_fusion.refs_0_, bf16[4,64,2176]{2,1,0:T(8,128)(2,1)S(1)} %collective-permute-done.19.refs_1_, ...), custom_call_target="tpu_custom_call" | custom-call | flops 4831838208 | bytes 25165824 | tf_op jit(solution)/shard_map/experts/pallas_call | solution.py:418
  193.4 2.6 %collective-permute-done.29 = bf16[128,2048]{1,0:T(8,128)(2,1)S(1)} collective-permute-done((bf16[128,2048]{1,0:T(8,128)(2,1)S(1)}, bf16[128,2048]{1,0:T(8,128)(2,1)S(1)}, u32[]{:S(2)}, u32[]{:S(2)}) %collective-permute-start.29) | collective-permute-done | bytes 524320 | tf_op jit(solution)/shard_map/ppermute | solution.py:136
  196.0 3.7 %collective-permute-done.30 = bf16[64,2048]{1,0:T(8,128)(2,1)S(1)} collective-permute-done((bf16[64,2048]{1,0:T(8,128)(2,1)S(1)}, bf16[64,2048]{1,0:T(8,128)(2,1)S(1)}, u32[]{:S(2)}, u32[]{:S(2)}) %collective-permute-start.30) | collective-permute-done | bytes 262176 | tf_op jit(solution)/shard_map/ppermute | solution.py:136
  200.1 2.4 collective-permute-start.33
  206.1 6.9 %collective-permute-done.40 = bf16[64,2048]{1,0:T(8,128)(2,1)S(1)} collective-permute-done((bf16[64,2048]{1,0:T(8,128)(2,1)S(1)}, bf16[64,2048]{1,0:T(8,128)(2,1)S(1)}, u32[]{:S(2)}, u32[]{:S(2)}) %collective-permute-start.40) | collective-permute-done | bytes 262176 | tf_op jit(solution)/shard_map/ppermute | solution.py:122
  216.7 9.8 %collective-permute-done.42 = bf16[64,2048]{1,0:T(8,128)(2,1)S(1)} collective-permute-done((bf16[64,2048]{1,0:T(8,128)(2,1)S(1)}, bf16[64,2048]{1,0:T(8,128)(2,1)S(1)}, u32[]{:S(2)}, u32[]{:S(2)}) %collective-permute-start.42) | collective-permute-done | bytes 262176 | tf_op jit(solution)/shard_map/ppermute | solution.py:122
  228.5 2.8 %collective-permute-start.45 = (bf16[16,2048]{1,0:T(8,128)(2,1)S(1)}, bf16[16,2048]{1,0:T(8,128)(2,1)S(1)}, u32[]{:S(2)}, u32[]{:S(2)}) collective-permute-start(bf16[16,2048]{1,0:T(8,128)(2,1)S(1)} %get-tuple-element.212), channel_id=1, source_target_pairs={{4,0},{5,1},{6,2},{7,3},{8,4},{9,5},{10,6},{11,7},{12,8},{13,9},{1... | collective-permute-start | bytes 196616 | tf_op jit(solution)/shard_map/ppermute | solution.py:112
  233.5 2.2 collective-permute-start.39
  235.7 2.0 collective-permute-done.44
  239.5 3.9 %collective-permute-done.38 = bf16[32,2048]{1,0:T(8,128)(2,1)S(1)} collective-permute-done((bf16[32,2048]{1,0:T(8,128)(2,1)S(1)}, bf16[32,2048]{1,0:T(8,128)(2,1)S(1)}, u32[]{:S(2)}, u32[]{:S(2)}) %collective-permute-start.38) | collective-permute-done | bytes 131104 | tf_op jit(solution)/shard_map/ppermute | solution.py:112
  (149 shorter events, 52.4 us)
Async XLA Ops:
  3.7 29.0 %collective-permute-start.4 = (bf16[448,768]{1,0:T(8,128)(2,1)}, bf16[448,768]{1,0:T(8,128)(2,1)}, u32[]{:S(2)}, u32[]{:S(2)}) collective-permute-start(bf16[448,768]{1,0:T(8,128)(2,1)} %get-tuple-element.101), channel_id=1, source_target_pairs={{0,16},{16,0},{1,17},{17,1},{2,18},{18,2},{3,19},{19,3},{4,20},{20... | collective-permute-start | bytes 2064392 | tf_op jit(solution)/shard_map/ppermute | solution.py:136
  6.7 14.6 %collective-permute-start = (bf16[1024,128]{1,0:T(8,128)(2,1)}, bf16[1024,128]{1,0:T(8,128)(2,1)S(1)}, u32[]{:S(2)}, u32[]{:S(2)}) collective-permute-start(bf16[1024,128]{1,0:T(8,128)(2,1)} %refs_0_.1), channel_id=1, source_target_pairs={{4,0},{5,1},{6,2},{7,3},{8,4},{9,5},{10,6},{11,7},{12,8},{13,9},{1... | collective-permute-start | bytes 786440 | tf_op jit(solution)/shard_map/ppermute | solution.py:112
  10.3 22.3 %collective-permute-start.1 = (bf16[1024,128]{1,0:T(8,128)(2,1)}, bf16[1024,128]{1,0:T(8,128)(2,1)}, u32[]{:S(2)}, u32[]{:S(2)}) collective-permute-start(bf16[1024,128]{1,0:T(8,128)(2,1)} %refs_0_.1), channel_id=1, source_target_pairs={{8,0},{9,1},{10,2},{11,3},{12,4},{13,5},{14,6},{15,7},{0,8},{1,9},... | collective-permute-start | bytes 786440 | tf_op jit(solution)/shard_map/ppermute | solution.py:112
  10.3 22.3 %collective-permute-start.2 = (bf16[1024,128]{1,0:T(8,128)(2,1)}, bf16[1024,128]{1,0:T(8,128)(2,1)}, u32[]{:S(2)}, u32[]{:S(2)}) collective-permute-start(bf16[1024,128]{1,0:T(8,128)(2,1)} %refs_0_.1), channel_id=1, source_target_pairs={{12,0},{13,1},{14,2},{15,3},{0,4},{1,5},{2,6},{3,7},{4,8},{5,9},{6... | collective-permute-start | bytes 786440 | tf_op jit(solution)/shard_map/ppermute | solution.py:112
  11.3 21.3 %collective-permute-start.3 = (bf16[1024,128]{1,0:T(8,128)(2,1)}, bf16[1024,128]{1,0:T(8,128)(2,1)}, u32[]{:S(2)}, u32[]{:S(2)}) collective-permute-start(bf16[1024,128]{1,0:T(8,128)(2,1)} %refs_0_.1), channel_id=1, source_target_pairs={{2,0},{3,1},{0,2},{1,3},{6,4},{7,5},{4,6},{5,7},{10,8},{11,9},{8,1... | collective-permute-start | bytes 786440 | tf_op jit(solution)/shard_map/ppermute | solution.py:122
  32.7 29.8 %collective-permute-start.11 = (bf16[704,2048]{1,0:T(8,128)(2,1)S(1)}, bf16[704,2048]{1,0:T(8,128)(2,1)}, u32[]{:S(2)}, u32[]{:S(2)}) collective-permute-start(bf16[704,2048]{1,0:T(8,128)(2,1)S(1)} %bitcast.7), channel_id=1, source_target_pairs={{1,0},{0,1},{3,2},{2,3},{5,4},{4,5},{7,6},{6,7},{9,8},{8,9},{11,10... | collective-permute-start | bytes 8650760 | tf_op jit(solution)/shard_map/ppermute | solution.py:132
  37.8 24.0 %collective-permute-start.10 = (bf16[1024,768]{1,0:T(8,128)(2,1)}, bf16[1024,768]{1,0:T(8,128)(2,1)}, u32[]{:S(2)}, u32[]{:S(2)}) collective-permute-start(bf16[1024,768]{1,0:T(8,128)(2,1)} %get-tuple-element.113.refs_8_), channel_id=1, source_target_pairs={{1,0},{0,1},{3,2},{2,3},{5,4},{4,5},{7,6},{6,7},{9,8},{8,9},{11,10... | collective-permute-start | bytes 4718600 | tf_op jit(solution)/shard_map/ppermute | solution.py:132
  38.3 24.1 %collective-permute-start.9 = (bf16[1024,768]{1,0:T(8,128)(2,1)}, bf16[1024,768]{1,0:T(8,128)(2,1)}, u32[]{:S(2)}, u32[]{:S(2)}) collective-permute-start(bf16[1024,768]{1,0:T(8,128)(2,1)} %get-tuple-element.111.refs_5_), channel_id=1, source_target_pairs={{1,0},{0,1},{3,2},{2,3},{5,4},{4,5},{7,6},{6,7},{9,8},{8,9},{11,10... | collective-permute-start | bytes 4718600 | tf_op jit(solution)/shard_map/ppermute | solution.py:132
  39.8 12.8 %collective-permute-start.7 = (bf16[1024,128]{1,0:T(8,128)(2,1)}, bf16[1024,128]{1,0:T(8,128)(2,1)S(1)}, u32[]{:S(2)}, u32[]{:S(2)}) collective-permute-start(bf16[1024,128]{1,0:T(8,128)(2,1)} %collective-permute-done.1.refs_2_), channel_id=1, source_target_pairs={{2,0},{3,1},{0,2},{1,3},{6,4},{7,5},{4,6},{5,7},{10,8},{11,9},{8,1... | collective-permute-start | bytes 786440 | tf_op jit(solution)/shard_map/ppermute | solution.py:122
  48.1 22.9 %collective-permute-start.12 = (bf16[576,768]{1,0:T(8,128)(2,1)}, bf16[576,768]{1,0:T(8,128)(2,1)}, u32[]{:S(2)}, u32[]{:S(2)}) collective-permute-start(bf16[576,768]{1,0:T(8,128)(2,1)} %get-tuple-element.121), channel_id=1, source_target_pairs={{0,16},{16,0},{1,17},{17,1},{2,18},{18,2},{3,19},{19,3},{4,20},{20... | collective-permute-start | bytes 2654216 | tf_op jit(solution)/shard_map/ppermute | solution.py:136
  61.8 17.6 %collective-permute-start.14 = (bf16[256,768]{1,0:T(8,128)(2,1)}, bf16[256,768]{1,0:T(8,128)(2,1)S(1)}, u32[]{:S(2)}, u32[]{:S(2)}) collective-permute-start(bf16[256,768]{1,0:T(8,128)(2,1)} %copy-done.18), channel_id=1, source_target_pairs={{0,16},{16,0},{1,17},{17,1},{2,18},{18,2},{3,19},{19,3},{4,20},{20... | collective-permute-start | bytes 1179656 | tf_op jit(solution)/shard_map/ppermute | solution.py:136
  71.0 12.2 %collective-permute-start.13 = (bf16[128,1024]{1,0:T(8,128)(2,1)S(1)}, bf16[128,1024]{1,0:T(8,128)(2,1)S(1)}, u32[]{:S(2)}, u32[]{:S(2)}) collective-permute-start(bf16[128,1024]{1,0:T(8,128)(2,1)S(1)} %get-tuple-element.123), channel_id=1, source_target_pairs={{0,16},{16,0},{1,17},{17,1},{2,18},{18,2},{3,19},{19,3},{4,20},{20... | collective-permute-start | bytes 786440 | tf_op jit(solution)/shard_map/ppermute | solution.py:136
  85.3 27.6 %collective-permute-start.17 = (bf16[64,2176]{1,0:T(8,128)(2,1)S(1)}, bf16[64,2176]{1,0:T(8,128)(2,1)S(1)}, u32[]{:S(2)}, u32[]{:S(2)}) collective-permute-start(bf16[64,2176]{1,0:T(8,128)(2,1)S(1)} %get-tuple-element.129), channel_id=1, source_target_pairs={{8,0},{9,1},{10,2},{11,3},{12,4},{13,5},{14,6},{15,7},{0,8},{1,9},... | collective-permute-start | bytes 835592 | tf_op jit(solution)/shard_map/ppermute | solution.py:112
  88.2 24.8 %collective-permute-start.18 = (bf16[64,2176]{1,0:T(8,128)(2,1)S(1)}, bf16[64,2176]{1,0:T(8,128)(2,1)S(1)}, u32[]{:S(2)}, u32[]{:S(2)}) collective-permute-start(bf16[64,2176]{1,0:T(8,128)(2,1)S(1)} %get-tuple-element.129), channel_id=1, source_target_pairs={{12,0},{13,1},{14,2},{15,3},{0,4},{1,5},{2,6},{3,7},{4,8},{5,9},{6... | collective-permute-start | bytes 835592 | tf_op jit(solution)/shard_map/ppermute | solution.py:112
  90.1 28.9 %collective-permute-start.20 = (bf16[768,768]{1,0:T(8,128)(2,1)S(1)}, bf16[768,768]{1,0:T(8,128)(2,1)S(1)}, u32[]{:S(2)}, u32[]{:S(2)}) collective-permute-start(bf16[768,768]{1,0:T(8,128)(2,1)S(1)} %copy-done.17), channel_id=1, source_target_pairs={{0,16},{16,0},{1,17},{17,1},{2,18},{18,2},{3,19},{19,3},{4,20},{20... | collective-permute-start | bytes 3538952 | tf_op jit(solution)/shard_map/ppermute | solution.py:136
  113.1 28.0 %collective-permute-start.19 = (bf16[4,64,2176]{2,1,0:T(8,128)(2,1)S(1)}, bf16[4,64,2176]{2,1,0:T(8,128)(2,1)S(1)}, u32[]{:S(2)}, u32[]{:S(2)}) collective-permute-start(bf16[4,64,2176]{2,1,0:T(8,128)(2,1)S(1)} %pad_maximum_fusion.refs_0_), channel_id=1, source_target_pairs={{0,16},{16,0},{1,17},{17,1},{2,18},{18,2},{3,19},{19,3},{4,20},{20... | collective-permute-start | bytes 3342344 | tf_op jit(solution)/shard_map/ppermute | solution.py:136
  113.7 29.6 %collective-permute-start.21 = (bf16[4,64,2176]{2,1,0:T(8,128)(2,1)S(1)}, bf16[4,64,2176]{2,1,0:T(8,128)(2,1)S(1)}, u32[]{:S(2)}, u32[]{:S(2)}) collective-permute-start(bf16[4,64,2176]{2,1,0:T(8,128)(2,1)S(1)} %pad_maximum_fusion.refs_0_), channel_id=1, source_target_pairs={{2,0},{3,1},{0,2},{1,3},{6,4},{7,5},{4,6},{5,7},{10,8},{11,9},{8,1... | collective-permute-start | bytes 3342344 | tf_op jit(solution)/shard_map/ppermute | solution.py:122
  141.2 17.0 %collective-permute-start.27 = (bf16[768,768]{1,0:T(8,128)(2,1)S(1)}, bf16[768,768]{1,0:T(8,128)(2,1)S(1)}, u32[]{:S(2)}, u32[]{:S(2)}) collective-permute-start(bf16[768,768]{1,0:T(8,128)(2,1)S(1)} %collective-permute-done.20.refs_10_), channel_id=1, source_target_pairs={{1,0},{0,1},{3,2},{2,3},{5,4},{4,5},{7,6},{6,7},{9,8},{8,9},{11,10... | collective-permute-start | bytes 3538952 | tf_op jit(solution)/shard_map/ppermute | solution.py:132
  141.7 15.1 %collective-permute-start.22 = (bf16[2,64,2176]{2,1,0:T(8,128)(2,1)S(1)}, bf16[2,64,2176]{2,1,0:T(8,128)(2,1)S(1)}, u32[]{:S(2)}, u32[]{:S(2)}) collective-permute-start(bf16[2,64,2176]{2,1,0:T(8,128)(2,1)S(1)} %slice.71), channel_id=1, source_target_pairs={{2,0},{3,1},{0,2},{1,3},{6,4},{7,5},{4,6},{5,7},{10,8},{11,9},{8,1... | collective-permute-start | bytes 1671176 | tf_op jit(solution)/shard_map/ppermute | solution.py:122
  143.4 14.8 %collective-permute-start.23 = (bf16[2,64,2176]{2,1,0:T(8,128)(2,1)S(1)}, bf16[2,64,2176]{2,1,0:T(8,128)(2,1)S(1)}, u32[]{:S(2)}, u32[]{:S(2)}) collective-permute-start(bf16[2,64,2176]{2,1,0:T(8,128)(2,1)S(1)} %slice.87), channel_id=1, source_target_pairs={{0,16},{16,0},{1,17},{17,1},{2,18},{18,2},{3,19},{19,3},{4,20},{20... | collective-permute-start | bytes 1671176 | tf_op jit(solution)/shard_map/ppermute | solution.py:136
  166.7 14.2 %collective-permute-start.28 = (bf16[64,2048]{1,0:T(8,128)(2,1)S(1)}, bf16[64,2048]{1,0:T(8,128)(2,1)S(1)}, u32[]{:S(2)}, u32[]{:S(2)}) collective-permute-start(bf16[64,2048]{1,0:T(8,128)(2,1)S(1)} %pad_maximum_fusion.2), channel_id=1, source_target_pairs={{2,0},{3,1},{0,2},{1,3},{6,4},{7,5},{4,6},{5,7},{10,8},{11,9},{8,1... | collective-permute-start | bytes 786440 | tf_op jit(solution)/shard_map/ppermute | solution.py:122
  181.0 14.9 %collective-permute-start.29 = (bf16[128,2048]{1,0:T(8,128)(2,1)S(1)}, bf16[128,2048]{1,0:T(8,128)(2,1)S(1)}, u32[]{:S(2)}, u32[]{:S(2)}) collective-permute-start(bf16[128,2048]{1,0:T(8,128)(2,1)S(1)} %pad_maximum_fusion.1), channel_id=1, source_target_pairs={{0,16},{16,0},{1,17},{17,1},{2,18},{18,2},{3,19},{19,3},{4,20},{20... | collective-permute-start | bytes 1572872 | tf_op jit(solution)/shard_map/ppermute | solution.py:136
  181.7 18.0 %collective-permute-start.30 = (bf16[64,2048]{1,0:T(8,128)(2,1)S(1)}, bf16[64,2048]{1,0:T(8,128)(2,1)S(1)}, u32[]{:S(2)}, u32[]{:S(2)}) collective-permute-start(bf16[64,2048]{1,0:T(8,128)(2,1)S(1)} %add_convert_fusion.2), channel_id=1, source_target_pairs={{0,16},{16,0},{1,17},{17,1},{2,18},{18,2},{3,19},{19,3},{4,20},{20... | collective-permute-start | bytes 786440 | tf_op jit(solution)/shard_map/ppermute | solution.py:136
  183.3 16.4 %collective-permute-start.31 = (bf16[64,2048]{1,0:T(8,128)(2,1)S(1)}, bf16[64,2048]{1,0:T(8,128)(2,1)S(1)}, u32[]{:S(2)}, u32[]{:S(2)}) collective-permute-start(bf16[64,2048]{1,0:T(8,128)(2,1)S(1)} %convert_element_type.102), channel_id=1, source_target_pairs={{2,0},{3,1},{0,2},{1,3},{6,4},{7,5},{4,6},{5,7},{10,8},{11,9},{8,1... | collective-permute-start | bytes 786440 | tf_op jit(solution)/shard_map/ppermute | solution.py:122
  199.8 13.8 %collective-permute-start.32 = (bf16[16,2048]{1,0:T(8,128)(2,1)S(1)}, bf16[16,2048]{1,0:T(8,128)(2,1)S(1)}, u32[]{:S(2)}, u32[]{:S(2)}) collective-permute-start(bf16[16,2048]{1,0:T(8,128)(2,1)S(1)} %get-tuple-element.208), channel_id=1, source_target_pairs={{12,0},{13,1},{14,2},{15,3},{0,4},{1,5},{2,6},{3,7},{4,8},{5,9},{6... | collective-permute-start | bytes 196616 | tf_op jit(solution)/shard_map/ppermute | solution.py:112
  200.1 15.1 %collective-permute-start.33 = (bf16[16,2048]{1,0:T(8,128)(2,1)S(1)}, bf16[16,2048]{1,0:T(8,128)(2,1)S(1)}, u32[]{:S(2)}, u32[]{:S(2)}) collective-permute-start(bf16[16,2048]{1,0:T(8,128)(2,1)S(1)} %get-tuple-element.210), channel_id=1, source_target_pairs={{8,0},{9,1},{10,2},{11,3},{12,4},{13,5},{14,6},{15,7},{0,8},{1,9},... | collective-permute-start | bytes 196616 | tf_op jit(solution)/shard_map/ppermute | solution.py:112
  202.6 14.1 %collective-permute-start.34 = (bf16[16,2048]{1,0:T(8,128)(2,1)S(1)}, bf16[16,2048]{1,0:T(8,128)(2,1)S(1)}, u32[]{:S(2)}, u32[]{:S(2)}) collective-permute-start(bf16[16,2048]{1,0:T(8,128)(2,1)S(1)} %get-tuple-element.209), channel_id=1, source_target_pairs={{4,0},{5,1},{6,2},{7,3},{8,4},{9,5},{10,6},{11,7},{12,8},{13,9},{1... | collective-permute-start | bytes 196616 | tf_op jit(solution)/shard_map/ppermute | solution.py:112
  205.4 25.9 %collective-permute-start.36 = (bf16[128,2048]{1,0:T(8,128)(2,1)S(1)}, bf16[128,2048]{1,0:T(8,128)(2,1)S(1)}, u32[]{:S(2)}, u32[]{:S(2)}) collective-permute-start(bf16[128,2048]{1,0:T(8,128)(2,1)S(1)} %add_convert_fusion), channel_id=1, source_target_pairs={{2,0},{3,1},{0,2},{1,3},{6,4},{7,5},{4,6},{5,7},{10,8},{11,9},{8,1... | collective-permute-start | bytes 1572872 | tf_op jit(solution)/shard_map/ppermute | solution.py:122
  213.0 18.3 %collective-permute-start.35 = (bf16[128,2048]{1,0:T(8,128)(2,1)S(1)}, bf16[128,2048]{1,0:T(8,128)(2,1)S(1)}, u32[]{:S(2)}, u32[]{:S(2)}) collective-permute-start(bf16[128,2048]{1,0:T(8,128)(2,1)S(1)} %convert_element_type.108), channel_id=1, source_target_pairs={{0,16},{16,0},{1,17},{17,1},{2,18},{18,2},{3,19},{19,3},{4,20},{20... | collective-permute-start | bytes 1572872 | tf_op jit(solution)/shard_map/ppermute | solution.py:136
  213.6 12.9 %collective-permute-start.42 = (bf16[64,2048]{1,0:T(8,128)(2,1)S(1)}, bf16[64,2048]{1,0:T(8,128)(2,1)S(1)}, u32[]{:S(2)}, u32[]{:S(2)}) collective-permute-start(bf16[64,2048]{1,0:T(8,128)(2,1)S(1)} %convert_element_type.119), channel_id=1, source_target_pairs={{2,0},{3,1},{0,2},{1,3},{6,4},{7,5},{4,6},{5,7},{10,8},{11,9},{8,1... | collective-permute-start | bytes 786440 | tf_op jit(solution)/shard_map/ppermute | solution.py:122
  215.2 11.3 %collective-permute-start.41 = (bf16[64,2048]{1,0:T(8,128)(2,1)S(1)}, bf16[64,2048]{1,0:T(8,128)(2,1)S(1)}, u32[]{:S(2)}, u32[]{:S(2)}) collective-permute-start(bf16[64,2048]{1,0:T(8,128)(2,1)S(1)} %add_convert_fusion.1), channel_id=1, source_target_pairs={{0,16},{16,0},{1,17},{17,1},{2,18},{18,2},{3,19},{19,3},{4,20},{20... | collective-permute-start | bytes 786440 | tf_op jit(solution)/shard_map/ppermute | solution.py:136
  231.6 11.8 %collective-permute-start.38 = (bf16[32,2048]{1,0:T(8,128)(2,1)S(1)}, bf16[32,2048]{1,0:T(8,128)(2,1)S(1)}, u32[]{:S(2)}, u32[]{:S(2)}) collective-permute-start(bf16[32,2048]{1,0:T(8,128)(2,1)S(1)} %get-tuple-element.205), channel_id=1, source_target_pairs={{8,0},{9,1},{10,2},{11,3},{12,4},{13,5},{14,6},{15,7},{0,8},{1,9},... | collective-permute-start | bytes 393224 | tf_op jit(solution)/shard_map/ppermute | solution.py:112
  (37 other events, 259.7 us)

commit v5 on v4

--- a/solution.py
+++ b/solution.py
@@ -136,6 +136,17 @@
     return lax.ppermute(values, "dp", [(0, 1), (1, 0)])
 
 
+def flip_xy(values, depth):
+    pairs = [
+        ((1 - x) * 4 * depth + place(z, 1 - y, c), x * 4 * depth + place(z, y, c))
+        for x in range(2)
+        for z in range(depth)
+        for y in range(2)
+        for c in range(2)
+    ]
+    return lax.ppermute(values, ("dp", "expert"), pairs)
+
+
 def attend_kernel(pages_ref, lens_ref, q_ref, kv_ref, out_ref):
     scale = 1.0 / math.sqrt(HD)
     seqs, slots = pages_ref.shape
@@ -186,7 +197,7 @@
 def project_kernel(depth, ctx_ref, other_ref, *refs):
     pieces, (kept_ref, sent_ref) = refs[:-2], refs[-2:]
     half = ctx_ref.shape[0] // 2
-    width = pieces[0].shape[1]
+    feats, width = pieces[0].shape
     me = lax.axis_index("expert")
     x = lax.axis_index("dp")
     y = lax.rem(lax.div(me, 2), 2)
@@ -199,7 +210,11 @@
     for flip in range(2):
         at_y = y if flip == 0 else 1 - y
         for r in range(depth):
-            total = jnp.dot(rows, pieces[flip * depth + r][...], preferred_element_type=jnp.float32)
+            if r == 0:
+                piece = pieces[2 * flip][...]
+            else:
+                piece = pieces[2 * flip + 1][(r - 1) * feats : r * feats, :]
+            total = jnp.dot(rows, piece, preferred_element_type=jnp.float32)
             index = lax.rem(z + r, depth) * 2 + at_y
             columns = pl.ds(pl.multiple_of(index * width, width), width)
             kept_ref[:, columns] = total[: 2 * half]
@@ -302,8 +317,8 @@
 SLOTS = 3
 
 
-def experts_kernel(tile, out_tile, first_row, count, n_gate, n_up, *refs):
-    per_expert = n_gate + n_up + 1
+def experts_kernel(tile, out_tile, first_row, count, split, *refs):
+    per_expert = 6
     pieces, refs = refs[:count], refs[count:]
     weights, refs = refs[: 2 * per_expert], refs[2 * per_expert :]
     outs, refs = refs[:count], refs[count:]
@@ -340,20 +355,25 @@
 
     def fetch(t):
         e, j = t // tiles, t % tiles
-        mine = weights[e * per_expert : (e + 1) * per_expert]
+        gate_own, gate_far, mixed, up_own, up_far, _ = weights[
+            e * per_expert : (e + 1) * per_expert
+        ]
         group = []
-        sem = (n_gate + n_up) * (t % SLOTS)
-        for sources, target in ((mine[:n_gate], gate), (mine[n_gate:-1], up)):
+        sem = 6 * (t % SLOTS)
+        gates = ((gate_own, 0), (gate_far, 0), (mixed, 0))
+        ups = ((up_own, 0), (mixed, split), (up_far, 0))
+        for sources, target in ((gates, gate), (ups, up)):
             depth_at = 0
-            for source in sources:
+            for source, start in sources:
+                end = split if source is mixed and start == 0 else source.shape[0]
                 copy = pltpu.make_async_copy(
-                    source.at[:, pl.ds(j * tile, tile)],
-                    target.at[t % SLOTS, pl.ds(depth_at, source.shape[0]), :],
+                    source.at[pl.ds(start, end - start), pl.ds(j * tile, tile)],
+                    target.at[t % SLOTS, pl.ds(depth_at, end - start), :],
                     weight_sem.at[sem],
                 )
                 copy.start()
                 group.append(copy)
-                depth_at += source.shape[0]
+                depth_at += end - start
                 sem += 1
         return group
 
@@ -402,13 +422,9 @@
             out[:, lanes] = total[first : first + part].astype(out.dtype)
 
 
-def run_experts(pieces, kinds, first_row, each, experts_weights):
-    feats = experts_weights[0][2].shape[1]
-    width = experts_weights[0][0][0].shape[1]
-    n_gate, n_up = len(experts_weights[0][0]), len(experts_weights[0][1])
-    weights = [
-        array for gate, up, down in experts_weights for array in list(gate) + list(up) + [down]
-    ]
+def run_experts(pieces, kinds, first_row, each, weights, split):
+    feats = weights[-1].shape[1]
+    width = weights[0].shape[1]
     count = len(pieces)
     blocks = sum(piece.shape[0] for piece in pieces)
     total = blocks * each
@@ -416,7 +432,7 @@
     any_spec = pl.BlockSpec(memory_space=pl.ANY)
     vmem_spec = pl.BlockSpec(memory_space=pltpu.VMEM)
     return pl.pallas_call(
-        functools.partial(experts_kernel, tile, 512, first_row, count, n_gate, n_up),
+        functools.partial(experts_kernel, tile, 512, first_row, count, split),
         out_shape=tuple(
             jax.ShapeDtypeStruct((piece.shape[0] * each, feats), kind)
             for piece, kind in zip(pieces, kinds)
@@ -431,7 +447,7 @@
             pltpu.VMEM((2 * width, feats), jnp.bfloat16),
             pltpu.VMEM((total, 2 * width), jnp.bfloat16),
             pltpu.SemaphoreType.DMA((3 * count,)),
-            pltpu.SemaphoreType.DMA((SLOTS * (n_gate + n_up),)),
+            pltpu.SemaphoreType.DMA((SLOTS * 6,)),
             pltpu.SemaphoreType.DMA((2,)),
         ],
         compiler_params=pltpu.CompilerParams(vmem_limit_bytes=30 * MIB),
@@ -444,20 +460,12 @@
     )(*pieces, *weights)
 
 
-def send_sides(out_l, out_x, out_y, far, k, depth):
-    if k % 2 == 0:
-        out_x = out_x + far.astype(jnp.float32)
-    else:
-        out_y = out_y + far.astype(jnp.float32)
-    return (
-        out_l,
-        flip_x(out_x.astype(jnp.bfloat16)),
-        flip_y(out_y.astype(jnp.bfloat16), depth),
-    )
-
-
-def send_line(out_l, back_x, back_y, depth):
-    full = out_l + back_x.astype(jnp.float32) + back_y.astype(jnp.float32)
+def diagonal(line_x, line_y, depth):
+    half = depth // 2
+    return flip_y(line_x[:half], depth), flip_x(line_y[half:])
+
+
+def send_line(full, depth):
     full = full.reshape(depth, -1, full.shape[1])
     total = full[0]
     for s in range(1, depth):
@@ -489,24 +497,39 @@
     width = -(-units_here // 256) * 256
     barrier = lax.optimization_barrier
 
-    near = [w_out] + [shift_z(w_out, depth, s) for s in range(1, depth)]
+    shifted = [shift_z(w_out, depth, s) for s in range(1, depth)]
     across_own = flip_y(w_out, depth)
 
     feats_here = w_gate.shape[1]
-    early = feats_here * 7 // 16
+    early = feats_here * 7 // 8
     gate_own, *gate_sent = cut(w_gate, width, (early, feats_here - early))
-    gate_far = [flip_x(piece) for piece in gate_sent]
-    queries, gate_sent = barrier((queries, gate_sent))
+    gate_far = flip_x(gate_sent[0])
+    split = feats_here - early
+    queries, gate_sent[1], gate_own = barrier((queries, gate_sent[1], gate_own))
     context = attend_here(queries, kv_pool, page_table, ctx_lens)
-    near[1:], across_own, gate_far[0], gate_sent[1], w_up, w_down, gate_own, context = barrier(
-        (near[1:], across_own, gate_far[0], gate_sent[1], w_up, w_down, gate_own, context)
+    context, w_up, w_down = barrier((context, w_up, w_down))
+    early = feats_here * 27 // 64
+    up_own, *up_sent = cut(w_up, width, (early, feats_here - early))
+    mixed_sent = jnp.concatenate([gate_sent[1], up_sent[0]], axis=0)
+    shifted, across_own, gate_far, mixed_sent, up_sent[1], gate_own, up_own, w_down, context = (
+        barrier(
+            (
+                shifted,
+                across_own,
+                gate_far,
+                mixed_sent,
+                up_sent[1],
+                gate_own,
+                up_own,
+                w_down,
+                context,
+            )
+        )
     )
+    shifted = jnp.concatenate(shifted, axis=0)
+    across = flip_y(shifted, depth)
+    mixed_far = flip_x(mixed_sent)
     other = flip_core(context, depth)
-    gate_far[1] = flip_x(gate_sent[1])
-    across = [across_own] + [flip_y(piece, depth) for piece in near[1:]]
-    early = feats_here // 4
-    up_own, *up_sent = cut(w_up, width, (early, feats_here - early))
-    up_early = flip_x(up_sent[0])
     down_own = w_down[0]
     here_core = [flip_core(array, depth) for array in (gate_own, up_own, down_own)]
 
@@ -518,56 +541,71 @@
         [share_high, share_low, jnp.zeros((block, 128 - 2 * experts), jnp.bfloat16)], axis=1
     )
 
-    across, share, here_core = barrier((across, share, here_core))
-    kept, sent = project(context, other, near + across, depth)
-    kept, sent, gate_far[1] = barrier((kept, sent, gate_far[1]))
-    received, up_sent[1], up_early = barrier((flip_x(sent), up_sent[1], up_early))
-    up_far = [up_early, flip_x(up_sent[1])]
-    gate_far_core = [flip_core(piece, depth) for piece in gate_far]
+    across, share, here_core, mixed_far = barrier((across, share, here_core, mixed_far))
+    kept, sent = project(context, other, [w_out, shifted, across_own, across], depth)
+    gate_far_core = flip_core(gate_far, depth)
+    mixed_far_core = flip_core(mixed_far, depth)
+    received, up_late = barrier((flip_x(sent), up_sent[1]))
+    up_far = flip_x(up_late)
     total = kept + received.astype(jnp.float32)
     back = flip_core(total[block:], depth)
     hidden_state, message = join(total[:block], back, residual, moe_gain, share, w_out.shape[1])
 
-    line = jnp.stack([message] + [shift_z(message, depth, s) for s in range(1, depth)])
-    line_x, up_far[1] = barrier((flip_x(line), up_far[1]))
-    line_y = flip_y(line, depth)
-    mid_z = depth // 2
-    low = flip_y(line_x[:mid_z], depth)
-    high = flip_x(line_y[mid_z:])
-    up_far_core = [flip_core(piece, depth) for piece in up_far]
-    weights = [
-        ([gate_own] + gate_far, [up_own] + up_far, down_own),
-        ([here_core[0]] + gate_far_core, [here_core[1]] + up_far_core, here_core[2]),
+    rows = block // 2
+    arrived = [message] + [shift_z(message, depth, s) for s in range(1, depth)]
+    ready = []
+    for k in range(2):
+        line = jnp.stack([piece[rows * k : rows * (k + 1)] for piece in arrived])
+        if k > 0:
+            line, ready[0][3], ready[0][4] = barrier((line, ready[0][3], ready[0][4]))
+        line_x = flip_x(line)
+        line_y = flip_y(line, depth)
+        if k == 0:
+            line_x, line_y, up_far = barrier((line_x, line_y, up_far))
+            ready.append([line, line_x, line_y, *diagonal(line_x, line_y, depth)])
+        else:
+            ready.append([line, line_x, line_y])
+
+    weights = [gate_own, gate_far, mixed_far, up_own, up_far, down_own]
+    weights += [
+        here_core[0],
+        gate_far_core,
+        mixed_far_core,
+        here_core[1],
+        flip_core(up_far, depth),
+        here_core[2],
     ]
 
-    moe = []
-    diagonal = []
-    sides = []
-    at = 0
-    quarter = block // 4
-    for k, each in enumerate((quarter, 2 * quarter, quarter)):
-        outs = run_experts(
-            [line, line_x, line_y, low, high],
-            (jnp.float32, jnp.float32, jnp.float32, jnp.bfloat16, jnp.bfloat16),
+    backs = []
+    last = None
+    for chunk, at, each in ((0, 0, rows), (1, 0, rows // 2), (1, rows // 2, rows // 2)):
+        pieces = ready[chunk]
+        if len(pieces) == 3:
+            pieces[1], pieces[2], last = barrier((pieces[1], pieces[2], last))
+            pieces += diagonal(pieces[1], pieces[2], depth)
+        elif last is not None:
+            pieces[0], last = barrier((pieces[0], last))
+        out_l, out_x, out_y, out_low, out_high = run_experts(
+            pieces,
+            (jnp.float32, jnp.bfloat16, jnp.bfloat16, jnp.bfloat16, jnp.bfloat16),
             at,
             each,
             weights,
+            split,
         )
-        at += each
-        if k > 0:
-            outs, diagonal[k - 1] = barrier((outs, diagonal[k - 1]))
-            sides.append(send_sides(*diagonal[k - 1], k - 1, depth))
-        if k > 1:
-            outs, sides[k - 2] = barrier((outs, sides[k - 2]))
-            moe.append(send_line(*sides[k - 2], depth))
-        line, outs = barrier((line, outs))
-        out_l, out_x, out_y, out_low, out_high = outs
+        last = out_low
         far = jnp.concatenate([out_low, out_high], axis=0)
-        far = flip_y(far, depth) if k % 2 == 0 else flip_x(far)
-        diagonal.append((out_l, out_x, out_y, far))
-    sides.append(send_sides(*diagonal[-1], len(diagonal) - 1, depth))
-    for side in sides[-2:]:
-        moe.append(send_line(*side, depth))
+        backs.append((out_l, flip_x(out_x), flip_y(out_y, depth), flip_xy(far, depth)))
+    moe = []
+    full = None
+    for back in backs:
+        if full is not None:
+            back, full = barrier((back, full))
+            moe.append(send_line(full, depth))
+        full = back[0]
+        for part in back[1:]:
+            full = full + part.astype(jnp.float32)
+    moe.append(send_line(full, depth))
     combined = hidden_state + jnp.concatenate(moe, axis=0)
     return normalize(combined, final_gain).astype(jnp.bfloat16)
 

time: 245 us -> 221 us (0.902)
  waiting for transfers between devices: 139 us -> 105 us
  starting transfers between devices: 47.7 us -> 59.5 us
  local copies, waits for them, and re-layouts: 12.8 us -> 10 us
    ppermute x11, waiting for transfers between devices: 47.8 us -> 28.7 us  [flip_x(): return lax.ppermute(values, 'dp', [(0, 1), (1, 0)])]
    ppermute x0 -> x3, starting transfers between devices: none -> 7.1 us  [flip_xy(): return lax.ppermute(values, ('dp', 'expert'), pairs)]
    ppermute x15, starting transfers between devices: 21.6 us -> 27.4 us  [shift_z(): return lax.ppermute(values, 'expert', pairs)]
    ppermute x15, waiting for transfers between devices: 41.9 us -> 36.6 us  [shift_z(): return lax.ppermute(values, 'expert', pairs)]
    ppermute x11 -> x9, waiting for transfers between devices: 44.4 us -> 39.3 us  [flip_y(): return lax.ppermute(values, 'expert', pairs)]
    ppermute x9 -> x8, waiting for transfers between devices: 4.81 us -> 0.02 us  [flip_core(): return lax.ppermute(values, 'expert', pairs)]
    unnamed x46 -> x36, local copies, waits for them, and re-layouts: 12.2 us -> 7.71 us
    ppermute x11 -> x9, starting transfers between devices: 14.1 us -> 10.6 us  [flip_y(): return lax.ppermute(values, 'expert', pairs)]
  transfers between devices with their start and end apart: 46 -> 46, of which waited for: 25 -> 19; matrix products, arithmetic and copies ran while one was open for 1% -> 3% of each run, Pallas kernels for 13% -> 17%
where the time goes in v5:
time: 221 us
  waiting for transfers between devices  105 us (48%)
  starting transfers between devices  59.5 us (27%)
  Pallas kernels  43.1 us (20%)
  local copies, waits for them, and re-layouts  10 us (5%)
  other arithmetic  3.17 us (1%)
    ppermute x9, waiting for transfers between devices, flip_y(): return lax.ppermute(values, 'expert', pairs)  39.3 us
    ppermute x15, waiting for transfers between devices, shift_z(): return lax.ppermute(values, 'expert', pairs)  36.6 us
    pallas_call x3, Pallas kernels, run_experts(): pl.pallas_call(functools.partial(experts_kernel, tile, 512, first_row, co...  31 us
    ppermute x11, waiting for transfers between devices, flip_x(): return lax.ppermute(values, 'dp', [(0, 1), (1, 0)])  28.7 us
    ppermute x15, starting transfers between devices, shift_z(): return lax.ppermute(values, 'expert', pairs)  27.4 us
    ppermute x11, starting transfers between devices, flip_x(): return lax.ppermute(values, 'dp', [(0, 1), (1, 0)])  13.2 us
    ppermute x9, starting transfers between devices, flip_y(): return lax.ppermute(values, 'expert', pairs)  10.6 us
    unnamed x36, local copies, waits for them, and re-layouts  7.71 us
  transfers between devices with their start and end apart: 46, of which 19 were waited for; matrix products, arithmetic and copies ran while one was open for 3% of the time, Pallas kernels for 17%

profile of v5, /device:TPU:0, one launch (start us, length us, event | category | flops | bytes accessed | tf_op | source)
XLA Modules:
  0.0 220.9 jit_solution(18300581933538654543)
XLA Ops:
  0.0 1.8 copy-done.1
  1.8 1.9 cut.2
  4.4 2.9 %collective-permute-start.4 = (bf16[896,768]{1,0:T(8,128)(2,1)}, bf16[896,768]{1,0:T(8,128)(2,1)}, u32[]{:S(2)}, u32[]{:S(2)}) collective-permute-start(bf16[896,768]{1,0:T(8,128)(2,1)} %get-tuple-element.74), channel_id=1, source_target_pairs={{0,16},{16,0},{1,17},{17,1},{2,18},{18,2},{3,19},{19,3},{4,20},{20... | collective-permute-start | bytes 4128776 | tf_op jit(solution)/shard_map/ppermute | solution.py:136
  7.3 3.6 %collective-permute-start = (bf16[1024,128]{1,0:T(8,128)(2,1)S(1)}, bf16[1024,128]{1,0:T(8,128)(2,1)}, u32[]{:S(2)}, u32[]{:S(2)}) collective-permute-start(bf16[1024,128]{1,0:T(8,128)(2,1)S(1)} %copy-done.5), channel_id=1, source_target_pairs={{4,0},{5,1},{6,2},{7,3},{8,4},{9,5},{10,6},{11,7},{12,8},{13,9},{1... | collective-permute-start | bytes 786440 | tf_op jit(solution)/shard_map/ppermute | solution.py:112
  13.6 5.8 %attend.1.ctx_ref = bf16[128,1024]{1,0:T(8,128)(2,1)S(1)} custom-call(s32[2,4]{1,0:T(2,128)S(1)} %copy-done.10, s32[128,1]{1,0:T(8,128)S(1)} %copy.20.lens_ref, bf16[128,1024]{1,0:T(8,128)(2,1)S(1)} %copy-done.4, bf16[2,8,64,1024]{3,2,1,0:T(8,128)(2,1)S(1)} %copy-done.3), custom_call_target="tpu_custom_call" | custom-call | flops 134217728 | bytes 2621440 | tf_op jit(solution)/shard_map/attend/pallas_call | solution.py:182
  19.4 1.8 copy-done.2
  23.7 9.3 %collective-permute-done.1 = bf16[1024,128]{1,0:T(8,128)(2,1)} collective-permute-done((bf16[1024,128]{1,0:T(8,128)(2,1)S(1)}, bf16[1024,128]{1,0:T(8,128)(2,1)}, u32[]{:S(2)}, u32[]{:S(2)}) %collective-permute-start.1) | collective-permute-done | bytes 262176 | tf_op jit(solution)/shard_map/ppermute | solution.py:112
  33.1 4.7 %collective-permute-done.4.refs_6_ = bf16[896,768]{1,0:T(8,128)(2,1)} collective-permute-done((bf16[896,768]{1,0:T(8,128)(2,1)}, bf16[896,768]{1,0:T(8,128)(2,1)}, u32[]{:S(2)}, u32[]{:S(2)}) %collective-permute-start.4) | collective-permute-done | bytes 1376288 | tf_op jit(solution)/shard_map/ppermute | solution.py:136
  43.4 1.8 collective-permute-start.6
  46.9 16.8 %collective-permute-done.6.refs_3_ = bf16[3072,128]{1,0:T(8,128)(2,1)} collective-permute-done((bf16[3072,128]{1,0:T(8,128)(2,1)}, bf16[3072,128]{1,0:T(8,128)(2,1)}, u32[]{:S(2)}, u32[]{:S(2)}) %collective-permute-start.6) | collective-permute-done | bytes 786464 | tf_op jit(solution)/shard_map/ppermute | solution.py:122
  63.8 2.9 %collective-permute-done.10.refs_7_ = bf16[560,768]{1,0:T(8,128)(2,1)} collective-permute-done((bf16[560,768]{1,0:T(8,128)(2,1)}, bf16[560,768]{1,0:T(8,128)(2,1)}, u32[]{:S(2)}, u32[]{:S(2)}) %collective-permute-start.10) | collective-permute-done | bytes 860192 | tf_op jit(solution)/shard_map/ppermute | solution.py:136
  66.7 2.7 %project.1 = (f32[128,1024]{1,0:T(8,128)S(1)}, bf16[128,1024]{1,0:T(8,128)(2,1)S(1)}) custom-call(bf16[128,1024]{1,0:T(8,128)(2,1)S(1)} %attend.1.ctx_ref, bf16[128,1024]{1,0:T(8,128)(2,1)S(1)} %collective-permute-done.5.other_ref, bf16[1024,128]{1,0:T(8,128)(2,1)S(1)} %copy-done.5, bf16[3072,128]{1,0:T(8,128)(2,1)} %constant_dynamic-update-slice_fusion.refs_1_, ...), custom_call_target="tpu_custom_call" | custom-call | flops 536870912 | bytes 2883584 | tf_op jit(solution)/shard_map/project/pallas_call | solution.py:227
  71.0 6.1 %collective-permute-done.11 = bf16[128,1024]{1,0:T(8,128)(2,1)S(1)} collective-permute-done((bf16[128,1024]{1,0:T(8,128)(2,1)S(1)}, bf16[128,1024]{1,0:T(8,128)(2,1)S(1)}, u32[]{:S(2)}, u32[]{:S(2)}) %collective-permute-start.11) | collective-permute-done | bytes 262176 | tf_op jit(solution)/shard_map/ppermute | solution.py:136
  79.1 3.7 %collective-permute-start.13 = (bf16[64,2176]{1,0:T(8,128)(2,1)S(1)}, bf16[64,2176]{1,0:T(8,128)(2,1)S(1)}, u32[]{:S(2)}, u32[]{:S(2)}) collective-permute-start(bf16[64,2176]{1,0:T(8,128)(2,1)S(1)} %get-tuple-element.102), channel_id=1, source_target_pairs={{4,0},{5,1},{6,2},{7,3},{8,4},{9,5},{10,6},{11,7},{12,8},{13,9},{1... | collective-permute-start | bytes 835592 | tf_op jit(solution)/shard_map/ppermute | solution.py:112
  83.8 6.1 %collective-permute-done.13 = bf16[64,2176]{1,0:T(8,128)(2,1)S(1)} collective-permute-done((bf16[64,2176]{1,0:T(8,128)(2,1)S(1)}, bf16[64,2176]{1,0:T(8,128)(2,1)S(1)}, u32[]{:S(2)}, u32[]{:S(2)}) %collective-permute-start.13) | collective-permute-done | bytes 278560 | tf_op jit(solution)/shard_map/ppermute | solution.py:112
  89.9 16.9 %collective-permute-done.14 = bf16[64,2176]{1,0:T(8,128)(2,1)S(1)} collective-permute-done((bf16[64,2176]{1,0:T(8,128)(2,1)S(1)}, bf16[64,2176]{1,0:T(8,128)(2,1)S(1)}, u32[]{:S(2)}, u32[]{:S(2)}) %collective-permute-start.14) | collective-permute-done | bytes 278560 | tf_op jit(solution)/shard_map/ppermute | solution.py:112
  109.5 11.4 %collective-permute-done.16.refs_1_ = bf16[4,32,2176]{2,1,0:T(8,128)(2,1)S(1)} collective-permute-done((bf16[4,32,2176]{2,1,0:T(8,128)(2,1)S(1)}, bf16[4,32,2176]{2,1,0:T(8,128)(2,1)S(1)}, u32[]{:S(2)}, u32[]{:S(2)}) %collective-permute-start.16) | collective-permute-done | bytes 557088 | tf_op jit(solution)/shard_map/ppermute | solution.py:136
  124.4 6.7 %collective-permute-done.19.refs_3_ = bf16[2,32,2176]{2,1,0:T(8,128)(2,1)S(1)} collective-permute-done((bf16[2,32,2176]{2,1,0:T(8,128)(2,1)S(1)}, bf16[2,32,2176]{2,1,0:T(8,128)(2,1)S(1)}, u32[]{:S(2)}, u32[]{:S(2)}) %collective-permute-start.19) | collective-permute-done | bytes 278560 | tf_op jit(solution)/shard_map/ppermute | solution.py:122
  133.6 13.6 %experts.3 = (f32[128,2048]{1,0:T(8,128)S(1)}, bf16[128,2048]{1,0:T(8,128)(2,1)S(1)}, bf16[128,2048]{1,0:T(8,128)(2,1)S(1)}, bf16[64,2048]{1,0:T(8,128)(2,1)S(1)}, bf16[64,2048]{1,0:T(8,128)(2,1)S(1)}) custom-call(bf16[4,32,2176]{2,1,0:T(8,128)(2,1)S(1)} %pad_maximum_fusion.2.refs_0_, bf16[4,32,2176]{2,1,0:T(8,128)(2,1)S(1)} %collective-permute-done.16.refs_1_, ...), custom_call_target="tpu_custom_call" | custom-call | flops 9663676416 | bytes 31457280 | tf_op jit(solution)/shard_map/experts/pallas_call | solution.py:434
  153.4 11.6 %collective-permute-done.26.refs_3_ = bf16[2,32,2176]{2,1,0:T(8,128)(2,1)S(1)} collective-permute-done((bf16[2,32,2176]{2,1,0:T(8,128)(2,1)S(1)}, bf16[2,32,2176]{2,1,0:T(8,128)(2,1)S(1)}, u32[]{:S(2)}, u32[]{:S(2)}) %collective-permute-start.26) | collective-permute-done | bytes 278560 | tf_op jit(solution)/shard_map/ppermute | solution.py:122
  165.0 8.8 %experts.4 = (f32[64,2048]{1,0:T(8,128)S(1)}, bf16[64,2048]{1,0:T(8,128)(2,1)S(1)}, bf16[64,2048]{1,0:T(8,128)(2,1)S(1)}, bf16[32,2048]{1,0:T(8,128)(2,1)S(1)}, bf16[32,2048]{1,0:T(8,128)(2,1)S(1)}) custom-call(bf16[4,32,2176]{2,1,0:T(8,128)(2,1)S(1)} %pad_maximum_fusion.1.refs_0_, bf16[4,32,2176]{2,1,0:T(8,128)(2,1)S(1)} %collective-permute-done.21.refs_1_, ...), custom_call_target="tpu_custom_call" | custom-call | flops 4831838208 | bytes 25165824 | tf_op jit(solution)/shard_map/experts/pallas_call | solution.py:434
  173.9 3.5 %collective-permute-start.30 = (bf16[64,2048]{1,0:T(8,128)(2,1)S(1)}, bf16[64,2048]{1,0:T(8,128)(2,1)S(1)}, u32[]{:S(2)}, u32[]{:S(2)}) collective-permute-start(bf16[64,2048]{1,0:T(8,128)(2,1)S(1)} %pad_maximum_fusion.4), channel_id=1, source_target_pairs={{18,0},{19,1},{16,2},{17,3},{22,4},{23,5},{20,6},{21,7},{26,8},{27... | collective-permute-start | bytes 786440 | tf_op jit(solution)/shard_map/ppermute | solution.py:147
  177.4 8.6 %experts.5 = (f32[64,2048]{1,0:T(8,128)S(1)}, bf16[64,2048]{1,0:T(8,128)(2,1)S(1)}, bf16[64,2048]{1,0:T(8,128)(2,1)S(1)}, bf16[32,2048]{1,0:T(8,128)(2,1)S(1)}, bf16[32,2048]{1,0:T(8,128)(2,1)S(1)}) custom-call(bf16[4,32,2176]{2,1,0:T(8,128)(2,1)S(1)} %pad_maximum_fusion.1.refs_0_, bf16[4,32,2176]{2,1,0:T(8,128)(2,1)S(1)} %collective-permute-done.21.refs_1_, ...), custom_call_target="tpu_custom_call" | custom-call | flops 4831838208 | bytes 25165824 | tf_op jit(solution)/shard_map/experts/pallas_call | solution.py:434
  187.1 2.5 %collective-permute-start.39 = (bf16[64,2048]{1,0:T(8,128)(2,1)S(1)}, bf16[64,2048]{1,0:T(8,128)(2,1)S(1)}, u32[]{:S(2)}, u32[]{:S(2)}) collective-permute-start(bf16[64,2048]{1,0:T(8,128)(2,1)S(1)} %pad_maximum_fusion.5), channel_id=1, source_target_pairs={{18,0},{19,1},{16,2},{17,3},{22,4},{23,5},{20,6},{21,7},{26,8},{27... | collective-permute-start | bytes 786440 | tf_op jit(solution)/shard_map/ppermute | solution.py:147
  191.8 3.1 %collective-permute-done.29 = bf16[64,2048]{1,0:T(8,128)(2,1)S(1)} collective-permute-done((bf16[64,2048]{1,0:T(8,128)(2,1)S(1)}, bf16[64,2048]{1,0:T(8,128)(2,1)S(1)}, u32[]{:S(2)}, u32[]{:S(2)}) %collective-permute-start.29) | collective-permute-done | bytes 262176 | tf_op jit(solution)/shard_map/ppermute | solution.py:122
  195.8 2.0 collective-permute-start.35
  197.9 2.0 collective-permute-done.37
  200.8 2.0 collective-permute-start.41
  202.8 2.8 %collective-permute-start.42 = (bf16[16,2048]{1,0:T(8,128)(2,1)S(1)}, bf16[16,2048]{1,0:T(8,128)(2,1)S(1)}, u32[]{:S(2)}, u32[]{:S(2)}) collective-permute-start(bf16[16,2048]{1,0:T(8,128)(2,1)S(1)} %get-tuple-element.159), channel_id=1, source_target_pairs={{4,0},{5,1},{6,2},{7,3},{8,4},{9,5},{10,6},{11,7},{12,8},{13,9},{1... | collective-permute-start | bytes 196616 | tf_op jit(solution)/shard_map/ppermute | solution.py:112
  206.2 3.7 %collective-permute-start.43 = (bf16[16,2048]{1,0:T(8,128)(2,1)S(1)}, bf16[16,2048]{1,0:T(8,128)(2,1)S(1)}, u32[]{:S(2)}, u32[]{:S(2)}) collective-permute-start(bf16[16,2048]{1,0:T(8,128)(2,1)S(1)} %get-tuple-element.161), channel_id=1, source_target_pairs={{12,0},{13,1},{14,2},{15,3},{0,4},{1,5},{2,6},{3,7},{4,8},{5,9},{6... | collective-permute-start | bytes 196616 | tf_op jit(solution)/shard_map/ppermute | solution.py:112
  211.8 2.9 %collective-permute-start.45 = (bf16[16,2048]{1,0:T(8,128)(2,1)S(1)}, bf16[16,2048]{1,0:T(8,128)(2,1)S(1)}, u32[]{:S(2)}, u32[]{:S(2)}) collective-permute-start(bf16[16,2048]{1,0:T(8,128)(2,1)S(1)} %get-tuple-element.162), channel_id=1, source_target_pairs={{4,0},{5,1},{6,2},{7,3},{8,4},{9,5},{10,6},{11,7},{12,8},{13,9},{1... | collective-permute-start | bytes 196616 | tf_op jit(solution)/shard_map/ppermute | solution.py:112
  216.7 3.1 %collective-permute-done.36 = bf16[32,2048]{1,0:T(8,128)(2,1)S(1)} collective-permute-done((bf16[32,2048]{1,0:T(8,128)(2,1)S(1)}, bf16[32,2048]{1,0:T(8,128)(2,1)S(1)}, u32[]{:S(2)}, u32[]{:S(2)}) %collective-permute-start.36) | collective-permute-done | bytes 131104 | tf_op jit(solution)/shard_map/ppermute | solution.py:112
  (144 shorter events, 43.3 us)
Async XLA Ops:
  4.4 33.4 %collective-permute-start.4 = (bf16[896,768]{1,0:T(8,128)(2,1)}, bf16[896,768]{1,0:T(8,128)(2,1)}, u32[]{:S(2)}, u32[]{:S(2)}) collective-permute-start(bf16[896,768]{1,0:T(8,128)(2,1)} %get-tuple-element.74), channel_id=1, source_target_pairs={{0,16},{16,0},{1,17},{17,1},{2,18},{18,2},{3,19},{19,3},{4,20},{20... | collective-permute-start | bytes 4128776 | tf_op jit(solution)/shard_map/ppermute | solution.py:136
  7.3 16.4 %collective-permute-start = (bf16[1024,128]{1,0:T(8,128)(2,1)S(1)}, bf16[1024,128]{1,0:T(8,128)(2,1)}, u32[]{:S(2)}, u32[]{:S(2)}) collective-permute-start(bf16[1024,128]{1,0:T(8,128)(2,1)S(1)} %copy-done.5), channel_id=1, source_target_pairs={{4,0},{5,1},{6,2},{7,3},{8,4},{9,5},{10,6},{11,7},{12,8},{13,9},{1... | collective-permute-start | bytes 786440 | tf_op jit(solution)/shard_map/ppermute | solution.py:112
  10.9 22.1 %collective-permute-start.1 = (bf16[1024,128]{1,0:T(8,128)(2,1)S(1)}, bf16[1024,128]{1,0:T(8,128)(2,1)}, u32[]{:S(2)}, u32[]{:S(2)}) collective-permute-start(bf16[1024,128]{1,0:T(8,128)(2,1)S(1)} %copy-done.5), channel_id=1, source_target_pairs={{8,0},{9,1},{10,2},{11,3},{12,4},{13,5},{14,6},{15,7},{0,8},{1,9},... | collective-permute-start | bytes 786440 | tf_op jit(solution)/shard_map/ppermute | solution.py:112
  10.9 22.1 %collective-permute-start.2 = (bf16[1024,128]{1,0:T(8,128)(2,1)S(1)}, bf16[1024,128]{1,0:T(8,128)(2,1)}, u32[]{:S(2)}, u32[]{:S(2)}) collective-permute-start(bf16[1024,128]{1,0:T(8,128)(2,1)S(1)} %copy-done.5), channel_id=1, source_target_pairs={{12,0},{13,1},{14,2},{15,3},{0,4},{1,5},{2,6},{3,7},{4,8},{5,9},{6... | collective-permute-start | bytes 786440 | tf_op jit(solution)/shard_map/ppermute | solution.py:112
  11.9 21.1 %collective-permute-start.3 = (bf16[1024,128]{1,0:T(8,128)(2,1)S(1)}, bf16[1024,128]{1,0:T(8,128)(2,1)}, u32[]{:S(2)}, u32[]{:S(2)}) collective-permute-start(bf16[1024,128]{1,0:T(8,128)(2,1)S(1)} %copy-done.5), channel_id=1, source_target_pairs={{2,0},{3,1},{0,2},{1,3},{6,4},{7,5},{4,6},{5,7},{10,8},{11,9},{8,1... | collective-permute-start | bytes 786440 | tf_op jit(solution)/shard_map/ppermute | solution.py:122
  37.8 28.9 %collective-permute-start.9 = (bf16[704,2048]{1,0:T(8,128)(2,1)S(1)}, bf16[704,2048]{1,0:T(8,128)(2,1)}, u32[]{:S(2)}, u32[]{:S(2)}) collective-permute-start(bf16[704,2048]{1,0:T(8,128)(2,1)S(1)} %bitcast.19), channel_id=1, source_target_pairs={{1,0},{0,1},{3,2},{2,3},{5,4},{4,5},{7,6},{6,7},{9,8},{8,9},{11,10... | collective-permute-start | bytes 8650760 | tf_op jit(solution)/shard_map/ppermute | solution.py:132
  37.8 28.9 %collective-permute-start.7 = (bf16[1024,768]{1,0:T(8,128)(2,1)}, bf16[1024,768]{1,0:T(8,128)(2,1)}, u32[]{:S(2)}, u32[]{:S(2)}) collective-permute-start(bf16[1024,768]{1,0:T(8,128)(2,1)} %get-tuple-element.91.refs_5_), channel_id=1, source_target_pairs={{1,0},{0,1},{3,2},{2,3},{5,4},{4,5},{7,6},{6,7},{9,8},{8,9},{11,10... | collective-permute-start | bytes 4718600 | tf_op jit(solution)/shard_map/ppermute | solution.py:132
  38.3 28.4 %collective-permute-start.8 = (bf16[1024,768]{1,0:T(8,128)(2,1)}, bf16[1024,768]{1,0:T(8,128)(2,1)}, u32[]{:S(2)}, u32[]{:S(2)}) collective-permute-start(bf16[1024,768]{1,0:T(8,128)(2,1)} %get-tuple-element.92.refs_8_), channel_id=1, source_target_pairs={{1,0},{0,1},{3,2},{2,3},{5,4},{4,5},{7,6},{6,7},{9,8},{8,9},{11,10... | collective-permute-start | bytes 4718600 | tf_op jit(solution)/shard_map/ppermute | solution.py:132
  43.4 20.2 %collective-permute-start.6 = (bf16[3072,128]{1,0:T(8,128)(2,1)}, bf16[3072,128]{1,0:T(8,128)(2,1)}, u32[]{:S(2)}, u32[]{:S(2)}) collective-permute-start(bf16[3072,128]{1,0:T(8,128)(2,1)} %constant_dynamic-update-slice_fusion.refs_1_), channel_id=1, source_target_pairs={{2,0},{3,1},{0,2},{1,3},{6,4},{7,5},{4,6},{5,7},{10,8},{11,9},{8,1... | collective-permute-start | bytes 2359304 | tf_op jit(solution)/shard_map/ppermute | solution.py:122
  45.2 21.5 %collective-permute-start.10 = (bf16[560,768]{1,0:T(8,128)(2,1)}, bf16[560,768]{1,0:T(8,128)(2,1)}, u32[]{:S(2)}, u32[]{:S(2)}) collective-permute-start(bf16[560,768]{1,0:T(8,128)(2,1)} %pad_maximum_fusion), channel_id=1, source_target_pairs={{0,16},{16,0},{1,17},{17,1},{2,18},{18,2},{3,19},{19,3},{4,20},{20... | collective-permute-start | bytes 2580488 | tf_op jit(solution)/shard_map/ppermute | solution.py:136
  77.3 32.2 %collective-permute-start.18 = (bf16[592,768]{1,0:T(8,128)(2,1)S(1)}, bf16[592,768]{1,0:T(8,128)(2,1)S(1)}, u32[]{:S(2)}, u32[]{:S(2)}) collective-permute-start(bf16[592,768]{1,0:T(8,128)(2,1)S(1)} %copy-done.12), channel_id=1, source_target_pairs={{0,16},{16,0},{1,17},{17,1},{2,18},{18,2},{3,19},{19,3},{4,20},{20... | collective-permute-start | bytes 2727944 | tf_op jit(solution)/shard_map/ppermute | solution.py:136
  79.1 10.8 %collective-permute-start.13 = (bf16[64,2176]{1,0:T(8,128)(2,1)S(1)}, bf16[64,2176]{1,0:T(8,128)(2,1)S(1)}, u32[]{:S(2)}, u32[]{:S(2)}) collective-permute-start(bf16[64,2176]{1,0:T(8,128)(2,1)S(1)} %get-tuple-element.102), channel_id=1, source_target_pairs={{4,0},{5,1},{6,2},{7,3},{8,4},{9,5},{10,6},{11,7},{12,8},{13,9},{1... | collective-permute-start | bytes 835592 | tf_op jit(solution)/shard_map/ppermute | solution.py:112
  82.8 24.0 %collective-permute-start.14 = (bf16[64,2176]{1,0:T(8,128)(2,1)S(1)}, bf16[64,2176]{1,0:T(8,128)(2,1)S(1)}, u32[]{:S(2)}, u32[]{:S(2)}) collective-permute-start(bf16[64,2176]{1,0:T(8,128)(2,1)S(1)} %get-tuple-element.102), channel_id=1, source_target_pairs={{8,0},{9,1},{10,2},{11,3},{12,4},{13,5},{14,6},{15,7},{0,8},{1,9},... | collective-permute-start | bytes 835592 | tf_op jit(solution)/shard_map/ppermute | solution.py:112
  82.8 24.1 %collective-permute-start.15 = (bf16[64,2176]{1,0:T(8,128)(2,1)S(1)}, bf16[64,2176]{1,0:T(8,128)(2,1)S(1)}, u32[]{:S(2)}, u32[]{:S(2)}) collective-permute-start(bf16[64,2176]{1,0:T(8,128)(2,1)S(1)} %get-tuple-element.102), channel_id=1, source_target_pairs={{12,0},{13,1},{14,2},{15,3},{0,4},{1,5},{2,6},{3,7},{4,8},{5,9},{6... | collective-permute-start | bytes 835592 | tf_op jit(solution)/shard_map/ppermute | solution.py:112
  107.0 13.9 %collective-permute-start.16 = (bf16[4,32,2176]{2,1,0:T(8,128)(2,1)S(1)}, bf16[4,32,2176]{2,1,0:T(8,128)(2,1)S(1)}, u32[]{:S(2)}, u32[]{:S(2)}) collective-permute-start(bf16[4,32,2176]{2,1,0:T(8,128)(2,1)S(1)} %pad_maximum_fusion.2.refs_0_), channel_id=1, source_target_pairs={{0,16},{16,0},{1,17},{17,1},{2,18},{18,2},{3,19},{19,3},{4,20},{20... | collective-permute-start | bytes 1671176 | tf_op jit(solution)/shard_map/ppermute | solution.py:136
  108.4 13.6 %collective-permute-start.17 = (bf16[4,32,2176]{2,1,0:T(8,128)(2,1)S(1)}, bf16[4,32,2176]{2,1,0:T(8,128)(2,1)S(1)}, u32[]{:S(2)}, u32[]{:S(2)}) collective-permute-start(bf16[4,32,2176]{2,1,0:T(8,128)(2,1)S(1)} %pad_maximum_fusion.2.refs_0_), channel_id=1, source_target_pairs={{2,0},{3,1},{0,2},{1,3},{6,4},{7,5},{4,6},{5,7},{10,8},{11,9},{8,1... | collective-permute-start | bytes 1671176 | tf_op jit(solution)/shard_map/ppermute | solution.py:122
  109.4 24.2 %collective-permute-start.23 = (bf16[896,768]{1,0:T(8,128)(2,1)}, bf16[896,768]{1,0:T(8,128)(2,1)S(1)}, u32[]{:S(2)}, u32[]{:S(2)}) collective-permute-start(bf16[896,768]{1,0:T(8,128)(2,1)} %collective-permute-done.4.refs_6_), channel_id=1, source_target_pairs={{1,0},{0,1},{3,2},{2,3},{5,4},{4,5},{7,6},{6,7},{9,8},{8,9},{11,10... | collective-permute-start | bytes 4128776 | tf_op jit(solution)/shard_map/ppermute | solution.py:132
  122.0 11.6 %collective-permute-start.25 = (bf16[592,768]{1,0:T(8,128)(2,1)S(1)}, bf16[592,768]{1,0:T(8,128)(2,1)S(1)}, u32[]{:S(2)}, u32[]{:S(2)}) collective-permute-start(bf16[592,768]{1,0:T(8,128)(2,1)S(1)} %collective-permute-done.18.refs_9_), channel_id=1, source_target_pairs={{1,0},{0,1},{3,2},{2,3},{5,4},{4,5},{7,6},{6,7},{9,8},{8,9},{11,10... | collective-permute-start | bytes 2727944 | tf_op jit(solution)/shard_map/ppermute | solution.py:132
  122.0 11.6 %collective-permute-start.24 = (bf16[560,768]{1,0:T(8,128)(2,1)}, bf16[560,768]{1,0:T(8,128)(2,1)S(1)}, u32[]{:S(2)}, u32[]{:S(2)}) collective-permute-start(bf16[560,768]{1,0:T(8,128)(2,1)} %collective-permute-done.10.refs_7_), channel_id=1, source_target_pairs={{1,0},{0,1},{3,2},{2,3},{5,4},{4,5},{7,6},{6,7},{9,8},{8,9},{11,10... | collective-permute-start | bytes 2580488 | tf_op jit(solution)/shard_map/ppermute | solution.py:132
  132.0 15.2 %collective-permute-start.21 = (bf16[4,32,2176]{2,1,0:T(8,128)(2,1)S(1)}, bf16[4,32,2176]{2,1,0:T(8,128)(2,1)S(1)}, u32[]{:S(2)}, u32[]{:S(2)}) collective-permute-start(bf16[4,32,2176]{2,1,0:T(8,128)(2,1)S(1)} %pad_maximum_fusion.1.refs_0_), channel_id=1, source_target_pairs={{0,16},{16,0},{1,17},{17,1},{2,18},{18,2},{3,19},{19,3},{4,20},{20... | collective-permute-start | bytes 1671176 | tf_op jit(solution)/shard_map/ppermute | solution.py:136
  132.6 14.6 %collective-permute-start.22 = (bf16[4,32,2176]{2,1,0:T(8,128)(2,1)S(1)}, bf16[4,32,2176]{2,1,0:T(8,128)(2,1)S(1)}, u32[]{:S(2)}, u32[]{:S(2)}) collective-permute-start(bf16[4,32,2176]{2,1,0:T(8,128)(2,1)S(1)} %pad_maximum_fusion.1.refs_0_), channel_id=1, source_target_pairs={{2,0},{3,1},{0,2},{1,3},{6,4},{7,5},{4,6},{5,7},{10,8},{11,9},{8,1... | collective-permute-start | bytes 1671176 | tf_op jit(solution)/shard_map/ppermute | solution.py:122
  147.3 17.8 %collective-permute-start.26 = (bf16[2,32,2176]{2,1,0:T(8,128)(2,1)S(1)}, bf16[2,32,2176]{2,1,0:T(8,128)(2,1)S(1)}, u32[]{:S(2)}, u32[]{:S(2)}) collective-permute-start(bf16[2,32,2176]{2,1,0:T(8,128)(2,1)S(1)} %slice.111), channel_id=1, source_target_pairs={{2,0},{3,1},{0,2},{1,3},{6,4},{7,5},{4,6},{5,7},{10,8},{11,9},{8,1... | collective-permute-start | bytes 835592 | tf_op jit(solution)/shard_map/ppermute | solution.py:122
  148.4 16.7 %collective-permute-start.27 = (bf16[2,32,2176]{2,1,0:T(8,128)(2,1)S(1)}, bf16[2,32,2176]{2,1,0:T(8,128)(2,1)S(1)}, u32[]{:S(2)}, u32[]{:S(2)}) collective-permute-start(bf16[2,32,2176]{2,1,0:T(8,128)(2,1)S(1)} %slice.112), channel_id=1, source_target_pairs={{0,16},{16,0},{1,17},{17,1},{2,18},{18,2},{3,19},{19,3},{4,20},{20... | collective-permute-start | bytes 835592 | tf_op jit(solution)/shard_map/ppermute | solution.py:136
  149.9 36.2 %collective-permute-start.33 = (bf16[128,2048]{1,0:T(8,128)(2,1)S(1)}, bf16[128,2048]{1,0:T(8,128)(2,1)S(1)}, u32[]{:S(2)}, u32[]{:S(2)}) collective-permute-start(bf16[128,2048]{1,0:T(8,128)(2,1)S(1)} %pad_maximum_fusion.3), channel_id=1, source_target_pairs={{18,0},{19,1},{16,2},{17,3},{22,4},{23,5},{20,6},{21,7},{26,8},{27... | collective-permute-start | bytes 1572872 | tf_op jit(solution)/shard_map/ppermute | solution.py:147
  151.0 36.1 %collective-permute-start.31 = (bf16[128,2048]{1,0:T(8,128)(2,1)S(1)}, bf16[128,2048]{1,0:T(8,128)(2,1)S(1)}, u32[]{:S(2)}, u32[]{:S(2)}) collective-permute-start(bf16[128,2048]{1,0:T(8,128)(2,1)S(1)} %get-tuple-element.124), channel_id=1, source_target_pairs={{0,16},{16,0},{1,17},{17,1},{2,18},{18,2},{3,19},{19,3},{4,20},{20... | collective-permute-start | bytes 1572872 | tf_op jit(solution)/shard_map/ppermute | solution.py:136
  152.4 37.2 %collective-permute-start.32 = (bf16[128,2048]{1,0:T(8,128)(2,1)S(1)}, bf16[128,2048]{1,0:T(8,128)(2,1)S(1)}, u32[]{:S(2)}, u32[]{:S(2)}) collective-permute-start(bf16[128,2048]{1,0:T(8,128)(2,1)S(1)} %get-tuple-element.125), channel_id=1, source_target_pairs={{2,0},{3,1},{0,2},{1,3},{6,4},{7,5},{4,6},{5,7},{10,8},{11,9},{8,1... | collective-permute-start | bytes 1572872 | tf_op jit(solution)/shard_map/ppermute | solution.py:122
  173.9 16.0 %collective-permute-start.30 = (bf16[64,2048]{1,0:T(8,128)(2,1)S(1)}, bf16[64,2048]{1,0:T(8,128)(2,1)S(1)}, u32[]{:S(2)}, u32[]{:S(2)}) collective-permute-start(bf16[64,2048]{1,0:T(8,128)(2,1)S(1)} %pad_maximum_fusion.4), channel_id=1, source_target_pairs={{18,0},{19,1},{16,2},{17,3},{22,4},{23,5},{20,6},{21,7},{26,8},{27... | collective-permute-start | bytes 786440 | tf_op jit(solution)/shard_map/ppermute | solution.py:147
  177.4 14.4 %collective-permute-start.28 = (bf16[64,2048]{1,0:T(8,128)(2,1)S(1)}, bf16[64,2048]{1,0:T(8,128)(2,1)S(1)}, u32[]{:S(2)}, u32[]{:S(2)}) collective-permute-start(bf16[64,2048]{1,0:T(8,128)(2,1)S(1)} %get-tuple-element.119), channel_id=1, source_target_pairs={{0,16},{16,0},{1,17},{17,1},{2,18},{18,2},{3,19},{19,3},{4,20},{20... | collective-permute-start | bytes 786440 | tf_op jit(solution)/shard_map/ppermute | solution.py:136
  187.1 10.8 %collective-permute-start.39 = (bf16[64,2048]{1,0:T(8,128)(2,1)S(1)}, bf16[64,2048]{1,0:T(8,128)(2,1)S(1)}, u32[]{:S(2)}, u32[]{:S(2)}) collective-permute-start(bf16[64,2048]{1,0:T(8,128)(2,1)S(1)} %pad_maximum_fusion.5), channel_id=1, source_target_pairs={{18,0},{19,1},{16,2},{17,3},{22,4},{23,5},{20,6},{21,7},{26,8},{27... | collective-permute-start | bytes 786440 | tf_op jit(solution)/shard_map/ppermute | solution.py:147
  189.6 10.3 %collective-permute-start.37 = (bf16[64,2048]{1,0:T(8,128)(2,1)S(1)}, bf16[64,2048]{1,0:T(8,128)(2,1)S(1)}, u32[]{:S(2)}, u32[]{:S(2)}) collective-permute-start(bf16[64,2048]{1,0:T(8,128)(2,1)S(1)} %get-tuple-element.130), channel_id=1, source_target_pairs={{0,16},{16,0},{1,17},{17,1},{2,18},{18,2},{3,19},{19,3},{4,20},{20... | collective-permute-start | bytes 786440 | tf_op jit(solution)/shard_map/ppermute | solution.py:136
  194.9 21.8 %collective-permute-start.34 = (bf16[32,2048]{1,0:T(8,128)(2,1)S(1)}, bf16[32,2048]{1,0:T(8,128)(2,1)S(1)}, u32[]{:S(2)}, u32[]{:S(2)}) collective-permute-start(bf16[32,2048]{1,0:T(8,128)(2,1)S(1)} %get-tuple-element.145), channel_id=1, source_target_pairs={{12,0},{13,1},{14,2},{15,3},{0,4},{1,5},{2,6},{3,7},{4,8},{5,9},{6... | collective-permute-start | bytes 393224 | tf_op jit(solution)/shard_map/ppermute | solution.py:112
  195.8 20.9 %collective-permute-start.35 = (bf16[32,2048]{1,0:T(8,128)(2,1)S(1)}, bf16[32,2048]{1,0:T(8,128)(2,1)S(1)}, u32[]{:S(2)}, u32[]{:S(2)}) collective-permute-start(bf16[32,2048]{1,0:T(8,128)(2,1)S(1)} %get-tuple-element.147), channel_id=1, source_target_pairs={{8,0},{9,1},{10,2},{11,3},{12,4},{13,5},{14,6},{15,7},{0,8},{1,9},... | collective-permute-start | bytes 393224 | tf_op jit(solution)/shard_map/ppermute | solution.py:112
  (31 other events, 283.3 us)

commit v6 on v5

--- a/solution.py
+++ b/solution.py
@@ -197,7 +197,7 @@
 def project_kernel(depth, ctx_ref, other_ref, *refs):
     pieces, (kept_ref, sent_ref) = refs[:-2], refs[-2:]
     half = ctx_ref.shape[0] // 2
-    feats, width = pieces[0].shape
+    width = pieces[0].shape[1]
     me = lax.axis_index("expert")
     x = lax.axis_index("dp")
     y = lax.rem(lax.div(me, 2), 2)
@@ -210,10 +210,7 @@
     for flip in range(2):
         at_y = y if flip == 0 else 1 - y
         for r in range(depth):
-            if r == 0:
-                piece = pieces[2 * flip][...]
-            else:
-                piece = pieces[2 * flip + 1][(r - 1) * feats : r * feats, :]
+            piece = pieces[flip * depth + r][...]
             total = jnp.dot(rows, piece, preferred_element_type=jnp.float32)
             index = lax.rem(z + r, depth) * 2 + at_y
             columns = pl.ds(pl.multiple_of(index * width, width), width)
@@ -303,7 +300,7 @@
     return pl.pallas_call(
         functools.partial(cut_kernel, width),
         out_shape=tuple(jax.ShapeDtypeStruct((n, width), weights.dtype) for n in shapes),
-        in_specs=[any_spec],
+        in_specs=[pl.BlockSpec(memory_space=pltpu.HBM)],
         out_specs=(pl.BlockSpec(memory_space=pltpu.VMEM),) * len(shapes),
         scratch_shapes=[pltpu.SemaphoreType.DMA((len(shapes),))],
         cost_estimate=pl.CostEstimate(
@@ -498,24 +495,24 @@
     barrier = lax.optimization_barrier
 
     shifted = [shift_z(w_out, depth, s) for s in range(1, depth)]
-    across_own = flip_y(w_out, depth)
+    across = [flip_y(w_out, depth), flip_y(shifted[0], depth)]
 
     feats_here = w_gate.shape[1]
-    early = feats_here * 7 // 8
+    early = feats_here * 3 // 4
     gate_own, *gate_sent = cut(w_gate, width, (early, feats_here - early))
     gate_far = flip_x(gate_sent[0])
     split = feats_here - early
     queries, gate_sent[1], gate_own = barrier((queries, gate_sent[1], gate_own))
     context = attend_here(queries, kv_pool, page_table, ctx_lens)
     context, w_up, w_down = barrier((context, w_up, w_down))
-    early = feats_here * 27 // 64
+    early = feats_here * 3 // 32
     up_own, *up_sent = cut(w_up, width, (early, feats_here - early))
     mixed_sent = jnp.concatenate([gate_sent[1], up_sent[0]], axis=0)
-    shifted, across_own, gate_far, mixed_sent, up_sent[1], gate_own, up_own, w_down, context = (
+    shifted, across, gate_far, mixed_sent, up_sent[1], gate_own, up_own, w_down, context = (
         barrier(
             (
                 shifted,
-                across_own,
+                across,
                 gate_far,
                 mixed_sent,
                 up_sent[1],
@@ -526,8 +523,7 @@
             )
         )
     )
-    shifted = jnp.concatenate(shifted, axis=0)
-    across = flip_y(shifted, depth)
+    across += [flip_y(piece, depth) for piece in shifted[1:]]
     mixed_far = flip_x(mixed_sent)
     other = flip_core(context, depth)
     down_own = w_down[0]
@@ -542,7 +538,7 @@
     )
 
     across, share, here_core, mixed_far = barrier((across, share, here_core, mixed_far))
-    kept, sent = project(context, other, [w_out, shifted, across_own, across], depth)
+    kept, sent = project(context, other, [w_out] + shifted + across, depth)
     gate_far_core = flip_core(gate_far, depth)
     mixed_far_core = flip_core(mixed_far, depth)
     received, up_late = barrier((flip_x(sent), up_sent[1]))
@@ -552,16 +548,19 @@
     hidden_state, message = join(total[:block], back, residual, moe_gain, share, w_out.shape[1])
 
     rows = block // 2
-    arrived = [message] + [shift_z(message, depth, s) for s in range(1, depth)]
+    lines = []
+    for k in range(2):
+        mine = message[rows * k : rows * (k + 1)]
+        lines.append([mine] + [shift_z(mine, depth, s) for s in range(1, depth)])
     ready = []
     for k in range(2):
-        line = jnp.stack([piece[rows * k : rows * (k + 1)] for piece in arrived])
+        line = jnp.stack(lines[k])
         if k > 0:
             line, ready[0][3], ready[0][4] = barrier((line, ready[0][3], ready[0][4]))
         line_x = flip_x(line)
         line_y = flip_y(line, depth)
         if k == 0:
-            line_x, line_y, up_far = barrier((line_x, line_y, up_far))
+            line_x, line_y, lines[1], up_far = barrier((line_x, line_y, lines[1], up_far))
             ready.append([line, line_x, line_y, *diagonal(line_x, line_y, depth)])
         else:
             ready.append([line, line_x, line_y])
@@ -576,36 +575,33 @@
         here_core[2],
     ]
 
-    backs = []
-    last = None
-    for chunk, at, each in ((0, 0, rows), (1, 0, rows // 2), (1, rows // 2, rows // 2)):
-        pieces = ready[chunk]
-        if len(pieces) == 3:
-            pieces[1], pieces[2], last = barrier((pieces[1], pieces[2], last))
-            pieces += diagonal(pieces[1], pieces[2], depth)
-        elif last is not None:
-            pieces[0], last = barrier((pieces[0], last))
-        out_l, out_x, out_y, out_low, out_high = run_experts(
-            pieces,
-            (jnp.float32, jnp.bfloat16, jnp.bfloat16, jnp.bfloat16, jnp.bfloat16),
-            at,
-            each,
-            weights,
-            split,
-        )
-        last = out_low
-        far = jnp.concatenate([out_low, out_high], axis=0)
-        backs.append((out_l, flip_x(out_x), flip_y(out_y, depth), flip_xy(far, depth)))
-    moe = []
-    full = None
+    kinds = (jnp.float32, jnp.bfloat16, jnp.bfloat16, jnp.bfloat16, jnp.bfloat16)
+    outs = run_experts(ready[0], kinds, 0, rows, weights, split)
+    ready[1][1], ready[1][2], outs = barrier((ready[1][1], ready[1][2], outs))
+    ready[1] += diagonal(ready[1][1], ready[1][2], depth)
+    ready[1], outs = barrier((ready[1], outs))
+    out_l, out_x, out_y, out_low, out_high = outs
+    far = jnp.concatenate([out_low, out_high], axis=0)
+    backs = [flip_x(out_x), flip_y(out_y, depth), flip_xy(far, depth)]
+
+    kinds = (jnp.float32, jnp.float32, jnp.float32, jnp.bfloat16, jnp.bfloat16)
+    last_l, last_x, last_y, last_low, last_high = run_experts(
+        ready[1], kinds, 0, rows, weights, split
+    )
+    back_low, back_high = flip_y(last_low, depth), flip_x(last_high)
+    full = out_l
     for back in backs:
-        if full is not None:
-            back, full = barrier((back, full))
-            moe.append(send_line(full, depth))
-        full = back[0]
-        for part in back[1:]:
-            full = full + part.astype(jnp.float32)
-    moe.append(send_line(full, depth))
+        full = full + back.astype(jnp.float32)
+    full, back_low, back_high = barrier((full, back_low, back_high))
+    first_rows = send_line(full, depth)
+    half = last_x.shape[0] // 2
+    sum_x = jnp.concatenate([last_x[:half] + back_low.astype(jnp.float32), last_x[half:]], axis=0)
+    sum_y = jnp.concatenate([last_y[:half], last_y[half:] + back_high.astype(jnp.float32)], axis=0)
+    back_x = flip_x(sum_x.astype(jnp.bfloat16))
+    back_y = flip_y(sum_y.astype(jnp.bfloat16), depth)
+    first_rows, back_x, back_y = barrier((first_rows, back_x, back_y))
+    full = last_l + back_x.astype(jnp.float32) + back_y.astype(jnp.float32)
+    moe = [first_rows, send_line(full, depth)]
     combined = hidden_state + jnp.concatenate(moe, axis=0)
     return normalize(combined, final_gain).astype(jnp.bfloat16)
 

time: 221 us -> 218 us (0.986)
  starting transfers between devices: 59.5 us -> 68.9 us
  waiting for transfers between devices: 105 us -> 97.2 us
  Pallas kernels: 43.1 us -> 39.2 us
    ppermute x15, starting transfers between devices: 27.4 us -> 38.8 us  [shift_z(): return lax.ppermute(values, 'expert', pairs)]
    ppermute x9 -> x11, waiting for transfers between devices: 39.3 us -> 31 us  [flip_y(): return lax.ppermute(values, 'expert', pairs)]
    ppermute x3 -> x1, starting transfers between devices: 7.1 us -> 0.55 us  [flip_xy(): return lax.ppermute(values, ('dp', 'expert'), pairs)]
    ppermute x15, waiting for transfers between devices: 36.6 us -> 41.6 us  [shift_z(): return lax.ppermute(values, 'expert', pairs)]
    ppermute x11, waiting for transfers between devices: 28.7 us -> 24.6 us  [flip_x(): return lax.ppermute(values, 'dp', [(0, 1), (1, 0)])]
    pallas_call x3 -> x2, Pallas kernels: 31 us -> 27.4 us  [run_experts(): pl.pallas_call(functools.partial(experts_kernel, tile, 512, first_row, co...]
    ppermute x11, starting transfers between devices: 13.2 us -> 16.1 us  [flip_x(): return lax.ppermute(values, 'dp', [(0, 1), (1, 0)])]
    ppermute x9 -> x11, starting transfers between devices: 10.6 us -> 12.3 us  [flip_y(): return lax.ppermute(values, 'expert', pairs)]
  transfers between devices with their start and end apart: 46 -> 46, of which waited for: 19 -> 25; matrix products, arithmetic and copies ran while one was open for 3% -> 1% of each run, Pallas kernels for 17% -> 16%
where the time goes in v6:
time: 218 us; the launch traced here: 217 us
  waiting for transfers between devices  97.2 us (45%)
  starting transfers between devices  68.9 us (32%)
  Pallas kernels  39.2 us (18%)
  local copies, waits for them, and re-layouts  8.61 us (4%)
  other arithmetic  3.02 us (1%)
    ppermute x15, waiting for transfers between devices, shift_z(): return lax.ppermute(values, 'expert', pairs)  41.6 us
    ppermute x15, starting transfers between devices, shift_z(): return lax.ppermute(values, 'expert', pairs)  38.8 us
    ppermute x11, waiting for transfers between devices, flip_y(): return lax.ppermute(values, 'expert', pairs)  31 us
    pallas_call x2, Pallas kernels, run_experts(): pl.pallas_call(functools.partial(experts_kernel, tile, 512, first_row, co...  27.4 us
    ppermute x11, waiting for transfers between devices, flip_x(): return lax.ppermute(values, 'dp', [(0, 1), (1, 0)])  24.6 us
    ppermute x11, starting transfers between devices, flip_x(): return lax.ppermute(values, 'dp', [(0, 1), (1, 0)])  16.1 us
    ppermute x11, starting transfers between devices, flip_y(): return lax.ppermute(values, 'expert', pairs)  12.3 us
    unnamed x30, local copies, waits for them, and re-layouts  7.33 us
  transfers between devices with their start and end apart: 46, of which 25 were waited for; matrix products, arithmetic and copies ran while one was open for 1% of the time, Pallas kernels for 16%

profile of v6, /device:TPU:0, one launch (start us, length us, event | category | flops | bytes accessed | tf_op | source)
XLA Modules:
  0.0 217.4 jit_solution(2351737660986742879)
XLA Ops:
  0.0 1.8 copy-done
  3.6 3.0 %collective-permute-start.5 = (bf16[768,768]{1,0:T(8,128)(2,1)}, bf16[768,768]{1,0:T(8,128)(2,1)}, u32[]{:S(2)}, u32[]{:S(2)}) collective-permute-start(bf16[768,768]{1,0:T(8,128)(2,1)} %get-tuple-element.87), channel_id=1, source_target_pairs={{0,16},{16,0},{1,17},{17,1},{2,18},{18,2},{3,19},{19,3},{4,20},{20... | collective-permute-start | bytes 3538952 | tf_op jit(solution)/shard_map/ppermute | solution.py:136
  6.6 3.6 %collective-permute-start = (bf16[1024,128]{1,0:T(8,128)(2,1)}, bf16[1024,128]{1,0:T(8,128)(2,1)}, u32[]{:S(2)}, u32[]{:S(2)}) collective-permute-start(bf16[1024,128]{1,0:T(8,128)(2,1)} %refs_0_.1), channel_id=1, source_target_pairs={{4,0},{5,1},{6,2},{7,3},{8,4},{9,5},{10,6},{11,7},{12,8},{13,9},{1... | collective-permute-start | bytes 786440 | tf_op jit(solution)/shard_map/ppermute | solution.py:112
  12.7 4.6 %collective-permute-done.refs_1_ = bf16[1024,128]{1,0:T(8,128)(2,1)} collective-permute-done((bf16[1024,128]{1,0:T(8,128)(2,1)}, bf16[1024,128]{1,0:T(8,128)(2,1)}, u32[]{:S(2)}, u32[]{:S(2)}) %collective-permute-start) | collective-permute-done | bytes 262176 | tf_op jit(solution)/shard_map/ppermute | solution.py:112
  22.9 5.8 %attend.1.ctx_ref = bf16[128,1024]{1,0:T(8,128)(2,1)S(1)} custom-call(s32[2,4]{1,0:T(2,128)S(1)} %copy-done.8, s32[128,1]{1,0:T(8,128)S(1)} %copy-done.6, bf16[128,1024]{1,0:T(8,128)(2,1)S(1)} %copy-done.3, bf16[2,8,64,1024]{3,2,1,0:T(8,128)(2,1)S(1)} %copy-done.2), custom_call_target="tpu_custom_call" | custom-call | flops 134217728 | bytes 2621440 | tf_op jit(solution)/shard_map/attend/pallas_call | solution.py:182
  33.4 1.8 collective-permute-start.7
  35.4 7.3 %collective-permute-done.7.refs_6_ = bf16[1024,128]{1,0:T(8,128)(2,1)S(1)} collective-permute-done((bf16[1024,128]{1,0:T(8,128)(2,1)}, bf16[1024,128]{1,0:T(8,128)(2,1)S(1)}, u32[]{:S(2)}, u32[]{:S(2)}) %collective-permute-start.7) | collective-permute-done | bytes 262176 | tf_op jit(solution)/shard_map/ppermute | solution.py:122
  44.6 3.3 %collective-permute-done.8.refs_7_ = bf16[1024,128]{1,0:T(8,128)(2,1)S(1)} collective-permute-done((bf16[1024,128]{1,0:T(8,128)(2,1)}, bf16[1024,128]{1,0:T(8,128)(2,1)S(1)}, u32[]{:S(2)}, u32[]{:S(2)}) %collective-permute-start.8) | collective-permute-done | bytes 262176 | tf_op jit(solution)/shard_map/ppermute | solution.py:122
  48.1 8.3 %collective-permute-done.12.refs_7_ = bf16[352,768]{1,0:T(8,128)(2,1)S(1)} collective-permute-done((bf16[352,768]{1,0:T(8,128)(2,1)}, bf16[352,768]{1,0:T(8,128)(2,1)S(1)}, u32[]{:S(2)}, u32[]{:S(2)}) %collective-permute-start.12) | collective-permute-done | bytes 540704 | tf_op jit(solution)/shard_map/ppermute | solution.py:136
  57.5 2.5 %project.1 = (f32[128,1024]{1,0:T(8,128)S(1)}, bf16[128,1024]{1,0:T(8,128)(2,1)S(1)}) custom-call(bf16[128,1024]{1,0:T(8,128)(2,1)S(1)} %attend.1.ctx_ref, bf16[128,1024]{1,0:T(8,128)(2,1)S(1)} %collective-permute-done.6.other_ref, bf16[1024,128]{1,0:T(8,128)(2,1)S(1)} %copy-done.4, bf16[1024,128]{1,0:T(8,128)(2,1)} %collective-permute-done.refs_1_, ...), custom_call_target="tpu_custom_call" | custom-call | flops 536870912 | bytes 2883584 | tf_op jit(solution)/shard_map/project/pallas_call | solution.py:224
  61.8 5.0 %collective-permute-done.13 = bf16[128,1024]{1,0:T(8,128)(2,1)S(1)} collective-permute-done((bf16[128,1024]{1,0:T(8,128)(2,1)S(1)}, bf16[128,1024]{1,0:T(8,128)(2,1)S(1)}, u32[]{:S(2)}, u32[]{:S(2)}) %collective-permute-start.13) | collective-permute-done | bytes 262176 | tf_op jit(solution)/shard_map/ppermute | solution.py:136
  69.0 10.6 %collective-permute-start.17 = (bf16[32,2176]{1,0:T(8,128)(2,1)S(1)}, bf16[32,2176]{1,0:T(8,128)(2,1)S(1)}, u32[]{:S(2)}, u32[]{:S(2)}) collective-permute-start(bf16[32,2176]{1,0:T(8,128)(2,1)S(1)} %get-tuple-element.181), channel_id=1, source_target_pairs={{12,0},{13,1},{14,2},{15,3},{0,4},{1,5},{2,6},{3,7},{4,8},{5,9},{6... | collective-permute-start | bytes 417800 | tf_op jit(solution)/shard_map/ppermute | solution.py:112
  79.6 2.4 %collective-permute-start.15 = (bf16[32,2176]{1,0:T(8,128)(2,1)S(1)}, bf16[32,2176]{1,0:T(8,128)(2,1)S(1)}, u32[]{:S(2)}, u32[]{:S(2)}) collective-permute-start(bf16[32,2176]{1,0:T(8,128)(2,1)S(1)} %get-tuple-element.181), channel_id=1, source_target_pairs={{4,0},{5,1},{6,2},{7,3},{8,4},{9,5},{10,6},{11,7},{12,8},{13,9},{1... | collective-permute-start | bytes 417800 | tf_op jit(solution)/shard_map/ppermute | solution.py:112
  83.6 5.2 %collective-permute-done.16 = bf16[32,2176]{1,0:T(8,128)(2,1)S(1)} collective-permute-done((bf16[32,2176]{1,0:T(8,128)(2,1)S(1)}, bf16[32,2176]{1,0:T(8,128)(2,1)S(1)}, u32[]{:S(2)}, u32[]{:S(2)}) %collective-permute-start.16) | collective-permute-done | bytes 139296 | tf_op jit(solution)/shard_map/ppermute | solution.py:112
  90.1 6.0 %collective-permute-start.20 = (bf16[32,2176]{1,0:T(8,128)(2,1)S(1)}, bf16[32,2176]{1,0:T(8,128)(2,1)S(1)}, u32[]{:S(2)}, u32[]{:S(2)}) collective-permute-start(bf16[32,2176]{1,0:T(8,128)(2,1)S(1)} %get-tuple-element.121), channel_id=1, source_target_pairs={{4,0},{5,1},{6,2},{7,3},{8,4},{9,5},{10,6},{11,7},{12,8},{13,9},{1... | collective-permute-start | bytes 417800 | tf_op jit(solution)/shard_map/ppermute | solution.py:112
  96.2 4.1 %collective-permute-done.20 = bf16[32,2176]{1,0:T(8,128)(2,1)S(1)} collective-permute-done((bf16[32,2176]{1,0:T(8,128)(2,1)S(1)}, bf16[32,2176]{1,0:T(8,128)(2,1)S(1)}, u32[]{:S(2)}, u32[]{:S(2)}) %collective-permute-start.20) | collective-permute-done | bytes 139296 | tf_op jit(solution)/shard_map/ppermute | solution.py:112
  100.3 5.2 %collective-permute-done.21 = bf16[32,2176]{1,0:T(8,128)(2,1)S(1)} collective-permute-done((bf16[32,2176]{1,0:T(8,128)(2,1)S(1)}, bf16[32,2176]{1,0:T(8,128)(2,1)S(1)}, u32[]{:S(2)}, u32[]{:S(2)}) %collective-permute-start.21) | collective-permute-done | bytes 139296 | tf_op jit(solution)/shard_map/ppermute | solution.py:112
  105.5 2.2 %collective-permute-done.22 = bf16[32,2176]{1,0:T(8,128)(2,1)S(1)} collective-permute-done((bf16[32,2176]{1,0:T(8,128)(2,1)S(1)}, bf16[32,2176]{1,0:T(8,128)(2,1)S(1)}, u32[]{:S(2)}, u32[]{:S(2)}) %collective-permute-start.22) | collective-permute-done | bytes 139296 | tf_op jit(solution)/shard_map/ppermute | solution.py:112
  107.7 4.8 %collective-permute-done.18.refs_1_ = bf16[4,32,2176]{2,1,0:T(8,128)(2,1)S(1)} collective-permute-done((bf16[4,32,2176]{2,1,0:T(8,128)(2,1)S(1)}, bf16[4,32,2176]{2,1,0:T(8,128)(2,1)S(1)}, u32[]{:S(2)}, u32[]{:S(2)}) %collective-permute-start.18) | collective-permute-done | bytes 557088 | tf_op jit(solution)/shard_map/ppermute | solution.py:136
  116.5 5.7 %collective-permute-done.24.refs_3_ = bf16[2,32,2176]{2,1,0:T(8,128)(2,1)S(1)} collective-permute-done((bf16[2,32,2176]{2,1,0:T(8,128)(2,1)S(1)}, bf16[2,32,2176]{2,1,0:T(8,128)(2,1)S(1)}, u32[]{:S(2)}, u32[]{:S(2)}) %collective-permute-start.24) | collective-permute-done | bytes 278560 | tf_op jit(solution)/shard_map/ppermute | solution.py:122
  125.7 13.7 %experts.2 = (f32[128,2048]{1,0:T(8,128)S(1)}, bf16[128,2048]{1,0:T(8,128)(2,1)S(1)}, bf16[128,2048]{1,0:T(8,128)(2,1)S(1)}, bf16[64,2048]{1,0:T(8,128)(2,1)S(1)}, bf16[64,2048]{1,0:T(8,128)(2,1)S(1)}) custom-call(bf16[4,32,2176]{2,1,0:T(8,128)(2,1)S(1)} %pad_maximum_fusion.refs_0_, bf16[4,32,2176]{2,1,0:T(8,128)(2,1)S(1)} %collective-permute-done.18.refs_1_, ...), custom_call_target="tpu_custom_call" | custom-call | flops 9663676416 | bytes 31457280 | tf_op jit(solution)/shard_map/experts/pallas_call | solution.py:431
  141.7 5.2 %collective-permute-done.31.refs_3_ = bf16[2,32,2176]{2,1,0:T(8,128)(2,1)S(1)} collective-permute-done((bf16[2,32,2176]{2,1,0:T(8,128)(2,1)S(1)}, bf16[2,32,2176]{2,1,0:T(8,128)(2,1)S(1)}, u32[]{:S(2)}, u32[]{:S(2)}) %collective-permute-start.31) | collective-permute-done | bytes 278560 | tf_op jit(solution)/shard_map/ppermute | solution.py:122
  151.8 13.7 %experts.3 = (f32[128,2048]{1,0:T(8,128)S(1)}, f32[128,2048]{1,0:T(8,128)S(1)}, f32[128,2048]{1,0:T(8,128)S(1)}, bf16[64,2048]{1,0:T(8,128)(2,1)S(1)}, bf16[64,2048]{1,0:T(8,128)(2,1)S(1)}) custom-call(bf16[4,32,2176]{2,1,0:T(8,128)(2,1)S(1)} %pad_maximum_fusion.1.refs_0_, bf16[4,32,2176]{2,1,0:T(8,128)(2,1)S(1)} %collective-permute-done.26.refs_1_, ...), custom_call_target="tpu_custom_call" | custom-call | flops 9663676416 | bytes 31457280 | tf_op jit(solution)/shard_map/experts/pallas_call | solution.py:431
  166.7 5.3 %collective-permute-done.34 = bf16[128,2048]{1,0:T(8,128)(2,1)S(1)} collective-permute-done((bf16[128,2048]{1,0:T(8,128)(2,1)S(1)}, bf16[128,2048]{1,0:T(8,128)(2,1)S(1)}, u32[]{:S(2)}, u32[]{:S(2)}) %collective-permute-start.34) | collective-permute-done | bytes 524320 | tf_op jit(solution)/shard_map/ppermute | solution.py:122
  172.0 1.8 collective-permute-done.33
  174.0 2.9 %collective-permute-done.36 = bf16[64,2048]{1,0:T(8,128)(2,1)S(1)} collective-permute-done((bf16[64,2048]{1,0:T(8,128)(2,1)S(1)}, bf16[64,2048]{1,0:T(8,128)(2,1)S(1)}, u32[]{:S(2)}, u32[]{:S(2)}) %collective-permute-start.36) | collective-permute-done | bytes 262176 | tf_op jit(solution)/shard_map/ppermute | solution.py:122
  177.0 3.6 %collective-permute-start.40 = (bf16[32,2048]{1,0:T(8,128)(2,1)S(1)}, bf16[32,2048]{1,0:T(8,128)(2,1)S(1)}, u32[]{:S(2)}, u32[]{:S(2)}) collective-permute-start(bf16[32,2048]{1,0:T(8,128)(2,1)S(1)} %get-tuple-element.175), channel_id=1, source_target_pairs={{4,0},{5,1},{6,2},{7,3},{8,4},{9,5},{10,6},{11,7},{12,8},{13,9},{1... | collective-permute-start | bytes 393224 | tf_op jit(solution)/shard_map/ppermute | solution.py:112
  180.6 7.2 %collective-permute-start.39 = (bf16[32,2048]{1,0:T(8,128)(2,1)S(1)}, bf16[32,2048]{1,0:T(8,128)(2,1)S(1)}, u32[]{:S(2)}, u32[]{:S(2)}) collective-permute-start(bf16[32,2048]{1,0:T(8,128)(2,1)S(1)} %get-tuple-element.176), channel_id=1, source_target_pairs={{8,0},{9,1},{10,2},{11,3},{12,4},{13,5},{14,6},{15,7},{0,8},{1,9},... | collective-permute-start | bytes 393224 | tf_op jit(solution)/shard_map/ppermute | solution.py:112
  190.4 9.2 %collective-permute-done.39 = bf16[32,2048]{1,0:T(8,128)(2,1)S(1)} collective-permute-done((bf16[32,2048]{1,0:T(8,128)(2,1)S(1)}, bf16[32,2048]{1,0:T(8,128)(2,1)S(1)}, u32[]{:S(2)}, u32[]{:S(2)}) %collective-permute-start.39) | collective-permute-done | bytes 131104 | tf_op jit(solution)/shard_map/ppermute | solution.py:112
  202.8 3.6 %collective-permute-start.45 = (bf16[32,2048]{1,0:T(8,128)(2,1)S(1)}, bf16[32,2048]{1,0:T(8,128)(2,1)S(1)}, u32[]{:S(2)}, u32[]{:S(2)}) collective-permute-start(bf16[32,2048]{1,0:T(8,128)(2,1)S(1)} %get-tuple-element.172), channel_id=1, source_target_pairs={{4,0},{5,1},{6,2},{7,3},{8,4},{9,5},{10,6},{11,7},{12,8},{13,9},{1... | collective-permute-start | bytes 393224 | tf_op jit(solution)/shard_map/ppermute | solution.py:112
  207.1 3.0 %collective-permute-done.45 = bf16[32,2048]{1,0:T(8,128)(2,1)S(1)} collective-permute-done((bf16[32,2048]{1,0:T(8,128)(2,1)S(1)}, bf16[32,2048]{1,0:T(8,128)(2,1)S(1)}, u32[]{:S(2)}, u32[]{:S(2)}) %collective-permute-start.45) | collective-permute-done | bytes 131104 | tf_op jit(solution)/shard_map/ppermute | solution.py:112
  210.1 6.2 %collective-permute-done.44 = bf16[32,2048]{1,0:T(8,128)(2,1)S(1)} collective-permute-done((bf16[32,2048]{1,0:T(8,128)(2,1)S(1)}, bf16[32,2048]{1,0:T(8,128)(2,1)S(1)}, u32[]{:S(2)}, u32[]{:S(2)}) %collective-permute-start.44) | collective-permute-done | bytes 131104 | tf_op jit(solution)/shard_map/ppermute | solution.py:112
  (133 shorter events, 48.3 us)
Async XLA Ops:
  3.6 29.3 %collective-permute-start.5 = (bf16[768,768]{1,0:T(8,128)(2,1)}, bf16[768,768]{1,0:T(8,128)(2,1)}, u32[]{:S(2)}, u32[]{:S(2)}) collective-permute-start(bf16[768,768]{1,0:T(8,128)(2,1)} %get-tuple-element.87), channel_id=1, source_target_pairs={{0,16},{16,0},{1,17},{17,1},{2,18},{18,2},{3,19},{19,3},{4,20},{20... | collective-permute-start | bytes 3538952 | tf_op jit(solution)/shard_map/ppermute | solution.py:136
  6.6 10.7 %collective-permute-start = (bf16[1024,128]{1,0:T(8,128)(2,1)}, bf16[1024,128]{1,0:T(8,128)(2,1)}, u32[]{:S(2)}, u32[]{:S(2)}) collective-permute-start(bf16[1024,128]{1,0:T(8,128)(2,1)} %refs_0_.1), channel_id=1, source_target_pairs={{4,0},{5,1},{6,2},{7,3},{8,4},{9,5},{10,6},{11,7},{12,8},{13,9},{1... | collective-permute-start | bytes 786440 | tf_op jit(solution)/shard_map/ppermute | solution.py:112
  10.2 22.3 %collective-permute-start.1 = (bf16[1024,128]{1,0:T(8,128)(2,1)}, bf16[1024,128]{1,0:T(8,128)(2,1)}, u32[]{:S(2)}, u32[]{:S(2)}) collective-permute-start(bf16[1024,128]{1,0:T(8,128)(2,1)} %refs_0_.1), channel_id=1, source_target_pairs={{8,0},{9,1},{10,2},{11,3},{12,4},{13,5},{14,6},{15,7},{0,8},{1,9},... | collective-permute-start | bytes 786440 | tf_op jit(solution)/shard_map/ppermute | solution.py:112
  10.2 22.3 %collective-permute-start.2 = (bf16[1024,128]{1,0:T(8,128)(2,1)}, bf16[1024,128]{1,0:T(8,128)(2,1)}, u32[]{:S(2)}, u32[]{:S(2)}) collective-permute-start(bf16[1024,128]{1,0:T(8,128)(2,1)} %refs_0_.1), channel_id=1, source_target_pairs={{12,0},{13,1},{14,2},{15,3},{0,4},{1,5},{2,6},{3,7},{4,8},{5,9},{6... | collective-permute-start | bytes 786440 | tf_op jit(solution)/shard_map/ppermute | solution.py:112
  11.2 21.3 %collective-permute-start.3 = (bf16[1024,128]{1,0:T(8,128)(2,1)}, bf16[1024,128]{1,0:T(8,128)(2,1)}, u32[]{:S(2)}, u32[]{:S(2)}) collective-permute-start(bf16[1024,128]{1,0:T(8,128)(2,1)} %refs_0_.1), channel_id=1, source_target_pairs={{2,0},{3,1},{0,2},{1,3},{6,4},{7,5},{4,6},{5,7},{10,8},{11,9},{8,1... | collective-permute-start | bytes 786440 | tf_op jit(solution)/shard_map/ppermute | solution.py:122
  17.3 15.2 %collective-permute-start.4 = (bf16[1024,128]{1,0:T(8,128)(2,1)}, bf16[1024,128]{1,0:T(8,128)(2,1)}, u32[]{:S(2)}, u32[]{:S(2)}) collective-permute-start(bf16[1024,128]{1,0:T(8,128)(2,1)} %collective-permute-done.refs_1_), channel_id=1, source_target_pairs={{2,0},{3,1},{0,2},{1,3},{6,4},{7,5},{4,6},{5,7},{10,8},{11,9},{8,1... | collective-permute-start | bytes 786440 | tf_op jit(solution)/shard_map/ppermute | solution.py:122
  32.9 23.6 %collective-permute-start.11 = (bf16[704,2048]{1,0:T(8,128)(2,1)}, bf16[704,2048]{1,0:T(8,128)(2,1)}, u32[]{:S(2)}, u32[]{:S(2)}) collective-permute-start(bf16[704,2048]{1,0:T(8,128)(2,1)} %bitcast.1.refs_10_), channel_id=1, source_target_pairs={{1,0},{0,1},{3,2},{2,3},{5,4},{4,5},{7,6},{6,7},{9,8},{8,9},{11,10... | collective-permute-start | bytes 8650760 | tf_op jit(solution)/shard_map/ppermute | solution.py:132
  32.9 23.6 %collective-permute-start.9 = (bf16[1024,768]{1,0:T(8,128)(2,1)}, bf16[1024,768]{1,0:T(8,128)(2,1)S(1)}, u32[]{:S(2)}, u32[]{:S(2)}) collective-permute-start(bf16[1024,768]{1,0:T(8,128)(2,1)} %get-tuple-element.105.refs_5_), channel_id=1, source_target_pairs={{1,0},{0,1},{3,2},{2,3},{5,4},{4,5},{7,6},{6,7},{9,8},{8,9},{11,10... | collective-permute-start | bytes 4718600 | tf_op jit(solution)/shard_map/ppermute | solution.py:132
  33.4 23.1 %collective-permute-start.10 = (bf16[1024,768]{1,0:T(8,128)(2,1)}, bf16[1024,768]{1,0:T(8,128)(2,1)}, u32[]{:S(2)}, u32[]{:S(2)}) collective-permute-start(bf16[1024,768]{1,0:T(8,128)(2,1)} %get-tuple-element.106.refs_8_), channel_id=1, source_target_pairs={{1,0},{0,1},{3,2},{2,3},{5,4},{4,5},{7,6},{6,7},{9,8},{8,9},{11,10... | collective-permute-start | bytes 4718600 | tf_op jit(solution)/shard_map/ppermute | solution.py:132
  35.1 12.8 %collective-permute-start.8 = (bf16[1024,128]{1,0:T(8,128)(2,1)}, bf16[1024,128]{1,0:T(8,128)(2,1)S(1)}, u32[]{:S(2)}, u32[]{:S(2)}) collective-permute-start(bf16[1024,128]{1,0:T(8,128)(2,1)} %collective-permute-done.2.refs_3_), channel_id=1, source_target_pairs={{2,0},{3,1},{0,2},{1,3},{6,4},{7,5},{4,6},{5,7},{10,8},{11,9},{8,1... | collective-permute-start | bytes 786440 | tf_op jit(solution)/shard_map/ppermute | solution.py:122
  42.7 13.8 %collective-permute-start.12 = (bf16[352,768]{1,0:T(8,128)(2,1)}, bf16[352,768]{1,0:T(8,128)(2,1)S(1)}, u32[]{:S(2)}, u32[]{:S(2)}) collective-permute-start(bf16[352,768]{1,0:T(8,128)(2,1)} %pad_maximum_fusion.2), channel_id=1, source_target_pairs={{0,16},{16,0},{1,17},{17,1},{2,18},{18,2},{3,19},{19,3},{4,20},{20... | collective-permute-start | bytes 1622024 | tf_op jit(solution)/shard_map/ppermute | solution.py:136
  66.9 45.6 %collective-permute-start.23 = (bf16[928,768]{1,0:T(8,128)(2,1)S(1)}, bf16[928,768]{1,0:T(8,128)(2,1)S(1)}, u32[]{:S(2)}, u32[]{:S(2)}) collective-permute-start(bf16[928,768]{1,0:T(8,128)(2,1)S(1)} %copy-done.10), channel_id=1, source_target_pairs={{0,16},{16,0},{1,17},{17,1},{2,18},{18,2},{3,19},{19,3},{4,20},{20... | collective-permute-start | bytes 4276232 | tf_op jit(solution)/shard_map/ppermute | solution.py:136
  69.0 14.7 %collective-permute-start.17 = (bf16[32,2176]{1,0:T(8,128)(2,1)S(1)}, bf16[32,2176]{1,0:T(8,128)(2,1)S(1)}, u32[]{:S(2)}, u32[]{:S(2)}) collective-permute-start(bf16[32,2176]{1,0:T(8,128)(2,1)S(1)} %get-tuple-element.181), channel_id=1, source_target_pairs={{12,0},{13,1},{14,2},{15,3},{0,4},{1,5},{2,6},{3,7},{4,8},{5,9},{6... | collective-permute-start | bytes 417800 | tf_op jit(solution)/shard_map/ppermute | solution.py:112
  88.9 23.6 %collective-permute-start.18 = (bf16[4,32,2176]{2,1,0:T(8,128)(2,1)S(1)}, bf16[4,32,2176]{2,1,0:T(8,128)(2,1)S(1)}, u32[]{:S(2)}, u32[]{:S(2)}) collective-permute-start(bf16[4,32,2176]{2,1,0:T(8,128)(2,1)S(1)} %pad_maximum_fusion.refs_0_), channel_id=1, source_target_pairs={{0,16},{16,0},{1,17},{17,1},{2,18},{18,2},{3,19},{19,3},{4,20},{20... | collective-permute-start | bytes 1671176 | tf_op jit(solution)/shard_map/ppermute | solution.py:136
  89.6 22.9 %collective-permute-start.19 = (bf16[4,32,2176]{2,1,0:T(8,128)(2,1)S(1)}, bf16[4,32,2176]{2,1,0:T(8,128)(2,1)S(1)}, u32[]{:S(2)}, u32[]{:S(2)}) collective-permute-start(bf16[4,32,2176]{2,1,0:T(8,128)(2,1)S(1)} %pad_maximum_fusion.refs_0_), channel_id=1, source_target_pairs={{2,0},{3,1},{0,2},{1,3},{6,4},{7,5},{4,6},{5,7},{10,8},{11,9},{8,1... | collective-permute-start | bytes 1671176 | tf_op jit(solution)/shard_map/ppermute | solution.py:122
  90.1 10.2 %collective-permute-start.20 = (bf16[32,2176]{1,0:T(8,128)(2,1)S(1)}, bf16[32,2176]{1,0:T(8,128)(2,1)S(1)}, u32[]{:S(2)}, u32[]{:S(2)}) collective-permute-start(bf16[32,2176]{1,0:T(8,128)(2,1)S(1)} %get-tuple-element.121), channel_id=1, source_target_pairs={{4,0},{5,1},{6,2},{7,3},{8,4},{9,5},{10,6},{11,7},{12,8},{13,9},{1... | collective-permute-start | bytes 417800 | tf_op jit(solution)/shard_map/ppermute | solution.py:112
  112.5 13.2 %collective-permute-start.30 = (bf16[928,768]{1,0:T(8,128)(2,1)S(1)}, bf16[928,768]{1,0:T(8,128)(2,1)S(1)}, u32[]{:S(2)}, u32[]{:S(2)}) collective-permute-start(bf16[928,768]{1,0:T(8,128)(2,1)S(1)} %collective-permute-done.23.refs_9_), channel_id=1, source_target_pairs={{1,0},{0,1},{3,2},{2,3},{5,4},{4,5},{7,6},{6,7},{9,8},{8,9},{11,10... | collective-permute-start | bytes 4276232 | tf_op jit(solution)/shard_map/ppermute | solution.py:132
  112.5 13.1 %collective-permute-start.28 = (bf16[768,768]{1,0:T(8,128)(2,1)}, bf16[768,768]{1,0:T(8,128)(2,1)S(1)}, u32[]{:S(2)}, u32[]{:S(2)}) collective-permute-start(bf16[768,768]{1,0:T(8,128)(2,1)} %collective-permute-done.5.refs_6_), channel_id=1, source_target_pairs={{1,0},{0,1},{3,2},{2,3},{5,4},{4,5},{7,6},{6,7},{9,8},{8,9},{11,10... | collective-permute-start | bytes 3538952 | tf_op jit(solution)/shard_map/ppermute | solution.py:132
  113.0 12.6 %collective-permute-start.29 = (bf16[352,768]{1,0:T(8,128)(2,1)S(1)}, bf16[352,768]{1,0:T(8,128)(2,1)S(1)}, u32[]{:S(2)}, u32[]{:S(2)}) collective-permute-start(bf16[352,768]{1,0:T(8,128)(2,1)S(1)} %collective-permute-done.12.refs_7_), channel_id=1, source_target_pairs={{1,0},{0,1},{3,2},{2,3},{5,4},{4,5},{7,6},{6,7},{9,8},{8,9},{11,10... | collective-permute-start | bytes 1622024 | tf_op jit(solution)/shard_map/ppermute | solution.py:132
  123.7 15.7 %collective-permute-start.26 = (bf16[4,32,2176]{2,1,0:T(8,128)(2,1)S(1)}, bf16[4,32,2176]{2,1,0:T(8,128)(2,1)S(1)}, u32[]{:S(2)}, u32[]{:S(2)}) collective-permute-start(bf16[4,32,2176]{2,1,0:T(8,128)(2,1)S(1)} %pad_maximum_fusion.1.refs_0_), channel_id=1, source_target_pairs={{0,16},{16,0},{1,17},{17,1},{2,18},{18,2},{3,19},{19,3},{4,20},{20... | collective-permute-start | bytes 1671176 | tf_op jit(solution)/shard_map/ppermute | solution.py:136
  125.2 14.2 %collective-permute-start.27 = (bf16[4,32,2176]{2,1,0:T(8,128)(2,1)S(1)}, bf16[4,32,2176]{2,1,0:T(8,128)(2,1)S(1)}, u32[]{:S(2)}, u32[]{:S(2)}) collective-permute-start(bf16[4,32,2176]{2,1,0:T(8,128)(2,1)S(1)} %pad_maximum_fusion.1.refs_0_), channel_id=1, source_target_pairs={{2,0},{3,1},{0,2},{1,3},{6,4},{7,5},{4,6},{5,7},{10,8},{11,9},{8,1... | collective-permute-start | bytes 1671176 | tf_op jit(solution)/shard_map/ppermute | solution.py:122
  148.2 18.5 %collective-permute-start.35 = (bf16[128,2048]{1,0:T(8,128)(2,1)S(1)}, bf16[128,2048]{1,0:T(8,128)(2,1)S(1)}, u32[]{:S(2)}, u32[]{:S(2)}) collective-permute-start(bf16[128,2048]{1,0:T(8,128)(2,1)S(1)} %pad_maximum_fusion.3), channel_id=1, source_target_pairs={{18,0},{19,1},{16,2},{17,3},{22,4},{23,5},{20,6},{21,7},{26,8},{27... | collective-permute-start | bytes 1572872 | tf_op jit(solution)/shard_map/ppermute | solution.py:147
  148.8 23.2 %collective-permute-start.34 = (bf16[128,2048]{1,0:T(8,128)(2,1)S(1)}, bf16[128,2048]{1,0:T(8,128)(2,1)S(1)}, u32[]{:S(2)}, u32[]{:S(2)}) collective-permute-start(bf16[128,2048]{1,0:T(8,128)(2,1)S(1)} %get-tuple-element.150), channel_id=1, source_target_pairs={{2,0},{3,1},{0,2},{1,3},{6,4},{7,5},{4,6},{5,7},{10,8},{11,9},{8,1... | collective-permute-start | bytes 1572872 | tf_op jit(solution)/shard_map/ppermute | solution.py:122
  150.3 23.5 %collective-permute-start.33 = (bf16[128,2048]{1,0:T(8,128)(2,1)S(1)}, bf16[128,2048]{1,0:T(8,128)(2,1)S(1)}, u32[]{:S(2)}, u32[]{:S(2)}) collective-permute-start(bf16[128,2048]{1,0:T(8,128)(2,1)S(1)} %get-tuple-element.149), channel_id=1, source_target_pairs={{0,16},{16,0},{1,17},{17,1},{2,18},{18,2},{3,19},{19,3},{4,20},{20... | collective-permute-start | bytes 1572872 | tf_op jit(solution)/shard_map/ppermute | solution.py:136
  165.5 11.4 %collective-permute-start.36 = (bf16[64,2048]{1,0:T(8,128)(2,1)S(1)}, bf16[64,2048]{1,0:T(8,128)(2,1)S(1)}, u32[]{:S(2)}, u32[]{:S(2)}) collective-permute-start(bf16[64,2048]{1,0:T(8,128)(2,1)S(1)} %get-tuple-element.158), channel_id=1, source_target_pairs={{2,0},{3,1},{0,2},{1,3},{6,4},{7,5},{4,6},{5,7},{10,8},{11,9},{8,1... | collective-permute-start | bytes 786440 | tf_op jit(solution)/shard_map/ppermute | solution.py:122
  166.1 10.8 %collective-permute-start.37 = (bf16[64,2048]{1,0:T(8,128)(2,1)S(1)}, bf16[64,2048]{1,0:T(8,128)(2,1)S(1)}, u32[]{:S(2)}, u32[]{:S(2)}) collective-permute-start(bf16[64,2048]{1,0:T(8,128)(2,1)S(1)} %get-tuple-element.159), channel_id=1, source_target_pairs={{0,16},{16,0},{1,17},{17,1},{2,18},{18,2},{3,19},{19,3},{4,20},{20... | collective-permute-start | bytes 786440 | tf_op jit(solution)/shard_map/ppermute | solution.py:136
  177.0 13.4 %collective-permute-start.40 = (bf16[32,2048]{1,0:T(8,128)(2,1)S(1)}, bf16[32,2048]{1,0:T(8,128)(2,1)S(1)}, u32[]{:S(2)}, u32[]{:S(2)}) collective-permute-start(bf16[32,2048]{1,0:T(8,128)(2,1)S(1)} %get-tuple-element.175), channel_id=1, source_target_pairs={{4,0},{5,1},{6,2},{7,3},{8,4},{9,5},{10,6},{11,7},{12,8},{13,9},{1... | collective-permute-start | bytes 393224 | tf_op jit(solution)/shard_map/ppermute | solution.py:112
  180.6 19.0 %collective-permute-start.39 = (bf16[32,2048]{1,0:T(8,128)(2,1)S(1)}, bf16[32,2048]{1,0:T(8,128)(2,1)S(1)}, u32[]{:S(2)}, u32[]{:S(2)}) collective-permute-start(bf16[32,2048]{1,0:T(8,128)(2,1)S(1)} %get-tuple-element.176), channel_id=1, source_target_pairs={{8,0},{9,1},{10,2},{11,3},{12,4},{13,5},{14,6},{15,7},{0,8},{1,9},... | collective-permute-start | bytes 393224 | tf_op jit(solution)/shard_map/ppermute | solution.py:112
  187.8 11.8 %collective-permute-start.38 = (bf16[32,2048]{1,0:T(8,128)(2,1)S(1)}, bf16[32,2048]{1,0:T(8,128)(2,1)S(1)}, u32[]{:S(2)}, u32[]{:S(2)}) collective-permute-start(bf16[32,2048]{1,0:T(8,128)(2,1)S(1)} %get-tuple-element.174), channel_id=1, source_target_pairs={{12,0},{13,1},{14,2},{15,3},{0,4},{1,5},{2,6},{3,7},{4,8},{5,9},{6... | collective-permute-start | bytes 393224 | tf_op jit(solution)/shard_map/ppermute | solution.py:112
  187.9 13.3 %collective-permute-start.41 = (bf16[128,2048]{1,0:T(8,128)(2,1)S(1)}, bf16[128,2048]{1,0:T(8,128)(2,1)S(1)}, u32[]{:S(2)}, u32[]{:S(2)}) collective-permute-start(bf16[128,2048]{1,0:T(8,128)(2,1)S(1)} %pad_maximum_fusion.4), channel_id=1, source_target_pairs={{0,16},{16,0},{1,17},{17,1},{2,18},{18,2},{3,19},{19,3},{4,20},{20... | collective-permute-start | bytes 1572872 | tf_op jit(solution)/shard_map/ppermute | solution.py:136
  189.6 13.0 %collective-permute-start.42 = (bf16[128,2048]{1,0:T(8,128)(2,1)S(1)}, bf16[128,2048]{1,0:T(8,128)(2,1)S(1)}, u32[]{:S(2)}, u32[]{:S(2)}) collective-permute-start(bf16[128,2048]{1,0:T(8,128)(2,1)S(1)} %pad_maximum_fusion.5), channel_id=1, source_target_pairs={{2,0},{3,1},{0,2},{1,3},{6,4},{7,5},{4,6},{5,7},{10,8},{11,9},{8,1... | collective-permute-start | bytes 1572872 | tf_op jit(solution)/shard_map/ppermute | solution.py:122
  206.4 9.9 %collective-permute-start.43 = (bf16[32,2048]{1,0:T(8,128)(2,1)S(1)}, bf16[32,2048]{1,0:T(8,128)(2,1)S(1)}, u32[]{:S(2)}, u32[]{:S(2)}) collective-permute-start(bf16[32,2048]{1,0:T(8,128)(2,1)S(1)} %get-tuple-element.171), channel_id=1, source_target_pairs={{12,0},{13,1},{14,2},{15,3},{0,4},{1,5},{2,6},{3,7},{4,8},{5,9},{6... | collective-permute-start | bytes 393224 | tf_op jit(solution)/shard_map/ppermute | solution.py:112
  (29 other events, 249.4 us)

commit v7 on v6

--- a/solution.py
+++ b/solution.py
@@ -395,6 +395,12 @@
     shares = share[...].reshape(total_rows, 128).astype(jnp.float32)
     lane = lax.broadcasted_iota(jnp.int32, (total_rows, 128), 1)
     experts = lax.axis_size("expert")
+
+    def activate(t, g, u, scale):
+        h = g / (1.0 + jnp.exp(-g)) * u * scale
+        mid[:, pl.ds(t * tile, tile)] = h.astype(mid.dtype)
+
+    pending = None
     for t in range(2 * tiles):
         e, j = t // tiles, t % tiles
         if j == 0:
@@ -406,10 +412,12 @@
         values = rows[...].reshape(total_rows, feats)
         g = jnp.dot(values, gate[t % SLOTS], preferred_element_type=jnp.float32)
         u = jnp.dot(values, up[t % SLOTS], preferred_element_type=jnp.float32)
-        h = g / (1.0 + jnp.exp(-g)) * u * scale
-        mid[:, pl.ds(t * tile, tile)] = h.astype(mid.dtype)
+        if pending is not None:
+            activate(*pending)
+        pending = (t, g, u, scale)
         if t + SLOTS < 2 * tiles:
             weight_copies.append(fetch(t + SLOTS))
+    activate(*pending)
     for copy in down_copies:
         copy.wait()
     for n in range(feats // out_tile):
@@ -505,7 +513,7 @@
     queries, gate_sent[1], gate_own = barrier((queries, gate_sent[1], gate_own))
     context = attend_here(queries, kv_pool, page_table, ctx_lens)
     context, w_up, w_down = barrier((context, w_up, w_down))
-    early = feats_here * 3 // 32
+    early = feats_here * 7 // 32
     up_own, *up_sent = cut(w_up, width, (early, feats_here - early))
     mixed_sent = jnp.concatenate([gate_sent[1], up_sent[0]], axis=0)
     shifted, across, gate_far, mixed_sent, up_sent[1], gate_own, up_own, w_down, context = (
@@ -548,19 +556,16 @@
     hidden_state, message = join(total[:block], back, residual, moe_gain, share, w_out.shape[1])
 
     rows = block // 2
-    lines = []
-    for k in range(2):
-        mine = message[rows * k : rows * (k + 1)]
-        lines.append([mine] + [shift_z(mine, depth, s) for s in range(1, depth)])
+    arrived = [message] + [shift_z(message, depth, s) for s in range(1, depth)]
     ready = []
     for k in range(2):
-        line = jnp.stack(lines[k])
+        line = jnp.stack([piece[rows * k : rows * (k + 1)] for piece in arrived])
         if k > 0:
             line, ready[0][3], ready[0][4] = barrier((line, ready[0][3], ready[0][4]))
         line_x = flip_x(line)
         line_y = flip_y(line, depth)
         if k == 0:
-            line_x, line_y, lines[1], up_far = barrier((line_x, line_y, lines[1], up_far))
+            line_x, line_y, up_far = barrier((line_x, line_y, up_far))
             ready.append([line, line_x, line_y, *diagonal(line_x, line_y, depth)])
         else:
             ready.append([line, line_x, line_y])
@@ -588,19 +593,27 @@
     last_l, last_x, last_y, last_low, last_high = run_experts(
         ready[1], kinds, 0, rows, weights, split
     )
+    half = last_x.shape[0] // 2
     back_low, back_high = flip_y(last_low, depth), flip_x(last_high)
+    plain_x = flip_x(last_x[half:].astype(jnp.bfloat16))
+    plain_y = flip_y(last_y[:half].astype(jnp.bfloat16), depth)
     full = out_l
     for back in backs:
         full = full + back.astype(jnp.float32)
-    full, back_low, back_high = barrier((full, back_low, back_high))
     first_rows = send_line(full, depth)
-    half = last_x.shape[0] // 2
-    sum_x = jnp.concatenate([last_x[:half] + back_low.astype(jnp.float32), last_x[half:]], axis=0)
-    sum_y = jnp.concatenate([last_y[:half], last_y[half:] + back_high.astype(jnp.float32)], axis=0)
-    back_x = flip_x(sum_x.astype(jnp.bfloat16))
-    back_y = flip_y(sum_y.astype(jnp.bfloat16), depth)
-    first_rows, back_x, back_y = barrier((first_rows, back_x, back_y))
-    full = last_l + back_x.astype(jnp.float32) + back_y.astype(jnp.float32)
+    back_low, back_high, plain_x, plain_y, _ = barrier(
+        (back_low, back_high, plain_x, plain_y, full)
+    )
+    sum_x = last_x[:half] + back_low.astype(jnp.float32)
+    sum_y = last_y[half:] + back_high.astype(jnp.float32)
+    sum_x = flip_x(sum_x.astype(jnp.bfloat16))
+    sum_y = flip_y(sum_y.astype(jnp.bfloat16), depth)
+    full = (
+        last_l
+        + jnp.concatenate([sum_x, plain_x], axis=0).astype(jnp.float32)
+        + jnp.concatenate([plain_y, sum_y], axis=0).astype(jnp.float32)
+    )
+    full, first_rows = barrier((full, first_rows))
     moe = [first_rows, send_line(full, depth)]
     combined = hidden_state + jnp.concatenate(moe, axis=0)
     return normalize(combined, final_gain).astype(jnp.bfloat16)

time: 218 us -> 209 us (0.959)
  starting transfers between devices: 68.9 us -> 52.2 us
  waiting for transfers between devices: 97.2 us -> 106 us
    ppermute x15 -> x12, starting transfers between devices: 38.8 us -> 19.2 us  [shift_z(): return lax.ppermute(values, 'expert', pairs)]
    ppermute x11 -> x12, waiting for transfers between devices: 24.6 us -> 34 us  [flip_x(): return lax.ppermute(values, 'dp', [(0, 1), (1, 0)])]
    ppermute x11 -> x12, starting transfers between devices: 12.3 us -> 16 us  [flip_y(): return lax.ppermute(values, 'expert', pairs)]
    ppermute x15 -> x12, waiting for transfers between devices: 41.6 us -> 40.4 us  [shift_z(): return lax.ppermute(values, 'expert', pairs)]
    ppermute x11 -> x12, starting transfers between devices: 16.1 us -> 15.2 us  [flip_x(): return lax.ppermute(values, 'dp', [(0, 1), (1, 0)])]
    ppermute x11 -> x12, waiting for transfers between devices: 31 us -> 31.7 us  [flip_y(): return lax.ppermute(values, 'expert', pairs)]
  transfers between devices with their start and end apart: 46 -> 45, of which waited for: 25 -> 23; matrix products, arithmetic and copies ran while one was open for 1% -> 1% of each run, Pallas kernels for 16% -> 17%
where the time goes in v7:
time: 209 us; the launch traced here: 208 us
  waiting for transfers between devices  106 us (51%)
  starting transfers between devices  52.2 us (25%)
  Pallas kernels  40 us (19%)
  local copies, waits for them, and re-layouts  6.57 us (3%)
  other arithmetic  3.04 us (1%)
    ppermute x12, waiting for transfers between devices, shift_z(): return lax.ppermute(values, 'expert', pairs)  40.4 us
    ppermute x12, waiting for transfers between devices, flip_x(): return lax.ppermute(values, 'dp', [(0, 1), (1, 0)])  34 us
    ppermute x12, waiting for transfers between devices, flip_y(): return lax.ppermute(values, 'expert', pairs)  31.7 us
    pallas_call x2, Pallas kernels, run_experts(): pl.pallas_call(functools.partial(experts_kernel, tile, 512, first_row, co...  28.3 us
    ppermute x12, starting transfers between devices, shift_z(): return lax.ppermute(values, 'expert', pairs)  19.2 us
    ppermute x12, starting transfers between devices, flip_y(): return lax.ppermute(values, 'expert', pairs)  16 us
    ppermute x12, starting transfers between devices, flip_x(): return lax.ppermute(values, 'dp', [(0, 1), (1, 0)])  15.2 us
    pallas_call x1, Pallas kernels, attend_here(): pl.pallas_call(attend_kernel, out_shape=jax.ShapeDtypeStruct(queries.shap...  5.81 us
  transfers between devices with their start and end apart: 45, of which 23 were waited for; matrix products, arithmetic and copies ran while one was open for 1% of the time, Pallas kernels for 17%

profile of v7, /device:TPU:0, one launch (start us, length us, event | category | flops | bytes accessed | tf_op | source)
XLA Modules:
  0.0 208.4 jit_solution(4520968732863196946)
XLA Ops:
  0.0 1.8 copy-done
  1.8 1.7 cut.2
  3.6 3.0 %collective-permute-start.5 = (bf16[768,768]{1,0:T(8,128)(2,1)}, bf16[768,768]{1,0:T(8,128)(2,1)}, u32[]{:S(2)}, u32[]{:S(2)}) collective-permute-start(bf16[768,768]{1,0:T(8,128)(2,1)} %get-tuple-element.83), channel_id=1, source_target_pairs={{0,16},{16,0},{1,17},{17,1},{2,18},{18,2},{3,19},{19,3},{4,20},{20... | collective-permute-start | bytes 3538952 | tf_op jit(solution)/shard_map/ppermute | solution.py:136
  6.6 3.6 %collective-permute-start = (bf16[1024,128]{1,0:T(8,128)(2,1)}, bf16[1024,128]{1,0:T(8,128)(2,1)}, u32[]{:S(2)}, u32[]{:S(2)}) collective-permute-start(bf16[1024,128]{1,0:T(8,128)(2,1)} %refs_0_.1), channel_id=1, source_target_pairs={{4,0},{5,1},{6,2},{7,3},{8,4},{9,5},{10,6},{11,7},{12,8},{13,9},{1... | collective-permute-start | bytes 786440 | tf_op jit(solution)/shard_map/ppermute | solution.py:112
  12.7 4.6 %collective-permute-done.refs_1_ = bf16[1024,128]{1,0:T(8,128)(2,1)} collective-permute-done((bf16[1024,128]{1,0:T(8,128)(2,1)}, bf16[1024,128]{1,0:T(8,128)(2,1)}, u32[]{:S(2)}, u32[]{:S(2)}) %collective-permute-start) | collective-permute-done | bytes 262176 | tf_op jit(solution)/shard_map/ppermute | solution.py:112
  19.6 1.6 copy-done.2
  22.9 5.8 %attend.1.ctx_ref = bf16[128,1024]{1,0:T(8,128)(2,1)S(1)} custom-call(s32[2,4]{1,0:T(2,128)S(1)} %copy-done.8, s32[128,1]{1,0:T(8,128)S(1)} %copy-done.6, bf16[128,1024]{1,0:T(8,128)(2,1)S(1)} %copy-done.3, bf16[2,8,64,1024]{3,2,1,0:T(8,128)(2,1)S(1)} %copy-done.2), custom_call_target="tpu_custom_call" | custom-call | flops 134217728 | bytes 2621440 | tf_op jit(solution)/shard_map/attend/pallas_call | solution.py:182
  33.4 1.8 collective-permute-start.7
  36.6 5.7 %collective-permute-done.7.refs_6_ = bf16[1024,128]{1,0:T(8,128)(2,1)S(1)} collective-permute-done((bf16[1024,128]{1,0:T(8,128)(2,1)}, bf16[1024,128]{1,0:T(8,128)(2,1)S(1)}, u32[]{:S(2)}, u32[]{:S(2)}) %collective-permute-start.7) | collective-permute-done | bytes 262176 | tf_op jit(solution)/shard_map/ppermute | solution.py:122
  42.3 1.7 collective-permute-start.8
  44.3 6.3 %collective-permute-done.8.refs_7_ = bf16[1024,128]{1,0:T(8,128)(2,1)S(1)} collective-permute-done((bf16[1024,128]{1,0:T(8,128)(2,1)}, bf16[1024,128]{1,0:T(8,128)(2,1)S(1)}, u32[]{:S(2)}, u32[]{:S(2)}) %collective-permute-start.8) | collective-permute-done | bytes 262176 | tf_op jit(solution)/shard_map/ppermute | solution.py:122
  50.8 3.3 %collective-permute-done.12.refs_7_ = bf16[480,768]{1,0:T(8,128)(2,1)} collective-permute-done((bf16[480,768]{1,0:T(8,128)(2,1)}, bf16[480,768]{1,0:T(8,128)(2,1)}, u32[]{:S(2)}, u32[]{:S(2)}) %collective-permute-start.12) | collective-permute-done | bytes 737312 | tf_op jit(solution)/shard_map/ppermute | solution.py:136
  54.1 2.5 %project.1 = (f32[128,1024]{1,0:T(8,128)S(1)}, bf16[128,1024]{1,0:T(8,128)(2,1)S(1)}) custom-call(bf16[128,1024]{1,0:T(8,128)(2,1)S(1)} %attend.1.ctx_ref, bf16[128,1024]{1,0:T(8,128)(2,1)S(1)} %collective-permute-done.6.other_ref, bf16[1024,128]{1,0:T(8,128)(2,1)S(1)} %copy-done.4, bf16[1024,128]{1,0:T(8,128)(2,1)} %collective-permute-done.refs_1_, ...), custom_call_target="tpu_custom_call" | custom-call | flops 536870912 | bytes 2883584 | tf_op jit(solution)/shard_map/project/pallas_call | solution.py:224
  58.2 6.1 %collective-permute-done.13 = bf16[128,1024]{1,0:T(8,128)(2,1)S(1)} collective-permute-done((bf16[128,1024]{1,0:T(8,128)(2,1)S(1)}, bf16[128,1024]{1,0:T(8,128)(2,1)S(1)}, u32[]{:S(2)}, u32[]{:S(2)}) %collective-permute-start.13) | collective-permute-done | bytes 262176 | tf_op jit(solution)/shard_map/ppermute | solution.py:136
  66.4 3.7 %collective-permute-start.15 = (bf16[64,2176]{1,0:T(8,128)(2,1)S(1)}, bf16[64,2176]{1,0:T(8,128)(2,1)S(1)}, u32[]{:S(2)}, u32[]{:S(2)}) collective-permute-start(bf16[64,2176]{1,0:T(8,128)(2,1)S(1)} %get-tuple-element.115), channel_id=1, source_target_pairs={{4,0},{5,1},{6,2},{7,3},{8,4},{9,5},{10,6},{11,7},{12,8},{13,9},{1... | collective-permute-start | bytes 835592 | tf_op jit(solution)/shard_map/ppermute | solution.py:112
  70.1 6.5 %collective-permute-start.16 = (bf16[64,2176]{1,0:T(8,128)(2,1)S(1)}, bf16[64,2176]{1,0:T(8,128)(2,1)S(1)}, u32[]{:S(2)}, u32[]{:S(2)}) collective-permute-start(bf16[64,2176]{1,0:T(8,128)(2,1)S(1)} %get-tuple-element.115), channel_id=1, source_target_pairs={{8,0},{9,1},{10,2},{11,3},{12,4},{13,5},{14,6},{15,7},{0,8},{1,9},... | collective-permute-start | bytes 835592 | tf_op jit(solution)/shard_map/ppermute | solution.py:112
  76.6 5.5 %collective-permute-done.15 = bf16[64,2176]{1,0:T(8,128)(2,1)S(1)} collective-permute-done((bf16[64,2176]{1,0:T(8,128)(2,1)S(1)}, bf16[64,2176]{1,0:T(8,128)(2,1)S(1)}, u32[]{:S(2)}, u32[]{:S(2)}) %collective-permute-start.15) | collective-permute-done | bytes 278560 | tf_op jit(solution)/shard_map/ppermute | solution.py:112
  82.1 19.1 %collective-permute-done.16 = bf16[64,2176]{1,0:T(8,128)(2,1)S(1)} collective-permute-done((bf16[64,2176]{1,0:T(8,128)(2,1)S(1)}, bf16[64,2176]{1,0:T(8,128)(2,1)S(1)}, u32[]{:S(2)}, u32[]{:S(2)}) %collective-permute-start.16) | collective-permute-done | bytes 278560 | tf_op jit(solution)/shard_map/ppermute | solution.py:112
  103.5 11.7 %collective-permute-done.18.refs_1_ = bf16[4,32,2176]{2,1,0:T(8,128)(2,1)S(1)} collective-permute-done((bf16[4,32,2176]{2,1,0:T(8,128)(2,1)S(1)}, bf16[4,32,2176]{2,1,0:T(8,128)(2,1)S(1)}, u32[]{:S(2)}, u32[]{:S(2)}) %collective-permute-start.18) | collective-permute-done | bytes 557088 | tf_op jit(solution)/shard_map/ppermute | solution.py:136
  116.1 1.6 collective-permute-start.21
  119.3 6.0 %collective-permute-done.21.refs_3_ = bf16[2,32,2176]{2,1,0:T(8,128)(2,1)S(1)} collective-permute-done((bf16[2,32,2176]{2,1,0:T(8,128)(2,1)S(1)}, bf16[2,32,2176]{2,1,0:T(8,128)(2,1)S(1)}, u32[]{:S(2)}, u32[]{:S(2)}) %collective-permute-start.21) | collective-permute-done | bytes 278560 | tf_op jit(solution)/shard_map/ppermute | solution.py:122
  128.5 14.1 %experts.2 = (f32[128,2048]{1,0:T(8,128)S(1)}, bf16[128,2048]{1,0:T(8,128)(2,1)S(1)}, bf16[128,2048]{1,0:T(8,128)(2,1)S(1)}, bf16[64,2048]{1,0:T(8,128)(2,1)S(1)}, bf16[64,2048]{1,0:T(8,128)(2,1)S(1)}) custom-call(bf16[4,32,2176]{2,1,0:T(8,128)(2,1)S(1)} %pad_maximum_fusion.2.refs_0_, bf16[4,32,2176]{2,1,0:T(8,128)(2,1)S(1)} %collective-permute-done.18.refs_1_, ...), custom_call_target="tpu_custom_call" | custom-call | flops 9663676416 | bytes 31457280 | tf_op jit(solution)/shard_map/experts/pallas_call | solution.py:439
  145.0 5.2 %collective-permute-done.28.refs_3_ = bf16[2,32,2176]{2,1,0:T(8,128)(2,1)S(1)} collective-permute-done((bf16[2,32,2176]{2,1,0:T(8,128)(2,1)S(1)}, bf16[2,32,2176]{2,1,0:T(8,128)(2,1)S(1)}, u32[]{:S(2)}, u32[]{:S(2)}) %collective-permute-start.28) | collective-permute-done | bytes 278560 | tf_op jit(solution)/shard_map/ppermute | solution.py:122
  155.1 14.1 %experts.3 = (f32[128,2048]{1,0:T(8,128)S(1)}, f32[128,2048]{1,0:T(8,128)S(1)}, f32[128,2048]{1,0:T(8,128)S(1)}, bf16[64,2048]{1,0:T(8,128)(2,1)S(1)}, bf16[64,2048]{1,0:T(8,128)(2,1)S(1)}) custom-call(bf16[4,32,2176]{2,1,0:T(8,128)(2,1)S(1)} %pad_maximum_fusion.1.refs_0_, bf16[4,32,2176]{2,1,0:T(8,128)(2,1)S(1)} %collective-permute-done.23.refs_1_, ...), custom_call_target="tpu_custom_call" | custom-call | flops 9663676416 | bytes 31457280 | tf_op jit(solution)/shard_map/experts/pallas_call | solution.py:439
  172.1 5.5 %collective-permute-done.34 = bf16[128,2048]{1,0:T(8,128)(2,1)S(1)} collective-permute-done((bf16[128,2048]{1,0:T(8,128)(2,1)S(1)}, bf16[128,2048]{1,0:T(8,128)(2,1)S(1)}, u32[]{:S(2)}, u32[]{:S(2)}) %collective-permute-start.34) | collective-permute-done | bytes 524320 | tf_op jit(solution)/shard_map/ppermute | solution.py:136
  178.7 4.0 %collective-permute-done.32 = bf16[64,2048]{1,0:T(8,128)(2,1)S(1)} collective-permute-done((bf16[64,2048]{1,0:T(8,128)(2,1)S(1)}, bf16[64,2048]{1,0:T(8,128)(2,1)S(1)}, u32[]{:S(2)}, u32[]{:S(2)}) %collective-permute-start.32) | collective-permute-done | bytes 262176 | tf_op jit(solution)/shard_map/ppermute | solution.py:136
  183.2 3.3 %collective-permute-done.30 = bf16[64,2048]{1,0:T(8,128)(2,1)S(1)} collective-permute-done((bf16[64,2048]{1,0:T(8,128)(2,1)S(1)}, bf16[64,2048]{1,0:T(8,128)(2,1)S(1)}, u32[]{:S(2)}, u32[]{:S(2)}) %collective-permute-start.30) | collective-permute-done | bytes 262176 | tf_op jit(solution)/shard_map/ppermute | solution.py:122
  187.9 1.9 collective-permute-done.40
  189.9 4.9 %collective-permute-done.38 = bf16[64,2048]{1,0:T(8,128)(2,1)S(1)} collective-permute-done((bf16[64,2048]{1,0:T(8,128)(2,1)S(1)}, bf16[64,2048]{1,0:T(8,128)(2,1)S(1)}, u32[]{:S(2)}, u32[]{:S(2)}) %collective-permute-start.38) | collective-permute-done | bytes 262176 | tf_op jit(solution)/shard_map/ppermute | solution.py:122
  196.2 3.2 %collective-permute-start.44 = (bf16[32,2048]{1,0:T(8,128)(2,1)S(1)}, bf16[32,2048]{1,0:T(8,128)(2,1)S(1)}, u32[]{:S(2)}, u32[]{:S(2)}) collective-permute-start(bf16[32,2048]{1,0:T(8,128)(2,1)S(1)} %get-tuple-element.164), channel_id=1, source_target_pairs={{4,0},{5,1},{6,2},{7,3},{8,4},{9,5},{10,6},{11,7},{12,8},{13,9},{1... | collective-permute-start | bytes 393224 | tf_op jit(solution)/shard_map/ppermute | solution.py:112
  199.3 4.5 %collective-permute-done.42 = bf16[32,2048]{1,0:T(8,128)(2,1)S(1)} collective-permute-done((bf16[32,2048]{1,0:T(8,128)(2,1)S(1)}, bf16[32,2048]{1,0:T(8,128)(2,1)S(1)}, u32[]{:S(2)}, u32[]{:S(2)}) %collective-permute-start.42) | collective-permute-done | bytes 131104 | tf_op jit(solution)/shard_map/ppermute | solution.py:112
  203.8 3.6 %collective-permute-done.43 = bf16[32,2048]{1,0:T(8,128)(2,1)S(1)} collective-permute-done((bf16[32,2048]{1,0:T(8,128)(2,1)S(1)}, bf16[32,2048]{1,0:T(8,128)(2,1)S(1)}, u32[]{:S(2)}, u32[]{:S(2)}) %collective-permute-start.43) | collective-permute-done | bytes 131104 | tf_op jit(solution)/shard_map/ppermute | solution.py:112
  (132 shorter events, 40.1 us)
Async XLA Ops:
  3.6 29.3 %collective-permute-start.5 = (bf16[768,768]{1,0:T(8,128)(2,1)}, bf16[768,768]{1,0:T(8,128)(2,1)}, u32[]{:S(2)}, u32[]{:S(2)}) collective-permute-start(bf16[768,768]{1,0:T(8,128)(2,1)} %get-tuple-element.83), channel_id=1, source_target_pairs={{0,16},{16,0},{1,17},{17,1},{2,18},{18,2},{3,19},{19,3},{4,20},{20... | collective-permute-start | bytes 3538952 | tf_op jit(solution)/shard_map/ppermute | solution.py:136
  6.6 10.7 %collective-permute-start = (bf16[1024,128]{1,0:T(8,128)(2,1)}, bf16[1024,128]{1,0:T(8,128)(2,1)}, u32[]{:S(2)}, u32[]{:S(2)}) collective-permute-start(bf16[1024,128]{1,0:T(8,128)(2,1)} %refs_0_.1), channel_id=1, source_target_pairs={{4,0},{5,1},{6,2},{7,3},{8,4},{9,5},{10,6},{11,7},{12,8},{13,9},{1... | collective-permute-start | bytes 786440 | tf_op jit(solution)/shard_map/ppermute | solution.py:112
  10.2 22.3 %collective-permute-start.1 = (bf16[1024,128]{1,0:T(8,128)(2,1)}, bf16[1024,128]{1,0:T(8,128)(2,1)}, u32[]{:S(2)}, u32[]{:S(2)}) collective-permute-start(bf16[1024,128]{1,0:T(8,128)(2,1)} %refs_0_.1), channel_id=1, source_target_pairs={{8,0},{9,1},{10,2},{11,3},{12,4},{13,5},{14,6},{15,7},{0,8},{1,9},... | collective-permute-start | bytes 786440 | tf_op jit(solution)/shard_map/ppermute | solution.py:112
  10.2 22.3 %collective-permute-start.2 = (bf16[1024,128]{1,0:T(8,128)(2,1)}, bf16[1024,128]{1,0:T(8,128)(2,1)}, u32[]{:S(2)}, u32[]{:S(2)}) collective-permute-start(bf16[1024,128]{1,0:T(8,128)(2,1)} %refs_0_.1), channel_id=1, source_target_pairs={{12,0},{13,1},{14,2},{15,3},{0,4},{1,5},{2,6},{3,7},{4,8},{5,9},{6... | collective-permute-start | bytes 786440 | tf_op jit(solution)/shard_map/ppermute | solution.py:112
  11.2 21.3 %collective-permute-start.3 = (bf16[1024,128]{1,0:T(8,128)(2,1)}, bf16[1024,128]{1,0:T(8,128)(2,1)}, u32[]{:S(2)}, u32[]{:S(2)}) collective-permute-start(bf16[1024,128]{1,0:T(8,128)(2,1)} %refs_0_.1), channel_id=1, source_target_pairs={{2,0},{3,1},{0,2},{1,3},{6,4},{7,5},{4,6},{5,7},{10,8},{11,9},{8,1... | collective-permute-start | bytes 786440 | tf_op jit(solution)/shard_map/ppermute | solution.py:122
  17.3 15.2 %collective-permute-start.4 = (bf16[1024,128]{1,0:T(8,128)(2,1)}, bf16[1024,128]{1,0:T(8,128)(2,1)}, u32[]{:S(2)}, u32[]{:S(2)}) collective-permute-start(bf16[1024,128]{1,0:T(8,128)(2,1)} %collective-permute-done.refs_1_), channel_id=1, source_target_pairs={{2,0},{3,1},{0,2},{1,3},{6,4},{7,5},{4,6},{5,7},{10,8},{11,9},{8,1... | collective-permute-start | bytes 786440 | tf_op jit(solution)/shard_map/ppermute | solution.py:122
  32.9 21.2 %collective-permute-start.11 = (bf16[704,2048]{1,0:T(8,128)(2,1)}, bf16[704,2048]{1,0:T(8,128)(2,1)}, u32[]{:S(2)}, u32[]{:S(2)}) collective-permute-start(bf16[704,2048]{1,0:T(8,128)(2,1)} %bitcast.1.refs_10_), channel_id=1, source_target_pairs={{1,0},{0,1},{3,2},{2,3},{5,4},{4,5},{7,6},{6,7},{9,8},{8,9},{11,10... | collective-permute-start | bytes 8650760 | tf_op jit(solution)/shard_map/ppermute | solution.py:132
  32.9 21.2 %collective-permute-start.10 = (bf16[1024,768]{1,0:T(8,128)(2,1)}, bf16[1024,768]{1,0:T(8,128)(2,1)S(1)}, u32[]{:S(2)}, u32[]{:S(2)}) collective-permute-start(bf16[1024,768]{1,0:T(8,128)(2,1)} %get-tuple-element.102.refs_8_), channel_id=1, source_target_pairs={{1,0},{0,1},{3,2},{2,3},{5,4},{4,5},{7,6},{6,7},{9,8},{8,9},{11,10... | collective-permute-start | bytes 4718600 | tf_op jit(solution)/shard_map/ppermute | solution.py:132
  33.4 20.7 %collective-permute-start.9 = (bf16[1024,768]{1,0:T(8,128)(2,1)}, bf16[1024,768]{1,0:T(8,128)(2,1)}, u32[]{:S(2)}, u32[]{:S(2)}) collective-permute-start(bf16[1024,768]{1,0:T(8,128)(2,1)} %get-tuple-element.101.refs_5_), channel_id=1, source_target_pairs={{1,0},{0,1},{3,2},{2,3},{5,4},{4,5},{7,6},{6,7},{9,8},{8,9},{11,10... | collective-permute-start | bytes 4718600 | tf_op jit(solution)/shard_map/ppermute | solution.py:132
  33.4 9.0 %collective-permute-start.7 = (bf16[1024,128]{1,0:T(8,128)(2,1)}, bf16[1024,128]{1,0:T(8,128)(2,1)S(1)}, u32[]{:S(2)}, u32[]{:S(2)}) collective-permute-start(bf16[1024,128]{1,0:T(8,128)(2,1)} %collective-permute-done.1.refs_2_), channel_id=1, source_target_pairs={{2,0},{3,1},{0,2},{1,3},{6,4},{7,5},{4,6},{5,7},{10,8},{11,9},{8,1... | collective-permute-start | bytes 786440 | tf_op jit(solution)/shard_map/ppermute | solution.py:122
  35.1 18.9 %collective-permute-start.12 = (bf16[480,768]{1,0:T(8,128)(2,1)}, bf16[480,768]{1,0:T(8,128)(2,1)}, u32[]{:S(2)}, u32[]{:S(2)}) collective-permute-start(bf16[480,768]{1,0:T(8,128)(2,1)} %pad_maximum_fusion), channel_id=1, source_target_pairs={{0,16},{16,0},{1,17},{17,1},{2,18},{18,2},{3,19},{19,3},{4,20},{20... | collective-permute-start | bytes 2211848 | tf_op jit(solution)/shard_map/ppermute | solution.py:136
  64.6 51.0 %collective-permute-start.20 = (bf16[800,768]{1,0:T(8,128)(2,1)S(1)}, bf16[800,768]{1,0:T(8,128)(2,1)S(1)}, u32[]{:S(2)}, u32[]{:S(2)}) collective-permute-start(bf16[800,768]{1,0:T(8,128)(2,1)S(1)} %copy-done.10), channel_id=1, source_target_pairs={{0,16},{16,0},{1,17},{17,1},{2,18},{18,2},{3,19},{19,3},{4,20},{20... | collective-permute-start | bytes 3686408 | tf_op jit(solution)/shard_map/ppermute | solution.py:136
  66.4 15.7 %collective-permute-start.15 = (bf16[64,2176]{1,0:T(8,128)(2,1)S(1)}, bf16[64,2176]{1,0:T(8,128)(2,1)S(1)}, u32[]{:S(2)}, u32[]{:S(2)}) collective-permute-start(bf16[64,2176]{1,0:T(8,128)(2,1)S(1)} %get-tuple-element.115), channel_id=1, source_target_pairs={{4,0},{5,1},{6,2},{7,3},{8,4},{9,5},{10,6},{11,7},{12,8},{13,9},{1... | collective-permute-start | bytes 835592 | tf_op jit(solution)/shard_map/ppermute | solution.py:112
  70.1 31.1 %collective-permute-start.16 = (bf16[64,2176]{1,0:T(8,128)(2,1)S(1)}, bf16[64,2176]{1,0:T(8,128)(2,1)S(1)}, u32[]{:S(2)}, u32[]{:S(2)}) collective-permute-start(bf16[64,2176]{1,0:T(8,128)(2,1)S(1)} %get-tuple-element.115), channel_id=1, source_target_pairs={{8,0},{9,1},{10,2},{11,3},{12,4},{13,5},{14,6},{15,7},{0,8},{1,9},... | collective-permute-start | bytes 835592 | tf_op jit(solution)/shard_map/ppermute | solution.py:112
  76.6 24.6 %collective-permute-start.17 = (bf16[64,2176]{1,0:T(8,128)(2,1)S(1)}, bf16[64,2176]{1,0:T(8,128)(2,1)S(1)}, u32[]{:S(2)}, u32[]{:S(2)}) collective-permute-start(bf16[64,2176]{1,0:T(8,128)(2,1)S(1)} %get-tuple-element.115), channel_id=1, source_target_pairs={{12,0},{13,1},{14,2},{15,3},{0,4},{1,5},{2,6},{3,7},{4,8},{5,9},{6... | collective-permute-start | bytes 835592 | tf_op jit(solution)/shard_map/ppermute | solution.py:112
  101.3 13.9 %collective-permute-start.18 = (bf16[4,32,2176]{2,1,0:T(8,128)(2,1)S(1)}, bf16[4,32,2176]{2,1,0:T(8,128)(2,1)S(1)}, u32[]{:S(2)}, u32[]{:S(2)}) collective-permute-start(bf16[4,32,2176]{2,1,0:T(8,128)(2,1)S(1)} %pad_maximum_fusion.2.refs_0_), channel_id=1, source_target_pairs={{0,16},{16,0},{1,17},{17,1},{2,18},{18,2},{3,19},{19,3},{4,20},{20... | collective-permute-start | bytes 1671176 | tf_op jit(solution)/shard_map/ppermute | solution.py:136
  102.0 13.6 %collective-permute-start.19 = (bf16[4,32,2176]{2,1,0:T(8,128)(2,1)S(1)}, bf16[4,32,2176]{2,1,0:T(8,128)(2,1)S(1)}, u32[]{:S(2)}, u32[]{:S(2)}) collective-permute-start(bf16[4,32,2176]{2,1,0:T(8,128)(2,1)S(1)} %pad_maximum_fusion.2.refs_0_), channel_id=1, source_target_pairs={{2,0},{3,1},{0,2},{1,3},{6,4},{7,5},{4,6},{5,7},{10,8},{11,9},{8,1... | collective-permute-start | bytes 1671176 | tf_op jit(solution)/shard_map/ppermute | solution.py:122
  115.6 12.9 %collective-permute-start.27 = (bf16[800,768]{1,0:T(8,128)(2,1)S(1)}, bf16[800,768]{1,0:T(8,128)(2,1)S(1)}, u32[]{:S(2)}, u32[]{:S(2)}) collective-permute-start(bf16[800,768]{1,0:T(8,128)(2,1)S(1)} %collective-permute-done.20.refs_9_), channel_id=1, source_target_pairs={{1,0},{0,1},{3,2},{2,3},{5,4},{4,5},{7,6},{6,7},{9,8},{8,9},{11,10... | collective-permute-start | bytes 3686408 | tf_op jit(solution)/shard_map/ppermute | solution.py:132
  115.6 12.9 %collective-permute-start.25 = (bf16[768,768]{1,0:T(8,128)(2,1)}, bf16[768,768]{1,0:T(8,128)(2,1)S(1)}, u32[]{:S(2)}, u32[]{:S(2)}) collective-permute-start(bf16[768,768]{1,0:T(8,128)(2,1)} %collective-permute-done.5.refs_6_), channel_id=1, source_target_pairs={{1,0},{0,1},{3,2},{2,3},{5,4},{4,5},{7,6},{6,7},{9,8},{8,9},{11,10... | collective-permute-start | bytes 3538952 | tf_op jit(solution)/shard_map/ppermute | solution.py:132
  116.1 12.4 %collective-permute-start.26 = (bf16[480,768]{1,0:T(8,128)(2,1)}, bf16[480,768]{1,0:T(8,128)(2,1)S(1)}, u32[]{:S(2)}, u32[]{:S(2)}) collective-permute-start(bf16[480,768]{1,0:T(8,128)(2,1)} %collective-permute-done.12.refs_7_), channel_id=1, source_target_pairs={{1,0},{0,1},{3,2},{2,3},{5,4},{4,5},{7,6},{6,7},{9,8},{8,9},{11,10... | collective-permute-start | bytes 2211848 | tf_op jit(solution)/shard_map/ppermute | solution.py:132
  116.1 9.1 %collective-permute-start.21 = (bf16[2,32,2176]{2,1,0:T(8,128)(2,1)S(1)}, bf16[2,32,2176]{2,1,0:T(8,128)(2,1)S(1)}, u32[]{:S(2)}, u32[]{:S(2)}) collective-permute-start(bf16[2,32,2176]{2,1,0:T(8,128)(2,1)S(1)} %slice.104), channel_id=1, source_target_pairs={{2,0},{3,1},{0,2},{1,3},{6,4},{7,5},{4,6},{5,7},{10,8},{11,9},{8,1... | collective-permute-start | bytes 835592 | tf_op jit(solution)/shard_map/ppermute | solution.py:122
  126.6 16.0 %collective-permute-start.23 = (bf16[4,32,2176]{2,1,0:T(8,128)(2,1)S(1)}, bf16[4,32,2176]{2,1,0:T(8,128)(2,1)S(1)}, u32[]{:S(2)}, u32[]{:S(2)}) collective-permute-start(bf16[4,32,2176]{2,1,0:T(8,128)(2,1)S(1)} %pad_maximum_fusion.1.refs_0_), channel_id=1, source_target_pairs={{0,16},{16,0},{1,17},{17,1},{2,18},{18,2},{3,19},{19,3},{4,20},{20... | collective-permute-start | bytes 1671176 | tf_op jit(solution)/shard_map/ppermute | solution.py:136
  128.0 14.7 %collective-permute-start.24 = (bf16[4,32,2176]{2,1,0:T(8,128)(2,1)S(1)}, bf16[4,32,2176]{2,1,0:T(8,128)(2,1)S(1)}, u32[]{:S(2)}, u32[]{:S(2)}) collective-permute-start(bf16[4,32,2176]{2,1,0:T(8,128)(2,1)S(1)} %pad_maximum_fusion.1.refs_0_), channel_id=1, source_target_pairs={{2,0},{3,1},{0,2},{1,3},{6,4},{7,5},{4,6},{5,7},{10,8},{11,9},{8,1... | collective-permute-start | bytes 1671176 | tf_op jit(solution)/shard_map/ppermute | solution.py:122
  151.5 19.1 %collective-permute-start.36 = (bf16[128,2048]{1,0:T(8,128)(2,1)S(1)}, bf16[128,2048]{1,0:T(8,128)(2,1)S(1)}, u32[]{:S(2)}, u32[]{:S(2)}) collective-permute-start(bf16[128,2048]{1,0:T(8,128)(2,1)S(1)} %pad_maximum_fusion.3), channel_id=1, source_target_pairs={{18,0},{19,1},{16,2},{17,3},{22,4},{23,5},{20,6},{21,7},{26,8},{27... | collective-permute-start | bytes 1572872 | tf_op jit(solution)/shard_map/ppermute | solution.py:147
  152.2 25.5 %collective-permute-start.34 = (bf16[128,2048]{1,0:T(8,128)(2,1)S(1)}, bf16[128,2048]{1,0:T(8,128)(2,1)S(1)}, u32[]{:S(2)}, u32[]{:S(2)}) collective-permute-start(bf16[128,2048]{1,0:T(8,128)(2,1)S(1)} %get-tuple-element.151), channel_id=1, source_target_pairs={{0,16},{16,0},{1,17},{17,1},{2,18},{18,2},{3,19},{19,3},{4,20},{20... | collective-permute-start | bytes 1572872 | tf_op jit(solution)/shard_map/ppermute | solution.py:136
  153.6 24.7 %collective-permute-start.35 = (bf16[128,2048]{1,0:T(8,128)(2,1)S(1)}, bf16[128,2048]{1,0:T(8,128)(2,1)S(1)}, u32[]{:S(2)}, u32[]{:S(2)}) collective-permute-start(bf16[128,2048]{1,0:T(8,128)(2,1)S(1)} %get-tuple-element.152), channel_id=1, source_target_pairs={{2,0},{3,1},{0,2},{1,3},{6,4},{7,5},{4,6},{5,7},{10,8},{11,9},{8,1... | collective-permute-start | bytes 1572872 | tf_op jit(solution)/shard_map/ppermute | solution.py:122
  169.3 13.5 %collective-permute-start.32 = (bf16[64,2048]{1,0:T(8,128)(2,1)S(1)}, bf16[64,2048]{1,0:T(8,128)(2,1)S(1)}, u32[]{:S(2)}, u32[]{:S(2)}) collective-permute-start(bf16[64,2048]{1,0:T(8,128)(2,1)S(1)} %slice.156), channel_id=1, source_target_pairs={{0,16},{16,0},{1,17},{17,1},{2,18},{18,2},{3,19},{19,3},{4,20},{20... | collective-permute-start | bytes 786440 | tf_op jit(solution)/shard_map/ppermute | solution.py:136
  170.0 12.7 %collective-permute-start.33 = (bf16[64,2048]{1,0:T(8,128)(2,1)S(1)}, bf16[64,2048]{1,0:T(8,128)(2,1)S(1)}, u32[]{:S(2)}, u32[]{:S(2)}) collective-permute-start(bf16[64,2048]{1,0:T(8,128)(2,1)S(1)} %slice.155), channel_id=1, source_target_pairs={{2,0},{3,1},{0,2},{1,3},{6,4},{7,5},{4,6},{5,7},{10,8},{11,9},{8,1... | collective-permute-start | bytes 786440 | tf_op jit(solution)/shard_map/ppermute | solution.py:122
  170.6 15.9 %collective-permute-start.30 = (bf16[64,2048]{1,0:T(8,128)(2,1)S(1)}, bf16[64,2048]{1,0:T(8,128)(2,1)S(1)}, u32[]{:S(2)}, u32[]{:S(2)}) collective-permute-start(bf16[64,2048]{1,0:T(8,128)(2,1)S(1)} %get-tuple-element.147), channel_id=1, source_target_pairs={{2,0},{3,1},{0,2},{1,3},{6,4},{7,5},{4,6},{5,7},{10,8},{11,9},{8,1... | collective-permute-start | bytes 786440 | tf_op jit(solution)/shard_map/ppermute | solution.py:122
  178.6 9.3 %collective-permute-start.39 = (bf16[32,2048]{1,0:T(8,128)(2,1)S(1)}, bf16[32,2048]{1,0:T(8,128)(2,1)S(1)}, u32[]{:S(2)}, u32[]{:S(2)}) collective-permute-start(bf16[32,2048]{1,0:T(8,128)(2,1)S(1)} %get-tuple-element.166), channel_id=1, source_target_pairs={{12,0},{13,1},{14,2},{15,3},{0,4},{1,5},{2,6},{3,7},{4,8},{5,9},{6... | collective-permute-start | bytes 393224 | tf_op jit(solution)/shard_map/ppermute | solution.py:112
  195.5 11.8 %collective-permute-start.43 = (bf16[32,2048]{1,0:T(8,128)(2,1)S(1)}, bf16[32,2048]{1,0:T(8,128)(2,1)S(1)}, u32[]{:S(2)}, u32[]{:S(2)}) collective-permute-start(bf16[32,2048]{1,0:T(8,128)(2,1)S(1)} %get-tuple-element.165), channel_id=1, source_target_pairs={{8,0},{9,1},{10,2},{11,3},{12,4},{13,5},{14,6},{15,7},{0,8},{1,9},... | collective-permute-start | bytes 393224 | tf_op jit(solution)/shard_map/ppermute | solution.py:112
  196.2 11.2 %collective-permute-start.44 = (bf16[32,2048]{1,0:T(8,128)(2,1)S(1)}, bf16[32,2048]{1,0:T(8,128)(2,1)S(1)}, u32[]{:S(2)}, u32[]{:S(2)}) collective-permute-start(bf16[32,2048]{1,0:T(8,128)(2,1)S(1)} %get-tuple-element.164), channel_id=1, source_target_pairs={{4,0},{5,1},{6,2},{7,3},{8,4},{9,5},{10,6},{11,7},{12,8},{13,9},{1... | collective-permute-start | bytes 393224 | tf_op jit(solution)/shard_map/ppermute | solution.py:112
  (28 other events, 264.7 us)

commit v8 on v7

--- a/solution.py
+++ b/solution.py
@@ -395,12 +395,6 @@
     shares = share[...].reshape(total_rows, 128).astype(jnp.float32)
     lane = lax.broadcasted_iota(jnp.int32, (total_rows, 128), 1)
     experts = lax.axis_size("expert")
-
-    def activate(t, g, u, scale):
-        h = g / (1.0 + jnp.exp(-g)) * u * scale
-        mid[:, pl.ds(t * tile, tile)] = h.astype(mid.dtype)
-
-    pending = None
     for t in range(2 * tiles):
         e, j = t // tiles, t % tiles
         if j == 0:
@@ -412,12 +406,10 @@
         values = rows[...].reshape(total_rows, feats)
         g = jnp.dot(values, gate[t % SLOTS], preferred_element_type=jnp.float32)
         u = jnp.dot(values, up[t % SLOTS], preferred_element_type=jnp.float32)
-        if pending is not None:
-            activate(*pending)
-        pending = (t, g, u, scale)
+        h = g / (1.0 + jnp.exp(-g)) * u * scale
+        mid[:, pl.ds(t * tile, tile)] = h.astype(mid.dtype)
         if t + SLOTS < 2 * tiles:
             weight_copies.append(fetch(t + SLOTS))
-    activate(*pending)
     for copy in down_copies:
         copy.wait()
     for n in range(feats // out_tile):
@@ -463,11 +455,6 @@
         ),
         name="experts",
     )(*pieces, *weights)
-
-
-def diagonal(line_x, line_y, depth):
-    half = depth // 2
-    return flip_y(line_x[:half], depth), flip_x(line_y[half:])
 
 
 def send_line(full, depth):
@@ -503,7 +490,7 @@
     barrier = lax.optimization_barrier
 
     shifted = [shift_z(w_out, depth, s) for s in range(1, depth)]
-    across = [flip_y(w_out, depth), flip_y(shifted[0], depth)]
+    across = [flip_y(piece, depth) for piece in [w_out] + shifted[:-1]]
 
     feats_here = w_gate.shape[1]
     early = feats_here * 3 // 4
@@ -513,7 +500,7 @@
     queries, gate_sent[1], gate_own = barrier((queries, gate_sent[1], gate_own))
     context = attend_here(queries, kv_pool, page_table, ctx_lens)
     context, w_up, w_down = barrier((context, w_up, w_down))
-    early = feats_here * 7 // 32
+    early = feats_here // 32
     up_own, *up_sent = cut(w_up, width, (early, feats_here - early))
     mixed_sent = jnp.concatenate([gate_sent[1], up_sent[0]], axis=0)
     shifted, across, gate_far, mixed_sent, up_sent[1], gate_own, up_own, w_down, context = (
@@ -531,7 +518,7 @@
             )
         )
     )
-    across += [flip_y(piece, depth) for piece in shifted[1:]]
+    across.append(flip_y(shifted[-1], depth))
     mixed_far = flip_x(mixed_sent)
     other = flip_core(context, depth)
     down_own = w_down[0]
@@ -561,14 +548,11 @@
     for k in range(2):
         line = jnp.stack([piece[rows * k : rows * (k + 1)] for piece in arrived])
         if k > 0:
-            line, ready[0][3], ready[0][4] = barrier((line, ready[0][3], ready[0][4]))
-        line_x = flip_x(line)
-        line_y = flip_y(line, depth)
+            line, ready[0] = barrier((line, ready[0]))
+        pieces = [line, flip_x(line), flip_y(line, depth), flip_xy(line, depth)]
         if k == 0:
-            line_x, line_y, up_far = barrier((line_x, line_y, up_far))
-            ready.append([line, line_x, line_y, *diagonal(line_x, line_y, depth)])
-        else:
-            ready.append([line, line_x, line_y])
+            pieces, up_far = barrier((pieces, up_far))
+        ready.append(pieces)
 
     weights = [gate_own, gate_far, mixed_far, up_own, up_far, down_own]
     weights += [
@@ -580,21 +564,16 @@
         here_core[2],
     ]
 
-    kinds = (jnp.float32, jnp.bfloat16, jnp.bfloat16, jnp.bfloat16, jnp.bfloat16)
+    kinds = (jnp.float32, jnp.bfloat16, jnp.bfloat16, jnp.bfloat16)
     outs = run_experts(ready[0], kinds, 0, rows, weights, split)
-    ready[1][1], ready[1][2], outs = barrier((ready[1][1], ready[1][2], outs))
-    ready[1] += diagonal(ready[1][1], ready[1][2], depth)
     ready[1], outs = barrier((ready[1], outs))
-    out_l, out_x, out_y, out_low, out_high = outs
-    far = jnp.concatenate([out_low, out_high], axis=0)
-    backs = [flip_x(out_x), flip_y(out_y, depth), flip_xy(far, depth)]
-
-    kinds = (jnp.float32, jnp.float32, jnp.float32, jnp.bfloat16, jnp.bfloat16)
-    last_l, last_x, last_y, last_low, last_high = run_experts(
-        ready[1], kinds, 0, rows, weights, split
-    )
+    out_l, out_x, out_y, out_far = outs
+    backs = [flip_x(out_x), flip_y(out_y, depth), flip_xy(out_far, depth)]
+
+    kinds = (jnp.float32, jnp.float32, jnp.float32, jnp.bfloat16)
+    last_l, last_x, last_y, last_far = run_experts(ready[1], kinds, 0, rows, weights, split)
     half = last_x.shape[0] // 2
-    back_low, back_high = flip_y(last_low, depth), flip_x(last_high)
+    back_low, back_high = flip_y(last_far[:half], depth), flip_x(last_far[half:])
     plain_x = flip_x(last_x[half:].astype(jnp.bfloat16))
     plain_y = flip_y(last_y[:half].astype(jnp.bfloat16), depth)
     full = out_l

time: 209 us -> 220 us (1.053)
  waiting for transfers between devices: 106 us -> 133 us
  starting transfers between devices: 52.2 us -> 36.4 us
    ppermute x1 -> x3, waiting for transfers between devices: 0.01 us -> 13.9 us  [flip_xy(): return lax.ppermute(values, ('dp', 'expert'), pairs)]
    ppermute x12, waiting for transfers between devices: 40.4 us -> 49 us  [shift_z(): return lax.ppermute(values, 'expert', pairs)]
    ppermute x12, starting transfers between devices: 19.2 us -> 10.6 us  [shift_z(): return lax.ppermute(values, 'expert', pairs)]
    ppermute x12 -> x10, starting transfers between devices: 16 us -> 10 us  [flip_y(): return lax.ppermute(values, 'expert', pairs)]
    ppermute x8, waiting for transfers between devices: 0.02 us -> 4.73 us  [flip_core(): return lax.ppermute(values, 'expert', pairs)]
    ppermute x12 -> x10, starting transfers between devices: 15.2 us -> 11.1 us  [flip_x(): return lax.ppermute(values, 'dp', [(0, 1), (1, 0)])]
    ppermute x1 -> x3, starting transfers between devices: 0.65 us -> 3.34 us  [flip_xy(): return lax.ppermute(values, ('dp', 'expert'), pairs)]
    ppermute x12 -> x10, waiting for transfers between devices: 31.7 us -> 31.1 us  [flip_y(): return lax.ppermute(values, 'expert', pairs)]
  transfers between devices with their start and end apart: 45 -> 43, of which waited for: 23 -> 23; matrix products, arithmetic and copies ran while one was open for 1% -> 1% of each run, Pallas kernels for 17% -> 16%
where the time goes in v8:
time: 220 us; the launch traced here: 219 us
  waiting for transfers between devices  133 us (60%)
  Pallas kernels  38.9 us (18%)
  starting transfers between devices  36.4 us (17%)
  local copies, waits for them, and re-layouts  8.64 us (4%)
    ppermute x12, waiting for transfers between devices, shift_z(): return lax.ppermute(values, 'expert', pairs)  49 us
    ppermute x10, waiting for transfers between devices, flip_x(): return lax.ppermute(values, 'dp', [(0, 1), (1, 0)])  34 us
    ppermute x10, waiting for transfers between devices, flip_y(): return lax.ppermute(values, 'expert', pairs)  31.1 us
    pallas_call x2, Pallas kernels, run_experts(): pl.pallas_call(functools.partial(experts_kernel, tile, 512, first_row, co...  27.1 us
    ppermute x3, waiting for transfers between devices, flip_xy(): return lax.ppermute(values, ('dp', 'expert'), pairs)  13.9 us
    ppermute x10, starting transfers between devices, flip_x(): return lax.ppermute(values, 'dp', [(0, 1), (1, 0)])  11.1 us
    ppermute x12, starting transfers between devices, shift_z(): return lax.ppermute(values, 'expert', pairs)  10.6 us
    ppermute x10, starting transfers between devices, flip_y(): return lax.ppermute(values, 'expert', pairs)  10 us
  transfers between devices with their start and end apart: 43, of which 23 were waited for; matrix products, arithmetic and copies ran while one was open for 1% of the time, Pallas kernels for 16%

profile of v8, /device:TPU:0, one launch (start us, length us, event | category | flops | bytes accessed | tf_op | source)
XLA Modules:
  0.0 219.2 jit_solution(6533575691590878163)
XLA Ops:
  0.0 1.8 copy-done
  1.8 1.7 cut.2
  3.6 3.0 %collective-permute-start.6 = (bf16[768,768]{1,0:T(8,128)(2,1)}, bf16[768,768]{1,0:T(8,128)(2,1)}, u32[]{:S(2)}, u32[]{:S(2)}) collective-permute-start(bf16[768,768]{1,0:T(8,128)(2,1)} %get-tuple-element.77), channel_id=1, source_target_pairs={{0,16},{16,0},{1,17},{17,1},{2,18},{18,2},{3,19},{19,3},{4,20},{20... | collective-permute-start | bytes 3538952 | tf_op jit(solution)/shard_map/ppermute | solution.py:136
  6.6 3.6 %collective-permute-start = (bf16[1024,128]{1,0:T(8,128)(2,1)}, bf16[1024,128]{1,0:T(8,128)(2,1)}, u32[]{:S(2)}, u32[]{:S(2)}) collective-permute-start(bf16[1024,128]{1,0:T(8,128)(2,1)} %refs_0_.1), channel_id=1, source_target_pairs={{4,0},{5,1},{6,2},{7,3},{8,4},{9,5},{10,6},{11,7},{12,8},{13,9},{1... | collective-permute-start | bytes 786440 | tf_op jit(solution)/shard_map/ppermute | solution.py:112
  11.2 1.5 collective-permute-start.3
  12.7 4.6 %collective-permute-done.refs_1_ = bf16[1024,128]{1,0:T(8,128)(2,1)} collective-permute-done((bf16[1024,128]{1,0:T(8,128)(2,1)}, bf16[1024,128]{1,0:T(8,128)(2,1)}, u32[]{:S(2)}, u32[]{:S(2)}) %collective-permute-start) | collective-permute-done | bytes 262176 | tf_op jit(solution)/shard_map/ppermute | solution.py:112
  17.3 1.5 collective-permute-start.4
  18.8 13.7 %collective-permute-done.1.refs_2_ = bf16[1024,128]{1,0:T(8,128)(2,1)} collective-permute-done((bf16[1024,128]{1,0:T(8,128)(2,1)}, bf16[1024,128]{1,0:T(8,128)(2,1)}, u32[]{:S(2)}, u32[]{:S(2)}) %collective-permute-start.1) | collective-permute-done | bytes 262176 | tf_op jit(solution)/shard_map/ppermute | solution.py:112
  32.5 1.5 collective-permute-start.5
  34.8 1.6 copy-done.2
  38.2 5.8 %attend.1.ctx_ref = bf16[128,1024]{1,0:T(8,128)(2,1)S(1)} custom-call(s32[2,4]{1,0:T(2,128)S(1)} %copy-done.8, s32[128,1]{1,0:T(8,128)S(1)} %copy-done.6, bf16[128,1024]{1,0:T(8,128)(2,1)S(1)} %copy-done.3, bf16[2,8,64,1024]{3,2,1,0:T(8,128)(2,1)S(1)} %copy-done.2), custom_call_target="tpu_custom_call" | custom-call | flops 134217728 | bytes 2621440 | tf_op jit(solution)/shard_map/attend/pallas_call | solution.py:182
  48.7 7.6 %collective-permute-done.8.refs_7_ = bf16[1024,128]{1,0:T(8,128)(2,1)S(1)} collective-permute-done((bf16[1024,128]{1,0:T(8,128)(2,1)}, bf16[1024,128]{1,0:T(8,128)(2,1)S(1)}, u32[]{:S(2)}, u32[]{:S(2)}) %collective-permute-start.8) | collective-permute-done | bytes 262176 | tf_op jit(solution)/shard_map/ppermute | solution.py:122
  56.5 4.0 %collective-permute-done.12.refs_6_ = bf16[288,768]{1,0:T(8,128)(2,1)S(1)} collective-permute-done((bf16[288,768]{1,0:T(8,128)(2,1)S(1)}, bf16[288,768]{1,0:T(8,128)(2,1)S(1)}, u32[]{:S(2)}, u32[]{:S(2)}) %collective-permute-start.12) | collective-permute-done | bytes 442400 | tf_op jit(solution)/shard_map/ppermute | solution.py:136
  61.4 2.6 %project.1 = (f32[128,1024]{1,0:T(8,128)S(1)}, bf16[128,1024]{1,0:T(8,128)(2,1)S(1)}) custom-call(bf16[128,1024]{1,0:T(8,128)(2,1)S(1)} %attend.1.ctx_ref, bf16[128,1024]{1,0:T(8,128)(2,1)S(1)} %collective-permute-done.7.other_ref, bf16[1024,128]{1,0:T(8,128)(2,1)S(1)} %copy-done.4, bf16[1024,128]{1,0:T(8,128)(2,1)} %collective-permute-done.refs_1_, ...), custom_call_target="tpu_custom_call" | custom-call | flops 536870912 | bytes 2883584 | tf_op jit(solution)/shard_map/project/pallas_call | solution.py:224
  64.6 7.0 %collective-permute-done.13 = bf16[128,1024]{1,0:T(8,128)(2,1)S(1)} collective-permute-done((bf16[128,1024]{1,0:T(8,128)(2,1)S(1)}, bf16[128,1024]{1,0:T(8,128)(2,1)S(1)}, u32[]{:S(2)}, u32[]{:S(2)}) %collective-permute-start.13) | collective-permute-done | bytes 262176 | tf_op jit(solution)/shard_map/ppermute | solution.py:136
  73.8 1.9 collective-permute-start.17
  75.7 7.9 %collective-permute-done.15 = bf16[64,2176]{1,0:T(8,128)(2,1)S(1)} collective-permute-done((bf16[64,2176]{1,0:T(8,128)(2,1)S(1)}, bf16[64,2176]{1,0:T(8,128)(2,1)S(1)}, u32[]{:S(2)}, u32[]{:S(2)}) %collective-permute-start.15) | collective-permute-done | bytes 278560 | tf_op jit(solution)/shard_map/ppermute | solution.py:112
  83.7 14.4 %collective-permute-done.16 = bf16[64,2176]{1,0:T(8,128)(2,1)S(1)} collective-permute-done((bf16[64,2176]{1,0:T(8,128)(2,1)S(1)}, bf16[64,2176]{1,0:T(8,128)(2,1)S(1)}, u32[]{:S(2)}, u32[]{:S(2)}) %collective-permute-start.16) | collective-permute-done | bytes 278560 | tf_op jit(solution)/shard_map/ppermute | solution.py:112
  98.9 1.5 collective-permute-start.19
  101.8 18.2 %collective-permute-done.18.refs_1_ = bf16[4,32,2176]{2,1,0:T(8,128)(2,1)S(1)} collective-permute-done((bf16[4,32,2176]{2,1,0:T(8,128)(2,1)S(1)}, bf16[4,32,2176]{2,1,0:T(8,128)(2,1)S(1)}, u32[]{:S(2)}, u32[]{:S(2)}) %collective-permute-start.18) | collective-permute-done | bytes 557088 | tf_op jit(solution)/shard_map/ppermute | solution.py:136
  120.0 12.4 %collective-permute-done.20.refs_3_ = bf16[4,32,2176]{2,1,0:T(8,128)(2,1)S(1)} collective-permute-done((bf16[4,32,2176]{2,1,0:T(8,128)(2,1)S(1)}, bf16[4,32,2176]{2,1,0:T(8,128)(2,1)S(1)}, u32[]{:S(2)}, u32[]{:S(2)}) %collective-permute-start.20) | collective-permute-done | bytes 557088 | tf_op jit(solution)/shard_map/ppermute | solution.py:147
  134.1 3.8 %collective-permute-done.25.refs_11_ = bf16[768,768]{1,0:T(8,128)(2,1)S(1)} collective-permute-done((bf16[768,768]{1,0:T(8,128)(2,1)}, bf16[768,768]{1,0:T(8,128)(2,1)S(1)}, u32[]{:S(2)}, u32[]{:S(2)}) %collective-permute-start.25) | collective-permute-done | bytes 1179680 | tf_op jit(solution)/shard_map/ppermute | solution.py:132
  138.4 13.4 %experts.2 = (f32[128,2048]{1,0:T(8,128)S(1)}, bf16[128,2048]{1,0:T(8,128)(2,1)S(1)}, bf16[128,2048]{1,0:T(8,128)(2,1)S(1)}, bf16[128,2048]{1,0:T(8,128)(2,1)S(1)}) custom-call(bf16[4,32,2176]{2,1,0:T(8,128)(2,1)S(1)} %pad_maximum_fusion.1.refs_0_, bf16[4,32,2176]{2,1,0:T(8,128)(2,1)S(1)} %collective-permute-done.18.refs_1_, ...), custom_call_target="tpu_custom_call" | custom-call | flops 9663676416 | bytes 31457280 | tf_op jit(solution)/shard_map/experts/pallas_call | solution.py:431
  151.9 8.5 %collective-permute-done.23.refs_2_ = bf16[4,32,2176]{2,1,0:T(8,128)(2,1)S(1)} collective-permute-done((bf16[4,32,2176]{2,1,0:T(8,128)(2,1)S(1)}, bf16[4,32,2176]{2,1,0:T(8,128)(2,1)S(1)}, u32[]{:S(2)}, u32[]{:S(2)}) %collective-permute-start.23) | collective-permute-done | bytes 557088 | tf_op jit(solution)/shard_map/ppermute | solution.py:122
  163.8 13.6 %experts.3 = (f32[128,2048]{1,0:T(8,128)S(1)}, f32[128,2048]{1,0:T(8,128)S(1)}, f32[128,2048]{1,0:T(8,128)S(1)}, bf16[128,2048]{1,0:T(8,128)(2,1)S(1)}) custom-call(bf16[4,32,2176]{2,1,0:T(8,128)(2,1)S(1)} %pad_maximum_fusion.refs_0_, bf16[4,32,2176]{2,1,0:T(8,128)(2,1)S(1)} %collective-permute-done.22.refs_1_, ...), custom_call_target="tpu_custom_call" | custom-call | flops 9663676416 | bytes 31457280 | tf_op jit(solution)/shard_map/experts/pallas_call | solution.py:431
  181.0 4.2 %collective-permute-done.33 = bf16[128,2048]{1,0:T(8,128)(2,1)S(1)} collective-permute-done((bf16[128,2048]{1,0:T(8,128)(2,1)S(1)}, bf16[128,2048]{1,0:T(8,128)(2,1)S(1)}, u32[]{:S(2)}, u32[]{:S(2)}) %collective-permute-start.33) | collective-permute-done | bytes 524320 | tf_op jit(solution)/shard_map/ppermute | solution.py:122
  187.5 4.2 %collective-permute-done.28 = bf16[64,2048]{1,0:T(8,128)(2,1)S(1)} collective-permute-done((bf16[64,2048]{1,0:T(8,128)(2,1)S(1)}, bf16[64,2048]{1,0:T(8,128)(2,1)S(1)}, u32[]{:S(2)}, u32[]{:S(2)}) %collective-permute-start.28) | collective-permute-done | bytes 262176 | tf_op jit(solution)/shard_map/ppermute | solution.py:122
  192.1 4.0 %collective-permute-done.30 = bf16[64,2048]{1,0:T(8,128)(2,1)S(1)} collective-permute-done((bf16[64,2048]{1,0:T(8,128)(2,1)S(1)}, bf16[64,2048]{1,0:T(8,128)(2,1)S(1)}, u32[]{:S(2)}, u32[]{:S(2)}) %collective-permute-start.30) | collective-permute-done | bytes 262176 | tf_op jit(solution)/shard_map/ppermute | solution.py:136
  200.0 5.6 %collective-permute-done.36 = bf16[64,2048]{1,0:T(8,128)(2,1)S(1)} collective-permute-done((bf16[64,2048]{1,0:T(8,128)(2,1)S(1)}, bf16[64,2048]{1,0:T(8,128)(2,1)S(1)}, u32[]{:S(2)}, u32[]{:S(2)}) %collective-permute-start.36) | collective-permute-done | bytes 262176 | tf_op jit(solution)/shard_map/ppermute | solution.py:122
  206.4 3.7 %collective-permute-start.42 = (bf16[32,2048]{1,0:T(8,128)(2,1)S(1)}, bf16[32,2048]{1,0:T(8,128)(2,1)S(1)}, u32[]{:S(2)}, u32[]{:S(2)}) collective-permute-start(bf16[32,2048]{1,0:T(8,128)(2,1)S(1)} %get-tuple-element.152), channel_id=1, source_target_pairs={{4,0},{5,1},{6,2},{7,3},{8,4},{9,5},{10,6},{11,7},{12,8},{13,9},{1... | collective-permute-start | bytes 393224 | tf_op jit(solution)/shard_map/ppermute | solution.py:112
  210.2 4.5 %collective-permute-done.40 = bf16[32,2048]{1,0:T(8,128)(2,1)S(1)} collective-permute-done((bf16[32,2048]{1,0:T(8,128)(2,1)S(1)}, bf16[32,2048]{1,0:T(8,128)(2,1)S(1)}, u32[]{:S(2)}, u32[]{:S(2)}) %collective-permute-start.40) | collective-permute-done | bytes 131104 | tf_op jit(solution)/shard_map/ppermute | solution.py:112
  214.6 3.5 %collective-permute-done.41 = bf16[32,2048]{1,0:T(8,128)(2,1)S(1)} collective-permute-done((bf16[32,2048]{1,0:T(8,128)(2,1)S(1)}, bf16[32,2048]{1,0:T(8,128)(2,1)S(1)}, u32[]{:S(2)}, u32[]{:S(2)}) %collective-permute-start.41) | collective-permute-done | bytes 131104 | tf_op jit(solution)/shard_map/ppermute | solution.py:112
  (124 shorter events, 31.8 us)
Async XLA Ops:
  3.6 43.2 %collective-permute-start.6 = (bf16[768,768]{1,0:T(8,128)(2,1)}, bf16[768,768]{1,0:T(8,128)(2,1)}, u32[]{:S(2)}, u32[]{:S(2)}) collective-permute-start(bf16[768,768]{1,0:T(8,128)(2,1)} %get-tuple-element.77), channel_id=1, source_target_pairs={{0,16},{16,0},{1,17},{17,1},{2,18},{18,2},{3,19},{19,3},{4,20},{20... | collective-permute-start | bytes 3538952 | tf_op jit(solution)/shard_map/ppermute | solution.py:136
  6.6 10.7 %collective-permute-start = (bf16[1024,128]{1,0:T(8,128)(2,1)}, bf16[1024,128]{1,0:T(8,128)(2,1)}, u32[]{:S(2)}, u32[]{:S(2)}) collective-permute-start(bf16[1024,128]{1,0:T(8,128)(2,1)} %refs_0_.1), channel_id=1, source_target_pairs={{4,0},{5,1},{6,2},{7,3},{8,4},{9,5},{10,6},{11,7},{12,8},{13,9},{1... | collective-permute-start | bytes 786440 | tf_op jit(solution)/shard_map/ppermute | solution.py:112
  10.2 22.3 %collective-permute-start.1 = (bf16[1024,128]{1,0:T(8,128)(2,1)}, bf16[1024,128]{1,0:T(8,128)(2,1)}, u32[]{:S(2)}, u32[]{:S(2)}) collective-permute-start(bf16[1024,128]{1,0:T(8,128)(2,1)} %refs_0_.1), channel_id=1, source_target_pairs={{8,0},{9,1},{10,2},{11,3},{12,4},{13,5},{14,6},{15,7},{0,8},{1,9},... | collective-permute-start | bytes 786440 | tf_op jit(solution)/shard_map/ppermute | solution.py:112
  10.2 36.5 %collective-permute-start.2 = (bf16[1024,128]{1,0:T(8,128)(2,1)}, bf16[1024,128]{1,0:T(8,128)(2,1)}, u32[]{:S(2)}, u32[]{:S(2)}) collective-permute-start(bf16[1024,128]{1,0:T(8,128)(2,1)} %refs_0_.1), channel_id=1, source_target_pairs={{12,0},{13,1},{14,2},{15,3},{0,4},{1,5},{2,6},{3,7},{4,8},{5,9},{6... | collective-permute-start | bytes 786440 | tf_op jit(solution)/shard_map/ppermute | solution.py:112
  11.2 35.5 %collective-permute-start.3 = (bf16[1024,128]{1,0:T(8,128)(2,1)}, bf16[1024,128]{1,0:T(8,128)(2,1)}, u32[]{:S(2)}, u32[]{:S(2)}) collective-permute-start(bf16[1024,128]{1,0:T(8,128)(2,1)} %refs_0_.1), channel_id=1, source_target_pairs={{2,0},{3,1},{0,2},{1,3},{6,4},{7,5},{4,6},{5,7},{10,8},{11,9},{8,1... | collective-permute-start | bytes 786440 | tf_op jit(solution)/shard_map/ppermute | solution.py:122
  17.3 29.4 %collective-permute-start.4 = (bf16[1024,128]{1,0:T(8,128)(2,1)}, bf16[1024,128]{1,0:T(8,128)(2,1)}, u32[]{:S(2)}, u32[]{:S(2)}) collective-permute-start(bf16[1024,128]{1,0:T(8,128)(2,1)} %collective-permute-done.refs_1_), channel_id=1, source_target_pairs={{2,0},{3,1},{0,2},{1,3},{6,4},{7,5},{4,6},{5,7},{10,8},{11,9},{8,1... | collective-permute-start | bytes 786440 | tf_op jit(solution)/shard_map/ppermute | solution.py:122
  32.5 14.2 %collective-permute-start.5 = (bf16[1024,128]{1,0:T(8,128)(2,1)}, bf16[1024,128]{1,0:T(8,128)(2,1)}, u32[]{:S(2)}, u32[]{:S(2)}) collective-permute-start(bf16[1024,128]{1,0:T(8,128)(2,1)} %collective-permute-done.1.refs_2_), channel_id=1, source_target_pairs={{2,0},{3,1},{0,2},{1,3},{6,4},{7,5},{4,6},{5,7},{10,8},{11,9},{8,1... | collective-permute-start | bytes 786440 | tf_op jit(solution)/shard_map/ppermute | solution.py:122
  46.8 13.7 %collective-permute-start.11 = (bf16[704,2048]{1,0:T(8,128)(2,1)}, bf16[704,2048]{1,0:T(8,128)(2,1)}, u32[]{:S(2)}, u32[]{:S(2)}) collective-permute-start(bf16[704,2048]{1,0:T(8,128)(2,1)} %bitcast.1.refs_9_), channel_id=1, source_target_pairs={{1,0},{0,1},{3,2},{2,3},{5,4},{4,5},{7,6},{6,7},{9,8},{8,9},{11,10... | collective-permute-start | bytes 8650760 | tf_op jit(solution)/shard_map/ppermute | solution.py:132
  46.8 13.6 %collective-permute-start.10 = (bf16[1024,768]{1,0:T(8,128)(2,1)}, bf16[1024,768]{1,0:T(8,128)(2,1)S(1)}, u32[]{:S(2)}, u32[]{:S(2)}) collective-permute-start(bf16[1024,768]{1,0:T(8,128)(2,1)} %get-tuple-element.97.refs_7_), channel_id=1, source_target_pairs={{1,0},{0,1},{3,2},{2,3},{5,4},{4,5},{7,6},{6,7},{9,8},{8,9},{11,10... | collective-permute-start | bytes 4718600 | tf_op jit(solution)/shard_map/ppermute | solution.py:132
  47.3 13.1 %collective-permute-start.9 = (bf16[1024,768]{1,0:T(8,128)(2,1)}, bf16[1024,768]{1,0:T(8,128)(2,1)}, u32[]{:S(2)}, u32[]{:S(2)}) collective-permute-start(bf16[1024,768]{1,0:T(8,128)(2,1)} %get-tuple-element.96.refs_4_), channel_id=1, source_target_pairs={{1,0},{0,1},{3,2},{2,3},{5,4},{4,5},{7,6},{6,7},{9,8},{8,9},{11,10... | collective-permute-start | bytes 4718600 | tf_op jit(solution)/shard_map/ppermute | solution.py:132
  47.4 8.9 %collective-permute-start.8 = (bf16[1024,128]{1,0:T(8,128)(2,1)}, bf16[1024,128]{1,0:T(8,128)(2,1)S(1)}, u32[]{:S(2)}, u32[]{:S(2)}) collective-permute-start(bf16[1024,128]{1,0:T(8,128)(2,1)} %collective-permute-done.2.refs_3_), channel_id=1, source_target_pairs={{2,0},{3,1},{0,2},{1,3},{6,4},{7,5},{4,6},{5,7},{10,8},{11,9},{8,1... | collective-permute-start | bytes 786440 | tf_op jit(solution)/shard_map/ppermute | solution.py:122
  48.1 12.3 %collective-permute-start.12 = (bf16[288,768]{1,0:T(8,128)(2,1)S(1)}, bf16[288,768]{1,0:T(8,128)(2,1)S(1)}, u32[]{:S(2)}, u32[]{:S(2)}) collective-permute-start(bf16[288,768]{1,0:T(8,128)(2,1)S(1)} %pad_maximum_fusion.2), channel_id=1, source_target_pairs={{0,16},{16,0},{1,17},{17,1},{2,18},{18,2},{3,19},{19,3},{4,20},{20... | collective-permute-start | bytes 1327112 | tf_op jit(solution)/shard_map/ppermute | solution.py:136
  71.8 60.6 %collective-permute-start.21 = (bf16[992,768]{1,0:T(8,128)(2,1)S(1)}, bf16[992,768]{1,0:T(8,128)(2,1)S(1)}, u32[]{:S(2)}, u32[]{:S(2)}) collective-permute-start(bf16[992,768]{1,0:T(8,128)(2,1)S(1)} %copy-done.10), channel_id=1, source_target_pairs={{0,16},{16,0},{1,17},{17,1},{2,18},{18,2},{3,19},{19,3},{4,20},{20... | collective-permute-start | bytes 4571144 | tf_op jit(solution)/shard_map/ppermute | solution.py:136
  73.6 10.0 %collective-permute-start.15 = (bf16[64,2176]{1,0:T(8,128)(2,1)S(1)}, bf16[64,2176]{1,0:T(8,128)(2,1)S(1)}, u32[]{:S(2)}, u32[]{:S(2)}) collective-permute-start(bf16[64,2176]{1,0:T(8,128)(2,1)S(1)} %get-tuple-element.110), channel_id=1, source_target_pairs={{4,0},{5,1},{6,2},{7,3},{8,4},{9,5},{10,6},{11,7},{12,8},{13,9},{1... | collective-permute-start | bytes 835592 | tf_op jit(solution)/shard_map/ppermute | solution.py:112
  73.7 24.4 %collective-permute-start.16 = (bf16[64,2176]{1,0:T(8,128)(2,1)S(1)}, bf16[64,2176]{1,0:T(8,128)(2,1)S(1)}, u32[]{:S(2)}, u32[]{:S(2)}) collective-permute-start(bf16[64,2176]{1,0:T(8,128)(2,1)S(1)} %get-tuple-element.110), channel_id=1, source_target_pairs={{8,0},{9,1},{10,2},{11,3},{12,4},{13,5},{14,6},{15,7},{0,8},{1,9},... | collective-permute-start | bytes 835592 | tf_op jit(solution)/shard_map/ppermute | solution.py:112
  73.8 24.3 %collective-permute-start.17 = (bf16[64,2176]{1,0:T(8,128)(2,1)S(1)}, bf16[64,2176]{1,0:T(8,128)(2,1)S(1)}, u32[]{:S(2)}, u32[]{:S(2)}) collective-permute-start(bf16[64,2176]{1,0:T(8,128)(2,1)S(1)} %get-tuple-element.110), channel_id=1, source_target_pairs={{12,0},{13,1},{14,2},{15,3},{0,4},{1,5},{2,6},{3,7},{4,8},{5,9},{6... | collective-permute-start | bytes 835592 | tf_op jit(solution)/shard_map/ppermute | solution.py:112
  98.3 21.7 %collective-permute-start.18 = (bf16[4,32,2176]{2,1,0:T(8,128)(2,1)S(1)}, bf16[4,32,2176]{2,1,0:T(8,128)(2,1)S(1)}, u32[]{:S(2)}, u32[]{:S(2)}) collective-permute-start(bf16[4,32,2176]{2,1,0:T(8,128)(2,1)S(1)} %pad_maximum_fusion.1.refs_0_), channel_id=1, source_target_pairs={{0,16},{16,0},{1,17},{17,1},{2,18},{18,2},{3,19},{19,3},{4,20},{20... | collective-permute-start | bytes 1671176 | tf_op jit(solution)/shard_map/ppermute | solution.py:136
  98.9 21.1 %collective-permute-start.19 = (bf16[4,32,2176]{2,1,0:T(8,128)(2,1)S(1)}, bf16[4,32,2176]{2,1,0:T(8,128)(2,1)S(1)}, u32[]{:S(2)}, u32[]{:S(2)}) collective-permute-start(bf16[4,32,2176]{2,1,0:T(8,128)(2,1)S(1)} %pad_maximum_fusion.1.refs_0_), channel_id=1, source_target_pairs={{2,0},{3,1},{0,2},{1,3},{6,4},{7,5},{4,6},{5,7},{10,8},{11,9},{8,1... | collective-permute-start | bytes 1671176 | tf_op jit(solution)/shard_map/ppermute | solution.py:122
  100.5 32.0 %collective-permute-start.20 = (bf16[4,32,2176]{2,1,0:T(8,128)(2,1)S(1)}, bf16[4,32,2176]{2,1,0:T(8,128)(2,1)S(1)}, u32[]{:S(2)}, u32[]{:S(2)}) collective-permute-start(bf16[4,32,2176]{2,1,0:T(8,128)(2,1)S(1)} %pad_maximum_fusion.1.refs_0_), channel_id=1, source_target_pairs={{18,0},{19,1},{16,2},{17,3},{22,4},{23,5},{20,6},{21,7},{26,8},{27... | collective-permute-start | bytes 1671176 | tf_op jit(solution)/shard_map/ppermute | solution.py:147
  133.0 18.8 %collective-permute-start.22 = (bf16[4,32,2176]{2,1,0:T(8,128)(2,1)S(1)}, bf16[4,32,2176]{2,1,0:T(8,128)(2,1)S(1)}, u32[]{:S(2)}, u32[]{:S(2)}) collective-permute-start(bf16[4,32,2176]{2,1,0:T(8,128)(2,1)S(1)} %pad_maximum_fusion.refs_0_), channel_id=1, source_target_pairs={{0,16},{16,0},{1,17},{17,1},{2,18},{18,2},{3,19},{19,3},{4,20},{20... | collective-permute-start | bytes 1671176 | tf_op jit(solution)/shard_map/ppermute | solution.py:136
  133.6 26.7 %collective-permute-start.23 = (bf16[4,32,2176]{2,1,0:T(8,128)(2,1)S(1)}, bf16[4,32,2176]{2,1,0:T(8,128)(2,1)S(1)}, u32[]{:S(2)}, u32[]{:S(2)}) collective-permute-start(bf16[4,32,2176]{2,1,0:T(8,128)(2,1)S(1)} %pad_maximum_fusion.refs_0_), channel_id=1, source_target_pairs={{2,0},{3,1},{0,2},{1,3},{6,4},{7,5},{4,6},{5,7},{10,8},{11,9},{8,1... | collective-permute-start | bytes 1671176 | tf_op jit(solution)/shard_map/ppermute | solution.py:122
  137.9 22.4 %collective-permute-start.24 = (bf16[4,32,2176]{2,1,0:T(8,128)(2,1)S(1)}, bf16[4,32,2176]{2,1,0:T(8,128)(2,1)S(1)}, u32[]{:S(2)}, u32[]{:S(2)}) collective-permute-start(bf16[4,32,2176]{2,1,0:T(8,128)(2,1)S(1)} %pad_maximum_fusion.refs_0_), channel_id=1, source_target_pairs={{18,0},{19,1},{16,2},{17,3},{22,4},{23,5},{20,6},{21,7},{26,8},{27... | collective-permute-start | bytes 1671176 | tf_op jit(solution)/shard_map/ppermute | solution.py:147
  160.3 19.3 %collective-permute-start.32 = (bf16[128,2048]{1,0:T(8,128)(2,1)S(1)}, bf16[128,2048]{1,0:T(8,128)(2,1)S(1)}, u32[]{:S(2)}, u32[]{:S(2)}) collective-permute-start(bf16[128,2048]{1,0:T(8,128)(2,1)S(1)} %get-tuple-element.140), channel_id=1, source_target_pairs={{0,16},{16,0},{1,17},{17,1},{2,18},{18,2},{3,19},{19,3},{4,20},{20... | collective-permute-start | bytes 1572872 | tf_op jit(solution)/shard_map/ppermute | solution.py:136
  161.8 23.3 %collective-permute-start.33 = (bf16[128,2048]{1,0:T(8,128)(2,1)S(1)}, bf16[128,2048]{1,0:T(8,128)(2,1)S(1)}, u32[]{:S(2)}, u32[]{:S(2)}) collective-permute-start(bf16[128,2048]{1,0:T(8,128)(2,1)S(1)} %get-tuple-element.141), channel_id=1, source_target_pairs={{2,0},{3,1},{0,2},{1,3},{6,4},{7,5},{4,6},{5,7},{10,8},{11,9},{8,1... | collective-permute-start | bytes 1572872 | tf_op jit(solution)/shard_map/ppermute | solution.py:122
  162.3 24.7 %collective-permute-start.34 = (bf16[128,2048]{1,0:T(8,128)(2,1)S(1)}, bf16[128,2048]{1,0:T(8,128)(2,1)S(1)}, u32[]{:S(2)}, u32[]{:S(2)}) collective-permute-start(bf16[128,2048]{1,0:T(8,128)(2,1)S(1)} %get-tuple-element.142), channel_id=1, source_target_pairs={{18,0},{19,1},{16,2},{17,3},{22,4},{23,5},{20,6},{21,7},{26,8},{27... | collective-permute-start | bytes 1572872 | tf_op jit(solution)/shard_map/ppermute | solution.py:147
  177.5 14.2 %collective-permute-start.28 = (bf16[64,2048]{1,0:T(8,128)(2,1)S(1)}, bf16[64,2048]{1,0:T(8,128)(2,1)S(1)}, u32[]{:S(2)}, u32[]{:S(2)}) collective-permute-start(bf16[64,2048]{1,0:T(8,128)(2,1)S(1)} %get-tuple-element.158), channel_id=1, source_target_pairs={{2,0},{3,1},{0,2},{1,3},{6,4},{7,5},{4,6},{5,7},{10,8},{11,9},{8,1... | collective-permute-start | bytes 786440 | tf_op jit(solution)/shard_map/ppermute | solution.py:122
  178.8 13.3 %collective-permute-start.29 = (bf16[64,2048]{1,0:T(8,128)(2,1)S(1)}, bf16[64,2048]{1,0:T(8,128)(2,1)S(1)}, u32[]{:S(2)}, u32[]{:S(2)}) collective-permute-start(bf16[64,2048]{1,0:T(8,128)(2,1)S(1)} %get-tuple-element.157), channel_id=1, source_target_pairs={{0,16},{16,0},{1,17},{17,1},{2,18},{18,2},{3,19},{19,3},{4,20},{20... | collective-permute-start | bytes 786440 | tf_op jit(solution)/shard_map/ppermute | solution.py:136
  179.7 16.5 %collective-permute-start.30 = (bf16[64,2048]{1,0:T(8,128)(2,1)S(1)}, bf16[64,2048]{1,0:T(8,128)(2,1)S(1)}, u32[]{:S(2)}, u32[]{:S(2)}) collective-permute-start(bf16[64,2048]{1,0:T(8,128)(2,1)S(1)} %slice.148), channel_id=1, source_target_pairs={{0,16},{16,0},{1,17},{17,1},{2,18},{18,2},{3,19},{19,3},{4,20},{20... | collective-permute-start | bytes 786440 | tf_op jit(solution)/shard_map/ppermute | solution.py:136
  185.1 12.1 %collective-permute-start.31 = (bf16[64,2048]{1,0:T(8,128)(2,1)S(1)}, bf16[64,2048]{1,0:T(8,128)(2,1)S(1)}, u32[]{:S(2)}, u32[]{:S(2)}) collective-permute-start(bf16[64,2048]{1,0:T(8,128)(2,1)S(1)} %slice.147), channel_id=1, source_target_pairs={{2,0},{3,1},{0,2},{1,3},{6,4},{7,5},{4,6},{5,7},{10,8},{11,9},{8,1... | collective-permute-start | bytes 786440 | tf_op jit(solution)/shard_map/ppermute | solution.py:122
  187.4 12.1 %collective-permute-start.37 = (bf16[32,2048]{1,0:T(8,128)(2,1)S(1)}, bf16[32,2048]{1,0:T(8,128)(2,1)S(1)}, u32[]{:S(2)}, u32[]{:S(2)}) collective-permute-start(bf16[32,2048]{1,0:T(8,128)(2,1)S(1)} %get-tuple-element.154), channel_id=1, source_target_pairs={{12,0},{13,1},{14,2},{15,3},{0,4},{1,5},{2,6},{3,7},{4,8},{5,9},{6... | collective-permute-start | bytes 393224 | tf_op jit(solution)/shard_map/ppermute | solution.py:112
  206.4 11.8 %collective-permute-start.41 = (bf16[32,2048]{1,0:T(8,128)(2,1)S(1)}, bf16[32,2048]{1,0:T(8,128)(2,1)S(1)}, u32[]{:S(2)}, u32[]{:S(2)}) collective-permute-start(bf16[32,2048]{1,0:T(8,128)(2,1)S(1)} %get-tuple-element.153), channel_id=1, source_target_pairs={{8,0},{9,1},{10,2},{11,3},{12,4},{13,5},{14,6},{15,7},{0,8},{1,9},... | collective-permute-start | bytes 393224 | tf_op jit(solution)/shard_map/ppermute | solution.py:112
  206.4 11.7 %collective-permute-start.42 = (bf16[32,2048]{1,0:T(8,128)(2,1)S(1)}, bf16[32,2048]{1,0:T(8,128)(2,1)S(1)}, u32[]{:S(2)}, u32[]{:S(2)}) collective-permute-start(bf16[32,2048]{1,0:T(8,128)(2,1)S(1)} %get-tuple-element.152), channel_id=1, source_target_pairs={{4,0},{5,1},{6,2},{7,3},{8,4},{9,5},{10,6},{11,7},{12,8},{13,9},{1... | collective-permute-start | bytes 393224 | tf_op jit(solution)/shard_map/ppermute | solution.py:112
  (26 other events, 231.9 us)

commit v9 on v7

--- a/solution.py
+++ b/solution.py
@@ -395,12 +395,6 @@
     shares = share[...].reshape(total_rows, 128).astype(jnp.float32)
     lane = lax.broadcasted_iota(jnp.int32, (total_rows, 128), 1)
     experts = lax.axis_size("expert")
-
-    def activate(t, g, u, scale):
-        h = g / (1.0 + jnp.exp(-g)) * u * scale
-        mid[:, pl.ds(t * tile, tile)] = h.astype(mid.dtype)
-
-    pending = None
     for t in range(2 * tiles):
         e, j = t // tiles, t % tiles
         if j == 0:
@@ -412,12 +406,10 @@
         values = rows[...].reshape(total_rows, feats)
         g = jnp.dot(values, gate[t % SLOTS], preferred_element_type=jnp.float32)
         u = jnp.dot(values, up[t % SLOTS], preferred_element_type=jnp.float32)
-        if pending is not None:
-            activate(*pending)
-        pending = (t, g, u, scale)
+        h = g / (1.0 + jnp.exp(-g)) * u * scale
+        mid[:, pl.ds(t * tile, tile)] = h.astype(mid.dtype)
         if t + SLOTS < 2 * tiles:
             weight_copies.append(fetch(t + SLOTS))
-    activate(*pending)
     for copy in down_copies:
         copy.wait()
     for n in range(feats // out_tile):

time: 209 us -> 208 us (level)
  no operation moved by 1% of the time
where the time goes in v9:
time: 208 us
  waiting for transfers between devices  107 us (51%)
  starting transfers between devices  52.2 us (25%)
  Pallas kernels  39.3 us (19%)
  local copies, waits for them, and re-layouts  6.57 us (3%)
  other arithmetic  3.04 us (1%)
    ppermute x12, waiting for transfers between devices, shift_z(): return lax.ppermute(values, 'expert', pairs)  40.4 us
    ppermute x12, waiting for transfers between devices, flip_x(): return lax.ppermute(values, 'dp', [(0, 1), (1, 0)])  34.4 us
    ppermute x12, waiting for transfers between devices, flip_y(): return lax.ppermute(values, 'expert', pairs)  31.7 us
    pallas_call x2, Pallas kernels, run_experts(): pl.pallas_call(functools.partial(experts_kernel, tile, 512, first_row, co...  27.5 us
    ppermute x12, starting transfers between devices, shift_z(): return lax.ppermute(values, 'expert', pairs)  19.2 us
    ppermute x12, starting transfers between devices, flip_y(): return lax.ppermute(values, 'expert', pairs)  16 us
    ppermute x12, starting transfers between devices, flip_x(): return lax.ppermute(values, 'dp', [(0, 1), (1, 0)])  15.2 us
    pallas_call x1, Pallas kernels, attend_here(): pl.pallas_call(attend_kernel, out_shape=jax.ShapeDtypeStruct(queries.shap...  5.81 us
  transfers between devices with their start and end apart: 45, of which 23 were waited for; matrix products, arithmetic and copies ran while one was open for 1% of the time, Pallas kernels for 17%

profile of v9, /device:TPU:0, one launch (start us, length us, event | category | flops | bytes accessed | tf_op | source)
XLA Modules:
  0.0 208.0 jit_solution(12364186877141782571)
XLA Ops:
  0.0 1.8 copy-done
  1.8 1.7 cut.2
  3.6 3.0 %collective-permute-start.5 = (bf16[768,768]{1,0:T(8,128)(2,1)}, bf16[768,768]{1,0:T(8,128)(2,1)}, u32[]{:S(2)}, u32[]{:S(2)}) collective-permute-start(bf16[768,768]{1,0:T(8,128)(2,1)} %get-tuple-element.83), channel_id=1, source_target_pairs={{0,16},{16,0},{1,17},{17,1},{2,18},{18,2},{3,19},{19,3},{4,20},{20... | collective-permute-start | bytes 3538952 | tf_op jit(solution)/shard_map/ppermute | solution.py:136
  6.6 3.6 %collective-permute-start = (bf16[1024,128]{1,0:T(8,128)(2,1)}, bf16[1024,128]{1,0:T(8,128)(2,1)}, u32[]{:S(2)}, u32[]{:S(2)}) collective-permute-start(bf16[1024,128]{1,0:T(8,128)(2,1)} %refs_0_.1), channel_id=1, source_target_pairs={{4,0},{5,1},{6,2},{7,3},{8,4},{9,5},{10,6},{11,7},{12,8},{13,9},{1... | collective-permute-start | bytes 786440 | tf_op jit(solution)/shard_map/ppermute | solution.py:112
  12.7 4.6 %collective-permute-done.refs_1_ = bf16[1024,128]{1,0:T(8,128)(2,1)} collective-permute-done((bf16[1024,128]{1,0:T(8,128)(2,1)}, bf16[1024,128]{1,0:T(8,128)(2,1)}, u32[]{:S(2)}, u32[]{:S(2)}) %collective-permute-start) | collective-permute-done | bytes 262176 | tf_op jit(solution)/shard_map/ppermute | solution.py:112
  19.6 1.6 copy-done.2
  22.9 5.8 %attend.1.ctx_ref = bf16[128,1024]{1,0:T(8,128)(2,1)S(1)} custom-call(s32[2,4]{1,0:T(2,128)S(1)} %copy-done.8, s32[128,1]{1,0:T(8,128)S(1)} %copy-done.6, bf16[128,1024]{1,0:T(8,128)(2,1)S(1)} %copy-done.3, bf16[2,8,64,1024]{3,2,1,0:T(8,128)(2,1)S(1)} %copy-done.2), custom_call_target="tpu_custom_call" | custom-call | flops 134217728 | bytes 2621440 | tf_op jit(solution)/shard_map/attend/pallas_call | solution.py:182
  33.4 1.8 collective-permute-start.7
  36.6 5.7 %collective-permute-done.7.refs_6_ = bf16[1024,128]{1,0:T(8,128)(2,1)S(1)} collective-permute-done((bf16[1024,128]{1,0:T(8,128)(2,1)}, bf16[1024,128]{1,0:T(8,128)(2,1)S(1)}, u32[]{:S(2)}, u32[]{:S(2)}) %collective-permute-start.7) | collective-permute-done | bytes 262176 | tf_op jit(solution)/shard_map/ppermute | solution.py:122
  42.3 1.7 collective-permute-start.8
  44.3 6.3 %collective-permute-done.8.refs_7_ = bf16[1024,128]{1,0:T(8,128)(2,1)S(1)} collective-permute-done((bf16[1024,128]{1,0:T(8,128)(2,1)}, bf16[1024,128]{1,0:T(8,128)(2,1)S(1)}, u32[]{:S(2)}, u32[]{:S(2)}) %collective-permute-start.8) | collective-permute-done | bytes 262176 | tf_op jit(solution)/shard_map/ppermute | solution.py:122
  50.8 3.3 %collective-permute-done.12.refs_7_ = bf16[480,768]{1,0:T(8,128)(2,1)} collective-permute-done((bf16[480,768]{1,0:T(8,128)(2,1)}, bf16[480,768]{1,0:T(8,128)(2,1)}, u32[]{:S(2)}, u32[]{:S(2)}) %collective-permute-start.12) | collective-permute-done | bytes 737312 | tf_op jit(solution)/shard_map/ppermute | solution.py:136
  54.1 2.5 %project.1 = (f32[128,1024]{1,0:T(8,128)S(1)}, bf16[128,1024]{1,0:T(8,128)(2,1)S(1)}) custom-call(bf16[128,1024]{1,0:T(8,128)(2,1)S(1)} %attend.1.ctx_ref, bf16[128,1024]{1,0:T(8,128)(2,1)S(1)} %collective-permute-done.6.other_ref, bf16[1024,128]{1,0:T(8,128)(2,1)S(1)} %copy-done.4, bf16[1024,128]{1,0:T(8,128)(2,1)} %collective-permute-done.refs_1_, ...), custom_call_target="tpu_custom_call" | custom-call | flops 536870912 | bytes 2883584 | tf_op jit(solution)/shard_map/project/pallas_call | solution.py:224
  58.2 6.1 %collective-permute-done.13 = bf16[128,1024]{1,0:T(8,128)(2,1)S(1)} collective-permute-done((bf16[128,1024]{1,0:T(8,128)(2,1)S(1)}, bf16[128,1024]{1,0:T(8,128)(2,1)S(1)}, u32[]{:S(2)}, u32[]{:S(2)}) %collective-permute-start.13) | collective-permute-done | bytes 262176 | tf_op jit(solution)/shard_map/ppermute | solution.py:136
  66.4 3.7 %collective-permute-start.15 = (bf16[64,2176]{1,0:T(8,128)(2,1)S(1)}, bf16[64,2176]{1,0:T(8,128)(2,1)S(1)}, u32[]{:S(2)}, u32[]{:S(2)}) collective-permute-start(bf16[64,2176]{1,0:T(8,128)(2,1)S(1)} %get-tuple-element.115), channel_id=1, source_target_pairs={{4,0},{5,1},{6,2},{7,3},{8,4},{9,5},{10,6},{11,7},{12,8},{13,9},{1... | collective-permute-start | bytes 835592 | tf_op jit(solution)/shard_map/ppermute | solution.py:112
  70.1 6.5 %collective-permute-start.16 = (bf16[64,2176]{1,0:T(8,128)(2,1)S(1)}, bf16[64,2176]{1,0:T(8,128)(2,1)S(1)}, u32[]{:S(2)}, u32[]{:S(2)}) collective-permute-start(bf16[64,2176]{1,0:T(8,128)(2,1)S(1)} %get-tuple-element.115), channel_id=1, source_target_pairs={{8,0},{9,1},{10,2},{11,3},{12,4},{13,5},{14,6},{15,7},{0,8},{1,9},... | collective-permute-start | bytes 835592 | tf_op jit(solution)/shard_map/ppermute | solution.py:112
  76.6 5.5 %collective-permute-done.15 = bf16[64,2176]{1,0:T(8,128)(2,1)S(1)} collective-permute-done((bf16[64,2176]{1,0:T(8,128)(2,1)S(1)}, bf16[64,2176]{1,0:T(8,128)(2,1)S(1)}, u32[]{:S(2)}, u32[]{:S(2)}) %collective-permute-start.15) | collective-permute-done | bytes 278560 | tf_op jit(solution)/shard_map/ppermute | solution.py:112
  82.1 19.1 %collective-permute-done.16 = bf16[64,2176]{1,0:T(8,128)(2,1)S(1)} collective-permute-done((bf16[64,2176]{1,0:T(8,128)(2,1)S(1)}, bf16[64,2176]{1,0:T(8,128)(2,1)S(1)}, u32[]{:S(2)}, u32[]{:S(2)}) %collective-permute-start.16) | collective-permute-done | bytes 278560 | tf_op jit(solution)/shard_map/ppermute | solution.py:112
  103.5 11.7 %collective-permute-done.18.refs_1_ = bf16[4,32,2176]{2,1,0:T(8,128)(2,1)S(1)} collective-permute-done((bf16[4,32,2176]{2,1,0:T(8,128)(2,1)S(1)}, bf16[4,32,2176]{2,1,0:T(8,128)(2,1)S(1)}, u32[]{:S(2)}, u32[]{:S(2)}) %collective-permute-start.18) | collective-permute-done | bytes 557088 | tf_op jit(solution)/shard_map/ppermute | solution.py:136
  116.1 1.6 collective-permute-start.21
  119.3 6.0 %collective-permute-done.21.refs_3_ = bf16[2,32,2176]{2,1,0:T(8,128)(2,1)S(1)} collective-permute-done((bf16[2,32,2176]{2,1,0:T(8,128)(2,1)S(1)}, bf16[2,32,2176]{2,1,0:T(8,128)(2,1)S(1)}, u32[]{:S(2)}, u32[]{:S(2)}) %collective-permute-start.21) | collective-permute-done | bytes 278560 | tf_op jit(solution)/shard_map/ppermute | solution.py:122
  128.5 13.8 %experts.2 = (f32[128,2048]{1,0:T(8,128)S(1)}, bf16[128,2048]{1,0:T(8,128)(2,1)S(1)}, bf16[128,2048]{1,0:T(8,128)(2,1)S(1)}, bf16[64,2048]{1,0:T(8,128)(2,1)S(1)}, bf16[64,2048]{1,0:T(8,128)(2,1)S(1)}) custom-call(bf16[4,32,2176]{2,1,0:T(8,128)(2,1)S(1)} %pad_maximum_fusion.2.refs_0_, bf16[4,32,2176]{2,1,0:T(8,128)(2,1)S(1)} %collective-permute-done.18.refs_1_, ...), custom_call_target="tpu_custom_call" | custom-call | flops 9663676416 | bytes 31457280 | tf_op jit(solution)/shard_map/experts/pallas_call | solution.py:431
  144.6 5.2 %collective-permute-done.28.refs_3_ = bf16[2,32,2176]{2,1,0:T(8,128)(2,1)S(1)} collective-permute-done((bf16[2,32,2176]{2,1,0:T(8,128)(2,1)S(1)}, bf16[2,32,2176]{2,1,0:T(8,128)(2,1)S(1)}, u32[]{:S(2)}, u32[]{:S(2)}) %collective-permute-start.28) | collective-permute-done | bytes 278560 | tf_op jit(solution)/shard_map/ppermute | solution.py:122
  154.7 13.8 %experts.3 = (f32[128,2048]{1,0:T(8,128)S(1)}, f32[128,2048]{1,0:T(8,128)S(1)}, f32[128,2048]{1,0:T(8,128)S(1)}, bf16[64,2048]{1,0:T(8,128)(2,1)S(1)}, bf16[64,2048]{1,0:T(8,128)(2,1)S(1)}) custom-call(bf16[4,32,2176]{2,1,0:T(8,128)(2,1)S(1)} %pad_maximum_fusion.1.refs_0_, bf16[4,32,2176]{2,1,0:T(8,128)(2,1)S(1)} %collective-permute-done.23.refs_1_, ...), custom_call_target="tpu_custom_call" | custom-call | flops 9663676416 | bytes 31457280 | tf_op jit(solution)/shard_map/experts/pallas_call | solution.py:431
  171.4 5.9 %collective-permute-done.34 = bf16[128,2048]{1,0:T(8,128)(2,1)S(1)} collective-permute-done((bf16[128,2048]{1,0:T(8,128)(2,1)S(1)}, bf16[128,2048]{1,0:T(8,128)(2,1)S(1)}, u32[]{:S(2)}, u32[]{:S(2)}) %collective-permute-start.34) | collective-permute-done | bytes 524320 | tf_op jit(solution)/shard_map/ppermute | solution.py:136
  178.3 4.0 %collective-permute-done.32 = bf16[64,2048]{1,0:T(8,128)(2,1)S(1)} collective-permute-done((bf16[64,2048]{1,0:T(8,128)(2,1)S(1)}, bf16[64,2048]{1,0:T(8,128)(2,1)S(1)}, u32[]{:S(2)}, u32[]{:S(2)}) %collective-permute-start.32) | collective-permute-done | bytes 262176 | tf_op jit(solution)/shard_map/ppermute | solution.py:136
  182.8 3.3 %collective-permute-done.30 = bf16[64,2048]{1,0:T(8,128)(2,1)S(1)} collective-permute-done((bf16[64,2048]{1,0:T(8,128)(2,1)S(1)}, bf16[64,2048]{1,0:T(8,128)(2,1)S(1)}, u32[]{:S(2)}, u32[]{:S(2)}) %collective-permute-start.30) | collective-permute-done | bytes 262176 | tf_op jit(solution)/shard_map/ppermute | solution.py:122
  187.6 1.9 collective-permute-done.40
  189.6 4.9 %collective-permute-done.38 = bf16[64,2048]{1,0:T(8,128)(2,1)S(1)} collective-permute-done((bf16[64,2048]{1,0:T(8,128)(2,1)S(1)}, bf16[64,2048]{1,0:T(8,128)(2,1)S(1)}, u32[]{:S(2)}, u32[]{:S(2)}) %collective-permute-start.38) | collective-permute-done | bytes 262176 | tf_op jit(solution)/shard_map/ppermute | solution.py:122
  195.8 3.2 %collective-permute-start.44 = (bf16[32,2048]{1,0:T(8,128)(2,1)S(1)}, bf16[32,2048]{1,0:T(8,128)(2,1)S(1)}, u32[]{:S(2)}, u32[]{:S(2)}) collective-permute-start(bf16[32,2048]{1,0:T(8,128)(2,1)S(1)} %get-tuple-element.164), channel_id=1, source_target_pairs={{4,0},{5,1},{6,2},{7,3},{8,4},{9,5},{10,6},{11,7},{12,8},{13,9},{1... | collective-permute-start | bytes 393224 | tf_op jit(solution)/shard_map/ppermute | solution.py:112
  199.0 4.5 %collective-permute-done.42 = bf16[32,2048]{1,0:T(8,128)(2,1)S(1)} collective-permute-done((bf16[32,2048]{1,0:T(8,128)(2,1)S(1)}, bf16[32,2048]{1,0:T(8,128)(2,1)S(1)}, u32[]{:S(2)}, u32[]{:S(2)}) %collective-permute-start.42) | collective-permute-done | bytes 131104 | tf_op jit(solution)/shard_map/ppermute | solution.py:112
  203.4 3.6 %collective-permute-done.43 = bf16[32,2048]{1,0:T(8,128)(2,1)S(1)} collective-permute-done((bf16[32,2048]{1,0:T(8,128)(2,1)S(1)}, bf16[32,2048]{1,0:T(8,128)(2,1)S(1)}, u32[]{:S(2)}, u32[]{:S(2)}) %collective-permute-start.43) | collective-permute-done | bytes 131104 | tf_op jit(solution)/shard_map/ppermute | solution.py:112
  (132 shorter events, 40.1 us)
Async XLA Ops:
  3.6 29.3 %collective-permute-start.5 = (bf16[768,768]{1,0:T(8,128)(2,1)}, bf16[768,768]{1,0:T(8,128)(2,1)}, u32[]{:S(2)}, u32[]{:S(2)}) collective-permute-start(bf16[768,768]{1,0:T(8,128)(2,1)} %get-tuple-element.83), channel_id=1, source_target_pairs={{0,16},{16,0},{1,17},{17,1},{2,18},{18,2},{3,19},{19,3},{4,20},{20... | collective-permute-start | bytes 3538952 | tf_op jit(solution)/shard_map/ppermute | solution.py:136
  6.6 10.7 %collective-permute-start = (bf16[1024,128]{1,0:T(8,128)(2,1)}, bf16[1024,128]{1,0:T(8,128)(2,1)}, u32[]{:S(2)}, u32[]{:S(2)}) collective-permute-start(bf16[1024,128]{1,0:T(8,128)(2,1)} %refs_0_.1), channel_id=1, source_target_pairs={{4,0},{5,1},{6,2},{7,3},{8,4},{9,5},{10,6},{11,7},{12,8},{13,9},{1... | collective-permute-start | bytes 786440 | tf_op jit(solution)/shard_map/ppermute | solution.py:112
  10.2 22.3 %collective-permute-start.1 = (bf16[1024,128]{1,0:T(8,128)(2,1)}, bf16[1024,128]{1,0:T(8,128)(2,1)}, u32[]{:S(2)}, u32[]{:S(2)}) collective-permute-start(bf16[1024,128]{1,0:T(8,128)(2,1)} %refs_0_.1), channel_id=1, source_target_pairs={{8,0},{9,1},{10,2},{11,3},{12,4},{13,5},{14,6},{15,7},{0,8},{1,9},... | collective-permute-start | bytes 786440 | tf_op jit(solution)/shard_map/ppermute | solution.py:112
  10.2 22.3 %collective-permute-start.2 = (bf16[1024,128]{1,0:T(8,128)(2,1)}, bf16[1024,128]{1,0:T(8,128)(2,1)}, u32[]{:S(2)}, u32[]{:S(2)}) collective-permute-start(bf16[1024,128]{1,0:T(8,128)(2,1)} %refs_0_.1), channel_id=1, source_target_pairs={{12,0},{13,1},{14,2},{15,3},{0,4},{1,5},{2,6},{3,7},{4,8},{5,9},{6... | collective-permute-start | bytes 786440 | tf_op jit(solution)/shard_map/ppermute | solution.py:112
  11.2 21.3 %collective-permute-start.3 = (bf16[1024,128]{1,0:T(8,128)(2,1)}, bf16[1024,128]{1,0:T(8,128)(2,1)}, u32[]{:S(2)}, u32[]{:S(2)}) collective-permute-start(bf16[1024,128]{1,0:T(8,128)(2,1)} %refs_0_.1), channel_id=1, source_target_pairs={{2,0},{3,1},{0,2},{1,3},{6,4},{7,5},{4,6},{5,7},{10,8},{11,9},{8,1... | collective-permute-start | bytes 786440 | tf_op jit(solution)/shard_map/ppermute | solution.py:122
  17.3 15.2 %collective-permute-start.4 = (bf16[1024,128]{1,0:T(8,128)(2,1)}, bf16[1024,128]{1,0:T(8,128)(2,1)}, u32[]{:S(2)}, u32[]{:S(2)}) collective-permute-start(bf16[1024,128]{1,0:T(8,128)(2,1)} %collective-permute-done.refs_1_), channel_id=1, source_target_pairs={{2,0},{3,1},{0,2},{1,3},{6,4},{7,5},{4,6},{5,7},{10,8},{11,9},{8,1... | collective-permute-start | bytes 786440 | tf_op jit(solution)/shard_map/ppermute | solution.py:122
  32.9 21.2 %collective-permute-start.11 = (bf16[704,2048]{1,0:T(8,128)(2,1)}, bf16[704,2048]{1,0:T(8,128)(2,1)}, u32[]{:S(2)}, u32[]{:S(2)}) collective-permute-start(bf16[704,2048]{1,0:T(8,128)(2,1)} %bitcast.1.refs_10_), channel_id=1, source_target_pairs={{1,0},{0,1},{3,2},{2,3},{5,4},{4,5},{7,6},{6,7},{9,8},{8,9},{11,10... | collective-permute-start | bytes 8650760 | tf_op jit(solution)/shard_map/ppermute | solution.py:132
  32.9 21.2 %collective-permute-start.10 = (bf16[1024,768]{1,0:T(8,128)(2,1)}, bf16[1024,768]{1,0:T(8,128)(2,1)S(1)}, u32[]{:S(2)}, u32[]{:S(2)}) collective-permute-start(bf16[1024,768]{1,0:T(8,128)(2,1)} %get-tuple-element.102.refs_8_), channel_id=1, source_target_pairs={{1,0},{0,1},{3,2},{2,3},{5,4},{4,5},{7,6},{6,7},{9,8},{8,9},{11,10... | collective-permute-start | bytes 4718600 | tf_op jit(solution)/shard_map/ppermute | solution.py:132
  33.4 20.7 %collective-permute-start.9 = (bf16[1024,768]{1,0:T(8,128)(2,1)}, bf16[1024,768]{1,0:T(8,128)(2,1)}, u32[]{:S(2)}, u32[]{:S(2)}) collective-permute-start(bf16[1024,768]{1,0:T(8,128)(2,1)} %get-tuple-element.101.refs_5_), channel_id=1, source_target_pairs={{1,0},{0,1},{3,2},{2,3},{5,4},{4,5},{7,6},{6,7},{9,8},{8,9},{11,10... | collective-permute-start | bytes 4718600 | tf_op jit(solution)/shard_map/ppermute | solution.py:132
  33.4 9.0 %collective-permute-start.7 = (bf16[1024,128]{1,0:T(8,128)(2,1)}, bf16[1024,128]{1,0:T(8,128)(2,1)S(1)}, u32[]{:S(2)}, u32[]{:S(2)}) collective-permute-start(bf16[1024,128]{1,0:T(8,128)(2,1)} %collective-permute-done.1.refs_2_), channel_id=1, source_target_pairs={{2,0},{3,1},{0,2},{1,3},{6,4},{7,5},{4,6},{5,7},{10,8},{11,9},{8,1... | collective-permute-start | bytes 786440 | tf_op jit(solution)/shard_map/ppermute | solution.py:122
  35.1 18.9 %collective-permute-start.12 = (bf16[480,768]{1,0:T(8,128)(2,1)}, bf16[480,768]{1,0:T(8,128)(2,1)}, u32[]{:S(2)}, u32[]{:S(2)}) collective-permute-start(bf16[480,768]{1,0:T(8,128)(2,1)} %pad_maximum_fusion), channel_id=1, source_target_pairs={{0,16},{16,0},{1,17},{17,1},{2,18},{18,2},{3,19},{19,3},{4,20},{20... | collective-permute-start | bytes 2211848 | tf_op jit(solution)/shard_map/ppermute | solution.py:136
  64.6 51.0 %collective-permute-start.20 = (bf16[800,768]{1,0:T(8,128)(2,1)S(1)}, bf16[800,768]{1,0:T(8,128)(2,1)S(1)}, u32[]{:S(2)}, u32[]{:S(2)}) collective-permute-start(bf16[800,768]{1,0:T(8,128)(2,1)S(1)} %copy-done.10), channel_id=1, source_target_pairs={{0,16},{16,0},{1,17},{17,1},{2,18},{18,2},{3,19},{19,3},{4,20},{20... | collective-permute-start | bytes 3686408 | tf_op jit(solution)/shard_map/ppermute | solution.py:136
  66.4 15.7 %collective-permute-start.15 = (bf16[64,2176]{1,0:T(8,128)(2,1)S(1)}, bf16[64,2176]{1,0:T(8,128)(2,1)S(1)}, u32[]{:S(2)}, u32[]{:S(2)}) collective-permute-start(bf16[64,2176]{1,0:T(8,128)(2,1)S(1)} %get-tuple-element.115), channel_id=1, source_target_pairs={{4,0},{5,1},{6,2},{7,3},{8,4},{9,5},{10,6},{11,7},{12,8},{13,9},{1... | collective-permute-start | bytes 835592 | tf_op jit(solution)/shard_map/ppermute | solution.py:112
  70.1 31.1 %collective-permute-start.16 = (bf16[64,2176]{1,0:T(8,128)(2,1)S(1)}, bf16[64,2176]{1,0:T(8,128)(2,1)S(1)}, u32[]{:S(2)}, u32[]{:S(2)}) collective-permute-start(bf16[64,2176]{1,0:T(8,128)(2,1)S(1)} %get-tuple-element.115), channel_id=1, source_target_pairs={{8,0},{9,1},{10,2},{11,3},{12,4},{13,5},{14,6},{15,7},{0,8},{1,9},... | collective-permute-start | bytes 835592 | tf_op jit(solution)/shard_map/ppermute | solution.py:112
  76.6 24.6 %collective-permute-start.17 = (bf16[64,2176]{1,0:T(8,128)(2,1)S(1)}, bf16[64,2176]{1,0:T(8,128)(2,1)S(1)}, u32[]{:S(2)}, u32[]{:S(2)}) collective-permute-start(bf16[64,2176]{1,0:T(8,128)(2,1)S(1)} %get-tuple-element.115), channel_id=1, source_target_pairs={{12,0},{13,1},{14,2},{15,3},{0,4},{1,5},{2,6},{3,7},{4,8},{5,9},{6... | collective-permute-start | bytes 835592 | tf_op jit(solution)/shard_map/ppermute | solution.py:112
  101.3 13.9 %collective-permute-start.18 = (bf16[4,32,2176]{2,1,0:T(8,128)(2,1)S(1)}, bf16[4,32,2176]{2,1,0:T(8,128)(2,1)S(1)}, u32[]{:S(2)}, u32[]{:S(2)}) collective-permute-start(bf16[4,32,2176]{2,1,0:T(8,128)(2,1)S(1)} %pad_maximum_fusion.2.refs_0_), channel_id=1, source_target_pairs={{0,16},{16,0},{1,17},{17,1},{2,18},{18,2},{3,19},{19,3},{4,20},{20... | collective-permute-start | bytes 1671176 | tf_op jit(solution)/shard_map/ppermute | solution.py:136
  102.0 13.6 %collective-permute-start.19 = (bf16[4,32,2176]{2,1,0:T(8,128)(2,1)S(1)}, bf16[4,32,2176]{2,1,0:T(8,128)(2,1)S(1)}, u32[]{:S(2)}, u32[]{:S(2)}) collective-permute-start(bf16[4,32,2176]{2,1,0:T(8,128)(2,1)S(1)} %pad_maximum_fusion.2.refs_0_), channel_id=1, source_target_pairs={{2,0},{3,1},{0,2},{1,3},{6,4},{7,5},{4,6},{5,7},{10,8},{11,9},{8,1... | collective-permute-start | bytes 1671176 | tf_op jit(solution)/shard_map/ppermute | solution.py:122
  115.6 12.9 %collective-permute-start.27 = (bf16[800,768]{1,0:T(8,128)(2,1)S(1)}, bf16[800,768]{1,0:T(8,128)(2,1)S(1)}, u32[]{:S(2)}, u32[]{:S(2)}) collective-permute-start(bf16[800,768]{1,0:T(8,128)(2,1)S(1)} %collective-permute-done.20.refs_9_), channel_id=1, source_target_pairs={{1,0},{0,1},{3,2},{2,3},{5,4},{4,5},{7,6},{6,7},{9,8},{8,9},{11,10... | collective-permute-start | bytes 3686408 | tf_op jit(solution)/shard_map/ppermute | solution.py:132
  115.6 12.9 %collective-permute-start.25 = (bf16[768,768]{1,0:T(8,128)(2,1)}, bf16[768,768]{1,0:T(8,128)(2,1)S(1)}, u32[]{:S(2)}, u32[]{:S(2)}) collective-permute-start(bf16[768,768]{1,0:T(8,128)(2,1)} %collective-permute-done.5.refs_6_), channel_id=1, source_target_pairs={{1,0},{0,1},{3,2},{2,3},{5,4},{4,5},{7,6},{6,7},{9,8},{8,9},{11,10... | collective-permute-start | bytes 3538952 | tf_op jit(solution)/shard_map/ppermute | solution.py:132
  116.1 12.4 %collective-permute-start.26 = (bf16[480,768]{1,0:T(8,128)(2,1)}, bf16[480,768]{1,0:T(8,128)(2,1)S(1)}, u32[]{:S(2)}, u32[]{:S(2)}) collective-permute-start(bf16[480,768]{1,0:T(8,128)(2,1)} %collective-permute-done.12.refs_7_), channel_id=1, source_target_pairs={{1,0},{0,1},{3,2},{2,3},{5,4},{4,5},{7,6},{6,7},{9,8},{8,9},{11,10... | collective-permute-start | bytes 2211848 | tf_op jit(solution)/shard_map/ppermute | solution.py:132
  116.1 9.1 %collective-permute-start.21 = (bf16[2,32,2176]{2,1,0:T(8,128)(2,1)S(1)}, bf16[2,32,2176]{2,1,0:T(8,128)(2,1)S(1)}, u32[]{:S(2)}, u32[]{:S(2)}) collective-permute-start(bf16[2,32,2176]{2,1,0:T(8,128)(2,1)S(1)} %slice.104), channel_id=1, source_target_pairs={{2,0},{3,1},{0,2},{1,3},{6,4},{7,5},{4,6},{5,7},{10,8},{11,9},{8,1... | collective-permute-start | bytes 835592 | tf_op jit(solution)/shard_map/ppermute | solution.py:122
  126.6 15.7 %collective-permute-start.23 = (bf16[4,32,2176]{2,1,0:T(8,128)(2,1)S(1)}, bf16[4,32,2176]{2,1,0:T(8,128)(2,1)S(1)}, u32[]{:S(2)}, u32[]{:S(2)}) collective-permute-start(bf16[4,32,2176]{2,1,0:T(8,128)(2,1)S(1)} %pad_maximum_fusion.1.refs_0_), channel_id=1, source_target_pairs={{0,16},{16,0},{1,17},{17,1},{2,18},{18,2},{3,19},{19,3},{4,20},{20... | collective-permute-start | bytes 1671176 | tf_op jit(solution)/shard_map/ppermute | solution.py:136
  128.0 14.3 %collective-permute-start.24 = (bf16[4,32,2176]{2,1,0:T(8,128)(2,1)S(1)}, bf16[4,32,2176]{2,1,0:T(8,128)(2,1)S(1)}, u32[]{:S(2)}, u32[]{:S(2)}) collective-permute-start(bf16[4,32,2176]{2,1,0:T(8,128)(2,1)S(1)} %pad_maximum_fusion.1.refs_0_), channel_id=1, source_target_pairs={{2,0},{3,1},{0,2},{1,3},{6,4},{7,5},{4,6},{5,7},{10,8},{11,9},{8,1... | collective-permute-start | bytes 1671176 | tf_op jit(solution)/shard_map/ppermute | solution.py:122
  151.2 18.7 %collective-permute-start.36 = (bf16[128,2048]{1,0:T(8,128)(2,1)S(1)}, bf16[128,2048]{1,0:T(8,128)(2,1)S(1)}, u32[]{:S(2)}, u32[]{:S(2)}) collective-permute-start(bf16[128,2048]{1,0:T(8,128)(2,1)S(1)} %pad_maximum_fusion.3), channel_id=1, source_target_pairs={{18,0},{19,1},{16,2},{17,3},{22,4},{23,5},{20,6},{21,7},{26,8},{27... | collective-permute-start | bytes 1572872 | tf_op jit(solution)/shard_map/ppermute | solution.py:147
  151.8 25.5 %collective-permute-start.34 = (bf16[128,2048]{1,0:T(8,128)(2,1)S(1)}, bf16[128,2048]{1,0:T(8,128)(2,1)S(1)}, u32[]{:S(2)}, u32[]{:S(2)}) collective-permute-start(bf16[128,2048]{1,0:T(8,128)(2,1)S(1)} %get-tuple-element.151), channel_id=1, source_target_pairs={{0,16},{16,0},{1,17},{17,1},{2,18},{18,2},{3,19},{19,3},{4,20},{20... | collective-permute-start | bytes 1572872 | tf_op jit(solution)/shard_map/ppermute | solution.py:136
  153.2 24.7 %collective-permute-start.35 = (bf16[128,2048]{1,0:T(8,128)(2,1)S(1)}, bf16[128,2048]{1,0:T(8,128)(2,1)S(1)}, u32[]{:S(2)}, u32[]{:S(2)}) collective-permute-start(bf16[128,2048]{1,0:T(8,128)(2,1)S(1)} %get-tuple-element.152), channel_id=1, source_target_pairs={{2,0},{3,1},{0,2},{1,3},{6,4},{7,5},{4,6},{5,7},{10,8},{11,9},{8,1... | collective-permute-start | bytes 1572872 | tf_op jit(solution)/shard_map/ppermute | solution.py:122
  168.5 13.8 %collective-permute-start.32 = (bf16[64,2048]{1,0:T(8,128)(2,1)S(1)}, bf16[64,2048]{1,0:T(8,128)(2,1)S(1)}, u32[]{:S(2)}, u32[]{:S(2)}) collective-permute-start(bf16[64,2048]{1,0:T(8,128)(2,1)S(1)} %slice.156), channel_id=1, source_target_pairs={{0,16},{16,0},{1,17},{17,1},{2,18},{18,2},{3,19},{19,3},{4,20},{20... | collective-permute-start | bytes 786440 | tf_op jit(solution)/shard_map/ppermute | solution.py:136
  169.3 13.1 %collective-permute-start.33 = (bf16[64,2048]{1,0:T(8,128)(2,1)S(1)}, bf16[64,2048]{1,0:T(8,128)(2,1)S(1)}, u32[]{:S(2)}, u32[]{:S(2)}) collective-permute-start(bf16[64,2048]{1,0:T(8,128)(2,1)S(1)} %slice.155), channel_id=1, source_target_pairs={{2,0},{3,1},{0,2},{1,3},{6,4},{7,5},{4,6},{5,7},{10,8},{11,9},{8,1... | collective-permute-start | bytes 786440 | tf_op jit(solution)/shard_map/ppermute | solution.py:122
  169.9 16.2 %collective-permute-start.30 = (bf16[64,2048]{1,0:T(8,128)(2,1)S(1)}, bf16[64,2048]{1,0:T(8,128)(2,1)S(1)}, u32[]{:S(2)}, u32[]{:S(2)}) collective-permute-start(bf16[64,2048]{1,0:T(8,128)(2,1)S(1)} %get-tuple-element.147), channel_id=1, source_target_pairs={{2,0},{3,1},{0,2},{1,3},{6,4},{7,5},{4,6},{5,7},{10,8},{11,9},{8,1... | collective-permute-start | bytes 786440 | tf_op jit(solution)/shard_map/ppermute | solution.py:122
  178.3 9.3 %collective-permute-start.39 = (bf16[32,2048]{1,0:T(8,128)(2,1)S(1)}, bf16[32,2048]{1,0:T(8,128)(2,1)S(1)}, u32[]{:S(2)}, u32[]{:S(2)}) collective-permute-start(bf16[32,2048]{1,0:T(8,128)(2,1)S(1)} %get-tuple-element.166), channel_id=1, source_target_pairs={{12,0},{13,1},{14,2},{15,3},{0,4},{1,5},{2,6},{3,7},{4,8},{5,9},{6... | collective-permute-start | bytes 393224 | tf_op jit(solution)/shard_map/ppermute | solution.py:112
  195.1 11.8 %collective-permute-start.43 = (bf16[32,2048]{1,0:T(8,128)(2,1)S(1)}, bf16[32,2048]{1,0:T(8,128)(2,1)S(1)}, u32[]{:S(2)}, u32[]{:S(2)}) collective-permute-start(bf16[32,2048]{1,0:T(8,128)(2,1)S(1)} %get-tuple-element.165), channel_id=1, source_target_pairs={{8,0},{9,1},{10,2},{11,3},{12,4},{13,5},{14,6},{15,7},{0,8},{1,9},... | collective-permute-start | bytes 393224 | tf_op jit(solution)/shard_map/ppermute | solution.py:112
  195.8 11.2 %collective-permute-start.44 = (bf16[32,2048]{1,0:T(8,128)(2,1)S(1)}, bf16[32,2048]{1,0:T(8,128)(2,1)S(1)}, u32[]{:S(2)}, u32[]{:S(2)}) collective-permute-start(bf16[32,2048]{1,0:T(8,128)(2,1)S(1)} %get-tuple-element.164), channel_id=1, source_target_pairs={{4,0},{5,1},{6,2},{7,3},{8,4},{9,5},{10,6},{11,7},{12,8},{13,9},{1... | collective-permute-start | bytes 393224 | tf_op jit(solution)/shard_map/ppermute | solution.py:112
  (28 other events, 264.7 us)
